TPU v7x, 256 devices: a whole 4x4x8 slice. The times are simulated.
256 devices in a mesh: tm: 32 (over x, y, core), state: 8 (over z).
Axes of the slice: x: 4, y: 4, z: 8, core: 2. Of those that a mesh axis runs over, the one named last changes fastest.
Arguments:
- observations: float32 [128, 4096], P('tm'), may hold values from -6 to 6
- precisions: float32 [128, 4096], P('tm'), may hold values from 0.25 to 4
- blocks: bfloat16 [128, 256, 64, 64], P('tm', 'state'), may hold values from -0.09375 to 0.09375
- block_rows: int32 [128, 256], P('tm', 'state'), may hold values from 0 to 63
- block_cols: int32 [128, 256], P('tm', 'state'), may hold values from 0 to 15
- transition: bfloat16 [128, 1024, 1024], P('tm', 'state'), may hold values from -1 to 1
- prior: float32 [1024], replicated, may hold values from -8 to 8
Outputs:
- filtered: float32 [128, 1024], P('tm', 'state')
All inputs are finite; a program needn't handle non-finite values.
Results may differ from a plain program's by a relative error of at most 0.014.
Values may be sent and summed in bfloat16 or wider, within the bound.
No kernel may reach another device: no remote copies, remote signals or barrier semaphores. Data moves between devices by JAX's collectives and lax.ppermute only.
A program may use at most 64 MiB of HBM per device.

v0:
```python
import jax
import jax.numpy as jnp
from jax import lax
from jax.sharding import PartitionSpec as P


def passed_along(block, axis, distance):
    devices = range(lax.axis_size(axis))
    route = [(i - distance, i) for i in devices if i - distance in devices]
    return lax.ppermute(block, axis, route)


def matvec(matrix, vector):
    return jnp.sum(matrix.astype(jnp.float32) * vector[None, :], axis=1)


def shards(observations, precisions, blocks, block_rows, block_cols, transition, prior):
    steps_here = transition.shape[0]
    width = transition.shape[2]
    side = blocks.shape[2]
    weighted = (precisions * observations).astype(jnp.bfloat16)
    pieces = weighted.reshape(steps_here, weighted.shape[1] // side, side)
    selected_entry = jnp.take_along_axis(pieces, block_rows[:, :, None], axis=1)
    terms = jnp.einsum("tbi,tbij->tbj", selected_entry, blocks, preferred_element_type=jnp.float32)
    onehot = (
        block_cols[:, :, None] == jnp.arange(width // side, dtype=jnp.int32)[None, None, :]
    ).astype(jnp.float32)
    partial_drive = jnp.einsum("tbc,tbj->tcj", onehot, terms).reshape(steps_here, width)
    drive = lax.psum_scatter(partial_drive, "state", scatter_dimension=1, tiled=True)
    prod = transition[0]
    local = drive[0].astype(jnp.bfloat16)
    prods = [prod]
    locals_list = [local]
    for j in range(1, steps_here):
        matrix = transition[j]
        new_prod = jnp.dot(
            matrix,
            lax.all_gather(prod, "state", axis=0, tiled=True),
            preferred_element_type=jnp.float32,
        )
        fresh_segment_factor = jnp.dot(
            matrix,
            lax.all_gather(local, "state", axis=0, tiled=True),
            preferred_element_type=jnp.float32,
        )
        prod = new_prod.astype(jnp.bfloat16)
        local = (fresh_segment_factor + drive[j]).astype(jnp.bfloat16)
        prods.append(prod)
        locals_list.append(local)
    prod_stack = jnp.stack(prods)
    local_stack = jnp.stack(locals_list)
    position = lax.axis_index("tm")
    count = lax.axis_size("tm")
    summary, summary_term = (
        lax.all_gather(prod, "state", axis=0, tiled=True),
        lax.all_gather(local, "state", axis=0, tiled=True),
    )
    aggregate_increment = summary_term.astype(jnp.float32)

    def turn(step, carry):
        value, begin = carry
        incoming = passed_along(value, "tm", 1)
        begin = jnp.where(position == 0, prior, incoming)
        value = matvec(summary, begin) + aggregate_increment
        return (value, begin)

    zeros_full = jnp.zeros((width,), jnp.float32)
    _, start_full = lax.fori_loop(0, count, turn, (zeros_full, zeros_full))
    filtered = jnp.sum(prod_stack.astype(jnp.float32) * start_full[None, None, :], axis=2)
    return filtered + local_stack.astype(jnp.float32)


def solution(mesh):
    return jax.shard_map(
        shards,
        mesh=mesh,
        in_specs=(
            P("tm", None),
            P("tm", None),
            P("tm", "state", None, None),
            P("tm", "state"),
            P("tm", "state"),
            P("tm", "state", None),
            P(),
        ),
        out_specs=P("tm", "state"),
        check_vma=False,
    )
```

profile of v0, /device:TPU:34, one launch (start us, length us, event | category | flops | bytes accessed | tf_op | source)
XLA Modules:
  0.0 538.1 jit_solution(6457294126489116327)
XLA Ops:
  8.4 44.1 %all-gather.16.cloned.1.call-done = bf16[1,1024,1024]{2,1,0:T(8,128)(2,1)} async-done(((bf16[1,128,1024]{2,1,0:T(8,128)(2,1)}), bf16[1,1024,1024]{2,1,0:T(8,128)(2,1)}) %all-gather.16.cloned.1.call-update) | async-done | bytes 2097168 | tf_op jit(solution)/shard_map/all_gather | solution.py:38
  55.5 39.8 %all-gather.10.cloned.1.call-done = bf16[1024,1024]{1,0:T(8,128)(2,1)} async-done(((bf16[128,1024]{1,0:T(8,128)(2,1)}), bf16[1024,1024]{1,0:T(8,128)(2,1)}) %all-gather.10.cloned.1.call-update) | async-done | bytes 2097168 | tf_op jit(solution)/shard_map/all_gather | solution.py:38
  101.5 36.3 %all-gather.12.cloned.1.call-done = bf16[1024,1024]{1,0:T(8,128)(2,1)} async-done(((bf16[128,1024]{1,0:T(8,128)(2,1)}), bf16[1024,1024]{1,0:T(8,128)(2,1)}) %all-gather.12.cloned.1.call-update) | async-done | bytes 2097168 | tf_op jit(solution)/shard_map/all_gather | solution.py:38
  140.6 35.1 %reduce-scatter.4.cloned.1.call-done = f32[128,4]{1,0:T(8,128)} async-done(((f32[1024,4]{1,0:T(8,128)}), f32[128,4]{1,0:T(8,128)}) %reduce-scatter.4.cloned.1.call-update) | async-done | bytes 2064
  177.9 14.3 %all-gather.1 = bf16[1,1024]{1,0:T(2,128)(2,1)S(1)} all-gather(bf16[1,128]{1,0:T(2,128)(2,1)S(1)} %copy.21), channel_id=3, replica_groups=mesh['tm'=32,'state'=8] {'state'}, dimensions={1}, use_global_device_ids=true | all-gather | bytes 2304 | tf_op jit(solution)/shard_map/all_gather | solution.py:43
  192.3 14.6 %all-gather.2 = bf16[8,1,128]{2,1,0:T(2,128)(2,1)S(1)} all-gather(bf16[1,1,128]{2,1,0:T(2,128)(2,1)S(1)} %bitcast.95), channel_id=1, replica_groups=mesh['tm'=32,'state'=8] {'state'}, dimensions={0}, use_global_device_ids=true | all-gather | bytes 2304 | tf_op jit(solution)/shard_map/all_gather | solution.py:43
  207.1 13.8 %all-gather.3 = bf16[8,1,128]{2,1,0:T(2,128)(2,1)S(1)} all-gather(bf16[1,1,128]{2,1,0:T(2,128)(2,1)S(1)} %bitcast.97), channel_id=1, replica_groups=mesh['tm'=32,'state'=8] {'state'}, dimensions={0}, use_global_device_ids=true | all-gather | bytes 2304 | tf_op jit(solution)/shard_map/all_gather | solution.py:43
  221.1 15.3 %all-gather.4 = bf16[8,1,128]{2,1,0:T(2,128)(2,1)S(1)} all-gather(bf16[1,1,128]{2,1,0:T(2,128)(2,1)S(1)} %bitcast.99), channel_id=1, replica_groups=mesh['tm'=32,'state'=8] {'state'}, dimensions={0}, use_global_device_ids=true | all-gather | bytes 2304 | tf_op jit(solution)/shard_map/all_gather | solution.py:56
  236.5 293.5 %while.15 = (s32[]{:T(128)}, f32[1024]{0:T(1024)S(1)}, f32[1024]{0:T(1024)}, bf16[1024,1024]{1,0:T(8,128)(2,1)}, pred[]{:T(512)}, /*index=5*/f32[1024]{0:T(1024)S(1)}, f32[1024]{0:T(1024)S(1)}, s32[]{:T(128)}, s32[]{:T(128)}) while((s32[]{:T(128)}, f32[1024]{0:T(1024)S(1)}, f32[1024]{0:T(1024)}, bf16[1024,1024]{1,0:T(8,128)(2,1)}, ...), condition=%wide.region_3.4_spmd.clone, body=%wide.region_1.0_spmd.clone.sunk | while | flops 3147779 | bytes 2171052 | solution.py:68
  238.5 5.1 collective-permute-done
  247.7 5.1 collective-permute-done
  256.9 5.1 collective-permute-done
  266.1 5.1 collective-permute-done
  275.2 5.1 collective-permute-done
  284.4 5.1 collective-permute-done
  293.6 5.1 collective-permute-done
  302.7 5.1 collective-permute-done
  311.9 5.1 collective-permute-done
  321.1 5.1 collective-permute-done
  330.2 5.1 collective-permute-done
  339.4 5.1 collective-permute-done
  348.6 5.1 collective-permute-done
  357.7 5.1 collective-permute-done
  366.9 5.1 collective-permute-done
  421.9 5.1 collective-permute-done
  431.1 5.1 collective-permute-done
  440.3 5.1 collective-permute-done
  449.4 5.1 collective-permute-done
  458.6 5.1 collective-permute-done
  467.8 5.1 collective-permute-done
  476.9 5.1 collective-permute-done
  486.1 5.1 collective-permute-done
  (294 shorter events, 192.4 us)
Async XLA Ops:
  6.5 46.0 %all-gather.16.cloned.1.call-start = ((), (), s32[]{:S(2)}) async-start(), calls=%async_computation.4 | async-start | bytes 2359296 | tf_op jit(solution)/shard_map/all_gather | solution.py:38
  8.4 86.8 %all-gather.10.cloned.1.call-start = ((), (), s32[]{:S(2)}) async-start(), calls=%async_computation.1 | async-start | bytes 2359296 | tf_op jit(solution)/shard_map/all_gather | solution.py:38
  55.4 82.4 %all-gather.12.cloned.1.call-start = ((), (), s32[]{:S(2)}) async-start(), calls=%async_computation.2 | async-start | bytes 2359296 | tf_op jit(solution)/shard_map/all_gather | solution.py:38
  98.0 77.7 %reduce-scatter.4.cloned.1.call-start = ((), (), s32[]{:S(2)}) async-start(), calls=%async_computation.5 | async-start | bytes 589824
  101.4 135.0 %all-gather.14.cloned.1.call-start = ((), (), s32[]{:S(2)}) async-start(), calls=%async_computation.3 | async-start | bytes 2359296 | tf_op jit(solution)/shard_map/all_gather | solution.py:55
  236.5 7.2 %collective-permute-start = (f32[1024]{0:T(1024)S(1)}, f32[1024]{0:T(1024)S(1)}, u32[]{:S(2)}, u32[]{:S(2)}) collective-permute-start(f32[1024]{0:T(1024)S(1)} %broadcast_select_fusion.4), channel_id=1, source_target_pairs={{0,8},{8,16},{16,24},{24,32},{32,40},{40,48},{48,56},{56,64},{64,7... | collective-permute-start | bytes 12296 | tf_op jit(solution)/shard_map/while/body/eval_jaxpr/ppermute | solution.py:10
  245.8 7.0 %collective-permute-start = (f32[1024]{0:T(1024)S(1)}, f32[1024]{0:T(1024)S(1)}, u32[]{:S(2)}, u32[]{:S(2)}) collective-permute-start(f32[1024]{0:T(1024)S(1)} %broadcast_select_fusion.4), channel_id=1, source_target_pairs={{0,8},{8,16},{16,24},{24,32},{32,40},{40,48},{48,56},{56,64},{64,7... | collective-permute-start | bytes 12296 | tf_op jit(solution)/shard_map/while/body/eval_jaxpr/ppermute | solution.py:10
  255.0 7.0 %collective-permute-start = (f32[1024]{0:T(1024)S(1)}, f32[1024]{0:T(1024)S(1)}, u32[]{:S(2)}, u32[]{:S(2)}) collective-permute-start(f32[1024]{0:T(1024)S(1)} %broadcast_select_fusion.4), channel_id=1, source_target_pairs={{0,8},{8,16},{16,24},{24,32},{32,40},{40,48},{48,56},{56,64},{64,7... | collective-permute-start | bytes 12296 | tf_op jit(solution)/shard_map/while/body/eval_jaxpr/ppermute | solution.py:10
  264.1 7.0 %collective-permute-start = (f32[1024]{0:T(1024)S(1)}, f32[1024]{0:T(1024)S(1)}, u32[]{:S(2)}, u32[]{:S(2)}) collective-permute-start(f32[1024]{0:T(1024)S(1)} %broadcast_select_fusion.4), channel_id=1, source_target_pairs={{0,8},{8,16},{16,24},{24,32},{32,40},{40,48},{48,56},{56,64},{64,7... | collective-permute-start | bytes 12296 | tf_op jit(solution)/shard_map/while/body/eval_jaxpr/ppermute | solution.py:10
  273.3 7.0 %collective-permute-start = (f32[1024]{0:T(1024)S(1)}, f32[1024]{0:T(1024)S(1)}, u32[]{:S(2)}, u32[]{:S(2)}) collective-permute-start(f32[1024]{0:T(1024)S(1)} %broadcast_select_fusion.4), channel_id=1, source_target_pairs={{0,8},{8,16},{16,24},{24,32},{32,40},{40,48},{48,56},{56,64},{64,7... | collective-permute-start | bytes 12296 | tf_op jit(solution)/shard_map/while/body/eval_jaxpr/ppermute | solution.py:10
  282.5 7.0 %collective-permute-start = (f32[1024]{0:T(1024)S(1)}, f32[1024]{0:T(1024)S(1)}, u32[]{:S(2)}, u32[]{:S(2)}) collective-permute-start(f32[1024]{0:T(1024)S(1)} %broadcast_select_fusion.4), channel_id=1, source_target_pairs={{0,8},{8,16},{16,24},{24,32},{32,40},{40,48},{48,56},{56,64},{64,7... | collective-permute-start | bytes 12296 | tf_op jit(solution)/shard_map/while/body/eval_jaxpr/ppermute | solution.py:10
  291.6 7.0 %collective-permute-start = (f32[1024]{0:T(1024)S(1)}, f32[1024]{0:T(1024)S(1)}, u32[]{:S(2)}, u32[]{:S(2)}) collective-permute-start(f32[1024]{0:T(1024)S(1)} %broadcast_select_fusion.4), channel_id=1, source_target_pairs={{0,8},{8,16},{16,24},{24,32},{32,40},{40,48},{48,56},{56,64},{64,7... | collective-permute-start | bytes 12296 | tf_op jit(solution)/shard_map/while/body/eval_jaxpr/ppermute | solution.py:10
  300.8 7.0 %collective-permute-start = (f32[1024]{0:T(1024)S(1)}, f32[1024]{0:T(1024)S(1)}, u32[]{:S(2)}, u32[]{:S(2)}) collective-permute-start(f32[1024]{0:T(1024)S(1)} %broadcast_select_fusion.4), channel_id=1, source_target_pairs={{0,8},{8,16},{16,24},{24,32},{32,40},{40,48},{48,56},{56,64},{64,7... | collective-permute-start | bytes 12296 | tf_op jit(solution)/shard_map/while/body/eval_jaxpr/ppermute | solution.py:10
  310.0 7.0 %collective-permute-start = (f32[1024]{0:T(1024)S(1)}, f32[1024]{0:T(1024)S(1)}, u32[]{:S(2)}, u32[]{:S(2)}) collective-permute-start(f32[1024]{0:T(1024)S(1)} %broadcast_select_fusion.4), channel_id=1, source_target_pairs={{0,8},{8,16},{16,24},{24,32},{32,40},{40,48},{48,56},{56,64},{64,7... | collective-permute-start | bytes 12296 | tf_op jit(solution)/shard_map/while/body/eval_jaxpr/ppermute | solution.py:10
  319.1 7.0 %collective-permute-start = (f32[1024]{0:T(1024)S(1)}, f32[1024]{0:T(1024)S(1)}, u32[]{:S(2)}, u32[]{:S(2)}) collective-permute-start(f32[1024]{0:T(1024)S(1)} %broadcast_select_fusion.4), channel_id=1, source_target_pairs={{0,8},{8,16},{16,24},{24,32},{32,40},{40,48},{48,56},{56,64},{64,7... | collective-permute-start | bytes 12296 | tf_op jit(solution)/shard_map/while/body/eval_jaxpr/ppermute | solution.py:10
  328.3 7.0 %collective-permute-start = (f32[1024]{0:T(1024)S(1)}, f32[1024]{0:T(1024)S(1)}, u32[]{:S(2)}, u32[]{:S(2)}) collective-permute-start(f32[1024]{0:T(1024)S(1)} %broadcast_select_fusion.4), channel_id=1, source_target_pairs={{0,8},{8,16},{16,24},{24,32},{32,40},{40,48},{48,56},{56,64},{64,7... | collective-permute-start | bytes 12296 | tf_op jit(solution)/shard_map/while/body/eval_jaxpr/ppermute | solution.py:10
  337.5 7.0 %collective-permute-start = (f32[1024]{0:T(1024)S(1)}, f32[1024]{0:T(1024)S(1)}, u32[]{:S(2)}, u32[]{:S(2)}) collective-permute-start(f32[1024]{0:T(1024)S(1)} %broadcast_select_fusion.4), channel_id=1, source_target_pairs={{0,8},{8,16},{16,24},{24,32},{32,40},{40,48},{48,56},{56,64},{64,7... | collective-permute-start | bytes 12296 | tf_op jit(solution)/shard_map/while/body/eval_jaxpr/ppermute | solution.py:10
  346.6 7.0 %collective-permute-start = (f32[1024]{0:T(1024)S(1)}, f32[1024]{0:T(1024)S(1)}, u32[]{:S(2)}, u32[]{:S(2)}) collective-permute-start(f32[1024]{0:T(1024)S(1)} %broadcast_select_fusion.4), channel_id=1, source_target_pairs={{0,8},{8,16},{16,24},{24,32},{32,40},{40,48},{48,56},{56,64},{64,7... | collective-permute-start | bytes 12296 | tf_op jit(solution)/shard_map/while/body/eval_jaxpr/ppermute | solution.py:10
  355.8 7.0 %collective-permute-start = (f32[1024]{0:T(1024)S(1)}, f32[1024]{0:T(1024)S(1)}, u32[]{:S(2)}, u32[]{:S(2)}) collective-permute-start(f32[1024]{0:T(1024)S(1)} %broadcast_select_fusion.4), channel_id=1, source_target_pairs={{0,8},{8,16},{16,24},{24,32},{32,40},{40,48},{48,56},{56,64},{64,7... | collective-permute-start | bytes 12296 | tf_op jit(solution)/shard_map/while/body/eval_jaxpr/ppermute | solution.py:10
  365.0 7.0 %collective-permute-start = (f32[1024]{0:T(1024)S(1)}, f32[1024]{0:T(1024)S(1)}, u32[]{:S(2)}, u32[]{:S(2)}) collective-permute-start(f32[1024]{0:T(1024)S(1)} %broadcast_select_fusion.4), channel_id=1, source_target_pairs={{0,8},{8,16},{16,24},{24,32},{32,40},{40,48},{48,56},{56,64},{64,7... | collective-permute-start | bytes 12296 | tf_op jit(solution)/shard_map/while/body/eval_jaxpr/ppermute | solution.py:10
  374.1 7.0 %collective-permute-start = (f32[1024]{0:T(1024)S(1)}, f32[1024]{0:T(1024)S(1)}, u32[]{:S(2)}, u32[]{:S(2)}) collective-permute-start(f32[1024]{0:T(1024)S(1)} %broadcast_select_fusion.4), channel_id=1, source_target_pairs={{0,8},{8,16},{16,24},{24,32},{32,40},{40,48},{48,56},{56,64},{64,7... | collective-permute-start | bytes 12296 | tf_op jit(solution)/shard_map/while/body/eval_jaxpr/ppermute | solution.py:10
  383.3 7.0 %collective-permute-start = (f32[1024]{0:T(1024)S(1)}, f32[1024]{0:T(1024)S(1)}, u32[]{:S(2)}, u32[]{:S(2)}) collective-permute-start(f32[1024]{0:T(1024)S(1)} %broadcast_select_fusion.4), channel_id=1, source_target_pairs={{0,8},{8,16},{16,24},{24,32},{32,40},{40,48},{48,56},{56,64},{64,7... | collective-permute-start | bytes 12296 | tf_op jit(solution)/shard_map/while/body/eval_jaxpr/ppermute | solution.py:10
  392.5 7.0 %collective-permute-start = (f32[1024]{0:T(1024)S(1)}, f32[1024]{0:T(1024)S(1)}, u32[]{:S(2)}, u32[]{:S(2)}) collective-permute-start(f32[1024]{0:T(1024)S(1)} %broadcast_select_fusion.4), channel_id=1, source_target_pairs={{0,8},{8,16},{16,24},{24,32},{32,40},{40,48},{48,56},{56,64},{64,7... | collective-permute-start | bytes 12296 | tf_op jit(solution)/shard_map/while/body/eval_jaxpr/ppermute | solution.py:10
  420.0 7.0 %collective-permute-start = (f32[1024]{0:T(1024)S(1)}, f32[1024]{0:T(1024)S(1)}, u32[]{:S(2)}, u32[]{:S(2)}) collective-permute-start(f32[1024]{0:T(1024)S(1)} %broadcast_select_fusion.4), channel_id=1, source_target_pairs={{0,8},{8,16},{16,24},{24,32},{32,40},{40,48},{48,56},{56,64},{64,7... | collective-permute-start | bytes 12296 | tf_op jit(solution)/shard_map/while/body/eval_jaxpr/ppermute | solution.py:10
  429.2 7.0 %collective-permute-start = (f32[1024]{0:T(1024)S(1)}, f32[1024]{0:T(1024)S(1)}, u32[]{:S(2)}, u32[]{:S(2)}) collective-permute-start(f32[1024]{0:T(1024)S(1)} %broadcast_select_fusion.4), channel_id=1, source_target_pairs={{0,8},{8,16},{16,24},{24,32},{32,40},{40,48},{48,56},{56,64},{64,7... | collective-permute-start | bytes 12296 | tf_op jit(solution)/shard_map/while/body/eval_jaxpr/ppermute | solution.py:10
  438.3 7.0 %collective-permute-start = (f32[1024]{0:T(1024)S(1)}, f32[1024]{0:T(1024)S(1)}, u32[]{:S(2)}, u32[]{:S(2)}) collective-permute-start(f32[1024]{0:T(1024)S(1)} %broadcast_select_fusion.4), channel_id=1, source_target_pairs={{0,8},{8,16},{16,24},{24,32},{32,40},{40,48},{48,56},{56,64},{64,7... | collective-permute-start | bytes 12296 | tf_op jit(solution)/shard_map/while/body/eval_jaxpr/ppermute | solution.py:10
  447.5 7.0 %collective-permute-start = (f32[1024]{0:T(1024)S(1)}, f32[1024]{0:T(1024)S(1)}, u32[]{:S(2)}, u32[]{:S(2)}) collective-permute-start(f32[1024]{0:T(1024)S(1)} %broadcast_select_fusion.4), channel_id=1, source_target_pairs={{0,8},{8,16},{16,24},{24,32},{32,40},{40,48},{48,56},{56,64},{64,7... | collective-permute-start | bytes 12296 | tf_op jit(solution)/shard_map/while/body/eval_jaxpr/ppermute | solution.py:10
  456.7 7.0 %collective-permute-start = (f32[1024]{0:T(1024)S(1)}, f32[1024]{0:T(1024)S(1)}, u32[]{:S(2)}, u32[]{:S(2)}) collective-permute-start(f32[1024]{0:T(1024)S(1)} %broadcast_select_fusion.4), channel_id=1, source_target_pairs={{0,8},{8,16},{16,24},{24,32},{32,40},{40,48},{48,56},{56,64},{64,7... | collective-permute-start | bytes 12296 | tf_op jit(solution)/shard_map/while/body/eval_jaxpr/ppermute | solution.py:10
  465.8 7.0 %collective-permute-start = (f32[1024]{0:T(1024)S(1)}, f32[1024]{0:T(1024)S(1)}, u32[]{:S(2)}, u32[]{:S(2)}) collective-permute-start(f32[1024]{0:T(1024)S(1)} %broadcast_select_fusion.4), channel_id=1, source_target_pairs={{0,8},{8,16},{16,24},{24,32},{32,40},{40,48},{48,56},{56,64},{64,7... | collective-permute-start | bytes 12296 | tf_op jit(solution)/shard_map/while/body/eval_jaxpr/ppermute | solution.py:10
  475.0 7.0 %collective-permute-start = (f32[1024]{0:T(1024)S(1)}, f32[1024]{0:T(1024)S(1)}, u32[]{:S(2)}, u32[]{:S(2)}) collective-permute-start(f32[1024]{0:T(1024)S(1)} %broadcast_select_fusion.4), channel_id=1, source_target_pairs={{0,8},{8,16},{16,24},{24,32},{32,40},{40,48},{48,56},{56,64},{64,7... | collective-permute-start | bytes 12296 | tf_op jit(solution)/shard_map/while/body/eval_jaxpr/ppermute | solution.py:10
  484.2 7.0 %collective-permute-start = (f32[1024]{0:T(1024)S(1)}, f32[1024]{0:T(1024)S(1)}, u32[]{:S(2)}, u32[]{:S(2)}) collective-permute-start(f32[1024]{0:T(1024)S(1)} %broadcast_select_fusion.4), channel_id=1, source_target_pairs={{0,8},{8,16},{16,24},{24,32},{32,40},{40,48},{48,56},{56,64},{64,7... | collective-permute-start | bytes 12296 | tf_op jit(solution)/shard_map/while/body/eval_jaxpr/ppermute | solution.py:10
  493.3 7.0 %collective-permute-start = (f32[1024]{0:T(1024)S(1)}, f32[1024]{0:T(1024)S(1)}, u32[]{:S(2)}, u32[]{:S(2)}) collective-permute-start(f32[1024]{0:T(1024)S(1)} %broadcast_select_fusion.4), channel_id=1, source_target_pairs={{0,8},{8,16},{16,24},{24,32},{32,40},{40,48},{48,56},{56,64},{64,7... | collective-permute-start | bytes 12296 | tf_op jit(solution)/shard_map/while/body/eval_jaxpr/ppermute | solution.py:10
  (48 other events, 1723.4 us)
Sparse Core Ops, SparseCore 0:
  9.1 43.3 all-gather.15
  55.5 39.6 all-gather.9
  98.1 39.6 all-gather.11
  140.2 35.4 reduce-scatter.3
  177.4 40.0 all-gather.13
where the time goes:
time: 541 us; the launch traced here: 538 us
  waiting for transfers between devices  319 us (59%)
  other arithmetic  68.4 us (13%)
  starting transfers between devices  61.8 us (11%)
  blocking collectives  58 us (11%)
  between operations  13.3 us (2%)
  matrix products  9.56 us (2%)
  local copies, waits for them, and re-layouts  6.58 us (1%)
    ppermute x32, waiting for transfers between devices, passed_along(): return lax.ppermute(block, axis, route)  163 us
    all_gather x4, waiting for transfers between devices, shards(): lax.all_gather(prod, 'state', axis=0, tiled=True)  120 us
    reduce_sum x32, other arithmetic, matvec(): return jnp.sum(matrix.astype(jnp.float32) * vector[None, :], axis=1)  66.3 us
    ppermute x32, starting transfers between devices, passed_along(): return lax.ppermute(block, axis, route)  61.6 us
    all_gather x4, blocking collectives, shards(): lax.all_gather(local, 'state', axis=0, tiled=True)  58 us
    unnamed x6, waiting for transfers between devices  35.2 us
  transfers between devices with their start and end apart: 37, of which 36 were waited for; matrix products, arithmetic and copies ran while one was open for 2% of the time, Pallas kernels for 0%

commit v1 on v0

v1 whole, which is shorter than its diff:
```python
import functools

import jax
import jax.numpy as jnp
from jax import lax
from jax.experimental import pallas as pl
from jax.experimental.pallas import tpu as pltpu
from jax.sharding import PartitionSpec as P

F32 = jnp.float32
BF16 = jnp.bfloat16
VMEM_LIMIT = 40 * 1024 * 1024
ROWS = 256


def split_rows(x):
    hi = x.astype(BF16).astype(F32)
    rest = x - hi
    mid = rest.astype(BF16).astype(F32)
    lo = rest - mid
    row = lax.broadcasted_iota(jnp.int32, (16, x.shape[1]), 0)
    zero = jnp.zeros((16, x.shape[1]), F32)
    out = jnp.where(row == 0, hi, jnp.where(row == 1, mid, jnp.where(row == 2, lo, zero)))
    return out.astype(BF16)


def joined(rows):
    return jnp.sum(rows.astype(F32), axis=0, keepdims=True)


def times_t(x, matrix):
    out = lax.dot_general(split_rows(x), matrix, (((1,), (1,)), ((), ())), preferred_element_type=F32)
    return joined(out)


def times(x, matrix):
    return joined(jnp.dot(split_rows(x), matrix, preferred_element_type=F32))


def matmul_into(left, right, store, size):
    def block(i, carry):
        at = pl.multiple_of(i * ROWS, ROWS)
        out = jnp.dot(left(pl.ds(at, ROWS)), right(), preferred_element_type=F32)
        store(pl.ds(at, ROWS), out.astype(BF16))
        return carry

    lax.fori_loop(0, size // ROWS, block, 0)


def products_kernel(count, place_ref, drive_ref, *refs):
    pieces = refs[: 2 * count]
    sum_ref, slabs_ref, locals_ref, t_ref, m_ref, n_ref, sems = refs[2 * count:]
    size = t_ref.shape[1]
    width = size // count
    place = place_ref[0]
    copies = []
    for half in range(2):
        for r in range(count):
            at = pl.multiple_of(lax.rem(place + r, count) * width, width)
            copy = pltpu.make_async_copy(
                pieces[half * count + r],
                t_ref.at[pl.ds(2 * half, 2), pl.ds(at, width), :],
                sems.at[half * count + r],
            )
            copy.start()
            copies.append(copy)
    for copy in copies[:count]:
        copy.wait()
    mine = pl.ds(pl.multiple_of(place * width, width), width)
    slabs_ref[0] = t_ref[0, mine, :]

    def put(ref):
        def store(rows, value):
            ref[rows, :] = value

        return store

    matmul_into(lambda rows: t_ref[1, rows, :], lambda: t_ref[0], put(m_ref), size)
    slabs_ref[1] = m_ref[mine, :]
    for copy in copies[count:]:
        copy.wait()
    matmul_into(lambda rows: t_ref[2, rows, :], lambda: m_ref[...], put(n_ref), size)
    slabs_ref[2] = n_ref[mine, :]
    matmul_into(lambda rows: t_ref[3, rows, :], lambda: n_ref[...], put(sum_ref), size)
    slabs_ref[3] = sum_ref[mine, :]
    local = drive_ref[0:1, :]
    locals_ref[0:1, :] = local
    for j in range(1, 4):
        local = times_t(local, t_ref[j]) + drive_ref[j:j + 1, :]
        locals_ref[j:j + 1, :] = local
    sum_ref[size:, :] = split_rows(local)


def pair_kernel(core_ref, own_ref, other_ref, qt_ref, q_ref, first_ref, second_ref):
    size = qt_ref.shape[0]

    @pl.when(core_ref[0] == 0)
    def _():
        first_ref[...] = own_ref[...]
        second_ref[...] = other_ref[...]

    @pl.when(core_ref[0] != 0)
    def _():
        first_ref[...] = other_ref[...]
        second_ref[...] = own_ref[...]

    def block(i, carry):
        at = pl.multiple_of(i * ROWS, ROWS)
        out = jnp.dot(second_ref[pl.ds(at, ROWS), :], first_ref[:size, :], preferred_element_type=F32)
        qt_ref[:, pl.ds(at, ROWS)] = out.T.astype(BF16)
        return carry

    lax.fori_loop(0, size // ROWS, block, 0)
    q_ref[...] = times_t(joined(first_ref[size:, :]), second_ref[:size, :]) + joined(second_ref[size:, :])


def hop_kernel(turn, chip_ref, begin_ref, came_ref, qt_ref, q_ref, held_ref, value_ref):
    here = chip_ref[0] == turn

    @pl.when(here)
    def _():
        begin = came_ref[...] if turn > 0 else begin_ref[...]
        held_ref[...] = begin
        value_ref[...] = times(begin, qt_ref[...]) + q_ref[...]

    @pl.when(jnp.logical_not(here))
    def _():
        held_ref[...] = begin_ref[...]
        value_ref[...] = begin_ref[...]


def out_kernel(core_ref, begin_ref, other_ref, slabs_ref, locals_ref, out_ref):
    steps, width, size = slabs_ref.shape

    def write(begin):
        flat = slabs_ref[...].reshape(steps * width, size)
        row = times_t(begin, flat)
        for j in range(steps):
            out_ref[j:j + 1, :] = row[:, j * width:(j + 1) * width] + locals_ref[j:j + 1, :]

    @pl.when(core_ref[0] == 0)
    def _():
        write(begin_ref[...])

    @pl.when(core_ref[0] != 0)
    def _():
        write(times_t(begin_ref[...], other_ref[:size, :]) + joined(other_ref[size:, :]))


def call(kernel, out_shape, spaces, scratch=(), flops=0, moved=0):
    return pl.pallas_call(
        kernel,
        out_shape=out_shape,
        in_specs=[pl.BlockSpec(memory_space=s) for s in spaces],
        out_specs=jax.tree.map(lambda _: pl.BlockSpec(memory_space=pltpu.VMEM), out_shape),
        scratch_shapes=list(scratch),
        compiler_params=pltpu.CompilerParams(vmem_limit_bytes=VMEM_LIMIT),
        cost_estimate=pl.CostEstimate(flops=flops, bytes_accessed=moved, transcendentals=0),
    )


def gathered(part, axis, last_forward):
    count = lax.axis_size(axis)
    forward = [(i, (i + 1) % count) for i in range(count)]
    backward = [((i + 1) % count, i) for i in range(count)]
    pieces = {0: part}
    for r in range(1, count // 2):
        pieces[count - r] = lax.ppermute(pieces[(count - r + 1) % count], axis, forward)
        pieces[r] = lax.ppermute(pieces[r - 1], axis, backward)
    half = count // 2
    if last_forward:
        pieces[half] = lax.ppermute(pieces[half + 1], axis, forward)
    else:
        pieces[half] = lax.ppermute(pieces[half - 1], axis, backward)
    return [pieces[r] for r in range(count)]


def partial_drive_of(observations, precisions, blocks, block_rows, block_cols, width):
    steps_here = blocks.shape[0]
    side = blocks.shape[2]
    weighted = (precisions * observations).astype(BF16)
    pieces = weighted.reshape(steps_here, weighted.shape[1] // side, side)
    selected_entry = jnp.take_along_axis(pieces, block_rows[:, :, None], axis=1)
    terms = jnp.einsum("tbi,tbij->tbj", selected_entry, blocks, preferred_element_type=F32)
    onehot = (
        block_cols[:, :, None] == jnp.arange(width // side, dtype=jnp.int32)[None, None, :]
    ).astype(F32)
    return jnp.einsum("tbc,tbj->tcj", onehot, terms, precision=lax.Precision.HIGHEST).reshape(steps_here, width)


def shards(observations, precisions, blocks, block_rows, block_cols, transition, prior):
    steps_here, width, size = transition.shape
    count = lax.axis_size("state")
    place = lax.axis_index("state")
    position = lax.axis_index("tm")
    blocks_of_time = lax.axis_size("tm")
    core = (position % 2).astype(jnp.int32).reshape(1)
    chip = (position // 2).astype(jnp.int32).reshape(1)
    V, S, A = pltpu.VMEM, pltpu.SMEM, pl.ANY

    drive = partial_drive_of(observations, precisions, blocks, block_rows, block_cols, size)
    for bit in (1, 2, 4):
        drive = drive + lax.ppermute(drive, "state", [(i, i ^ bit) for i in range(count)])

    first = gathered(transition[:2], "state", True)
    second = gathered(transition[2:], "state", False)

    summed, slabs, locals_ = call(
        functools.partial(products_kernel, count),
        (
            jax.ShapeDtypeStruct((size + 16, size), BF16),
            jax.ShapeDtypeStruct((steps_here, width, size), BF16),
            jax.ShapeDtypeStruct((steps_here, size), F32),
        ),
        [S, V] + [A] * (2 * count),
        [
            pltpu.VMEM((steps_here, size, size), BF16),
            pltpu.VMEM((size, size), BF16),
            pltpu.VMEM((size, size), BF16),
            pltpu.SemaphoreType.DMA((2 * count,)),
        ],
        flops=6 * size ** 3,
        moved=12 * size ** 2,
    )(place.astype(jnp.int32).reshape(1), drive, *first, *second)

    swap = [(i, i ^ 1) for i in range(blocks_of_time)]
    other = lax.ppermute(summed, "tm", swap)
    turned, term = call(
        pair_kernel,
        (jax.ShapeDtypeStruct((size, size), BF16), jax.ShapeDtypeStruct((1, size), F32)),
        [S, V, V],
        [pltpu.VMEM((size + 16, size), BF16)] * 2,
        flops=2 * size ** 3,
        moved=6 * size ** 2,
    )(core, summed, other)

    begin = prior.reshape(1, size)
    came = begin
    chips = blocks_of_time // 2
    for turn in range(chips):
        begin, value = call(
            functools.partial(hop_kernel, turn),
            (jax.ShapeDtypeStruct((1, size), F32),) * 2,
            [S, V, V, V, V],
            flops=32 * size ** 2,
            moved=2 * size ** 2,
        )(chip, begin, came, turned, term)
        if turn + 1 < chips:
            came = lax.ppermute(value, "tm", [(2 * turn + c, 2 * turn + 2 + c) for c in (0, 1)])

    mine = lax.dynamic_slice_in_dim(locals_, place * width, width, axis=1)
    return call(
        out_kernel,
        jax.ShapeDtypeStruct((steps_here, width), F32),
        [S, V, V, V, V],
        flops=32 * size ** 2,
        moved=4 * size ** 2,
    )(core, begin, other, slabs, mine)


def solution(mesh):
    return jax.shard_map(
        shards,
        mesh=mesh,
        in_specs=(
            P("tm", None),
            P("tm", None),
            P("tm", "state", None, None),
            P("tm", "state"),
            P("tm", "state"),
            P("tm", "state", None),
            P(),
        ),
        out_specs=P("tm", "state"),
        check_vma=False,
    )
```

time: 541 us -> 202 us (0.37)
  the two profiles are of different devices: /device:TPU:34 before, /device:TPU:30 now
where the time goes in v1:
time: 202 us
  waiting for transfers between devices  117 us (58%)
  starting transfers between devices  45.2 us (22%)
  Pallas kernels  23.8 us (12%)
  local copies, waits for them, and re-layouts  13.9 us (7%)
    ppermute x15, waiting for transfers between devices, shards(): lax.ppermute(value, 'tm', [(2 * turn + c, 2 * turn + 2 + c) for c in (0,...  55.6 us
    ppermute x6, waiting for transfers between devices, gathered(): lax.ppermute(pieces[(count - r + 1) % count], axis, forward)  24.9 us
    ppermute x3, waiting for transfers between devices, shards(): lax.ppermute(drive, 'state', [(i, i ^ bit) for i in range(count)])  20.2 us
    ppermute x6, starting transfers between devices, gathered(): pieces[r] = lax.ppermute(pieces[r - 1], axis, backward)  20 us
    pallas_call x1, Pallas kernels, shards(): call(functools.partial(products_kernel, count), (jax.ShapeDtypeStruct((si...  13.7 us
    ppermute x6, waiting for transfers between devices, gathered(): pieces[r] = lax.ppermute(pieces[r - 1], axis, backward)  12 us
    unnamed x40, local copies, waits for them, and re-layouts  11.1 us
    ppermute x15, starting transfers between devices, shards(): lax.ppermute(value, 'tm', [(2 * turn + c, 2 * turn + 2 + c) for c in (0,...  10.5 us
  transfers between devices with their start and end apart: 33, of which 10 were waited for; matrix products, arithmetic and copies ran while one was open for 1% of the time, Pallas kernels for 0%

profile of v1, /device:TPU:30, one launch (start us, length us, event | category | flops | bytes accessed | tf_op | source)
XLA Modules:
  0.0 201.7 jit_solution(6548196648731311478)
XLA Ops:
  0.0 1.4 fusion.4
  1.5 2.0 collective-permute-start.6
  3.4 4.0 %collective-permute-start.10 = (bf16[2,128,1024]{2,1,0:T(8,128)(2,1)S(1)}, bf16[2,128,1024]{2,1,0:T(8,128)(2,1)S(1)}, u32[]{:S(2)}, u32[]{:S(2)}) collective-permute-start(bf16[2,128,1024]{2,1,0:T(8,128)(2,1)S(1)} %get-tuple-element.77.refs_8_), channel_id=1, source_target_pairs={{1,0},{2,1},{3,2},{4,3},{5,4},{6,5},{7,6},{0,7},{9,8},{10,9},{11,1... | collective-permute-start | bytes 1572872 | tf_op jit(solution)/shard_map/ppermute | solution.py:169
  7.5 1.9 collective-permute-start.3
  11.1 9.0 %collective-permute-done.6.refs_7_ = bf16[2,128,1024]{2,1,0:T(8,128)(2,1)S(1)} collective-permute-done((bf16[2,128,1024]{2,1,0:T(8,128)(2,1)S(1)}, bf16[2,128,1024]{2,1,0:T(8,128)(2,1)S(1)}, u32[]{:S(2)}, u32[]{:S(2)}) %collective-permute-start.6) | collective-permute-done | bytes 524320 | tf_op jit(solution)/shard_map/ppermute | solution.py:168
  21.0 3.2 %collective-permute-start.11 = (bf16[2,128,1024]{2,1,0:T(8,128)(2,1)S(1)}, bf16[2,128,1024]{2,1,0:T(8,128)(2,1)}, u32[]{:S(2)}, u32[]{:S(2)}) collective-permute-start(bf16[2,128,1024]{2,1,0:T(8,128)(2,1)S(1)} %collective-permute-done.10.refs_9_), channel_id=1, source_target_pairs={{1,0},{2,1},{3,2},{4,3},{5,4},{6,5},{7,6},{0,7},{9,8},{10,9},{11,1... | collective-permute-start | bytes 1572872 | tf_op jit(solution)/shard_map/ppermute | solution.py:169
  25.0 6.0 %collective-permute-done.3.refs_1_ = bf16[2,128,1024]{2,1,0:T(8,128)(2,1)S(1)} collective-permute-done((bf16[2,128,1024]{2,1,0:T(8,128)(2,1)S(1)}, bf16[2,128,1024]{2,1,0:T(8,128)(2,1)S(1)}, u32[]{:S(2)}, u32[]{:S(2)}) %collective-permute-start.3) | collective-permute-done | bytes 524320 | tf_op jit(solution)/shard_map/ppermute | solution.py:169
  31.0 3.7 %collective-permute-start.4 = (bf16[2,128,1024]{2,1,0:T(8,128)(2,1)S(1)}, bf16[2,128,1024]{2,1,0:T(8,128)(2,1)}, u32[]{:S(2)}, u32[]{:S(2)}) collective-permute-start(bf16[2,128,1024]{2,1,0:T(8,128)(2,1)S(1)} %collective-permute-done.3.refs_1_), channel_id=1, source_target_pairs={{1,0},{2,1},{3,2},{4,3},{5,4},{6,5},{7,6},{0,7},{9,8},{10,9},{11,1... | collective-permute-start | bytes 1572872 | tf_op jit(solution)/shard_map/ppermute | solution.py:169
  34.7 8.0 %collective-permute-done.7.refs_6_ = bf16[2,128,1024]{2,1,0:T(8,128)(2,1)} collective-permute-done((bf16[2,128,1024]{2,1,0:T(8,128)(2,1)S(1)}, bf16[2,128,1024]{2,1,0:T(8,128)(2,1)}, u32[]{:S(2)}, u32[]{:S(2)}) %collective-permute-start.7) | collective-permute-done | bytes 524320 | tf_op jit(solution)/shard_map/ppermute | solution.py:168
  42.7 3.4 %collective-permute-start.12 = (bf16[2,128,1024]{2,1,0:T(8,128)(2,1)}, bf16[2,128,1024]{2,1,0:T(8,128)(2,1)}, u32[]{:S(2)}, u32[]{:S(2)}) collective-permute-start(bf16[2,128,1024]{2,1,0:T(8,128)(2,1)} %collective-permute-done.11.refs_10_), channel_id=1, source_target_pairs={{1,0},{2,1},{3,2},{4,3},{5,4},{6,5},{7,6},{0,7},{9,8},{10,9},{11,1... | collective-permute-start | bytes 1572872 | tf_op jit(solution)/shard_map/ppermute | solution.py:169
  46.3 1.1 gather_fusion
  47.5 6.0 %collective-permute-done.4.refs_2_ = bf16[2,128,1024]{2,1,0:T(8,128)(2,1)} collective-permute-done((bf16[2,128,1024]{2,1,0:T(8,128)(2,1)S(1)}, bf16[2,128,1024]{2,1,0:T(8,128)(2,1)}, u32[]{:S(2)}, u32[]{:S(2)}) %collective-permute-start.4) | collective-permute-done | bytes 524320 | tf_op jit(solution)/shard_map/ppermute | solution.py:169
  53.5 3.8 %collective-permute-start.5 = (bf16[2,128,1024]{2,1,0:T(8,128)(2,1)}, bf16[2,128,1024]{2,1,0:T(8,128)(2,1)}, u32[]{:S(2)}, u32[]{:S(2)}) collective-permute-start(bf16[2,128,1024]{2,1,0:T(8,128)(2,1)} %collective-permute-done.4.refs_2_), channel_id=1, source_target_pairs={{1,0},{2,1},{3,2},{4,3},{5,4},{6,5},{7,6},{0,7},{9,8},{10,9},{11,1... | collective-permute-start | bytes 1572872 | tf_op jit(solution)/shard_map/ppermute | solution.py:169
  57.3 7.9 %collective-permute-done.8.refs_5_ = bf16[2,128,1024]{2,1,0:T(8,128)(2,1)} collective-permute-done((bf16[2,128,1024]{2,1,0:T(8,128)(2,1)}, bf16[2,128,1024]{2,1,0:T(8,128)(2,1)}, u32[]{:S(2)}, u32[]{:S(2)}) %collective-permute-start.8) | collective-permute-done | bytes 524320 | tf_op jit(solution)/shard_map/ppermute | solution.py:168
  65.2 3.4 %collective-permute-start.13 = (bf16[2,128,1024]{2,1,0:T(8,128)(2,1)}, bf16[2,128,1024]{2,1,0:T(8,128)(2,1)}, u32[]{:S(2)}, u32[]{:S(2)}) collective-permute-start(bf16[2,128,1024]{2,1,0:T(8,128)(2,1)} %collective-permute-done.12.refs_11_), channel_id=1, source_target_pairs={{1,0},{2,1},{3,2},{4,3},{5,4},{6,5},{7,6},{0,7},{9,8},{10,9},{11,1... | collective-permute-start | bytes 1572872 | tf_op jit(solution)/shard_map/ppermute | solution.py:174
  69.5 15.3 %collective-permute-done = f32[4,1024]{1,0:T(4,128)S(1)} collective-permute-done((f32[4,1024]{1,0:T(4,128)S(1)}, f32[4,1024]{1,0:T(4,128)S(1)}, u32[]{:S(2)}, u32[]{:S(2)}) %collective-permute-start) | collective-permute-done | bytes 16416 | tf_op jit(solution)/shard_map/ppermute | solution.py:203
  84.8 4.7 %collective-permute-start.1 = (f32[4,1024]{1,0:T(4,128)S(1)}, f32[4,1024]{1,0:T(4,128)S(1)}, u32[]{:S(2)}, u32[]{:S(2)}) collective-permute-start(f32[4,1024]{1,0:T(4,128)S(1)} %add.29), channel_id=1, source_target_pairs={{0,2},{1,3},{2,0},{3,1},{4,6},{5,7},{6,4},{7,5},{8,10},{9,11},{10,... | collective-permute-start | bytes 49160 | tf_op jit(solution)/shard_map/ppermute | solution.py:203
  89.4 1.7 collective-permute-done.1
  91.2 4.4 %collective-permute-start.2 = (f32[4,1024]{1,0:T(4,128)S(1)}, f32[4,1024]{1,0:T(4,128)S(1)}, u32[]{:S(2)}, u32[]{:S(2)}) collective-permute-start(f32[4,1024]{1,0:T(4,128)S(1)} %add.30), channel_id=1, source_target_pairs={{0,4},{1,5},{2,6},{3,7},{4,0},{5,1},{6,2},{7,3},{8,12},{9,13},{10,... | collective-permute-start | bytes 49160 | tf_op jit(solution)/shard_map/ppermute | solution.py:203
  95.6 3.2 %collective-permute-done.2 = f32[4,1024]{1,0:T(4,128)S(1)} collective-permute-done((f32[4,1024]{1,0:T(4,128)S(1)}, f32[4,1024]{1,0:T(4,128)S(1)}, u32[]{:S(2)}, u32[]{:S(2)}) %collective-permute-start.2) | collective-permute-done | bytes 16416 | tf_op jit(solution)/shard_map/ppermute | solution.py:203
  99.9 1.0 copy-done.6
  101.0 1.0 copy-done.9
  102.0 1.0 copy-done.11
  103.0 1.0 copy-done.13
  104.1 1.0 copy-done.15
  105.1 13.7 %shard_map.73 = (bf16[1040,1024]{1,0:T(8,128)(2,1)}, bf16[4,128,1024]{2,1,0:T(8,128)(2,1)S(1)}, f32[4,1024]{1,0:T(4,128)S(1)}) custom-call(s32[1]{0:T(128)} %bitcast.3.place_ref, f32[4,1024]{1,0:T(4,128)S(1)} %add.31.drive_ref, bf16[2,128,1024]{2,1,0:T(8,128)(2,1)S(1)} %copy-done.6, bf16[2,128,1024]{2,1,0:T(8,128)(2,1)S(1)} %copy-done.13, ...), custom_call_target="tpu_custom_call" | custom-call | flops 6442450944 | bytes 12582912 | tf_op jit(solution)/shard_map/pallas_call | solution.py:208
  118.9 4.5 %collective-permute-done.17.other_ref = bf16[1040,1024]{1,0:T(8,128)(2,1)} collective-permute-done((bf16[1040,1024]{1,0:T(8,128)(2,1)}, bf16[1040,1024]{1,0:T(8,128)(2,1)}, u32[]{:S(2)}, u32[]{:S(2)}) %collective-permute-start.17) | collective-permute-done | bytes 2129952 | tf_op jit(solution)/shard_map/ppermute | solution.py:227
  123.4 6.3 %shard_map.74 = (bf16[1024,1024]{1,0:T(8,128)(2,1)S(1)}, f32[1,1024]{1,0:T(1,128)S(1)}) custom-call(s32[1]{0:T(128)} %bitcast.core_ref, bf16[1040,1024]{1,0:T(8,128)(2,1)} %get-tuple-element.41.own_ref, bf16[1040,1024]{1,0:T(8,128)(2,1)} %collective-permute-done.17.other_ref), custom_call_target="tpu_custom_call" | custom-call | flops 2147483648 | bytes 6291456 | tf_op jit(solution)/shard_map/pallas_call | solution.py:228
  139.7 1.6 copy-done.2
  141.3 1.3 collective-permute-start.32
  142.6 55.5 %collective-permute-done.32.came_ref = f32[1,1024]{1,0:T(1,128)S(1)} collective-permute-done((f32[1,1024]{1,0:T(1,128)S(1)}, f32[1,1024]{1,0:T(1,128)S(1)}, u32[]{:S(2)}, u32[]{:S(2)}) %collective-permute-start.32) | collective-permute-done | bytes 4128 | tf_op jit(solution)/shard_map/ppermute | solution.py:249
  199.1 2.6 %shard_map.91 = f32[4,128]{1,0:T(4,128)} custom-call(s32[1]{0:T(128)} %bitcast.core_ref, f32[1,1024]{1,0:T(1,128)S(1)} %get-tuple-element.74.begin_ref, bf16[1040,1024]{1,0:T(8,128)(2,1)} %collective-permute-done.17.other_ref, bf16[4,128,1024]{2,1,0:T(8,128)(2,1)S(1)} %get-tuple-element.75.slabs_ref, f32[4,128]{1,0:T(4,128)S(1)} %constant_dynamic-slice_fusion.locals_ref), custom_call_target="tpu_custom_call" | custom-call | flops 33554432 | bytes 4194304 | tf_op jit(solution)/shard_map/pallas_call | solution.py:252
  (108 shorter events, 16.3 us)
Async XLA Ops:
  1.5 18.7 %collective-permute-start.6 = (bf16[2,128,1024]{2,1,0:T(8,128)(2,1)S(1)}, bf16[2,128,1024]{2,1,0:T(8,128)(2,1)S(1)}, u32[]{:S(2)}, u32[]{:S(2)}) collective-permute-start(bf16[2,128,1024]{2,1,0:T(8,128)(2,1)S(1)} %get-tuple-element.78.refs_0_), channel_id=1, source_target_pairs={{0,1},{1,2},{2,3},{3,4},{4,5},{5,6},{6,7},{7,0},{8,9},{9,10},{10,1... | collective-permute-start | bytes 1572872 | tf_op jit(solution)/shard_map/ppermute | solution.py:168
  3.4 17.5 %collective-permute-start.10 = (bf16[2,128,1024]{2,1,0:T(8,128)(2,1)S(1)}, bf16[2,128,1024]{2,1,0:T(8,128)(2,1)S(1)}, u32[]{:S(2)}, u32[]{:S(2)}) collective-permute-start(bf16[2,128,1024]{2,1,0:T(8,128)(2,1)S(1)} %get-tuple-element.77.refs_8_), channel_id=1, source_target_pairs={{1,0},{2,1},{3,2},{4,3},{5,4},{6,5},{7,6},{0,7},{9,8},{10,9},{11,1... | collective-permute-start | bytes 1572872 | tf_op jit(solution)/shard_map/ppermute | solution.py:169
  7.5 23.6 %collective-permute-start.3 = (bf16[2,128,1024]{2,1,0:T(8,128)(2,1)S(1)}, bf16[2,128,1024]{2,1,0:T(8,128)(2,1)S(1)}, u32[]{:S(2)}, u32[]{:S(2)}) collective-permute-start(bf16[2,128,1024]{2,1,0:T(8,128)(2,1)S(1)} %get-tuple-element.78.refs_0_), channel_id=1, source_target_pairs={{1,0},{2,1},{3,2},{4,3},{5,4},{6,5},{7,6},{0,7},{9,8},{10,9},{11,1... | collective-permute-start | bytes 1572872 | tf_op jit(solution)/shard_map/ppermute | solution.py:169
  10.2 24.5 %collective-permute-start.14 = (bf16[2,128,1024]{2,1,0:T(8,128)(2,1)S(1)}, bf16[2,128,1024]{2,1,0:T(8,128)(2,1)S(1)}, u32[]{:S(2)}, u32[]{:S(2)}) collective-permute-start(bf16[2,128,1024]{2,1,0:T(8,128)(2,1)S(1)} %get-tuple-element.77.refs_8_), channel_id=1, source_target_pairs={{0,1},{1,2},{2,3},{3,4},{4,5},{5,6},{6,7},{7,0},{8,9},{9,10},{10,1... | collective-permute-start | bytes 1572872 | tf_op jit(solution)/shard_map/ppermute | solution.py:168
  20.1 22.6 %collective-permute-start.7 = (bf16[2,128,1024]{2,1,0:T(8,128)(2,1)S(1)}, bf16[2,128,1024]{2,1,0:T(8,128)(2,1)}, u32[]{:S(2)}, u32[]{:S(2)}) collective-permute-start(bf16[2,128,1024]{2,1,0:T(8,128)(2,1)S(1)} %collective-permute-done.6.refs_7_), channel_id=1, source_target_pairs={{0,1},{1,2},{2,3},{3,4},{4,5},{5,6},{6,7},{7,0},{8,9},{9,10},{10,1... | collective-permute-start | bytes 1572872 | tf_op jit(solution)/shard_map/ppermute | solution.py:168
  21.0 21.8 %collective-permute-start.11 = (bf16[2,128,1024]{2,1,0:T(8,128)(2,1)S(1)}, bf16[2,128,1024]{2,1,0:T(8,128)(2,1)}, u32[]{:S(2)}, u32[]{:S(2)}) collective-permute-start(bf16[2,128,1024]{2,1,0:T(8,128)(2,1)S(1)} %collective-permute-done.10.refs_9_), channel_id=1, source_target_pairs={{1,0},{2,1},{3,2},{4,3},{5,4},{6,5},{7,6},{0,7},{9,8},{10,9},{11,1... | collective-permute-start | bytes 1572872 | tf_op jit(solution)/shard_map/ppermute | solution.py:169
  31.0 22.5 %collective-permute-start.4 = (bf16[2,128,1024]{2,1,0:T(8,128)(2,1)S(1)}, bf16[2,128,1024]{2,1,0:T(8,128)(2,1)}, u32[]{:S(2)}, u32[]{:S(2)}) collective-permute-start(bf16[2,128,1024]{2,1,0:T(8,128)(2,1)S(1)} %collective-permute-done.3.refs_1_), channel_id=1, source_target_pairs={{1,0},{2,1},{3,2},{4,3},{5,4},{6,5},{7,6},{0,7},{9,8},{10,9},{11,1... | collective-permute-start | bytes 1572872 | tf_op jit(solution)/shard_map/ppermute | solution.py:169
  34.7 22.6 %collective-permute-start.15 = (bf16[2,128,1024]{2,1,0:T(8,128)(2,1)S(1)}, bf16[2,128,1024]{2,1,0:T(8,128)(2,1)}, u32[]{:S(2)}, u32[]{:S(2)}) collective-permute-start(bf16[2,128,1024]{2,1,0:T(8,128)(2,1)S(1)} %collective-permute-done.14.refs_15_), channel_id=1, source_target_pairs={{0,1},{1,2},{2,3},{3,4},{4,5},{5,6},{6,7},{7,0},{8,9},{9,10},{10,1... | collective-permute-start | bytes 1572872 | tf_op jit(solution)/shard_map/ppermute | solution.py:168
  42.7 22.5 %collective-permute-start.8 = (bf16[2,128,1024]{2,1,0:T(8,128)(2,1)}, bf16[2,128,1024]{2,1,0:T(8,128)(2,1)}, u32[]{:S(2)}, u32[]{:S(2)}) collective-permute-start(bf16[2,128,1024]{2,1,0:T(8,128)(2,1)} %collective-permute-done.7.refs_6_), channel_id=1, source_target_pairs={{0,1},{1,2},{2,3},{3,4},{4,5},{5,6},{6,7},{7,0},{8,9},{9,10},{10,1... | collective-permute-start | bytes 1572872 | tf_op jit(solution)/shard_map/ppermute | solution.py:168
  42.7 22.5 %collective-permute-start.12 = (bf16[2,128,1024]{2,1,0:T(8,128)(2,1)}, bf16[2,128,1024]{2,1,0:T(8,128)(2,1)}, u32[]{:S(2)}, u32[]{:S(2)}) collective-permute-start(bf16[2,128,1024]{2,1,0:T(8,128)(2,1)} %collective-permute-done.11.refs_10_), channel_id=1, source_target_pairs={{1,0},{2,1},{3,2},{4,3},{5,4},{6,5},{7,6},{0,7},{9,8},{10,9},{11,1... | collective-permute-start | bytes 1572872 | tf_op jit(solution)/shard_map/ppermute | solution.py:169
  53.5 45.3 %collective-permute-start.5 = (bf16[2,128,1024]{2,1,0:T(8,128)(2,1)}, bf16[2,128,1024]{2,1,0:T(8,128)(2,1)}, u32[]{:S(2)}, u32[]{:S(2)}) collective-permute-start(bf16[2,128,1024]{2,1,0:T(8,128)(2,1)} %collective-permute-done.4.refs_2_), channel_id=1, source_target_pairs={{1,0},{2,1},{3,2},{4,3},{5,4},{6,5},{7,6},{0,7},{9,8},{10,9},{11,1... | collective-permute-start | bytes 1572872 | tf_op jit(solution)/shard_map/ppermute | solution.py:169
  57.3 41.5 %collective-permute-start.16 = (bf16[2,128,1024]{2,1,0:T(8,128)(2,1)}, bf16[2,128,1024]{2,1,0:T(8,128)(2,1)}, u32[]{:S(2)}, u32[]{:S(2)}) collective-permute-start(bf16[2,128,1024]{2,1,0:T(8,128)(2,1)} %collective-permute-done.15.refs_14_), channel_id=1, source_target_pairs={{0,1},{1,2},{2,3},{3,4},{4,5},{5,6},{6,7},{7,0},{8,9},{9,10},{10,1... | collective-permute-start | bytes 1572872 | tf_op jit(solution)/shard_map/ppermute | solution.py:168
  65.2 33.6 %collective-permute-start.9 = (bf16[2,128,1024]{2,1,0:T(8,128)(2,1)}, bf16[2,128,1024]{2,1,0:T(8,128)(2,1)}, u32[]{:S(2)}, u32[]{:S(2)}) collective-permute-start(bf16[2,128,1024]{2,1,0:T(8,128)(2,1)} %collective-permute-done.8.refs_5_), channel_id=1, source_target_pairs={{0,1},{1,2},{2,3},{3,4},{4,5},{5,6},{6,7},{7,0},{8,9},{9,10},{10,1... | collective-permute-start | bytes 1572872 | tf_op jit(solution)/shard_map/ppermute | solution.py:172
  65.2 33.6 %collective-permute-start.13 = (bf16[2,128,1024]{2,1,0:T(8,128)(2,1)}, bf16[2,128,1024]{2,1,0:T(8,128)(2,1)}, u32[]{:S(2)}, u32[]{:S(2)}) collective-permute-start(bf16[2,128,1024]{2,1,0:T(8,128)(2,1)} %collective-permute-done.12.refs_11_), channel_id=1, source_target_pairs={{1,0},{2,1},{3,2},{4,3},{5,4},{6,5},{7,6},{0,7},{9,8},{10,9},{11,1... | collective-permute-start | bytes 1572872 | tf_op jit(solution)/shard_map/ppermute | solution.py:174
  69.4 15.3 %collective-permute-start = (f32[4,1024]{1,0:T(4,128)S(1)}, f32[4,1024]{1,0:T(4,128)S(1)}, u32[]{:S(2)}, u32[]{:S(2)}) collective-permute-start(f32[4,1024]{1,0:T(4,128)S(1)} %reshape.32), channel_id=1, source_target_pairs={{0,1},{1,0},{2,3},{3,2},{4,5},{5,4},{6,7},{7,6},{8,9},{9,8},{10,11... | collective-permute-start | bytes 49160 | tf_op jit(solution)/shard_map/ppermute | solution.py:203
  84.8 6.4 %collective-permute-start.1 = (f32[4,1024]{1,0:T(4,128)S(1)}, f32[4,1024]{1,0:T(4,128)S(1)}, u32[]{:S(2)}, u32[]{:S(2)}) collective-permute-start(f32[4,1024]{1,0:T(4,128)S(1)} %add.29), channel_id=1, source_target_pairs={{0,2},{1,3},{2,0},{3,1},{4,6},{5,7},{6,4},{7,5},{8,10},{9,11},{10,... | collective-permute-start | bytes 49160 | tf_op jit(solution)/shard_map/ppermute | solution.py:203
  91.2 7.6 %collective-permute-start.2 = (f32[4,1024]{1,0:T(4,128)S(1)}, f32[4,1024]{1,0:T(4,128)S(1)}, u32[]{:S(2)}, u32[]{:S(2)}) collective-permute-start(f32[4,1024]{1,0:T(4,128)S(1)} %add.30), channel_id=1, source_target_pairs={{0,4},{1,5},{2,6},{3,7},{4,0},{5,1},{6,2},{7,3},{8,12},{9,13},{10,... | collective-permute-start | bytes 49160 | tf_op jit(solution)/shard_map/ppermute | solution.py:203
  118.8 4.6 %collective-permute-start.17 = (bf16[1040,1024]{1,0:T(8,128)(2,1)}, bf16[1040,1024]{1,0:T(8,128)(2,1)}, u32[]{:S(2)}, u32[]{:S(2)}) collective-permute-start(bf16[1040,1024]{1,0:T(8,128)(2,1)} %get-tuple-element.41.own_ref), channel_id=1, source_target_pairs={{0,8},{8,0},{16,24},{24,16},{32,40},{40,32},{48,56},{56,48},{64,72... | collective-permute-start | bytes 6389768 | tf_op jit(solution)/shard_map/ppermute | solution.py:227
  129.8 0.7 collective-permute-start.18
  130.5 0.7 collective-permute-start.19
  131.2 0.7 collective-permute-start.20
  131.9 0.7 collective-permute-start.21
  132.6 0.7 collective-permute-start.22
  133.3 0.7 collective-permute-start.23
  134.0 0.7 collective-permute-start.24
  134.7 0.7 collective-permute-start.25
  135.4 0.7 collective-permute-start.26
  136.1 0.7 collective-permute-start.27
  136.9 0.7 collective-permute-start.28
  137.6 0.7 collective-permute-start.29
  139.0 0.7 collective-permute-start.31
  141.3 56.8 %collective-permute-start.32 = (f32[1,1024]{1,0:T(1,128)S(1)}, f32[1,1024]{1,0:T(1,128)S(1)}, u32[]{:S(2)}, u32[]{:S(2)}) collective-permute-start(f32[1,1024]{1,0:T(1,128)S(1)} %get-tuple-element.73), channel_id=1, source_target_pairs={{224,240},{232,248},{225,241},{233,249},{226,242},{234,250},{227,2... | collective-permute-start | bytes 12296 | tf_op jit(solution)/shard_map/ppermute | solution.py:249
  (21 other events, 393.0 us)

commit v2 on v0

v2 whole, which is shorter than its diff:
```python
import functools

import jax
import jax.numpy as jnp
from jax import lax
from jax.experimental import pallas as pl
from jax.experimental.pallas import tpu as pltpu
from jax.sharding import PartitionSpec as P

F32 = jnp.float32
BF16 = jnp.bfloat16
VMEM_LIMIT = 24 * 1024 * 1024
COLUMNS = 256
LANES = 128


def three_parts(x):
    hi = x.astype(BF16).astype(F32)
    rest = x - hi
    mid = rest.astype(BF16).astype(F32)
    return hi, mid, rest - mid


def split_rows(x):
    hi, mid, lo = three_parts(x)
    row = lax.broadcasted_iota(jnp.int32, (16, x.shape[1]), 0)
    out = jnp.where(row == 0, hi, jnp.where(row == 1, mid, jnp.where(row == 2, lo, 0.0)))
    return out.astype(BF16)


def split_columns(x):
    hi, mid, lo = three_parts(x)
    column = lax.broadcasted_iota(jnp.int32, (x.shape[0], LANES), 1)
    out = jnp.where(column == 0, hi, jnp.where(column == 1, mid, jnp.where(column == 2, lo, 0.0)))
    return out.astype(BF16)


def joined(rows):
    return jnp.sum(rows.astype(F32), axis=0, keepdims=True)


def times_t(x, matrix):
    out = lax.dot_general(split_rows(x), matrix, (((1,), (1,)), ((), ())), preferred_element_type=F32)
    return joined(out)


def times(x, matrix):
    return joined(jnp.dot(split_rows(x), matrix, preferred_element_type=F32))


def times_column(matrix, x):
    out = jnp.dot(matrix, split_columns(x), preferred_element_type=F32)
    return jnp.sum(out, axis=1, keepdims=True)


def matmul(left_ref, right_ref, out_ref):
    size = left_ref.shape[0]

    def block(i, carry):
        at = pl.ds(pl.multiple_of(i * COLUMNS, COLUMNS), COLUMNS)
        out = jnp.dot(left_ref[...], right_ref[:, at], preferred_element_type=F32)
        out_ref[:size, at] = out.astype(BF16)
        return carry

    lax.fori_loop(0, right_ref.shape[1] // COLUMNS, block, 0)


def fetched(count, place, pieces, j, whole_ref, sems, first):
    width = pieces[0].shape[1]
    copies = []
    for r in range(count):
        at = pl.multiple_of(lax.rem(place + r, count) * width, width)
        copy = pltpu.make_async_copy(pieces[r].at[j], whole_ref.at[pl.ds(at, width), :], sems.at[first + r])
        copy.start()
        copies.append(copy)
    return copies


def two_kernel(count, place_ref, drive_ref, *refs):
    pieces, (two_ref, slab_ref, local_ref, one_ref, next_ref, sems) = refs[:count], refs[count:]
    width = slab_ref.shape[0]
    place = place_ref[0]
    copies = fetched(count, place, pieces, 0, one_ref, sems, 0)
    copies += fetched(count, place, pieces, 1, next_ref, sems, count)
    for copy in copies:
        copy.wait()
    matmul(next_ref, one_ref, two_ref)
    slab_ref[...] = two_ref[pl.ds(pl.multiple_of(place * width, width), width), :]
    local_ref[...] = times_column(next_ref[...], drive_ref[:, 0:1]) + drive_ref[:, 1:2]


def four_kernel(count, place_ref, drive_ref, local_ref, two_ref, *refs):
    pieces = refs[:count]
    sum_ref, slab3_ref, slab4_ref, locals_ref, three_ref, third_ref, fourth_ref, sems = refs[count:]
    width, size = slab3_ref.shape
    place = place_ref[0]
    thirds = fetched(count, place, pieces, 0, third_ref, sems, 0)
    fourths = fetched(count, place, pieces, 1, fourth_ref, sems, count)
    mine = pl.ds(pl.multiple_of(place * width, width), width)
    for copy in thirds:
        copy.wait()
    matmul(third_ref, two_ref, three_ref)
    slab3_ref[...] = three_ref[mine, :]
    local2 = local_ref[...]
    local3 = times_column(third_ref[...], local2) + drive_ref[:, 2:3]
    for copy in fourths:
        copy.wait()
    matmul(fourth_ref, three_ref, sum_ref)
    slab4_ref[...] = sum_ref[mine, :]
    local4 = times_column(fourth_ref[...], local3) + drive_ref[:, 3:4]
    column = lax.broadcasted_iota(jnp.int32, (size, LANES), 1)
    first = jnp.broadcast_to(drive_ref[:, 0:1], (size, LANES))
    side = jnp.where(column == 0, first, jnp.where(column == 1, local2, jnp.where(column == 2, local3, local4)))
    rows = side.T
    locals_ref[...] = rows[:8, :]
    sum_ref[size:, :] = split_rows(rows[3:4, :])


def both(core_ref, own_ref, other_ref, write):
    @pl.when(core_ref[0] == 0)
    def _():
        write(own_ref, other_ref)

    @pl.when(core_ref[0] != 0)
    def _():
        write(other_ref, own_ref)


def pair_kernel(core_ref, own_ref, other_ref, after_ref, qt_ref, q_ref):
    size = qt_ref.shape[0]

    @pl.when(core_ref[0] != 0)
    def _():
        def block(i, carry):
            at = pl.ds(pl.multiple_of(i * COLUMNS, COLUMNS), COLUMNS)
            out = jnp.dot(own_ref[at, :], other_ref[:size, :], preferred_element_type=F32)
            qt_ref[:, at] = out.T.astype(BF16)
            return carry

        lax.fori_loop(0, size // COLUMNS, block, 0)
        q_ref[...] = times_t(joined(other_ref[size:, :]), own_ref[:size, :]) + joined(own_ref[size:, :])


def early_hop_kernel(turn, core_ref, chip_ref, begin_ref, came_ref, own_ref, other_ref, held_ref, value_ref):
    size = begin_ref.shape[1]
    held_ref[...] = begin_ref[...]
    value_ref[...] = begin_ref[...]

    @pl.when(jnp.logical_and(chip_ref[0] == turn, core_ref[0] != 0))
    def _():
        begin = came_ref[...] if turn > 0 else begin_ref[...]
        held_ref[...] = begin
        between = times_t(begin, other_ref[:size, :]) + joined(other_ref[size:, :])
        value_ref[...] = times_t(between, own_ref[:size, :]) + joined(own_ref[size:, :])


def hop_kernel(turn, core_ref, chip_ref, begin_ref, came_ref, qt_ref, q_ref, held_ref, value_ref):
    here = jnp.logical_and(chip_ref[0] == turn, core_ref[0] != 0)

    @pl.when(here)
    def _():
        begin = came_ref[...]
        held_ref[...] = begin
        value_ref[...] = times(begin, qt_ref[...]) + q_ref[...]

    @pl.when(jnp.logical_not(here))
    def _():
        held_ref[...] = begin_ref[...]
        value_ref[...] = begin_ref[...]


def ready_kernel(core_ref, place_ref, other_ref, locals_ref, after_ref, *refs):
    slabs, (maps_ref, terms_ref) = refs[:-2], refs[-2:]
    width, size = slabs[0].shape
    mine = pl.ds(pl.multiple_of(place_ref[0] * width, width), width)
    for j, slab_ref in enumerate(slabs):
        at = slice(j * width, (j + 1) * width)

        @pl.when(core_ref[0] == 0)
        def _():
            maps_ref[:, at] = slab_ref[...].astype(F32).T.astype(BF16)
            terms_ref[j:j + 1, :] = locals_ref[j:j + 1, mine]

        @pl.when(core_ref[0] != 0)
        def _():
            out = jnp.dot(slab_ref[...], other_ref[:size, :], preferred_element_type=F32)
            maps_ref[:, at] = out.T.astype(BF16)
            term = times_t(joined(other_ref[size:, :]), slab_ref[...])
            terms_ref[j:j + 1, :] = term + locals_ref[j:j + 1, mine]


def out_kernel(core_ref, begin_ref, got_ref, maps_ref, terms_ref, out_ref):
    steps, width = out_ref.shape
    begin = jnp.where(core_ref[0] == 0, got_ref[...], begin_ref[...])
    row = times(begin, maps_ref[...])
    for j in range(steps):
        out_ref[j:j + 1, :] = row[:, j * width:(j + 1) * width] + terms_ref[j:j + 1, :]


def call(kernel, out_shape, spaces, scratch=(), flops=0, moved=0):
    return pl.pallas_call(
        kernel,
        out_shape=out_shape,
        in_specs=[pl.BlockSpec(memory_space=s) for s in spaces],
        out_specs=jax.tree.map(lambda _: pl.BlockSpec(memory_space=pltpu.VMEM), out_shape),
        scratch_shapes=list(scratch),
        compiler_params=pltpu.CompilerParams(vmem_limit_bytes=VMEM_LIMIT),
        cost_estimate=pl.CostEstimate(flops=flops, bytes_accessed=moved, transcendentals=0),
    )


def after(value, *needed):
    return lax.optimization_barrier((value, needed))[0]


def ring_rounds(parts, axis, needed):
    count = lax.axis_size(axis)
    forward = [(i, (i + 1) % count) for i in range(count)]
    backward = [((i + 1) % count, i) for i in range(count)]
    half = count // 2
    found = [{0: part} for part in parts]
    for r in range(1, half + 1):
        for i, pieces in enumerate(found):
            left, right = pieces[(count - r + 1) % count], pieces[r - 1]
            more = needed(r, i, found)
            if more:
                left, right = after((left, right), *more)
            if r < half or i % 2 == 0:
                pieces[count - r] = lax.ppermute(left, axis, forward)
            if r < half or i % 2 == 1:
                pieces[r] = lax.ppermute(right, axis, backward)
    return [[pieces[r] for r in range(count)] for pieces in found]


def partial_drive_of(observations, precisions, blocks, block_rows, block_cols, width):
    steps_here = blocks.shape[0]
    side = blocks.shape[2]
    weighted = (precisions * observations).astype(BF16)
    pieces = weighted.reshape(steps_here, weighted.shape[1] // side, side)
    selected_entry = jnp.take_along_axis(pieces, block_rows[:, :, None], axis=1)
    terms = jnp.einsum("tbi,tbij->tbj", selected_entry, blocks, preferred_element_type=F32)
    onehot = (
        block_cols[:, :, None] == jnp.arange(width // side, dtype=jnp.int32)[None, None, :]
    ).astype(F32)
    return jnp.einsum("tbc,tbj->tcj", onehot, terms, precision=lax.Precision.HIGHEST).reshape(steps_here, width)


def shards(observations, precisions, blocks, block_rows, block_cols, transition, prior):
    steps_here, width, size = transition.shape
    count = lax.axis_size("state")
    place = lax.axis_index("state")
    position = lax.axis_index("tm")
    blocks_of_time = lax.axis_size("tm")
    core = (position % 2).astype(jnp.int32).reshape(1)
    chip = (position // 2).astype(jnp.int32).reshape(1)
    at = place.astype(jnp.int32).reshape(1)
    V, S, H = pltpu.VMEM, pltpu.SMEM, pltpu.HBM

    def added(drive, bit):
        return drive + lax.ppermute(drive, "state", [(i, i ^ bit) for i in range(count)])

    drive = partial_drive_of(observations, precisions, blocks, block_rows, block_cols, size)
    drive1 = added(drive, 1)
    drive2 = added(drive1, 2)
    drive4 = added(drive2, 4)
    needs = {(2, 0): drive, (3, 0): drive1, (4, 0): drive2}

    def needed(r, i, found):
        return (needs[r, i],) if (r, i) in needs else ()

    early, late = ring_rounds([transition[:2], transition[2:]], "state", needed)
    columns = jnp.pad(drive4.T, ((0, 0), (0, LANES - steps_here)))

    matrix = jax.ShapeDtypeStruct((size, size), BF16)
    longer = jax.ShapeDtypeStruct((size + 16, size), BF16)
    slab = jax.ShapeDtypeStruct((width, size), BF16)
    column = jax.ShapeDtypeStruct((size, 1), F32)
    row = jax.ShapeDtypeStruct((1, size), F32)
    whole = pltpu.VMEM((size, size), BF16)
    semaphores = pltpu.SemaphoreType.DMA((2 * count,))
    two, slab2, local2 = call(
        functools.partial(two_kernel, count), (matrix, slab, column), [S, V] + [H] * count,
        [whole, whole, semaphores], flops=2 * size ** 3, moved=6 * size ** 2,
    )(at, columns, *early)
    own, slab3, slab4, locals_ = call(
        functools.partial(four_kernel, count),
        (longer, slab, slab, jax.ShapeDtypeStruct((8, size), F32)),
        [S, V, V, V] + [H] * count,
        [whole, whole, whole, semaphores], flops=4 * size ** 3, moved=8 * size ** 2,
    )(at, columns, local2, two, *late)

    other = lax.ppermute(own, "tm", [(i, i + 1) for i in range(0, blocks_of_time, 2)])

    def hop(value, turn):
        return lax.ppermute(value, "tm", [(2 * turn + 1, 2 * turn + 3)])

    begin = prior.reshape(1, size)
    came = begin
    chips = blocks_of_time // 2
    for turn in range(2):
        begin, value = call(
            functools.partial(early_hop_kernel, turn), (row, row), [S, S] + [V] * 4,
            flops=64 * size ** 2, moved=4 * size ** 2,
        )(core, chip, begin, came, own, other)
        came = hop(value, turn)
    turned, term = call(
        pair_kernel, (matrix, row), [S, V, V, V], flops=2 * size ** 3, moved=6 * size ** 2
    )(core, own, other, value)
    for turn in range(2, chips):
        begin, value = call(
            functools.partial(hop_kernel, turn), (row, row), [S, S, V, V, V, V],
            flops=32 * size ** 2, moved=2 * size ** 2,
        )(core, chip, begin, came, turned, term)
        if turn == 2:
            maps, terms = call(
                ready_kernel,
                (jax.ShapeDtypeStruct((size, steps_here * width), BF16), jax.ShapeDtypeStruct((steps_here, width), F32)),
                [S, S] + [V] * 7, flops=size ** 3, moved=4 * size ** 2,
            )(core, at, other, locals_, value, transition[0], slab2, slab3, slab4)
        if turn + 1 < chips:
            came = hop(value, turn)
    got = lax.ppermute(begin, "tm", [(i + 1, i) for i in range(0, blocks_of_time, 2)])
    return call(
        out_kernel, jax.ShapeDtypeStruct((steps_here, width), F32), [S, V, V, V, V],
        flops=16 * size ** 2, moved=size ** 2,
    )(core, begin, got, maps, terms)


def solution(mesh):
    return jax.shard_map(
        shards,
        mesh=mesh,
        in_specs=(
            P("tm", None),
            P("tm", None),
            P("tm", "state", None, None),
            P("tm", "state"),
            P("tm", "state"),
            P("tm", "state", None),
            P(),
        ),
        out_specs=P("tm", "state"),
        check_vma=False,
    )
```

time: 541 us -> 255 us (0.47)
  the two profiles are of different devices: /device:TPU:34 before, /device:TPU:95 now
where the time goes in v2:
time: 255 us
  waiting for transfers between devices  166 us (65%)
  starting transfers between devices  39.3 us (15%)
  Pallas kernels  35.7 us (14%)
  local copies, waits for them, and re-layouts  8.81 us (3%)
  other arithmetic  3.39 us (1%)
    ppermute x3, waiting for transfers between devices, added(): lax.ppermute(drive, 'state', [(i, i ^ bit) for i in range(count)])  108 us
    ppermute x15, waiting for transfers between devices, hop(): return lax.ppermute(value, 'tm', [(2 * turn + 1, 2 * turn + 3)])  36.3 us
    ppermute x7, waiting for transfers between devices, ring_rounds(): pieces[r] = lax.ppermute(right, axis, backward)  13.9 us
    ppermute x7, starting transfers between devices, ring_rounds(): pieces[count - r] = lax.ppermute(left, axis, forward)  13.8 us
    pallas_call x1, Pallas kernels, shards(): call(functools.partial(four_kernel, count), (longer, slab, slab, jax.Shap...  12.3 us
    ppermute x15, starting transfers between devices, hop(): return lax.ppermute(value, 'tm', [(2 * turn + 1, 2 * turn + 3)])  10.7 us
    ppermute x3, starting transfers between devices, added(): lax.ppermute(drive, 'state', [(i, i ^ bit) for i in range(count)])  8.7 us
    ppermute x1, waiting for transfers between devices, shards(): lax.ppermute(own, 'tm', [(i, i + 1) for i in range(0, blocks_of_time, 2)])  7.38 us
  transfers between devices with their start and end apart: 34, of which 7 were waited for; matrix products, arithmetic and copies ran while one was open for 3% of the time, Pallas kernels for 7%

profile of v2, /device:TPU:95, one launch (start us, length us, event | category | flops | bytes accessed | tf_op | source)
XLA Modules:
  0.0 254.6 jit_solution(2038298655006187080)
XLA Ops:
  0.0 1.4 fusion.4
  1.5 1.7 collective-permute-start.4
  3.5 1.1 gather_fusion
  5.6 1.1 copy.8
  6.6 8.2 %collective-permute-done.3.refs_1_ = bf16[2,128,1024]{2,1,0:T(8,128)(2,1)} collective-permute-done((bf16[2,128,1024]{2,1,0:T(8,128)(2,1)S(1)}, bf16[2,128,1024]{2,1,0:T(8,128)(2,1)}, u32[]{:S(2)}, u32[]{:S(2)}) %collective-permute-start.3) | collective-permute-done | bytes 524320 | tf_op jit(solution)/shard_map/ppermute | solution.py:231
  14.8 3.4 %collective-permute-start.5 = (bf16[2,128,1024]{2,1,0:T(8,128)(2,1)}, bf16[2,128,1024]{2,1,0:T(8,128)(2,1)S(1)}, u32[]{:S(2)}, u32[]{:S(2)}) collective-permute-start(bf16[2,128,1024]{2,1,0:T(8,128)(2,1)} %collective-permute-done.3.refs_1_), channel_id=1, source_target_pairs={{1,0},{2,1},{3,2},{4,3},{5,4},{6,5},{7,6},{0,7},{9,8},{10,9},{11,1... | collective-permute-start | bytes 1572872 | tf_op jit(solution)/shard_map/ppermute | solution.py:231
  18.2 2.1 collective-permute-start.14
  20.3 5.7 %collective-permute-done.10.refs_1_ = bf16[2,128,1024]{2,1,0:T(8,128)(2,1)} collective-permute-done((bf16[2,128,1024]{2,1,0:T(8,128)(2,1)S(1)}, bf16[2,128,1024]{2,1,0:T(8,128)(2,1)}, u32[]{:S(2)}, u32[]{:S(2)}) %collective-permute-start.10) | collective-permute-done | bytes 524320 | tf_op jit(solution)/shard_map/ppermute | solution.py:231
  26.1 2.8 %collective-permute-start = (f32[4,1024]{0,1:T(8,128)}, f32[4,1024]{0,1:T(8,128)S(1)}, u32[]{:S(2)}, u32[]{:S(2)}) collective-permute-start(f32[4,1024]{0,1:T(8,128)} %bitcast.23), channel_id=1, source_target_pairs={{0,1},{1,0},{2,3},{3,2},{4,5},{5,4},{6,7},{7,6},{8,9},{9,8},{10,11... | collective-permute-start | bytes 49160 | tf_op jit(solution)/shard_map/ppermute | solution.py:260
  28.9 30.7 %collective-permute-done = f32[4,1024]{0,1:T(8,128)S(1)} collective-permute-done((f32[4,1024]{0,1:T(8,128)}, f32[4,1024]{0,1:T(8,128)S(1)}, u32[]{:S(2)}, u32[]{:S(2)}) %collective-permute-start) | collective-permute-done | bytes 16416 | tf_op jit(solution)/shard_map/ppermute | solution.py:260
  59.6 1.1 bitcast_add_fusion
  61.7 1.5 collective-permute-start.8
  64.0 2.7 %collective-permute-start.15 = (bf16[2,128,1024]{2,1,0:T(8,128)(2,1)S(1)}, bf16[2,128,1024]{2,1,0:T(8,128)(2,1)}, u32[]{:S(2)}, u32[]{:S(2)}) collective-permute-start(bf16[2,128,1024]{2,1,0:T(8,128)(2,1)S(1)} %collective-permute-done.14.refs_7_), channel_id=1, source_target_pairs={{0,1},{1,2},{2,3},{3,4},{4,5},{5,6},{6,7},{7,0},{8,9},{9,10},{10,1... | collective-permute-start | bytes 1572872 | tf_op jit(solution)/shard_map/ppermute | solution.py:229
  67.4 1.8 collective-permute-start.1
  69.2 35.6 %collective-permute-done.1 = f32[4,1024]{0,1:T(8,128)S(1)} collective-permute-done((f32[4,1024]{0,1:T(8,128)S(1)}, f32[4,1024]{0,1:T(8,128)S(1)}, u32[]{:S(2)}, u32[]{:S(2)}) %collective-permute-start.1) | collective-permute-done | bytes 16416 | tf_op jit(solution)/shard_map/ppermute | solution.py:260
  106.5 3.9 %collective-permute-start.9 = (bf16[2,128,1024]{2,1,0:T(8,128)(2,1)}, bf16[2,128,1024]{2,1,0:T(8,128)(2,1)}, u32[]{:S(2)}, u32[]{:S(2)}) collective-permute-start(bf16[2,128,1024]{2,1,0:T(8,128)(2,1)} %collective-permute-done.8.refs_5_), channel_id=1, source_target_pairs={{0,1},{1,2},{2,3},{3,4},{4,5},{5,6},{6,7},{7,0},{8,9},{9,10},{10,1... | collective-permute-start | bytes 1572872 | tf_op jit(solution)/shard_map/ppermute | solution.py:229
  110.4 1.9 collective-permute-start.16
  112.3 4.1 %collective-permute-start.2 = (f32[4,1024]{0,1:T(8,128)}, f32[4,1024]{0,1:T(8,128)}, u32[]{:S(2)}, u32[]{:S(2)}) collective-permute-start(f32[4,1024]{0,1:T(8,128)} %add.29), channel_id=1, source_target_pairs={{0,4},{1,5},{2,6},{3,7},{4,0},{5,1},{6,2},{7,3},{8,12},{9,13},{10,... | collective-permute-start | bytes 49160 | tf_op jit(solution)/shard_map/ppermute | solution.py:260
  116.4 42.0 %collective-permute-done.2 = f32[4,1024]{0,1:T(8,128)} collective-permute-done((f32[4,1024]{0,1:T(8,128)}, f32[4,1024]{0,1:T(8,128)}, u32[]{:S(2)}, u32[]{:S(2)}) %collective-permute-start.2) | collective-permute-done | bytes 16416 | tf_op jit(solution)/shard_map/ppermute | solution.py:260
  158.4 1.3 add_bitcast_fusion
  159.8 6.8 %shard_map.73 = (bf16[1024,1024]{1,0:T(8,128)(2,1)S(1)}, bf16[128,1024]{1,0:T(8,128)(2,1)S(1)}, f32[1024,1]{1,0:T(8,128)S(1)}) custom-call(s32[1]{0:T(128)} %bitcast.3.place_ref, f32[1024,128]{1,0:T(8,128)S(1)} %pad.4.drive_ref, bf16[2,128,1024]{2,1,0:T(8,128)(2,1)S(1)} %get-tuple-element.100.refs_0_, bf16[2,128,1024]{2,1,0:T(8,128)(2,1)} %collective-permute-done.3.refs_1_, ...), custom_call_target="tpu_custom_call" | custom-call | flops 2147483648 | bytes 6291456 | tf_op jit(solution)/shard_map/pallas_call | solution.py:281
  166.7 12.3 %shard_map.74 = (bf16[1040,1024]{1,0:T(8,128)(2,1)}, bf16[128,1024]{1,0:T(8,128)(2,1)S(1)}, bf16[128,1024]{1,0:T(8,128)(2,1)S(1)}, f32[8,1024]{1,0:T(8,128)S(1)}) custom-call(s32[1]{0:T(128)} %bitcast.3.place_ref, f32[1024,128]{1,0:T(8,128)S(1)} %pad.4.drive_ref, f32[1024,1]{1,0:T(8,128)S(1)} %get-tuple-element.57.local_ref, ...), custom_call_target="tpu_custom_call" | custom-call | flops 4294967296 | bytes 8388608 | tf_op jit(solution)/shard_map/pallas_call | solution.py:285
  179.7 1.3 collective-permute-start.17
  181.0 7.4 %collective-permute-done.17.other_ref = bf16[1040,1024]{1,0:T(8,128)(2,1)} collective-permute-done((bf16[1040,1024]{1,0:T(8,128)(2,1)}, bf16[1040,1024]{1,0:T(8,128)(2,1)}, u32[]{:S(2)}, u32[]{:S(2)}) %collective-permute-start.17) | collective-permute-done | bytes 2129952 | tf_op jit(solution)/shard_map/ppermute | solution.py:292
  188.4 2.2 shard_map.75
  191.3 2.2 shard_map.76
  194.2 6.1 %shard_map.77 = (bf16[1024,1024]{1,0:T(8,128)(2,1)S(1)}, f32[1,1024]{1,0:T(1,128)S(1)}) custom-call(s32[1]{0:T(128)} %bitcast.core_ref, bf16[1040,1024]{1,0:T(8,128)(2,1)} %get-tuple-element.59.own_ref, bf16[1040,1024]{1,0:T(8,128)(2,1)} %collective-permute-done.17.other_ref, f32[1,1024]{1,0:T(1,128)S(1)} %get-tuple-element.63.after_ref), custom_call_target="tpu_custom_call" | custom-call | flops 2147483648 | bytes 6291456 | tf_op jit(solution)/shard_map/pallas_call | solution.py:306
  209.0 1.4 collective-permute-start.32
  211.4 36.3 %collective-permute-done.32.came_ref = f32[1,1024]{1,0:T(1,128)S(1)} collective-permute-done((f32[1,1024]{1,0:T(1,128)S(1)}, f32[1,1024]{1,0:T(1,128)S(1)}, u32[]{:S(2)}, u32[]{:S(2)}) %collective-permute-start.32) | collective-permute-done | bytes 4128 | tf_op jit(solution)/shard_map/ppermute | solution.py:295
  247.6 1.0 shard_map.91
  248.6 1.3 collective-permute-start.33
  249.9 3.8 %shard_map.92 = (bf16[1024,512]{1,0:T(8,128)(2,1)S(1)}, f32[4,128]{1,0:T(4,128)S(1)}) custom-call(s32[1]{0:T(128)} %bitcast.core_ref, s32[1]{0:T(128)} %bitcast.3.place_ref, bf16[1040,1024]{1,0:T(8,128)(2,1)} %collective-permute-done.17.other_ref, f32[8,1024]{1,0:T(8,128)S(1)} %get-tuple-element.93.locals_ref, f32[1,1024]{1,0:T(1,128)S(1)} %get-tuple-element.67.after_ref, ...), custom_call_target="tpu_custom_call" | custom-call | flops 1073741824 | bytes 4194304 | tf_op jit(solution)/shard_map/pallas_call | solution.py:315
  (109 shorter events, 17.8 us)
Async XLA Ops:
  1.5 13.4 %collective-permute-start.3 = (bf16[2,128,1024]{2,1,0:T(8,128)(2,1)S(1)}, bf16[2,128,1024]{2,1,0:T(8,128)(2,1)}, u32[]{:S(2)}, u32[]{:S(2)}) collective-permute-start(bf16[2,128,1024]{2,1,0:T(8,128)(2,1)S(1)} %get-tuple-element.100.refs_0_), channel_id=1, source_target_pairs={{1,0},{2,1},{3,2},{4,3},{5,4},{6,5},{7,6},{0,7},{9,8},{10,9},{11,1... | collective-permute-start | bytes 1572872 | tf_op jit(solution)/shard_map/ppermute | solution.py:231
  1.5 13.3 %collective-permute-start.4 = (bf16[2,128,1024]{2,1,0:T(8,128)(2,1)S(1)}, bf16[2,128,1024]{2,1,0:T(8,128)(2,1)}, u32[]{:S(2)}, u32[]{:S(2)}) collective-permute-start(bf16[2,128,1024]{2,1,0:T(8,128)(2,1)S(1)} %get-tuple-element.100.refs_0_), channel_id=1, source_target_pairs={{0,1},{1,2},{2,3},{3,4},{4,5},{5,6},{6,7},{7,0},{8,9},{9,10},{10,1... | collective-permute-start | bytes 1572872 | tf_op jit(solution)/shard_map/ppermute | solution.py:229
  3.3 22.8 %collective-permute-start.10 = (bf16[2,128,1024]{2,1,0:T(8,128)(2,1)S(1)}, bf16[2,128,1024]{2,1,0:T(8,128)(2,1)}, u32[]{:S(2)}, u32[]{:S(2)}) collective-permute-start(bf16[2,128,1024]{2,1,0:T(8,128)(2,1)S(1)} %get-tuple-element.99.refs_0_), channel_id=1, source_target_pairs={{1,0},{2,1},{3,2},{4,3},{5,4},{6,5},{7,6},{0,7},{9,8},{10,9},{11,1... | collective-permute-start | bytes 1572872 | tf_op jit(solution)/shard_map/ppermute | solution.py:231
  14.8 46.0 %collective-permute-start.5 = (bf16[2,128,1024]{2,1,0:T(8,128)(2,1)}, bf16[2,128,1024]{2,1,0:T(8,128)(2,1)S(1)}, u32[]{:S(2)}, u32[]{:S(2)}) collective-permute-start(bf16[2,128,1024]{2,1,0:T(8,128)(2,1)} %collective-permute-done.3.refs_1_), channel_id=1, source_target_pairs={{1,0},{2,1},{3,2},{4,3},{5,4},{6,5},{7,6},{0,7},{9,8},{10,9},{11,1... | collective-permute-start | bytes 1572872 | tf_op jit(solution)/shard_map/ppermute | solution.py:231
  18.2 42.6 %collective-permute-start.6 = (bf16[2,128,1024]{2,1,0:T(8,128)(2,1)}, bf16[2,128,1024]{2,1,0:T(8,128)(2,1)S(1)}, u32[]{:S(2)}, u32[]{:S(2)}) collective-permute-start(bf16[2,128,1024]{2,1,0:T(8,128)(2,1)} %collective-permute-done.4.refs_7_), channel_id=1, source_target_pairs={{0,1},{1,2},{2,3},{3,4},{4,5},{5,6},{6,7},{7,0},{8,9},{9,10},{10,1... | collective-permute-start | bytes 1572872 | tf_op jit(solution)/shard_map/ppermute | solution.py:229
  18.2 45.8 %collective-permute-start.14 = (bf16[2,128,1024]{2,1,0:T(8,128)(2,1)S(1)}, bf16[2,128,1024]{2,1,0:T(8,128)(2,1)S(1)}, u32[]{:S(2)}, u32[]{:S(2)}) collective-permute-start(bf16[2,128,1024]{2,1,0:T(8,128)(2,1)S(1)} %get-tuple-element.99.refs_0_), channel_id=1, source_target_pairs={{0,1},{1,2},{2,3},{3,4},{4,5},{5,6},{6,7},{7,0},{8,9},{9,10},{10,1... | collective-permute-start | bytes 1572872 | tf_op jit(solution)/shard_map/ppermute | solution.py:229
  26.0 41.3 %collective-permute-start.11 = (bf16[2,128,1024]{2,1,0:T(8,128)(2,1)}, bf16[2,128,1024]{2,1,0:T(8,128)(2,1)S(1)}, u32[]{:S(2)}, u32[]{:S(2)}) collective-permute-start(bf16[2,128,1024]{2,1,0:T(8,128)(2,1)} %collective-permute-done.10.refs_1_), channel_id=1, source_target_pairs={{1,0},{2,1},{3,2},{4,3},{5,4},{6,5},{7,6},{0,7},{9,8},{10,9},{11,1... | collective-permute-start | bytes 1572872 | tf_op jit(solution)/shard_map/ppermute | solution.py:231
  26.1 33.6 %collective-permute-start = (f32[4,1024]{0,1:T(8,128)}, f32[4,1024]{0,1:T(8,128)S(1)}, u32[]{:S(2)}, u32[]{:S(2)}) collective-permute-start(f32[4,1024]{0,1:T(8,128)} %bitcast.23), channel_id=1, source_target_pairs={{0,1},{1,0},{2,3},{3,2},{4,5},{5,4},{6,7},{7,6},{8,9},{9,8},{10,11... | collective-permute-start | bytes 49160 | tf_op jit(solution)/shard_map/ppermute | solution.py:260
  60.8 44.8 %collective-permute-start.7 = (bf16[2,128,1024]{2,1,0:T(8,128)(2,1)S(1)}, bf16[2,128,1024]{2,1,0:T(8,128)(2,1)S(1)}, u32[]{:S(2)}, u32[]{:S(2)}) collective-permute-start(bf16[2,128,1024]{2,1,0:T(8,128)(2,1)S(1)} %collective-permute-done.5.refs_2_), channel_id=1, source_target_pairs={{1,0},{2,1},{3,2},{4,3},{5,4},{6,5},{7,6},{0,7},{9,8},{10,9},{11,1... | collective-permute-start | bytes 1572872 | tf_op jit(solution)/shard_map/ppermute | solution.py:231
  61.7 44.8 %collective-permute-start.8 = (bf16[2,128,1024]{2,1,0:T(8,128)(2,1)S(1)}, bf16[2,128,1024]{2,1,0:T(8,128)(2,1)}, u32[]{:S(2)}, u32[]{:S(2)}) collective-permute-start(bf16[2,128,1024]{2,1,0:T(8,128)(2,1)S(1)} %collective-permute-done.6.refs_6_), channel_id=1, source_target_pairs={{0,1},{1,2},{2,3},{3,4},{4,5},{5,6},{6,7},{7,0},{8,9},{9,10},{10,1... | collective-permute-start | bytes 1572872 | tf_op jit(solution)/shard_map/ppermute | solution.py:229
  64.0 46.5 %collective-permute-start.15 = (bf16[2,128,1024]{2,1,0:T(8,128)(2,1)S(1)}, bf16[2,128,1024]{2,1,0:T(8,128)(2,1)}, u32[]{:S(2)}, u32[]{:S(2)}) collective-permute-start(bf16[2,128,1024]{2,1,0:T(8,128)(2,1)S(1)} %collective-permute-done.14.refs_7_), channel_id=1, source_target_pairs={{0,1},{1,2},{2,3},{3,4},{4,5},{5,6},{6,7},{7,0},{8,9},{9,10},{10,1... | collective-permute-start | bytes 1572872 | tf_op jit(solution)/shard_map/ppermute | solution.py:229
  67.4 44.9 %collective-permute-start.12 = (bf16[2,128,1024]{2,1,0:T(8,128)(2,1)S(1)}, bf16[2,128,1024]{2,1,0:T(8,128)(2,1)}, u32[]{:S(2)}, u32[]{:S(2)}) collective-permute-start(bf16[2,128,1024]{2,1,0:T(8,128)(2,1)S(1)} %collective-permute-done.11.refs_2_), channel_id=1, source_target_pairs={{1,0},{2,1},{3,2},{4,3},{5,4},{6,5},{7,6},{0,7},{9,8},{10,9},{11,1... | collective-permute-start | bytes 1572872 | tf_op jit(solution)/shard_map/ppermute | solution.py:231
  67.4 37.3 %collective-permute-start.1 = (f32[4,1024]{0,1:T(8,128)S(1)}, f32[4,1024]{0,1:T(8,128)S(1)}, u32[]{:S(2)}, u32[]{:S(2)}) collective-permute-start(f32[4,1024]{0,1:T(8,128)S(1)} %bitcast_add_fusion), channel_id=1, source_target_pairs={{0,2},{1,3},{2,0},{3,1},{4,6},{5,7},{6,4},{7,5},{8,10},{9,11},{10,... | collective-permute-start | bytes 49160 | tf_op jit(solution)/shard_map/ppermute | solution.py:260
  106.5 53.3 %collective-permute-start.9 = (bf16[2,128,1024]{2,1,0:T(8,128)(2,1)}, bf16[2,128,1024]{2,1,0:T(8,128)(2,1)}, u32[]{:S(2)}, u32[]{:S(2)}) collective-permute-start(bf16[2,128,1024]{2,1,0:T(8,128)(2,1)} %collective-permute-done.8.refs_5_), channel_id=1, source_target_pairs={{0,1},{1,2},{2,3},{3,4},{4,5},{5,6},{6,7},{7,0},{8,9},{9,10},{10,1... | collective-permute-start | bytes 1572872 | tf_op jit(solution)/shard_map/ppermute | solution.py:229
  110.4 56.2 %collective-permute-start.16 = (bf16[2,128,1024]{2,1,0:T(8,128)(2,1)}, bf16[2,128,1024]{2,1,0:T(8,128)(2,1)}, u32[]{:S(2)}, u32[]{:S(2)}) collective-permute-start(bf16[2,128,1024]{2,1,0:T(8,128)(2,1)} %collective-permute-done.15.refs_6_), channel_id=1, source_target_pairs={{0,1},{1,2},{2,3},{3,4},{4,5},{5,6},{6,7},{7,0},{8,9},{9,10},{10,1... | collective-permute-start | bytes 1572872 | tf_op jit(solution)/shard_map/ppermute | solution.py:229
  112.3 54.3 %collective-permute-start.13 = (bf16[2,128,1024]{2,1,0:T(8,128)(2,1)}, bf16[2,128,1024]{2,1,0:T(8,128)(2,1)}, u32[]{:S(2)}, u32[]{:S(2)}) collective-permute-start(bf16[2,128,1024]{2,1,0:T(8,128)(2,1)} %collective-permute-done.12.refs_3_), channel_id=1, source_target_pairs={{1,0},{2,1},{3,2},{4,3},{5,4},{6,5},{7,6},{0,7},{9,8},{10,9},{11,1... | collective-permute-start | bytes 1572872 | tf_op jit(solution)/shard_map/ppermute | solution.py:231
  112.3 46.1 %collective-permute-start.2 = (f32[4,1024]{0,1:T(8,128)}, f32[4,1024]{0,1:T(8,128)}, u32[]{:S(2)}, u32[]{:S(2)}) collective-permute-start(f32[4,1024]{0,1:T(8,128)} %add.29), channel_id=1, source_target_pairs={{0,4},{1,5},{2,6},{3,7},{4,0},{5,1},{6,2},{7,3},{8,12},{9,13},{10,... | collective-permute-start | bytes 49160 | tf_op jit(solution)/shard_map/ppermute | solution.py:260
  179.7 8.7 %collective-permute-start.17 = (bf16[1040,1024]{1,0:T(8,128)(2,1)}, bf16[1040,1024]{1,0:T(8,128)(2,1)}, u32[]{:S(2)}, u32[]{:S(2)}) collective-permute-start(bf16[1040,1024]{1,0:T(8,128)(2,1)} %get-tuple-element.59.own_ref), channel_id=1, source_target_pairs={{0,8},{16,24},{32,40},{48,56},{64,72},{80,88},{96,104},{112,120},{... | collective-permute-start | bytes 6389768 | tf_op jit(solution)/shard_map/ppermute | solution.py:292
  193.5 6.7 %collective-permute-start.19 = (f32[1,1024]{1,0:T(1,128)S(1)}, f32[1,1024]{1,0:T(1,128)S(1)}, u32[]{:S(2)}, u32[]{:S(2)}) collective-permute-start(f32[1,1024]{1,0:T(1,128)S(1)} %get-tuple-element.63.after_ref), channel_id=1, source_target_pairs={{24,40},{25,41},{26,42},{27,43},{28,44},{29,45},{30,46},{31,47}} | collective-permute-start | bytes 12296 | tf_op jit(solution)/shard_map/ppermute | solution.py:295
  200.3 0.7 collective-permute-start.20
  201.0 0.7 collective-permute-start.21
  201.7 0.7 collective-permute-start.22
  202.4 0.7 collective-permute-start.23
  203.1 0.7 collective-permute-start.24
  203.8 0.7 collective-permute-start.25
  204.7 0.7 collective-permute-start.26
  205.4 0.7 collective-permute-start.27
  206.1 0.7 collective-permute-start.28
  206.8 0.7 collective-permute-start.29
  207.5 0.7 collective-permute-start.30
  209.0 38.7 %collective-permute-start.32 = (f32[1,1024]{1,0:T(1,128)S(1)}, f32[1,1024]{1,0:T(1,128)S(1)}, u32[]{:S(2)}, u32[]{:S(2)}) collective-permute-start(f32[1,1024]{1,0:T(1,128)S(1)} %get-tuple-element.91), channel_id=1, source_target_pairs={{232,248},{233,249},{234,250},{235,251},{236,252},{237,253},{238,2... | collective-permute-start | bytes 12296 | tf_op jit(solution)/shard_map/ppermute | solution.py:295
  248.6 5.1 %collective-permute-start.33 = (f32[1,1024]{1,0:T(1,128)S(1)}, f32[1,1024]{1,0:T(1,128)S(1)}, u32[]{:S(2)}, u32[]{:S(2)}) collective-permute-start(f32[1,1024]{1,0:T(1,128)S(1)} %get-tuple-element.92.begin_ref), channel_id=1, source_target_pairs={{8,0},{24,16},{40,32},{56,48},{72,64},{88,80},{104,96},{120,112},{... | collective-permute-start | bytes 12296 | tf_op jit(solution)/shard_map/ppermute | solution.py:322
  (20 other events, 274.8 us)

commit v3 on v2

v3 whole, which is shorter than its diff:
```python
import functools

import jax
import jax.numpy as jnp
from jax import lax
from jax.experimental import pallas as pl
from jax.experimental.pallas import tpu as pltpu
from jax.sharding import PartitionSpec as P

F32 = jnp.float32
BF16 = jnp.bfloat16
VMEM_LIMIT = 24 * 1024 * 1024
ROWS = 512


def three_parts(x):
    hi = x.astype(BF16).astype(F32)
    rest = x - hi
    mid = rest.astype(BF16).astype(F32)
    return hi, mid, rest - mid


def split_rows(x):
    hi, mid, lo = three_parts(x)
    row = lax.broadcasted_iota(jnp.int32, (16, x.shape[1]), 0)
    out = jnp.where(row == 0, hi, jnp.where(row == 1, mid, jnp.where(row == 2, lo, 0.0)))
    return out.astype(BF16)


def joined(rows):
    return jnp.sum(rows.astype(F32), axis=0, keepdims=True)


def times_t(x, matrix):
    out = lax.dot_general(split_rows(x), matrix, (((1,), (1,)), ((), ())), preferred_element_type=F32)
    return joined(out)


def times(x, matrix):
    return joined(jnp.dot(split_rows(x), matrix, preferred_element_type=F32))


def matmul(left_ref, right_ref, out_ref):
    def block(i, carry):
        at = pl.ds(pl.multiple_of(i * ROWS, ROWS), ROWS)
        out_ref[at, :] = jnp.dot(left_ref[at, :], right_ref[...], preferred_element_type=F32).astype(BF16)
        return carry

    lax.fori_loop(0, left_ref.shape[0] // ROWS, block, 0)


def core_here():
    return lax.rem(lax.axis_index("tm"), 2)


def chip_here():
    return lax.div(lax.axis_index("tm"), 2)


def drive_kernel(rows_ref, cols_ref, observations_ref, precisions_ref, blocks_ref, drive_ref, weighted_ref):
    steps, count, side, _ = blocks_ref.shape
    weighted_ref[...] = (precisions_ref[...] * observations_ref[...]).astype(BF16).astype(F32)
    drive_ref[...] = jnp.zeros_like(drive_ref)
    for t in range(steps):
        def block(b, carry):
            left = jnp.broadcast_to(weighted_ref[t, pl.ds(rows_ref[t, b], 1), :], (16, side)).astype(BF16)
            term = jnp.dot(left, blocks_ref[t, b], preferred_element_type=F32)
            at = pl.ds(cols_ref[t, b], 1)
            drive_ref[t, at, :] = drive_ref[t, at, :] + term[0:1, :]
            return carry

        lax.fori_loop(0, count, block, 0, unroll=4)


def add_kernel(one_ref, other_ref, out_ref):
    out_ref[...] = one_ref[...] + other_ref[...]


def row_of(drive_ref, j, row_ref):
    side = drive_ref.shape[2]
    for c in range(drive_ref.shape[1]):
        row_ref[0:1, c * side:(c + 1) * side] = drive_ref[j, c:c + 1, :]
    return row_ref[0:1, :]


def fetched(count, place, pieces, j, whole_ref, sems, first):
    width = pieces[0].shape[1]
    copies = []
    for r in range(count):
        at = pl.multiple_of(lax.rem(place + r, count) * width, width)
        copy = pltpu.make_async_copy(pieces[r].at[j], whole_ref.at[pl.ds(at, width), :], sems.at[first + r])
        copy.start()
        copies.append(copy)
    return copies


def two_kernel(count, drive_ref, *refs):
    pieces = refs[:count]
    two_ref, slab_ref, locals_ref, one_ref, next_ref, row_ref, sems = refs[count:]
    width = slab_ref.shape[0]
    place = lax.axis_index("state")
    ones = fetched(count, place, pieces, 0, one_ref, sems, 0)
    nexts = fetched(count, place, pieces, 1, next_ref, sems, count)
    for copy in ones + nexts:
        copy.wait()
    matmul(next_ref, one_ref, two_ref)
    slab_ref[...] = two_ref[pl.ds(pl.multiple_of(place * width, width), width), :]
    first = row_of(drive_ref, 0, row_ref)
    locals_ref[0:1, :] = first
    locals_ref[1:2, :] = times_t(first, next_ref[...]) + row_of(drive_ref, 1, row_ref)


def four_kernel(count, two_ref, *refs):
    pieces = refs[:count]
    four_ref, slab3_ref, slab4_ref, third_ref, fourth_ref, three_ref, sems = refs[count:]
    width = slab3_ref.shape[0]
    place = lax.axis_index("state")
    thirds = fetched(count, place, pieces, 0, third_ref, sems, 0)
    fourths = fetched(count, place, pieces, 1, fourth_ref, sems, count)
    mine = pl.ds(pl.multiple_of(place * width, width), width)
    for copy in thirds:
        copy.wait()
    matmul(third_ref, two_ref, three_ref)
    slab3_ref[...] = three_ref[mine, :]
    for copy in fourths:
        copy.wait()
    matmul(fourth_ref, three_ref, four_ref)
    slab4_ref[...] = four_ref[mine, :]


def local_kernel(drive_ref, before_ref, third_ref, fourth_ref, locals_ref, term_ref, row_ref):
    locals_ref[0:2, :] = before_ref[0:2, :]
    local = times_t(before_ref[1:2, :], third_ref[...]) + row_of(drive_ref, 2, row_ref)
    locals_ref[2:3, :] = local
    local = times_t(local, fourth_ref[...]) + row_of(drive_ref, 3, row_ref)
    locals_ref[3:4, :] = local
    term_ref[...] = split_rows(local)


def pair_kernel(own_ref, own_term_ref, other_ref, other_term_ref, after_ref, qt_ref, q_ref):
    @pl.when(core_here() != 0)
    def _():
        def block(i, carry):
            at = pl.ds(pl.multiple_of(i * ROWS, ROWS), ROWS)
            out = jnp.dot(own_ref[at, :], other_ref[...], preferred_element_type=F32)
            qt_ref[:, at] = out.T.astype(BF16)
            return carry

        lax.fori_loop(0, own_ref.shape[0] // ROWS, block, 0)
        q_ref[...] = times_t(joined(other_term_ref[...]), own_ref[...]) + joined(own_term_ref[...])


def early_hop_kernel(
    turn, begin_ref, came_ref, own_ref, own_term_ref, other_ref, other_term_ref, held_ref, value_ref
):
    held_ref[...] = begin_ref[...]
    value_ref[...] = begin_ref[...]

    @pl.when(jnp.logical_and(chip_here() == turn, core_here() != 0))
    def _():
        begin = came_ref[...] if turn > 0 else begin_ref[...]
        held_ref[...] = begin
        between = times_t(begin, other_ref[...]) + joined(other_term_ref[...])
        value_ref[...] = times_t(between, own_ref[...]) + joined(own_term_ref[...])


def hop_kernel(turn, begin_ref, came_ref, qt_ref, q_ref, held_ref, value_ref):
    here = jnp.logical_and(chip_here() == turn, core_here() != 0)

    @pl.when(here)
    def _():
        begin = came_ref[...]
        held_ref[...] = begin
        value_ref[...] = times(begin, qt_ref[...]) + q_ref[...]

    @pl.when(jnp.logical_not(here))
    def _():
        held_ref[...] = begin_ref[...]
        value_ref[...] = begin_ref[...]


def ready_kernel(other_ref, other_term_ref, locals_ref, after_ref, maps0_ref, *refs):
    slabs, (maps_ref, terms_ref) = (maps0_ref.at[0],) + refs[:-2], refs[-2:]
    width = slabs[0].shape[0]
    mine = pl.ds(pl.multiple_of(lax.axis_index("state") * width, width), width)
    for j, slab_ref in enumerate(slabs):
        at = slice(j * width, (j + 1) * width)

        @pl.when(core_here() == 0)
        def _():
            maps_ref[:, at] = slab_ref[...].astype(F32).T.astype(BF16)
            terms_ref[j:j + 1, :] = locals_ref[j:j + 1, mine]

        @pl.when(core_here() != 0)
        def _():
            out = jnp.dot(slab_ref[...], other_ref[...], preferred_element_type=F32)
            maps_ref[:, at] = out.T.astype(BF16)
            term = times_t(joined(other_term_ref[...]), slab_ref[...])
            terms_ref[j:j + 1, :] = term + locals_ref[j:j + 1, mine]


def out_kernel(begin_ref, got_ref, maps_ref, terms_ref, out_ref):
    steps, width = out_ref.shape
    begin = jnp.where(core_here() == 0, got_ref[...], begin_ref[...])
    row = times(begin, maps_ref[...])
    for j in range(steps):
        out_ref[j:j + 1, :] = row[:, j * width:(j + 1) * width] + terms_ref[j:j + 1, :]


def call(kernel, out_shape, spaces, scratch=(), flops=0, moved=0):
    return pl.pallas_call(
        kernel,
        out_shape=out_shape,
        in_specs=[pl.BlockSpec(memory_space=s) for s in spaces],
        out_specs=jax.tree.map(lambda _: pl.BlockSpec(memory_space=pltpu.VMEM), out_shape),
        scratch_shapes=list(scratch),
        compiler_params=pltpu.CompilerParams(vmem_limit_bytes=VMEM_LIMIT),
        cost_estimate=pl.CostEstimate(flops=flops, bytes_accessed=moved, transcendentals=0),
    )


def after(value, *needed):
    return lax.optimization_barrier((value, needed))[0]


def ring_rounds(parts, axis, needed):
    count = lax.axis_size(axis)
    forward = [(i, (i + 1) % count) for i in range(count)]
    backward = [((i + 1) % count, i) for i in range(count)]
    half = count // 2
    found = [{0: part} for part in parts]
    for r in range(1, half + 1):
        for i, pieces in enumerate(found):
            left, right = pieces[(count - r + 1) % count], pieces[r - 1]
            more = needed(r, i, found)
            if more:
                left, right = after((left, right), *more)
            if r < half or i % 2 == 0:
                pieces[count - r] = lax.ppermute(left, axis, forward)
            if r < half or i % 2 == 1:
                pieces[r] = lax.ppermute(right, axis, backward)
    return [[pieces[r] for r in range(count)] for pieces in found]


def shards(observations, precisions, blocks, block_rows, block_cols, transition, prior):
    steps_here, width, size = transition.shape
    side = blocks.shape[2]
    count = lax.axis_size("state")
    blocks_of_time = lax.axis_size("tm")
    V, S, A = pltpu.VMEM, pltpu.SMEM, pl.ANY

    matrix = jax.ShapeDtypeStruct((size, size), BF16)
    slab = jax.ShapeDtypeStruct((width, size), BF16)
    rows = jax.ShapeDtypeStruct((16, size), BF16)
    steps = jax.ShapeDtypeStruct((steps_here, size), F32)
    row = jax.ShapeDtypeStruct((1, size), F32)
    whole = pltpu.VMEM((size, size), BF16)
    single = pltpu.VMEM((1, size), F32)
    semaphores = pltpu.SemaphoreType.DMA((2 * count,))

    pieces = (steps_here, observations.shape[1] // side, side)
    parts = jax.ShapeDtypeStruct((steps_here, size // side, side), F32)
    drive = call(
        drive_kernel, parts, [S, S, V, V, V], [pltpu.VMEM(pieces, F32)], flops=10 ** 7, moved=2 ** 21
    )(block_rows, block_cols, observations.reshape(pieces), precisions.reshape(pieces), blocks)

    def added(drive, bit):
        came = lax.ppermute(drive, "state", [(i, i ^ bit) for i in range(count)])
        return call(add_kernel, parts, [V, V], flops=4096, moved=2 ** 16)(drive, came)

    drive1 = added(drive, 1)
    drive2 = added(drive1, 2)
    drive4 = added(drive2, 4)
    needs = {(2, 0): drive, (3, 0): drive1, (4, 0): drive2}

    def needed(r, i, found):
        return (needs[r, i],) if (r, i) in needs else ()

    early, late = ring_rounds([transition[:2], transition[2:]], "state", needed)
    two, slab2, before = call(
        functools.partial(two_kernel, count), (matrix, slab, steps), [V] + [A] * count,
        [whole, whole, single, semaphores], flops=2 * size ** 3, moved=6 * size ** 2,
    )(drive4, *early)
    own, slab3, slab4, third, fourth = call(
        functools.partial(four_kernel, count), (matrix, slab, slab, matrix, matrix), [V] + [A] * count,
        [whole, semaphores], flops=4 * size ** 3, moved=8 * size ** 2,
    )(two, *late)

    swap = [(i, i + 1) for i in range(0, blocks_of_time, 2)]
    other = lax.ppermute(own, "tm", swap)
    locals_, own_term = call(
        local_kernel, (steps, rows), [V] * 4, [single], flops=64 * size ** 2, moved=4 * size ** 2
    )(drive4, before, third, fourth)
    other_term = lax.ppermute(own_term, "tm", swap)

    def hop(value, turn):
        return lax.ppermute(value, "tm", [(2 * turn + 1, 2 * turn + 3)])

    begin = prior.reshape(1, size)
    came = begin
    chips = blocks_of_time // 2
    for turn in range(2):
        begin, value = call(
            functools.partial(early_hop_kernel, turn), (row, row), [V] * 6,
            flops=64 * size ** 2, moved=4 * size ** 2,
        )(begin, came, own, own_term, other, other_term)
        came = hop(value, turn)
    turned, term = call(
        pair_kernel, (matrix, row), [V] * 5, flops=2 * size ** 3, moved=6 * size ** 2
    )(own, own_term, other, other_term, value)
    for turn in range(2, chips):
        begin, value = call(
            functools.partial(hop_kernel, turn), (row, row), [V] * 4,
            flops=32 * size ** 2, moved=2 * size ** 2,
        )(begin, came, turned, term)
        if turn == 2:
            maps, terms = call(
                ready_kernel,
                (jax.ShapeDtypeStruct((size, steps_here * width), BF16), jax.ShapeDtypeStruct((steps_here, width), F32)),
                [V] * 8, flops=size ** 3, moved=4 * size ** 2,
            )(other, other_term, locals_, value, early[0], slab2, slab3, slab4)
        if turn + 1 < chips:
            came = hop(value, turn)
    got = lax.ppermute(begin, "tm", [(i + 1, i) for i in range(0, blocks_of_time, 2)])
    return call(
        out_kernel, jax.ShapeDtypeStruct((steps_here, width), F32), [V] * 4,
        flops=16 * size ** 2, moved=size ** 2,
    )(begin, got, maps, terms)


def solution(mesh):
    return jax.shard_map(
        shards,
        mesh=mesh,
        in_specs=(
            P("tm", None),
            P("tm", None),
            P("tm", "state", None, None),
            P("tm", "state"),
            P("tm", "state"),
            P("tm", "state", None),
            P(),
        ),
        out_specs=P("tm", "state"),
        check_vma=False,
    )
```

time: 255 us -> 182 us (0.71)
  the two profiles are of different devices: /device:TPU:95 before, /device:TPU:30 now
where the time goes in v3:
time: 182 us; the launch traced here: 180 us
  waiting for transfers between devices  112 us (62%)
  starting transfers between devices  45.6 us (25%)
  Pallas kernels  19.7 us (11%)
    ppermute x3, waiting for transfers between devices, added(): came = lax.ppermute(drive, 'state', [(i, i ^ bit) for i in range(count)])  54.3 us
    ppermute x1, waiting for transfers between devices, shards(): lax.ppermute(begin, 'tm', [(i + 1, i) for i in range(0, blocks_of_time, 2)])  44.1 us
    ppermute x7, starting transfers between devices, ring_rounds(): pieces[r] = lax.ppermute(right, axis, backward)  21.6 us
    ppermute x15, starting transfers between devices, hop(): return lax.ppermute(value, 'tm', [(2 * turn + 1, 2 * turn + 3)])  9.91 us
    ppermute x7, waiting for transfers between devices, ring_rounds(): pieces[r] = lax.ppermute(right, axis, backward)  7.83 us
    pallas_call x1, Pallas kernels, shards(): call(functools.partial(four_kernel, count), (matrix, slab, slab, matrix,...  6.2 us
    ppermute x7, starting transfers between devices, ring_rounds(): pieces[count - r] = lax.ppermute(left, axis, forward)  5.39 us
    pallas_call x1, Pallas kernels, shards(): call(drive_kernel, parts, [S, S, V, V, V], [pltpu.VMEM(pieces, F32)], flo...  4.99 us
  transfers between devices with their start and end apart: 35, of which 8 were waited for; matrix products, arithmetic and copies ran while one was open for 0% of the time, Pallas kernels for 6%

profile of v3, /device:TPU:30, one launch (start us, length us, event | category | flops | bytes accessed | tf_op | source)
XLA Modules:
  0.0 179.6 jit_solution(6326147992679083082)
XLA Ops:
  0.0 1.4 fusion
  1.5 2.0 %collective-permute-start.4 = (bf16[2,128,1024]{2,1,0:T(8,128)(2,1)S(1)}, bf16[2,128,1024]{2,1,0:T(8,128)(2,1)}, u32[]{:S(2)}, u32[]{:S(2)}) collective-permute-start(bf16[2,128,1024]{2,1,0:T(8,128)(2,1)S(1)} %get-tuple-element.106.refs_0_.maps0_ref), channel_id=1, source_target_pairs={{0,1},{1,2},{2,3},{3,4},{4,5},{5,6},{6,7},{7,0},{8,9},{9,10},{10,1... | collective-permute-start | bytes 1572872 | tf_op jit(solution)/shard_map/ppermute | solution.py:239
  3.4 4.0 %collective-permute-start.3 = (bf16[2,128,1024]{2,1,0:T(8,128)(2,1)S(1)}, bf16[2,128,1024]{2,1,0:T(8,128)(2,1)}, u32[]{:S(2)}, u32[]{:S(2)}) collective-permute-start(bf16[2,128,1024]{2,1,0:T(8,128)(2,1)S(1)} %get-tuple-element.106.refs_0_.maps0_ref), channel_id=1, source_target_pairs={{1,0},{2,1},{3,2},{4,3},{5,4},{6,5},{7,6},{0,7},{9,8},{10,9},{11,1... | collective-permute-start | bytes 1572872 | tf_op jit(solution)/shard_map/ppermute | solution.py:241
  7.5 1.9 %collective-permute-start.10 = (bf16[2,128,1024]{2,1,0:T(8,128)(2,1)S(1)}, bf16[2,128,1024]{2,1,0:T(8,128)(2,1)}, u32[]{:S(2)}, u32[]{:S(2)}) collective-permute-start(bf16[2,128,1024]{2,1,0:T(8,128)(2,1)S(1)} %get-tuple-element.105.refs_0_), channel_id=1, source_target_pairs={{1,0},{2,1},{3,2},{4,3},{5,4},{6,5},{7,6},{0,7},{9,8},{10,9},{11,1... | collective-permute-start | bytes 1572872 | tf_op jit(solution)/shard_map/ppermute | solution.py:241
  9.7 5.0 %shard_map.73.one_ref = f32[4,16,64]{2,1,0:T(8,128)S(1)} custom-call(s32[4,32]{1,0:T(4,128)S(1)} %copy-done.2, s32[4,32]{1,0:T(4,128)S(1)} %copy-done.3, f32[4,64,64]{2,1,0:T(8,128)S(1)} %reshape.10.observations_ref, f32[4,64,64]{2,1,0:T(8,128)S(1)} %reshape.11.precisions_ref, bf16[4,32,64,64]{3,2,1,0:T(8,128)(2,1)S(1)} %copy-done), custom_call_target="tpu_custom_call" | custom-call | flops 10000000 | bytes 2097152 | tf_op jit(solution)/shard_map/pallas_call | solution.py:263
  14.7 4.7 %collective-permute-done.4.refs_7_ = bf16[2,128,1024]{2,1,0:T(8,128)(2,1)} collective-permute-done((bf16[2,128,1024]{2,1,0:T(8,128)(2,1)S(1)}, bf16[2,128,1024]{2,1,0:T(8,128)(2,1)}, u32[]{:S(2)}, u32[]{:S(2)}) %collective-permute-start.4) | collective-permute-done | bytes 524320 | tf_op jit(solution)/shard_map/ppermute | solution.py:239
  19.8 3.8 %collective-permute-start.5 = (bf16[2,128,1024]{2,1,0:T(8,128)(2,1)}, bf16[2,128,1024]{2,1,0:T(8,128)(2,1)S(1)}, u32[]{:S(2)}, u32[]{:S(2)}) collective-permute-start(bf16[2,128,1024]{2,1,0:T(8,128)(2,1)} %collective-permute-done.3.refs_1_), channel_id=1, source_target_pairs={{1,0},{2,1},{3,2},{4,3},{5,4},{6,5},{7,6},{0,7},{9,8},{10,9},{11,1... | collective-permute-start | bytes 1572872 | tf_op jit(solution)/shard_map/ppermute | solution.py:241
  23.6 7.4 %collective-permute-done.10.refs_1_ = bf16[2,128,1024]{2,1,0:T(8,128)(2,1)} collective-permute-done((bf16[2,128,1024]{2,1,0:T(8,128)(2,1)S(1)}, bf16[2,128,1024]{2,1,0:T(8,128)(2,1)}, u32[]{:S(2)}, u32[]{:S(2)}) %collective-permute-start.10) | collective-permute-done | bytes 524320 | tf_op jit(solution)/shard_map/ppermute | solution.py:241
  31.0 3.8 %collective-permute-start.11 = (bf16[2,128,1024]{2,1,0:T(8,128)(2,1)}, bf16[2,128,1024]{2,1,0:T(8,128)(2,1)S(1)}, u32[]{:S(2)}, u32[]{:S(2)}) collective-permute-start(bf16[2,128,1024]{2,1,0:T(8,128)(2,1)} %collective-permute-done.10.refs_1_), channel_id=1, source_target_pairs={{1,0},{2,1},{3,2},{4,3},{5,4},{6,5},{7,6},{0,7},{9,8},{10,9},{11,1... | collective-permute-start | bytes 1572872 | tf_op jit(solution)/shard_map/ppermute | solution.py:241
  34.8 16.6 %collective-permute-done.other_ref = f32[4,16,64]{2,1,0:T(8,128)S(1)} collective-permute-done((f32[4,16,64]{2,1,0:T(8,128)S(1)}, f32[4,16,64]{2,1,0:T(8,128)S(1)}, u32[]{:S(2)}, u32[]{:S(2)}) %collective-permute-start) | collective-permute-done | bytes 16416 | tf_op jit(solution)/shard_map/ppermute | solution.py:268
  51.4 3.4 %collective-permute-start.7 = (bf16[2,128,1024]{2,1,0:T(8,128)(2,1)S(1)}, bf16[2,128,1024]{2,1,0:T(8,128)(2,1)S(1)}, u32[]{:S(2)}, u32[]{:S(2)}) collective-permute-start(bf16[2,128,1024]{2,1,0:T(8,128)(2,1)S(1)} %collective-permute-done.5.refs_2_), channel_id=1, source_target_pairs={{1,0},{2,1},{3,2},{4,3},{5,4},{6,5},{7,6},{0,7},{9,8},{10,9},{11,1... | collective-permute-start | bytes 1572872 | tf_op jit(solution)/shard_map/ppermute | solution.py:241
  54.8 1.8 %collective-permute-start.15 = (bf16[2,128,1024]{2,1,0:T(8,128)(2,1)S(1)}, bf16[2,128,1024]{2,1,0:T(8,128)(2,1)S(1)}, u32[]{:S(2)}, u32[]{:S(2)}) collective-permute-start(bf16[2,128,1024]{2,1,0:T(8,128)(2,1)S(1)} %collective-permute-done.14.refs_7_), channel_id=1, source_target_pairs={{0,1},{1,2},{2,3},{3,4},{4,5},{5,6},{6,7},{7,0},{8,9},{9,10},{10,1... | collective-permute-start | bytes 1572872 | tf_op jit(solution)/shard_map/ppermute | solution.py:239
  56.7 1.5 collective-permute-start.12
  58.1 1.9 %collective-permute-start.1 = (f32[4,16,64]{2,1,0:T(8,128)S(1)}, f32[4,16,64]{2,1,0:T(8,128)S(1)}, u32[]{:S(2)}, u32[]{:S(2)}) collective-permute-start(f32[4,16,64]{2,1,0:T(8,128)S(1)} %shard_map.74.one_ref), channel_id=1, source_target_pairs={{0,2},{1,3},{2,0},{3,1},{4,6},{5,7},{6,4},{7,5},{8,10},{9,11},{10,... | collective-permute-start | bytes 49160 | tf_op jit(solution)/shard_map/ppermute | solution.py:268
  60.1 19.3 %collective-permute-done.1.other_ref = f32[4,16,64]{2,1,0:T(8,128)S(1)} collective-permute-done((f32[4,16,64]{2,1,0:T(8,128)S(1)}, f32[4,16,64]{2,1,0:T(8,128)S(1)}, u32[]{:S(2)}, u32[]{:S(2)}) %collective-permute-start.1) | collective-permute-done | bytes 16416 | tf_op jit(solution)/shard_map/ppermute | solution.py:268
  79.4 1.5 collective-permute-start.9
  80.9 3.1 %collective-permute-start.13 = (bf16[2,128,1024]{2,1,0:T(8,128)(2,1)S(1)}, bf16[2,128,1024]{2,1,0:T(8,128)(2,1)S(1)}, u32[]{:S(2)}, u32[]{:S(2)}) collective-permute-start(bf16[2,128,1024]{2,1,0:T(8,128)(2,1)S(1)} %collective-permute-done.12.refs_3_), channel_id=1, source_target_pairs={{1,0},{2,1},{3,2},{4,3},{5,4},{6,5},{7,6},{0,7},{9,8},{10,9},{11,1... | collective-permute-start | bytes 1572872 | tf_op jit(solution)/shard_map/ppermute | solution.py:241
  84.1 2.8 %collective-permute-start.2 = (f32[4,16,64]{2,1,0:T(8,128)S(1)}, f32[4,16,64]{2,1,0:T(8,128)S(1)}, u32[]{:S(2)}, u32[]{:S(2)}) collective-permute-start(f32[4,16,64]{2,1,0:T(8,128)S(1)} %shard_map.75.one_ref), channel_id=1, source_target_pairs={{0,4},{1,5},{2,6},{3,7},{4,0},{5,1},{6,2},{7,3},{8,12},{9,13},{10,... | collective-permute-start | bytes 49160 | tf_op jit(solution)/shard_map/ppermute | solution.py:268
  86.9 18.4 %collective-permute-done.2.other_ref = f32[4,16,64]{2,1,0:T(8,128)S(1)} collective-permute-done((f32[4,16,64]{2,1,0:T(8,128)S(1)}, f32[4,16,64]{2,1,0:T(8,128)S(1)}, u32[]{:S(2)}, u32[]{:S(2)}) %collective-permute-start.2) | collective-permute-done | bytes 16416 | tf_op jit(solution)/shard_map/ppermute | solution.py:268
  105.3 4.7 %shard_map.77 = (bf16[1024,1024]{1,0:T(8,128)(2,1)S(1)}, bf16[128,1024]{1,0:T(8,128)(2,1)S(1)}, f32[4,1024]{1,0:T(4,128)S(1)}) custom-call(f32[4,16,64]{2,1,0:T(8,128)S(1)} %shard_map.76.drive_ref, bf16[2,128,1024]{2,1,0:T(8,128)(2,1)S(1)} %get-tuple-element.106.refs_0_.maps0_ref, bf16[2,128,1024]{2,1,0:T(8,128)(2,1)} %collective-permute-done.3.refs_1_, ...), custom_call_target="tpu_custom_call" | custom-call | flops 2147483648 | bytes 6291456 | tf_op jit(solution)/shard_map/pallas_call | solution.py:280
  110.0 6.2 %shard_map.78 = (bf16[1024,1024]{1,0:T(8,128)(2,1)S(1)}, bf16[128,1024]{1,0:T(8,128)(2,1)S(1)}, bf16[128,1024]{1,0:T(8,128)(2,1)S(1)}, bf16[1024,1024]{1,0:T(8,128)(2,1)S(1)}, bf16[1024,1024]{1,0:T(8,128)(2,1)S(1)}) custom-call(bf16[1024,1024]{1,0:T(8,128)(2,1)S(1)} %get-tuple-element.60.two_ref, bf16[2,128,1024]{2,1,0:T(8,128)(2,1)S(1)} %get-tuple-element.105.refs_0_, ...), custom_call_target="tpu_custom_call" | custom-call | flops 4294967296 | bytes 8388608 | tf_op jit(solution)/shard_map/pallas_call | solution.py:284
  116.2 1.4 collective-permute-start.17
  117.6 1.2 shard_map.79
  118.9 1.3 collective-permute-start.18
  120.2 1.1 collective-permute-done.18.other_term_ref
  122.0 0.7 collective-permute-start.20
  122.8 0.7 collective-permute-start.21
  123.5 0.7 collective-permute-start.22
  124.2 0.7 collective-permute-start.23
  132.8 1.3 collective-permute-start.34
  134.7 44.1 %collective-permute-done.34.got_ref = f32[1,1024]{1,0:T(1,128)S(1)} collective-permute-done((f32[1,1024]{1,0:T(1,128)S(1)}, f32[1,1024]{1,0:T(1,128)S(1)}, u32[]{:S(2)}, u32[]{:S(2)}) %collective-permute-start.34) | collective-permute-done | bytes 4128 | tf_op jit(solution)/shard_map/ppermute | solution.py:324
  178.7 0.8 shard_map.98
  (79 shorter events, 9.9 us)
Async XLA Ops:
  1.5 18.0 %collective-permute-start.4 = (bf16[2,128,1024]{2,1,0:T(8,128)(2,1)S(1)}, bf16[2,128,1024]{2,1,0:T(8,128)(2,1)}, u32[]{:S(2)}, u32[]{:S(2)}) collective-permute-start(bf16[2,128,1024]{2,1,0:T(8,128)(2,1)S(1)} %get-tuple-element.106.refs_0_.maps0_ref), channel_id=1, source_target_pairs={{0,1},{1,2},{2,3},{3,4},{4,5},{5,6},{6,7},{7,0},{8,9},{9,10},{10,1... | collective-permute-start | bytes 1572872 | tf_op jit(solution)/shard_map/ppermute | solution.py:239
  3.4 16.4 %collective-permute-start.3 = (bf16[2,128,1024]{2,1,0:T(8,128)(2,1)S(1)}, bf16[2,128,1024]{2,1,0:T(8,128)(2,1)}, u32[]{:S(2)}, u32[]{:S(2)}) collective-permute-start(bf16[2,128,1024]{2,1,0:T(8,128)(2,1)S(1)} %get-tuple-element.106.refs_0_.maps0_ref), channel_id=1, source_target_pairs={{1,0},{2,1},{3,2},{4,3},{5,4},{6,5},{7,6},{0,7},{9,8},{10,9},{11,1... | collective-permute-start | bytes 1572872 | tf_op jit(solution)/shard_map/ppermute | solution.py:241
  7.5 23.6 %collective-permute-start.10 = (bf16[2,128,1024]{2,1,0:T(8,128)(2,1)S(1)}, bf16[2,128,1024]{2,1,0:T(8,128)(2,1)}, u32[]{:S(2)}, u32[]{:S(2)}) collective-permute-start(bf16[2,128,1024]{2,1,0:T(8,128)(2,1)S(1)} %get-tuple-element.105.refs_0_), channel_id=1, source_target_pairs={{1,0},{2,1},{3,2},{4,3},{5,4},{6,5},{7,6},{0,7},{9,8},{10,9},{11,1... | collective-permute-start | bytes 1572872 | tf_op jit(solution)/shard_map/ppermute | solution.py:241
  19.8 31.6 %collective-permute-start.5 = (bf16[2,128,1024]{2,1,0:T(8,128)(2,1)}, bf16[2,128,1024]{2,1,0:T(8,128)(2,1)S(1)}, u32[]{:S(2)}, u32[]{:S(2)}) collective-permute-start(bf16[2,128,1024]{2,1,0:T(8,128)(2,1)} %collective-permute-done.3.refs_1_), channel_id=1, source_target_pairs={{1,0},{2,1},{3,2},{4,3},{5,4},{6,5},{7,6},{0,7},{9,8},{10,9},{11,1... | collective-permute-start | bytes 1572872 | tf_op jit(solution)/shard_map/ppermute | solution.py:241
  23.6 27.8 %collective-permute-start.6 = (bf16[2,128,1024]{2,1,0:T(8,128)(2,1)}, bf16[2,128,1024]{2,1,0:T(8,128)(2,1)S(1)}, u32[]{:S(2)}, u32[]{:S(2)}) collective-permute-start(bf16[2,128,1024]{2,1,0:T(8,128)(2,1)} %collective-permute-done.4.refs_7_), channel_id=1, source_target_pairs={{0,1},{1,2},{2,3},{3,4},{4,5},{5,6},{6,7},{7,0},{8,9},{9,10},{10,1... | collective-permute-start | bytes 1572872 | tf_op jit(solution)/shard_map/ppermute | solution.py:239
  23.6 31.2 %collective-permute-start.14 = (bf16[2,128,1024]{2,1,0:T(8,128)(2,1)S(1)}, bf16[2,128,1024]{2,1,0:T(8,128)(2,1)S(1)}, u32[]{:S(2)}, u32[]{:S(2)}) collective-permute-start(bf16[2,128,1024]{2,1,0:T(8,128)(2,1)S(1)} %get-tuple-element.105.refs_0_), channel_id=1, source_target_pairs={{0,1},{1,2},{2,3},{3,4},{4,5},{5,6},{6,7},{7,0},{8,9},{9,10},{10,1... | collective-permute-start | bytes 1572872 | tf_op jit(solution)/shard_map/ppermute | solution.py:239
  31.0 25.6 %collective-permute-start.11 = (bf16[2,128,1024]{2,1,0:T(8,128)(2,1)}, bf16[2,128,1024]{2,1,0:T(8,128)(2,1)S(1)}, u32[]{:S(2)}, u32[]{:S(2)}) collective-permute-start(bf16[2,128,1024]{2,1,0:T(8,128)(2,1)} %collective-permute-done.10.refs_1_), channel_id=1, source_target_pairs={{1,0},{2,1},{3,2},{4,3},{5,4},{6,5},{7,6},{0,7},{9,8},{10,9},{11,1... | collective-permute-start | bytes 1572872 | tf_op jit(solution)/shard_map/ppermute | solution.py:241
  34.8 16.6 %collective-permute-start = (f32[4,16,64]{2,1,0:T(8,128)S(1)}, f32[4,16,64]{2,1,0:T(8,128)S(1)}, u32[]{:S(2)}, u32[]{:S(2)}) collective-permute-start(f32[4,16,64]{2,1,0:T(8,128)S(1)} %shard_map.73.one_ref), channel_id=1, source_target_pairs={{0,1},{1,0},{2,3},{3,2},{4,5},{5,4},{6,7},{7,6},{8,9},{9,8},{10,11... | collective-permute-start | bytes 49160 | tf_op jit(solution)/shard_map/ppermute | solution.py:268
  51.4 27.9 %collective-permute-start.7 = (bf16[2,128,1024]{2,1,0:T(8,128)(2,1)S(1)}, bf16[2,128,1024]{2,1,0:T(8,128)(2,1)S(1)}, u32[]{:S(2)}, u32[]{:S(2)}) collective-permute-start(bf16[2,128,1024]{2,1,0:T(8,128)(2,1)S(1)} %collective-permute-done.5.refs_2_), channel_id=1, source_target_pairs={{1,0},{2,1},{3,2},{4,3},{5,4},{6,5},{7,6},{0,7},{9,8},{10,9},{11,1... | collective-permute-start | bytes 1572872 | tf_op jit(solution)/shard_map/ppermute | solution.py:241
  54.8 24.5 %collective-permute-start.8 = (bf16[2,128,1024]{2,1,0:T(8,128)(2,1)S(1)}, bf16[2,128,1024]{2,1,0:T(8,128)(2,1)S(1)}, u32[]{:S(2)}, u32[]{:S(2)}) collective-permute-start(bf16[2,128,1024]{2,1,0:T(8,128)(2,1)S(1)} %collective-permute-done.6.refs_6_), channel_id=1, source_target_pairs={{0,1},{1,2},{2,3},{3,4},{4,5},{5,6},{6,7},{7,0},{8,9},{9,10},{10,1... | collective-permute-start | bytes 1572872 | tf_op jit(solution)/shard_map/ppermute | solution.py:239
  54.8 26.0 %collective-permute-start.15 = (bf16[2,128,1024]{2,1,0:T(8,128)(2,1)S(1)}, bf16[2,128,1024]{2,1,0:T(8,128)(2,1)S(1)}, u32[]{:S(2)}, u32[]{:S(2)}) collective-permute-start(bf16[2,128,1024]{2,1,0:T(8,128)(2,1)S(1)} %collective-permute-done.14.refs_7_), channel_id=1, source_target_pairs={{0,1},{1,2},{2,3},{3,4},{4,5},{5,6},{6,7},{7,0},{8,9},{9,10},{10,1... | collective-permute-start | bytes 1572872 | tf_op jit(solution)/shard_map/ppermute | solution.py:239
  56.7 24.3 %collective-permute-start.12 = (bf16[2,128,1024]{2,1,0:T(8,128)(2,1)S(1)}, bf16[2,128,1024]{2,1,0:T(8,128)(2,1)S(1)}, u32[]{:S(2)}, u32[]{:S(2)}) collective-permute-start(bf16[2,128,1024]{2,1,0:T(8,128)(2,1)S(1)} %collective-permute-done.11.refs_2_), channel_id=1, source_target_pairs={{1,0},{2,1},{3,2},{4,3},{5,4},{6,5},{7,6},{0,7},{9,8},{10,9},{11,1... | collective-permute-start | bytes 1572872 | tf_op jit(solution)/shard_map/ppermute | solution.py:241
  58.1 21.2 %collective-permute-start.1 = (f32[4,16,64]{2,1,0:T(8,128)S(1)}, f32[4,16,64]{2,1,0:T(8,128)S(1)}, u32[]{:S(2)}, u32[]{:S(2)}) collective-permute-start(f32[4,16,64]{2,1,0:T(8,128)S(1)} %shard_map.74.one_ref), channel_id=1, source_target_pairs={{0,2},{1,3},{2,0},{3,1},{4,6},{5,7},{6,4},{7,5},{8,10},{9,11},{10,... | collective-permute-start | bytes 49160 | tf_op jit(solution)/shard_map/ppermute | solution.py:268
  79.4 25.9 %collective-permute-start.9 = (bf16[2,128,1024]{2,1,0:T(8,128)(2,1)S(1)}, bf16[2,128,1024]{2,1,0:T(8,128)(2,1)S(1)}, u32[]{:S(2)}, u32[]{:S(2)}) collective-permute-start(bf16[2,128,1024]{2,1,0:T(8,128)(2,1)S(1)} %collective-permute-done.8.refs_5_), channel_id=1, source_target_pairs={{0,1},{1,2},{2,3},{3,4},{4,5},{5,6},{6,7},{7,0},{8,9},{9,10},{10,1... | collective-permute-start | bytes 1572872 | tf_op jit(solution)/shard_map/ppermute | solution.py:239
  80.8 29.1 %collective-permute-start.16 = (bf16[2,128,1024]{2,1,0:T(8,128)(2,1)S(1)}, bf16[2,128,1024]{2,1,0:T(8,128)(2,1)S(1)}, u32[]{:S(2)}, u32[]{:S(2)}) collective-permute-start(bf16[2,128,1024]{2,1,0:T(8,128)(2,1)S(1)} %collective-permute-done.15.refs_6_), channel_id=1, source_target_pairs={{0,1},{1,2},{2,3},{3,4},{4,5},{5,6},{6,7},{7,0},{8,9},{9,10},{10,1... | collective-permute-start | bytes 1572872 | tf_op jit(solution)/shard_map/ppermute | solution.py:239
  80.9 29.0 %collective-permute-start.13 = (bf16[2,128,1024]{2,1,0:T(8,128)(2,1)S(1)}, bf16[2,128,1024]{2,1,0:T(8,128)(2,1)S(1)}, u32[]{:S(2)}, u32[]{:S(2)}) collective-permute-start(bf16[2,128,1024]{2,1,0:T(8,128)(2,1)S(1)} %collective-permute-done.12.refs_3_), channel_id=1, source_target_pairs={{1,0},{2,1},{3,2},{4,3},{5,4},{6,5},{7,6},{0,7},{9,8},{10,9},{11,1... | collective-permute-start | bytes 1572872 | tf_op jit(solution)/shard_map/ppermute | solution.py:241
  84.1 21.2 %collective-permute-start.2 = (f32[4,16,64]{2,1,0:T(8,128)S(1)}, f32[4,16,64]{2,1,0:T(8,128)S(1)}, u32[]{:S(2)}, u32[]{:S(2)}) collective-permute-start(f32[4,16,64]{2,1,0:T(8,128)S(1)} %shard_map.75.one_ref), channel_id=1, source_target_pairs={{0,4},{1,5},{2,6},{3,7},{4,0},{5,1},{6,2},{7,3},{8,12},{9,13},{10,... | collective-permute-start | bytes 49160 | tf_op jit(solution)/shard_map/ppermute | solution.py:268
  116.2 5.1 %collective-permute-start.17 = (bf16[1024,1024]{1,0:T(8,128)(2,1)S(1)}, bf16[1024,1024]{1,0:T(8,128)(2,1)S(1)}, u32[]{:S(2)}, u32[]{:S(2)}) collective-permute-start(bf16[1024,1024]{1,0:T(8,128)(2,1)S(1)} %get-tuple-element.61.own_ref), channel_id=1, source_target_pairs={{0,8},{16,24},{32,40},{48,56},{64,72},{80,88},{96,104},{112,120},{... | collective-permute-start | bytes 6291464 | tf_op jit(solution)/shard_map/ppermute | solution.py:290
  118.9 2.4 %collective-permute-start.18 = (bf16[16,1024]{1,0:T(8,128)(2,1)S(1)}, bf16[16,1024]{1,0:T(8,128)(2,1)S(1)}, u32[]{:S(2)}, u32[]{:S(2)}) collective-permute-start(bf16[16,1024]{1,0:T(8,128)(2,1)S(1)} %get-tuple-element.65.own_term_ref), channel_id=1, source_target_pairs={{0,8},{16,24},{32,40},{48,56},{64,72},{80,88},{96,104},{112,120},{... | collective-permute-start | bytes 98312 | tf_op jit(solution)/shard_map/ppermute | solution.py:294
  122.0 0.7 collective-permute-start.20
  122.8 0.7 collective-permute-start.21
  123.5 0.7 collective-permute-start.22
  124.2 0.7 collective-permute-start.23
  124.9 0.7 collective-permute-start.24
  125.6 0.7 collective-permute-start.25
  126.3 0.7 collective-permute-start.26
  127.0 0.7 collective-permute-start.27
  127.7 0.7 collective-permute-start.28
  128.4 0.7 collective-permute-start.29
  130.8 0.7 collective-permute-start.32
  131.5 0.7 collective-permute-start.33
  132.8 45.9 %collective-permute-start.34 = (f32[1,1024]{1,0:T(1,128)S(1)}, f32[1,1024]{1,0:T(1,128)S(1)}, u32[]{:S(2)}, u32[]{:S(2)}) collective-permute-start(f32[1,1024]{1,0:T(1,128)S(1)} %get-tuple-element.98.begin_ref), channel_id=1, source_target_pairs={{8,0},{24,16},{40,32},{56,48},{72,64},{88,80},{104,96},{120,112},{... | collective-permute-start | bytes 12296 | tf_op jit(solution)/shard_map/ppermute | solution.py:324
  (9 other events, 53.6 us)

commit v4 on v3

v4 whole, which is shorter than its diff:
```python
import functools

import jax
import jax.numpy as jnp
from jax import lax
from jax.experimental import pallas as pl
from jax.experimental.pallas import tpu as pltpu
from jax.sharding import PartitionSpec as P

F32 = jnp.float32
BF16 = jnp.bfloat16
VMEM_LIMIT = 24 * 1024 * 1024
ROWS = 512


def three_parts(x):
    hi = x.astype(BF16).astype(F32)
    rest = x - hi
    mid = rest.astype(BF16).astype(F32)
    return hi, mid, rest - mid


def split_rows(x):
    hi, mid, lo = three_parts(x)
    row = lax.broadcasted_iota(jnp.int32, (16, x.shape[1]), 0)
    out = jnp.where(row == 0, hi, jnp.where(row == 1, mid, jnp.where(row == 2, lo, 0.0)))
    return out.astype(BF16)


def joined(rows):
    return jnp.sum(rows.astype(F32), axis=0, keepdims=True)


def times_t(x, matrix):
    out = lax.dot_general(split_rows(x), matrix, (((1,), (1,)), ((), ())), preferred_element_type=F32)
    return joined(out)


def times(x, matrix):
    return joined(jnp.dot(split_rows(x), matrix, preferred_element_type=F32))


def matmul(left_ref, right_ref, out_ref):
    def block(i, carry):
        at = pl.ds(pl.multiple_of(i * ROWS, ROWS), ROWS)
        out_ref[at, :] = jnp.dot(left_ref[at, :], right_ref[...], preferred_element_type=F32).astype(BF16)
        return carry

    lax.fori_loop(0, left_ref.shape[0] // ROWS, block, 0)


def core_here():
    return lax.rem(lax.axis_index("tm"), 2)


def chip_here():
    return lax.div(lax.axis_index("tm"), 2)


def drive_kernel(
    rows_ref, cols_ref, observations_ref, precisions_ref, blocks_ref, maps_ref, out_ref, weighted_ref, drive_ref, parts_ref, sems
):
    steps, count, side, _ = blocks_ref.shape
    width = maps_ref.shape[1]
    copies = []
    for j in range(steps // 2):
        rows = pl.ds(j * width, width)
        copies.append(pltpu.make_async_copy(maps_ref.at[steps // 2 + j], out_ref.at[rows, :], sems.at[j]))
        copies[j].start()
    weighted_ref[...] = (precisions_ref[...] * observations_ref[...]).astype(BF16).astype(F32)
    drive_ref[...] = jnp.zeros_like(drive_ref)
    parts_ref[...] = jnp.zeros_like(parts_ref)
    for t in range(steps):
        def block(b, carry):
            left = jnp.broadcast_to(weighted_ref[t, pl.ds(rows_ref[t, b], 1), :], (16, side)).astype(BF16)
            term = jnp.dot(left, blocks_ref[t, b], preferred_element_type=F32)
            at = pl.ds(cols_ref[t, b], 1)
            drive_ref[t, at, :] = drive_ref[t, at, :] + term[0:1, :]
            return carry

        lax.fori_loop(0, count, block, 0, unroll=4)
    for t in range(steps):
        for c in range(drive_ref.shape[1]):
            for i, part in enumerate(three_parts(drive_ref[t, c:c + 1, :])):
                parts_ref[3 * t + i:3 * t + i + 1, c * side:(c + 1) * side] = part
    out_ref[(steps // 2) * width:, :] = parts_ref[...].astype(BF16)
    for copy in copies:
        copy.wait()


def fetched(count, place, pieces, j, whole_ref, sems, first):
    width = whole_ref.shape[0] // count
    copies = []
    for r in range(count):
        at = pl.multiple_of(lax.rem(place + r, count) * width, width)
        copy = pltpu.make_async_copy(
            pieces[r].at[pl.ds(j * width, width), :], whole_ref.at[pl.ds(at, width), :], sems.at[first + r]
        )
        copy.start()
        copies.append(copy)
    return copies


def two_kernel(count, *refs):
    pieces, (two_ref, slab_ref, next_ref, one_ref, sems) = refs[:count], refs[count:]
    width = slab_ref.shape[0]
    place = lax.axis_index("state")
    ones = fetched(count, place, pieces, 0, one_ref, sems, 0)
    nexts = fetched(count, place, pieces, 1, next_ref, sems, count)
    for copy in ones + nexts:
        copy.wait()
    matmul(next_ref, one_ref, two_ref)
    slab_ref[...] = two_ref[pl.ds(pl.multiple_of(place * width, width), width), :]


def four_kernel(count, two_ref, *refs):
    pieces = refs[:count]
    four_ref, slab3_ref, slab4_ref, third_ref, fourth_ref, drive_ref, three_ref, parts_ref, sems = refs[count:]
    width = slab3_ref.shape[0]
    place = lax.axis_index("state")
    thirds = fetched(count, place, pieces, 0, third_ref, sems, 0)
    fourths = fetched(count, place, pieces, 1, fourth_ref, sems, count)
    parts = []
    for r in range(count):
        parts.append(pltpu.make_async_copy(pieces[r].at[pl.ds(2 * width, 16), :], parts_ref.at[r], sems.at[2 * count + r]))
        parts[r].start()
    mine = pl.ds(pl.multiple_of(place * width, width), width)
    for copy in thirds:
        copy.wait()
    matmul(third_ref, two_ref, three_ref)
    slab3_ref[...] = three_ref[mine, :]
    for copy in fourths:
        copy.wait()
    matmul(fourth_ref, three_ref, four_ref)
    slab4_ref[...] = four_ref[mine, :]
    for copy in parts:
        copy.wait()
    drive_ref[...] = jnp.sum(parts_ref[...].astype(F32), axis=0)


def local_kernel(drive_ref, prior_ref, second_ref, third_ref, fourth_ref, four_ref, locals_ref, term_ref, mean_ref):
    local = joined(drive_ref[0:3, :])
    locals_ref[0:1, :] = local
    for j, map_ref in enumerate((second_ref, third_ref, fourth_ref)):
        local = times_t(local, map_ref[...]) + joined(drive_ref[3 * j + 3:3 * j + 6, :])
        locals_ref[j + 1:j + 2, :] = local
    term_ref[...] = split_rows(local)
    mean_ref[...] = local

    @pl.when(lax.axis_index("tm") == 0)
    def _():
        mean_ref[...] = times_t(prior_ref[...], four_ref[...]) + local


def pair_kernel(own_ref, own_term_ref, other_ref, other_term_ref, after_ref, qt_ref, q_ref):
    @pl.when(core_here() != 0)
    def _():
        def block(i, carry):
            at = pl.ds(pl.multiple_of(i * ROWS, ROWS), ROWS)
            out = jnp.dot(own_ref[at, :], other_ref[...], preferred_element_type=F32)
            qt_ref[:, at] = out.T.astype(BF16)
            return carry

        lax.fori_loop(0, own_ref.shape[0] // ROWS, block, 0)
        q_ref[...] = times_t(joined(other_term_ref[...]), own_ref[...]) + joined(own_term_ref[...])


def first_hop_kernel(mean_ref, own_ref, term_ref, value_ref):
    value_ref[...] = mean_ref[...]

    @pl.when(lax.axis_index("tm") == 1)
    def _():
        value_ref[...] = times_t(mean_ref[...], own_ref[...]) + joined(term_ref[...])


def second_hop_kernel(begin_ref, came_ref, own_ref, own_term_ref, other_ref, other_term_ref, held_ref, value_ref):
    held_ref[...] = begin_ref[...]
    value_ref[...] = begin_ref[...]

    @pl.when(lax.axis_index("tm") == 3)
    def _():
        begin = came_ref[...]
        held_ref[...] = begin
        between = times_t(begin, other_ref[...]) + joined(other_term_ref[...])
        value_ref[...] = times_t(between, own_ref[...]) + joined(own_term_ref[...])


def hop_kernel(turn, begin_ref, came_ref, qt_ref, q_ref, held_ref, value_ref):
    here = jnp.logical_and(chip_here() == turn, core_here() != 0)

    @pl.when(here)
    def _():
        begin = came_ref[...]
        held_ref[...] = begin
        value_ref[...] = times(begin, qt_ref[...]) + q_ref[...]

    @pl.when(jnp.logical_not(here))
    def _():
        held_ref[...] = begin_ref[...]
        value_ref[...] = begin_ref[...]


def ready_kernel(other_ref, other_term_ref, other0_ref, other0_term_ref, locals_ref, after_ref, *refs):
    slabs, (maps_ref, terms_ref) = refs[:-2], refs[-2:]
    width, size = slabs[1].shape
    mine = pl.ds(pl.multiple_of(lax.axis_index("state") * width, width), width)

    def write(whole_ref, term_ref):
        for j, slab_ref in enumerate(slabs):
            at = slice(j * width, (j + 1) * width)
            out = jnp.dot(slab_ref[:width, :], whole_ref[...], preferred_element_type=F32)
            maps_ref[:, at] = out.T.astype(BF16)
            term = times_t(joined(term_ref[...]), slab_ref[:width, :])
            terms_ref[j:j + 1, :] = term + locals_ref[j:j + 1, mine]

    @pl.when(core_here() == 0)
    def _():
        for j, slab_ref in enumerate(slabs):
            maps_ref[:, j * width:(j + 1) * width] = slab_ref[:width, :].astype(F32).T.astype(BF16)
            terms_ref[j:j + 1, :] = locals_ref[j:j + 1, mine]

    @pl.when(lax.axis_index("tm") == 1)
    def _():
        write(other0_ref, other0_term_ref)

    @pl.when(jnp.logical_and(core_here() != 0, lax.axis_index("tm") != 1))
    def _():
        write(other_ref, other_term_ref)


def out_kernel(last, begin_ref, came_ref, got_ref, last_ref, maps_ref, terms_ref, out_ref):
    steps, width = out_ref.shape
    first, second = (got_ref[...], last_ref[...]), (begin_ref[...], came_ref[...])
    at_last = chip_here() == last
    begin = jnp.where(
        core_here() == 0, jnp.where(at_last, first[1], first[0]), jnp.where(at_last, second[1], second[0])
    )
    row = times(begin, maps_ref[...])
    for j in range(steps):
        out_ref[j:j + 1, :] = row[:, j * width:(j + 1) * width] + terms_ref[j:j + 1, :]


def call(kernel, out_shape, spaces, scratch=(), flops=0, moved=0):
    return pl.pallas_call(
        kernel,
        out_shape=out_shape,
        in_specs=[pl.BlockSpec(memory_space=s) for s in spaces],
        out_specs=jax.tree.map(lambda _: pl.BlockSpec(memory_space=pltpu.VMEM), out_shape),
        scratch_shapes=list(scratch),
        compiler_params=pltpu.CompilerParams(vmem_limit_bytes=VMEM_LIMIT),
        cost_estimate=pl.CostEstimate(flops=flops, bytes_accessed=moved, transcendentals=0),
    )


def after(value, *needed):
    return lax.optimization_barrier((value, needed))[0]


def ring_rounds(parts, axis, needed):
    count = lax.axis_size(axis)
    forward = [(i, (i + 1) % count) for i in range(count)]
    backward = [((i + 1) % count, i) for i in range(count)]
    half = count // 2
    found = [{0: part} for part in parts]
    for r in range(1, half + 1):
        for i, pieces in enumerate(found):
            left, right = pieces[(count - r + 1) % count], pieces[r - 1]
            more = needed(r, i, found)
            if more:
                left, right = after((left, right), *more)
            if r < half or i % 2 == 0:
                pieces[count - r] = lax.ppermute(left, axis, forward)
            if r < half or i % 2 == 1:
                pieces[r] = lax.ppermute(right, axis, backward)
    return [[pieces[r] for r in range(count)] for pieces in found]


def shards(observations, precisions, blocks, block_rows, block_cols, transition, prior):
    steps_here, width, size = transition.shape
    side = blocks.shape[2]
    count = lax.axis_size("state")
    blocks_of_time = lax.axis_size("tm")
    V, S, A = pltpu.VMEM, pltpu.SMEM, pl.ANY

    matrix = jax.ShapeDtypeStruct((size, size), BF16)
    slab = jax.ShapeDtypeStruct((width, size), BF16)
    rows = jax.ShapeDtypeStruct((16, size), BF16)
    steps = jax.ShapeDtypeStruct((steps_here, size), F32)
    row = jax.ShapeDtypeStruct((1, size), F32)
    whole = pltpu.VMEM((size, size), BF16)

    half = steps_here // 2
    pieces = (steps_here, observations.shape[1] // side, side)
    packed = call(
        drive_kernel, jax.ShapeDtypeStruct((half * width + 16, size), BF16), [S, S, V, V, V, A],
        [
            pltpu.VMEM(pieces, F32),
            pltpu.VMEM((steps_here, size // side, side), F32),
            pltpu.VMEM((16, size), F32),
            pltpu.SemaphoreType.DMA((half,)),
        ],
        flops=10 ** 7, moved=2 ** 21,
    )(block_rows, block_cols, observations.reshape(pieces), precisions.reshape(pieces), blocks, transition)
    early, late = ring_rounds(
        [transition[:half].reshape(half * width, size), packed], "state",
        lambda r, i, found: (packed,) if (r, i) == (2, 0) else (),
    )
    two, slab2, second = call(
        functools.partial(two_kernel, count), (matrix, slab, matrix), [A] * count,
        [whole, pltpu.SemaphoreType.DMA((2 * count,))], flops=2 * size ** 3, moved=6 * size ** 2,
    )(*early)
    own, slab3, slab4, third, fourth, drive = call(
        functools.partial(four_kernel, count),
        (matrix, slab, slab, matrix, matrix, jax.ShapeDtypeStruct((16, size), F32)),
        [V] + [A] * count,
        [whole, pltpu.VMEM((count, 16, size), BF16), pltpu.SemaphoreType.DMA((3 * count,))],
        flops=4 * size ** 3, moved=8 * size ** 2,
    )(two, *late)

    begin = prior.reshape(1, size)
    pairs = [(i, i + 1) for i in range(0, blocks_of_time, 2)]
    other = lax.ppermute(own, "tm", pairs[1:])
    locals_, own_term, mean = call(
        local_kernel, (steps, rows, row), [V] * 6, flops=128 * size ** 2, moved=8 * size ** 2
    )(drive, begin, second, third, fourth, own)
    mean = lax.ppermute(mean, "tm", pairs[:1])
    other_term = lax.ppermute(own_term, "tm", pairs[1:])

    def hop(value, turn):
        return lax.ppermute(value, "tm", [(2 * turn + 1, 2 * turn + 3)])

    chips = blocks_of_time // 2
    value = call(first_hop_kernel, row, [V] * 3, flops=32 * size ** 2, moved=2 * size ** 2)(mean, own, own_term)
    came = hop(value, 0)
    begin, value = call(
        second_hop_kernel, (row, row), [V] * 6, flops=64 * size ** 2, moved=4 * size ** 2
    )(begin, came, own, own_term, other, other_term)
    came = hop(value, 1)
    turned, term = call(
        pair_kernel, (matrix, row), [V] * 5, flops=2 * size ** 3, moved=6 * size ** 2
    )(own, own_term, other, other_term, value)
    for turn in range(2, chips - 1):
        begin, value = call(
            functools.partial(hop_kernel, turn), (row, row), [V] * 4,
            flops=32 * size ** 2, moved=2 * size ** 2,
        )(begin, came, turned, term)
        came = hop(value, turn)
        if turn == 2:
            other0, other0_term = lax.ppermute(after((own, own_term), value), "tm", pairs[:1])
        if turn == 3:
            maps, terms = call(
                ready_kernel,
                (jax.ShapeDtypeStruct((size, steps_here * width), BF16), jax.ShapeDtypeStruct((steps_here, width), F32)),
                [V] * 10, flops=size ** 3, moved=4 * size ** 2,
            )(other, other_term, other0, other0_term, locals_, value, early[0], slab2, slab3, slab4)
        if turn == 4:
            came = after(came, maps)
    got = lax.ppermute(begin, "tm", [(b, a) for a, b in pairs[:-1]])
    last = lax.ppermute(came, "tm", [(b, a) for a, b in pairs[-1:]])
    return call(
        functools.partial(out_kernel, chips - 1), jax.ShapeDtypeStruct((steps_here, width), F32), [V] * 6,
        flops=16 * size ** 2, moved=size ** 2,
    )(begin, came, got, last, maps, terms)


def solution(mesh):
    return jax.shard_map(
        shards,
        mesh=mesh,
        in_specs=(
            P("tm", None),
            P("tm", None),
            P("tm", "state", None, None),
            P("tm", "state"),
            P("tm", "state"),
            P("tm", "state", None),
            P(),
        ),
        out_specs=P("tm", "state"),
        check_vma=False,
    )
```

time: 182 us -> 163 us (0.90)
  waiting for transfers between devices: 112 us -> 93.6 us
  local copies, waits for them, and re-layouts: 1.7 us -> 6.06 us
  starting transfers between devices: 45.6 us -> 43.2 us
  Pallas kernels: 19.7 us -> 17.8 us
    ppermute x6 -> x7, waiting for transfers between devices: 99.5 us -> 42.7 us  [the longest x1 42.7 us: shards(): last = lax.ppermute(came, 'tm', [(b, a) for a, b in pairs[-1:]])]
    ppermute x7, waiting for transfers between devices: 4.75 us -> 26.8 us  [ring_rounds(): pieces[count - r] = lax.ppermute(left, axis, forward)]
    ppermute x7, waiting for transfers between devices: 7.83 us -> 24 us  [ring_rounds(): pieces[r] = lax.ppermute(right, axis, backward)]
    unnamed x12 -> x10, local copies, waits for them, and re-layouts: 0.03 us -> 2.96 us
    ppermute x6 -> x7, starting transfers between devices: 8.69 us -> 6.79 us  [the longest x2 1.46 us: shards(): lax.ppermute(after((own, own_term), value), 'tm', pairs[:1])]
    pallas_call x9 -> x6, Pallas kernels: 11.8 us -> 10.9 us  [the longest x1 5.22 us: shards(): call(drive_kernel, jax.ShapeDtypeStruct((half * width + 16, size), BF16),...]
  transfers between devices with their start and end apart: 35 -> 36, of which waited for: 8 -> 10; matrix products, arithmetic and copies ran while one was open for 0% -> 1% of each run, Pallas kernels for 6% -> 7%
where the time goes in v4:
time: 163 us; the launch traced here: 161 us
  waiting for transfers between devices  93.6 us (57%)
  starting transfers between devices  43.2 us (27%)
  Pallas kernels  17.8 us (11%)
  local copies, waits for them, and re-layouts  6.06 us (4%)
    ppermute x1, waiting for transfers between devices, shards(): last = lax.ppermute(came, 'tm', [(b, a) for a, b in pairs[-1:]])  42.7 us
    ppermute x7, waiting for transfers between devices, ring_rounds(): pieces[count - r] = lax.ppermute(left, axis, forward)  26.8 us
    ppermute x7, waiting for transfers between devices, ring_rounds(): pieces[r] = lax.ppermute(right, axis, backward)  24 us
    ppermute x7, starting transfers between devices, ring_rounds(): pieces[r] = lax.ppermute(right, axis, backward)  20.1 us
    ppermute x15, starting transfers between devices, hop(): return lax.ppermute(value, 'tm', [(2 * turn + 1, 2 * turn + 3)])  9.92 us
    ppermute x7, starting transfers between devices, ring_rounds(): pieces[count - r] = lax.ppermute(left, axis, forward)  6.4 us
    pallas_call x1, Pallas kernels, shards(): call(functools.partial(four_kernel, count), (matrix, slab, slab, matrix,...  6.04 us
    pallas_call x1, Pallas kernels, shards(): call(drive_kernel, jax.ShapeDtypeStruct((half * width + 16, size), BF16),...  5.22 us
  transfers between devices with their start and end apart: 36, of which 10 were waited for; matrix products, arithmetic and copies ran while one was open for 1% of the time, Pallas kernels for 7%

profile of v4, /device:TPU:30, one launch (start us, length us, event | category | flops | bytes accessed | tf_op | source)
XLA Modules:
  0.0 161.2 jit_solution(14855079016353515516)
XLA Ops:
  0.0 1.2 slice.3
  1.2 2.0 %collective-permute-start.1 = (bf16[256,1024]{1,0:T(8,128)(2,1)S(1)}, bf16[256,1024]{1,0:T(8,128)(2,1)S(1)}, u32[]{:S(2)}, u32[]{:S(2)}) collective-permute-start(bf16[256,1024]{1,0:T(8,128)(2,1)S(1)} %bitcast.2), channel_id=1, source_target_pairs={{0,1},{1,2},{2,3},{3,4},{4,5},{5,6},{6,7},{7,0},{8,9},{9,10},{10,1... | collective-permute-start | bytes 1572872 | tf_op jit(solution)/shard_map/ppermute | solution.py:272
  3.2 4.0 %collective-permute-start = (bf16[256,1024]{1,0:T(8,128)(2,1)S(1)}, bf16[256,1024]{1,0:T(8,128)(2,1)S(1)}, u32[]{:S(2)}, u32[]{:S(2)}) collective-permute-start(bf16[256,1024]{1,0:T(8,128)(2,1)S(1)} %bitcast.3), channel_id=1, source_target_pairs={{1,0},{2,1},{3,2},{4,3},{5,4},{6,5},{7,6},{0,7},{9,8},{10,9},{11,1... | collective-permute-start | bytes 1572872 | tf_op jit(solution)/shard_map/ppermute | solution.py:274
  7.2 1.0 reshape.14.observations_ref
  8.2 1.0 reshape.15.precisions_ref
  9.1 1.6 copy-done.1
  10.7 0.7 copy-done.3
  11.4 0.7 copy-done.4
  12.1 5.2 %shard_map.73.refs_0_ = bf16[272,1024]{1,0:T(8,128)(2,1)S(1)} custom-call(s32[4,32]{1,0:T(4,128)S(1)} %copy-done.3, s32[4,32]{1,0:T(4,128)S(1)} %copy-done.4, f32[4,64,64]{2,1,0:T(8,128)S(1)} %reshape.14.observations_ref, f32[4,64,64]{2,1,0:T(8,128)S(1)} %reshape.15.precisions_ref, bf16[4,32,64,64]{3,2,1,0:T(8,128)(2,1)S(1)} %copy-done.1, ...), custom_call_target="tpu_custom_call" | custom-call | flops 10000000 | bytes 2097152 | tf_op jit(solution)/shard_map/pallas_call | solution.py:294
  17.3 2.0 %collective-permute-start.7 = (bf16[272,1024]{1,0:T(8,128)(2,1)S(1)}, bf16[272,1024]{1,0:T(8,128)(2,1)S(1)}, u32[]{:S(2)}, u32[]{:S(2)}) collective-permute-start(bf16[272,1024]{1,0:T(8,128)(2,1)S(1)} %shard_map.73.refs_0_), channel_id=1, source_target_pairs={{1,0},{2,1},{3,2},{4,3},{5,4},{6,5},{7,6},{0,7},{9,8},{10,9},{11,1... | collective-permute-start | bytes 1671176 | tf_op jit(solution)/shard_map/ppermute | solution.py:274
  19.6 3.1 %collective-permute-start.11 = (bf16[272,1024]{1,0:T(8,128)(2,1)S(1)}, bf16[272,1024]{1,0:T(8,128)(2,1)S(1)}, u32[]{:S(2)}, u32[]{:S(2)}) collective-permute-start(bf16[272,1024]{1,0:T(8,128)(2,1)S(1)} %shard_map.73.refs_0_), channel_id=1, source_target_pairs={{0,1},{1,2},{2,3},{3,4},{4,5},{5,6},{6,7},{7,0},{8,9},{9,10},{10,1... | collective-permute-start | bytes 1671176 | tf_op jit(solution)/shard_map/ppermute | solution.py:272
  22.7 8.7 %collective-permute-done.7.refs_1_ = bf16[272,1024]{1,0:T(8,128)(2,1)S(1)} collective-permute-done((bf16[272,1024]{1,0:T(8,128)(2,1)S(1)}, bf16[272,1024]{1,0:T(8,128)(2,1)S(1)}, u32[]{:S(2)}, u32[]{:S(2)}) %collective-permute-start.7) | collective-permute-done | bytes 557088 | tf_op jit(solution)/shard_map/ppermute | solution.py:274
  31.5 2.9 %collective-permute-start.8 = (bf16[272,1024]{1,0:T(8,128)(2,1)S(1)}, bf16[272,1024]{1,0:T(8,128)(2,1)S(1)}, u32[]{:S(2)}, u32[]{:S(2)}) collective-permute-start(bf16[272,1024]{1,0:T(8,128)(2,1)S(1)} %collective-permute-done.7.refs_1_), channel_id=1, source_target_pairs={{1,0},{2,1},{3,2},{4,3},{5,4},{6,5},{7,6},{0,7},{9,8},{10,9},{11,1... | collective-permute-start | bytes 1671176 | tf_op jit(solution)/shard_map/ppermute | solution.py:274
  34.5 0.9 collective-permute-done.4.refs_6_
  35.4 1.0 collective-permute-start.5
  36.4 11.0 %collective-permute-done.11.refs_7_ = bf16[272,1024]{1,0:T(8,128)(2,1)S(1)} collective-permute-done((bf16[272,1024]{1,0:T(8,128)(2,1)S(1)}, bf16[272,1024]{1,0:T(8,128)(2,1)S(1)}, u32[]{:S(2)}, u32[]{:S(2)}) %collective-permute-start.11) | collective-permute-done | bytes 557088 | tf_op jit(solution)/shard_map/ppermute | solution.py:272
  47.4 3.7 %collective-permute-start.9 = (bf16[272,1024]{1,0:T(8,128)(2,1)S(1)}, bf16[272,1024]{1,0:T(8,128)(2,1)S(1)}, u32[]{:S(2)}, u32[]{:S(2)}) collective-permute-start(bf16[272,1024]{1,0:T(8,128)(2,1)S(1)} %collective-permute-done.8.refs_2_), channel_id=1, source_target_pairs={{1,0},{2,1},{3,2},{4,3},{5,4},{6,5},{7,6},{0,7},{9,8},{10,9},{11,1... | collective-permute-start | bytes 1671176 | tf_op jit(solution)/shard_map/ppermute | solution.py:274
  51.1 7.5 %collective-permute-done.2.refs_2_ = bf16[256,1024]{1,0:T(8,128)(2,1)S(1)} collective-permute-done((bf16[256,1024]{1,0:T(8,128)(2,1)S(1)}, bf16[256,1024]{1,0:T(8,128)(2,1)S(1)}, u32[]{:S(2)}, u32[]{:S(2)}) %collective-permute-start.2) | collective-permute-done | bytes 524320 | tf_op jit(solution)/shard_map/ppermute | solution.py:274
  58.7 3.7 %collective-permute-start.3 = (bf16[256,1024]{1,0:T(8,128)(2,1)S(1)}, bf16[256,1024]{1,0:T(8,128)(2,1)S(1)}, u32[]{:S(2)}, u32[]{:S(2)}) collective-permute-start(bf16[256,1024]{1,0:T(8,128)(2,1)S(1)} %collective-permute-done.2.refs_2_), channel_id=1, source_target_pairs={{1,0},{2,1},{3,2},{4,3},{5,4},{6,5},{7,6},{0,7},{9,8},{10,9},{11,1... | collective-permute-start | bytes 1572872 | tf_op jit(solution)/shard_map/ppermute | solution.py:274
  62.4 8.1 %collective-permute-done.12.refs_6_ = bf16[272,1024]{1,0:T(8,128)(2,1)S(1)} collective-permute-done((bf16[272,1024]{1,0:T(8,128)(2,1)S(1)}, bf16[272,1024]{1,0:T(8,128)(2,1)S(1)}, u32[]{:S(2)}, u32[]{:S(2)}) %collective-permute-start.12) | collective-permute-done | bytes 557088 | tf_op jit(solution)/shard_map/ppermute | solution.py:272
  70.6 3.7 %collective-permute-start.10 = (bf16[272,1024]{1,0:T(8,128)(2,1)S(1)}, bf16[272,1024]{1,0:T(8,128)(2,1)S(1)}, u32[]{:S(2)}, u32[]{:S(2)}) collective-permute-start(bf16[272,1024]{1,0:T(8,128)(2,1)S(1)} %collective-permute-done.9.refs_3_), channel_id=1, source_target_pairs={{1,0},{2,1},{3,2},{4,3},{5,4},{6,5},{7,6},{0,7},{9,8},{10,9},{11,1... | collective-permute-start | bytes 1671176 | tf_op jit(solution)/shard_map/ppermute | solution.py:274
  74.3 7.5 %collective-permute-done.3.refs_3_ = bf16[256,1024]{1,0:T(8,128)(2,1)S(1)} collective-permute-done((bf16[256,1024]{1,0:T(8,128)(2,1)S(1)}, bf16[256,1024]{1,0:T(8,128)(2,1)S(1)}, u32[]{:S(2)}, u32[]{:S(2)}) %collective-permute-start.3) | collective-permute-done | bytes 524320 | tf_op jit(solution)/shard_map/ppermute | solution.py:274
  81.8 3.0 %shard_map.74 = (bf16[1024,1024]{1,0:T(8,128)(2,1)S(1)}, bf16[128,1024]{1,0:T(8,128)(2,1)S(1)}, bf16[1024,1024]{1,0:T(8,128)(2,1)S(1)}) custom-call(bf16[256,1024]{1,0:T(8,128)(2,1)S(1)} %bitcast.4, bf16[256,1024]{1,0:T(8,128)(2,1)S(1)} %collective-permute-done.refs_1_, bf16[256,1024]{1,0:T(8,128)(2,1)S(1)} %collective-permute-done.2.refs_2_, ...), custom_call_target="tpu_custom_call" | custom-call | flops 2147483648 | bytes 6291456 | tf_op jit(solution)/shard_map/pallas_call | solution.py:308
  84.9 6.8 %collective-permute-done.13.refs_5_ = bf16[272,1024]{1,0:T(8,128)(2,1)S(1)} collective-permute-done((bf16[272,1024]{1,0:T(8,128)(2,1)S(1)}, bf16[272,1024]{1,0:T(8,128)(2,1)S(1)}, u32[]{:S(2)}, u32[]{:S(2)}) %collective-permute-start.13) | collective-permute-done | bytes 557088 | tf_op jit(solution)/shard_map/ppermute | solution.py:272
  91.7 6.0 %shard_map.75 = (bf16[1024,1024]{1,0:T(8,128)(2,1)S(1)}, bf16[128,1024]{1,0:T(8,128)(2,1)S(1)}, bf16[128,1024]{1,0:T(8,128)(2,1)S(1)}, bf16[1024,1024]{1,0:T(8,1...) custom-call(bf16[1024,1024]{1,0:T(8,128)(2,1)S(1)} %get-tuple-element.56.two_ref, ...), custom_call_target="tpu_custom_call" | custom-call | flops 4294967296 | bytes 8388608 | tf_op jit(solution)/shard_map/pallas_call | solution.py:312
  97.7 1.4 collective-permute-start.16
  99.2 1.8 %shard_map.76 = (f32[4,1024]{1,0:T(4,128)S(1)}, bf16[16,1024]{1,0:T(8,128)(2,1)S(1)}, f32[1,1024]{1,0:T(1,128)S(1)}) custom-call(f32[16,1024]{1,0:T(8,128)S(1)} %get-tuple-element.57.drive_ref, f32[1,1024]{1,0:T(1,128)S(1)} %bitcast.6, bf16[1024,1024]{1,0:T(8,128)(2,1)S(1)} %get-tuple-element.58.second_ref, ...), custom_call_target="tpu_custom_call" | custom-call | flops 134217728 | bytes 8388608 | tf_op jit(solution)/shard_map/pallas_call | solution.py:323
  100.9 1.3 collective-permute-start.17
  104.4 0.8 collective-permute-start.22
  116.4 1.3 collective-permute-start.35
  117.7 42.7 %collective-permute-done.35.last_ref = f32[1,1024]{1,0:T(1,128)S(1)} collective-permute-done((f32[1,1024]{1,0:T(1,128)S(1)}, f32[1,1024]{1,0:T(1,128)S(1)}, u32[]{:S(2)}, u32[]{:S(2)}) %collective-permute-start.35) | collective-permute-done | bytes 4128 | tf_op jit(solution)/shard_map/ppermute | solution.py:359
  160.4 0.8 shard_map.94
  (75 shorter events, 13.5 us)
Async XLA Ops:
  1.2 18.1 %collective-permute-start.1 = (bf16[256,1024]{1,0:T(8,128)(2,1)S(1)}, bf16[256,1024]{1,0:T(8,128)(2,1)S(1)}, u32[]{:S(2)}, u32[]{:S(2)}) collective-permute-start(bf16[256,1024]{1,0:T(8,128)(2,1)S(1)} %bitcast.2), channel_id=1, source_target_pairs={{0,1},{1,2},{2,3},{3,4},{4,5},{5,6},{6,7},{7,0},{8,9},{9,10},{10,1... | collective-permute-start | bytes 1572872 | tf_op jit(solution)/shard_map/ppermute | solution.py:272
  3.2 16.2 %collective-permute-start = (bf16[256,1024]{1,0:T(8,128)(2,1)S(1)}, bf16[256,1024]{1,0:T(8,128)(2,1)S(1)}, u32[]{:S(2)}, u32[]{:S(2)}) collective-permute-start(bf16[256,1024]{1,0:T(8,128)(2,1)S(1)} %bitcast.3), channel_id=1, source_target_pairs={{1,0},{2,1},{3,2},{4,3},{5,4},{6,5},{7,6},{0,7},{9,8},{10,9},{11,1... | collective-permute-start | bytes 1572872 | tf_op jit(solution)/shard_map/ppermute | solution.py:274
  17.3 14.2 %collective-permute-start.7 = (bf16[272,1024]{1,0:T(8,128)(2,1)S(1)}, bf16[272,1024]{1,0:T(8,128)(2,1)S(1)}, u32[]{:S(2)}, u32[]{:S(2)}) collective-permute-start(bf16[272,1024]{1,0:T(8,128)(2,1)S(1)} %shard_map.73.refs_0_), channel_id=1, source_target_pairs={{1,0},{2,1},{3,2},{4,3},{5,4},{6,5},{7,6},{0,7},{9,8},{10,9},{11,1... | collective-permute-start | bytes 1671176 | tf_op jit(solution)/shard_map/ppermute | solution.py:274
  19.3 16.1 %collective-permute-start.4 = (bf16[256,1024]{1,0:T(8,128)(2,1)S(1)}, bf16[256,1024]{1,0:T(8,128)(2,1)S(1)}, u32[]{:S(2)}, u32[]{:S(2)}) collective-permute-start(bf16[256,1024]{1,0:T(8,128)(2,1)S(1)} %collective-permute-done.1.refs_7_), channel_id=1, source_target_pairs={{0,1},{1,2},{2,3},{3,4},{4,5},{5,6},{6,7},{7,0},{8,9},{9,10},{10,1... | collective-permute-start | bytes 1572872 | tf_op jit(solution)/shard_map/ppermute | solution.py:272
  19.6 27.7 %collective-permute-start.11 = (bf16[272,1024]{1,0:T(8,128)(2,1)S(1)}, bf16[272,1024]{1,0:T(8,128)(2,1)S(1)}, u32[]{:S(2)}, u32[]{:S(2)}) collective-permute-start(bf16[272,1024]{1,0:T(8,128)(2,1)S(1)} %shard_map.73.refs_0_), channel_id=1, source_target_pairs={{0,1},{1,2},{2,3},{3,4},{4,5},{5,6},{6,7},{7,0},{8,9},{9,10},{10,1... | collective-permute-start | bytes 1671176 | tf_op jit(solution)/shard_map/ppermute | solution.py:272
  31.5 15.9 %collective-permute-start.8 = (bf16[272,1024]{1,0:T(8,128)(2,1)S(1)}, bf16[272,1024]{1,0:T(8,128)(2,1)S(1)}, u32[]{:S(2)}, u32[]{:S(2)}) collective-permute-start(bf16[272,1024]{1,0:T(8,128)(2,1)S(1)} %collective-permute-done.7.refs_1_), channel_id=1, source_target_pairs={{1,0},{2,1},{3,2},{4,3},{5,4},{6,5},{7,6},{0,7},{9,8},{10,9},{11,1... | collective-permute-start | bytes 1671176 | tf_op jit(solution)/shard_map/ppermute | solution.py:274
  34.3 24.3 %collective-permute-start.2 = (bf16[256,1024]{1,0:T(8,128)(2,1)S(1)}, bf16[256,1024]{1,0:T(8,128)(2,1)S(1)}, u32[]{:S(2)}, u32[]{:S(2)}) collective-permute-start(bf16[256,1024]{1,0:T(8,128)(2,1)S(1)} %collective-permute-done.refs_1_), channel_id=1, source_target_pairs={{1,0},{2,1},{3,2},{4,3},{5,4},{6,5},{7,6},{0,7},{9,8},{10,9},{11,1... | collective-permute-start | bytes 1572872 | tf_op jit(solution)/shard_map/ppermute | solution.py:274
  35.4 27.0 %collective-permute-start.5 = (bf16[256,1024]{1,0:T(8,128)(2,1)S(1)}, bf16[256,1024]{1,0:T(8,128)(2,1)S(1)}, u32[]{:S(2)}, u32[]{:S(2)}) collective-permute-start(bf16[256,1024]{1,0:T(8,128)(2,1)S(1)} %collective-permute-done.4.refs_6_), channel_id=1, source_target_pairs={{0,1},{1,2},{2,3},{3,4},{4,5},{5,6},{6,7},{7,0},{8,9},{9,10},{10,1... | collective-permute-start | bytes 1572872 | tf_op jit(solution)/shard_map/ppermute | solution.py:272
  47.3 23.2 %collective-permute-start.12 = (bf16[272,1024]{1,0:T(8,128)(2,1)S(1)}, bf16[272,1024]{1,0:T(8,128)(2,1)S(1)}, u32[]{:S(2)}, u32[]{:S(2)}) collective-permute-start(bf16[272,1024]{1,0:T(8,128)(2,1)S(1)} %collective-permute-done.11.refs_7_), channel_id=1, source_target_pairs={{0,1},{1,2},{2,3},{3,4},{4,5},{5,6},{6,7},{7,0},{8,9},{9,10},{10,1... | collective-permute-start | bytes 1671176 | tf_op jit(solution)/shard_map/ppermute | solution.py:272
  47.4 23.2 %collective-permute-start.9 = (bf16[272,1024]{1,0:T(8,128)(2,1)S(1)}, bf16[272,1024]{1,0:T(8,128)(2,1)S(1)}, u32[]{:S(2)}, u32[]{:S(2)}) collective-permute-start(bf16[272,1024]{1,0:T(8,128)(2,1)S(1)} %collective-permute-done.8.refs_2_), channel_id=1, source_target_pairs={{1,0},{2,1},{3,2},{4,3},{5,4},{6,5},{7,6},{0,7},{9,8},{10,9},{11,1... | collective-permute-start | bytes 1671176 | tf_op jit(solution)/shard_map/ppermute | solution.py:274
  58.7 23.2 %collective-permute-start.3 = (bf16[256,1024]{1,0:T(8,128)(2,1)S(1)}, bf16[256,1024]{1,0:T(8,128)(2,1)S(1)}, u32[]{:S(2)}, u32[]{:S(2)}) collective-permute-start(bf16[256,1024]{1,0:T(8,128)(2,1)S(1)} %collective-permute-done.2.refs_2_), channel_id=1, source_target_pairs={{1,0},{2,1},{3,2},{4,3},{5,4},{6,5},{7,6},{0,7},{9,8},{10,9},{11,1... | collective-permute-start | bytes 1572872 | tf_op jit(solution)/shard_map/ppermute | solution.py:274
  62.4 19.5 %collective-permute-start.6 = (bf16[256,1024]{1,0:T(8,128)(2,1)S(1)}, bf16[256,1024]{1,0:T(8,128)(2,1)S(1)}, u32[]{:S(2)}, u32[]{:S(2)}) collective-permute-start(bf16[256,1024]{1,0:T(8,128)(2,1)S(1)} %collective-permute-done.5.refs_5_), channel_id=1, source_target_pairs={{0,1},{1,2},{2,3},{3,4},{4,5},{5,6},{6,7},{7,0},{8,9},{9,10},{10,1... | collective-permute-start | bytes 1572872 | tf_op jit(solution)/shard_map/ppermute | solution.py:272
  70.5 21.1 %collective-permute-start.13 = (bf16[272,1024]{1,0:T(8,128)(2,1)S(1)}, bf16[272,1024]{1,0:T(8,128)(2,1)S(1)}, u32[]{:S(2)}, u32[]{:S(2)}) collective-permute-start(bf16[272,1024]{1,0:T(8,128)(2,1)S(1)} %collective-permute-done.12.refs_6_), channel_id=1, source_target_pairs={{0,1},{1,2},{2,3},{3,4},{4,5},{5,6},{6,7},{7,0},{8,9},{9,10},{10,1... | collective-permute-start | bytes 1671176 | tf_op jit(solution)/shard_map/ppermute | solution.py:272
  70.6 21.1 %collective-permute-start.10 = (bf16[272,1024]{1,0:T(8,128)(2,1)S(1)}, bf16[272,1024]{1,0:T(8,128)(2,1)S(1)}, u32[]{:S(2)}, u32[]{:S(2)}) collective-permute-start(bf16[272,1024]{1,0:T(8,128)(2,1)S(1)} %collective-permute-done.9.refs_3_), channel_id=1, source_target_pairs={{1,0},{2,1},{3,2},{4,3},{5,4},{6,5},{7,6},{0,7},{9,8},{10,9},{11,1... | collective-permute-start | bytes 1671176 | tf_op jit(solution)/shard_map/ppermute | solution.py:274
  97.7 5.9 %collective-permute-start.16 = (bf16[1024,1024]{1,0:T(8,128)(2,1)S(1)}, bf16[1024,1024]{1,0:T(8,128)(2,1)S(1)}, u32[]{:S(2)}, u32[]{:S(2)}) collective-permute-start(bf16[1024,1024]{1,0:T(8,128)(2,1)S(1)} %get-tuple-element.74.four_ref.own_ref), channel_id=1, source_target_pairs={{16,24},{32,40},{48,56},{64,72},{80,88},{96,104},{112,120},{128,13... | collective-permute-start | bytes 6291464 | tf_op jit(solution)/shard_map/ppermute | solution.py:322
  100.9 2.7 %collective-permute-start.17 = (bf16[16,1024]{1,0:T(8,128)(2,1)S(1)}, bf16[16,1024]{1,0:T(8,128)(2,1)S(1)}, u32[]{:S(2)}, u32[]{:S(2)}) collective-permute-start(bf16[16,1024]{1,0:T(8,128)(2,1)S(1)} %get-tuple-element.75.term_ref.own_term_ref), channel_id=1, source_target_pairs={{16,24},{32,40},{48,56},{64,72},{80,88},{96,104},{112,120},{128,13... | collective-permute-start | bytes 98312 | tf_op jit(solution)/shard_map/ppermute | solution.py:327
  102.2 0.7 collective-permute-start.14
  102.9 0.7 collective-permute-start.15
  103.6 0.7 collective-permute-start.18
  104.4 3.6 %collective-permute-start.22 = (bf16[1024,1024]{1,0:T(8,128)(2,1)S(1)}, bf16[1024,1024]{1,0:T(8,128)(2,1)S(1)}, u32[]{:S(2)}, u32[]{:S(2)}) collective-permute-start(bf16[1024,1024]{1,0:T(8,128)(2,1)S(1)} %get-tuple-element.74.four_ref.own_ref), channel_id=1, source_target_pairs={{0,8},{1,9},{2,10},{3,11},{4,12},{5,13},{6,14},{7,15}} | collective-permute-start | bytes 6291464 | tf_op jit(solution)/shard_map/ppermute | solution.py:349
  105.2 2.8 %collective-permute-start.23 = (bf16[16,1024]{1,0:T(8,128)(2,1)S(1)}, bf16[16,1024]{1,0:T(8,128)(2,1)S(1)}, u32[]{:S(2)}, u32[]{:S(2)}) collective-permute-start(bf16[16,1024]{1,0:T(8,128)(2,1)S(1)} %get-tuple-element.75.term_ref.own_term_ref), channel_id=1, source_target_pairs={{0,8},{1,9},{2,10},{3,11},{4,12},{5,13},{6,14},{7,15}} | collective-permute-start | bytes 98312 | tf_op jit(solution)/shard_map/ppermute | solution.py:349
  105.9 0.7 collective-permute-start.19
  106.6 0.7 collective-permute-start.20
  107.3 1.3 collective-permute-start.21
  108.6 0.7 collective-permute-start.24
  109.3 0.7 collective-permute-start.25
  110.0 0.7 collective-permute-start.26
  113.6 0.7 collective-permute-start.31
  114.3 0.7 collective-permute-start.32
  115.0 1.3 collective-permute-start.33
  115.7 2.0 %collective-permute-start.34 = (f32[1,1024]{1,0:T(1,128)S(1)}, f32[1,1024]{1,0:T(1,128)S(1)}, u32[]{:S(2)}, u32[]{:S(2)}) collective-permute-start(f32[1,1024]{1,0:T(1,128)S(1)} %get-tuple-element.100.begin_ref), channel_id=1, source_target_pairs={{8,0},{24,16},{40,32},{56,48},{72,64},{88,80},{104,96},{120,112},{... | collective-permute-start | bytes 12296 | tf_op jit(solution)/shard_map/ppermute | solution.py:358
  116.4 44.0 %collective-permute-start.35 = (f32[1,1024]{1,0:T(1,128)S(1)}, f32[1,1024]{1,0:T(1,128)S(1)}, u32[]{:S(2)}, u32[]{:S(2)}) collective-permute-start(f32[1,1024]{1,0:T(1,128)S(1)} %collective-permute-done.33.came_ref), channel_id=1, source_target_pairs={{248,240},{249,241},{250,242},{251,243},{252,244},{253,245},{254,2... | collective-permute-start | bytes 12296 | tf_op jit(solution)/shard_map/ppermute | solution.py:359
  (9 other events, 22.3 us)

commit v5 on v4

--- a/solution.py
+++ b/solution.py
@@ -58,32 +58,38 @@
 
 
 def drive_kernel(
-    rows_ref, cols_ref, observations_ref, precisions_ref, blocks_ref, maps_ref, out_ref, weighted_ref, drive_ref, parts_ref, sems
+    rows_ref, cols_ref, values_ref, blocks_ref, maps_ref, out_ref, weighted_ref, parts_ref, sems
 ):
     steps, count, side, _ = blocks_ref.shape
-    width = maps_ref.shape[1]
+    later, width, size = maps_ref.shape
     copies = []
-    for j in range(steps // 2):
-        rows = pl.ds(j * width, width)
-        copies.append(pltpu.make_async_copy(maps_ref.at[steps // 2 + j], out_ref.at[rows, :], sems.at[j]))
+    for j in range(later):
+        copies.append(pltpu.make_async_copy(maps_ref.at[j], out_ref.at[pl.ds(j * width, width), :], sems.at[j]))
         copies[j].start()
-    weighted_ref[...] = (precisions_ref[...] * observations_ref[...]).astype(BF16).astype(F32)
-    drive_ref[...] = jnp.zeros_like(drive_ref)
+    weighted = values_ref[...].astype(F32)
+    pieces = weighted_ref.shape[0]
+    for r in range(pieces):
+        weighted_ref[r] = weighted[:, r * side:(r + 1) * side]
     parts_ref[...] = jnp.zeros_like(parts_ref)
+    piece = lax.broadcasted_iota(jnp.int32, (pieces, count), 0)
+    column = lax.broadcasted_iota(jnp.int32, (size // side, count), 0)
+    own = lax.broadcasted_iota(jnp.int32, (count, count * side), 0) == (
+        lax.broadcasted_iota(jnp.int32, (count, count * side), 1) // side
+    )
     for t in range(steps):
-        def block(b, carry):
-            left = jnp.broadcast_to(weighted_ref[t, pl.ds(rows_ref[t, b], 1), :], (16, side)).astype(BF16)
-            term = jnp.dot(left, blocks_ref[t, b], preferred_element_type=F32)
-            at = pl.ds(cols_ref[t, b], 1)
-            drive_ref[t, at, :] = drive_ref[t, at, :] + term[0:1, :]
-            return carry
-
-        lax.fori_loop(0, count, block, 0, unroll=4)
-    for t in range(steps):
-        for c in range(drive_ref.shape[1]):
-            for i, part in enumerate(three_parts(drive_ref[t, c:c + 1, :])):
-                parts_ref[3 * t + i:3 * t + i + 1, c * side:(c + 1) * side] = part
-    out_ref[(steps // 2) * width:, :] = parts_ref[...].astype(BF16)
+        chosen = (piece == rows_ref[t:t + 1, :]).astype(F32).astype(BF16)
+        left = lax.dot_general(
+            chosen, weighted_ref[:, t, :].astype(BF16), (((0,), (0,)), ((), ())), preferred_element_type=F32
+        )
+        left = jnp.concatenate([left] * count, axis=1)
+        left = jnp.where(own, left, 0.0).astype(BF16)
+        terms = jnp.dot(left, blocks_ref[t].reshape(count * side, side), preferred_element_type=F32)
+        chosen = (column == cols_ref[t:t + 1, :]).astype(F32).astype(BF16)
+        drive = sum(jnp.dot(chosen, part.astype(BF16), preferred_element_type=F32) for part in three_parts(terms))
+        for i, part in enumerate(three_parts(drive)):
+            for c in range(size // side):
+                parts_ref[3 * t + i:3 * t + i + 1, c * side:(c + 1) * side] = part[c:c + 1, :]
+    out_ref[later * width:, :] = parts_ref[...].astype(BF16)
     for copy in copies:
         copy.wait()
 
@@ -102,7 +108,7 @@
 
 
 def two_kernel(count, *refs):
-    pieces, (two_ref, slab_ref, next_ref, one_ref, sems) = refs[:count], refs[count:]
+    pieces, (two_ref, slab_ref, one_ref, next_ref, sems) = refs[:count], refs[count:]
     width = slab_ref.shape[0]
     place = lax.axis_index("state")
     ones = fetched(count, place, pieces, 0, one_ref, sems, 0)
@@ -113,43 +119,46 @@
     slab_ref[...] = two_ref[pl.ds(pl.multiple_of(place * width, width), width), :]
 
 
-def four_kernel(count, two_ref, *refs):
+def gather_kernel(count, prior_ref, first_ref, second_ref, *refs):
     pieces = refs[:count]
-    four_ref, slab3_ref, slab4_ref, third_ref, fourth_ref, drive_ref, three_ref, parts_ref, sems = refs[count:]
-    width = slab3_ref.shape[0]
+    third_ref, fourth_ref, drive_ref, mean_ref, parts_ref, sems = refs[count:]
+    width = third_ref.shape[0] // count
     place = lax.axis_index("state")
-    thirds = fetched(count, place, pieces, 0, third_ref, sems, 0)
-    fourths = fetched(count, place, pieces, 1, fourth_ref, sems, count)
+    copies = fetched(count, place, pieces, 0, third_ref, sems, 0)
+    copies += fetched(count, place, pieces, 1, fourth_ref, sems, count)
     parts = []
     for r in range(count):
         parts.append(pltpu.make_async_copy(pieces[r].at[pl.ds(2 * width, 16), :], parts_ref.at[r], sems.at[2 * count + r]))
         parts[r].start()
-    mine = pl.ds(pl.multiple_of(place * width, width), width)
-    for copy in thirds:
+    for copy in copies + parts:
         copy.wait()
+    drive_ref[...] = jnp.sum(parts_ref[...].astype(F32), axis=0)
+    mean_ref[...] = prior_ref[...]
+
+    @pl.when(lax.axis_index("tm") == 0)
+    def _():
+        mean = prior_ref[...]
+        for j, map_ref in enumerate((first_ref, second_ref, third_ref, fourth_ref)):
+            mean = times_t(mean, map_ref[...]) + joined(drive_ref[3 * j:3 * j + 3, :])
+        mean_ref[...] = mean
+
+
+def four_kernel(two_ref, third_ref, fourth_ref, four_ref, slab3_ref, slab4_ref, three_ref):
+    width = slab3_ref.shape[0]
+    mine = pl.ds(pl.multiple_of(lax.axis_index("state") * width, width), width)
     matmul(third_ref, two_ref, three_ref)
     slab3_ref[...] = three_ref[mine, :]
-    for copy in fourths:
-        copy.wait()
     matmul(fourth_ref, three_ref, four_ref)
     slab4_ref[...] = four_ref[mine, :]
-    for copy in parts:
-        copy.wait()
-    drive_ref[...] = jnp.sum(parts_ref[...].astype(F32), axis=0)
-
-
-def local_kernel(drive_ref, prior_ref, second_ref, third_ref, fourth_ref, four_ref, locals_ref, term_ref, mean_ref):
+
+
+def local_kernel(drive_ref, second_ref, third_ref, fourth_ref, locals_ref, term_ref):
     local = joined(drive_ref[0:3, :])
     locals_ref[0:1, :] = local
     for j, map_ref in enumerate((second_ref, third_ref, fourth_ref)):
         local = times_t(local, map_ref[...]) + joined(drive_ref[3 * j + 3:3 * j + 6, :])
         locals_ref[j + 1:j + 2, :] = local
     term_ref[...] = split_rows(local)
-    mean_ref[...] = local
-
-    @pl.when(lax.axis_index("tm") == 0)
-    def _():
-        mean_ref[...] = times_t(prior_ref[...], four_ref[...]) + local
 
 
 def pair_kernel(own_ref, own_term_ref, other_ref, other_term_ref, after_ref, qt_ref, q_ref):
@@ -290,40 +299,41 @@
     whole = pltpu.VMEM((size, size), BF16)
 
     half = steps_here // 2
-    pieces = (steps_here, observations.shape[1] // side, side)
+    pieces = observations.shape[1] // side
     packed = call(
-        drive_kernel, jax.ShapeDtypeStruct((half * width + 16, size), BF16), [S, S, V, V, V, A],
+        drive_kernel, jax.ShapeDtypeStruct((half * width + 16, size), BF16), [V] * 4 + [A],
         [
-            pltpu.VMEM(pieces, F32),
-            pltpu.VMEM((steps_here, size // side, side), F32),
+            pltpu.VMEM((pieces, steps_here, side), F32),
             pltpu.VMEM((16, size), F32),
             pltpu.SemaphoreType.DMA((half,)),
         ],
         flops=10 ** 7, moved=2 ** 21,
-    )(block_rows, block_cols, observations.reshape(pieces), precisions.reshape(pieces), blocks, transition)
+    )(block_rows, block_cols, (precisions * observations).astype(BF16), blocks, transition[half:])
     early, late = ring_rounds(
         [transition[:half].reshape(half * width, size), packed], "state",
         lambda r, i, found: (packed,) if (r, i) == (2, 0) else (),
     )
-    two, slab2, second = call(
-        functools.partial(two_kernel, count), (matrix, slab, matrix), [A] * count,
-        [whole, pltpu.SemaphoreType.DMA((2 * count,))], flops=2 * size ** 3, moved=6 * size ** 2,
+    begin = prior.reshape(1, size)
+    two, slab2, first, second = call(
+        functools.partial(two_kernel, count), (matrix, slab, matrix, matrix), [A] * count,
+        [pltpu.SemaphoreType.DMA((2 * count,))], flops=2 * size ** 3, moved=6 * size ** 2,
     )(*early)
-    own, slab3, slab4, third, fourth, drive = call(
-        functools.partial(four_kernel, count),
-        (matrix, slab, slab, matrix, matrix, jax.ShapeDtypeStruct((16, size), F32)),
-        [V] + [A] * count,
-        [whole, pltpu.VMEM((count, 16, size), BF16), pltpu.SemaphoreType.DMA((3 * count,))],
-        flops=4 * size ** 3, moved=8 * size ** 2,
-    )(two, *late)
-
-    begin = prior.reshape(1, size)
+    third, fourth, drive, mean = call(
+        functools.partial(gather_kernel, count),
+        (matrix, matrix, jax.ShapeDtypeStruct((16, size), F32), row),
+        [V] * 3 + [A] * count,
+        [pltpu.VMEM((count, 16, size), BF16), pltpu.SemaphoreType.DMA((3 * count,))],
+        flops=128 * size ** 2, moved=8 * size ** 2,
+    )(begin, first, second, *late)
     pairs = [(i, i + 1) for i in range(0, blocks_of_time, 2)]
+    mean = lax.ppermute(mean, "tm", pairs[:1])
+    own, slab3, slab4 = call(
+        four_kernel, (matrix, slab, slab), [V] * 3, [whole], flops=4 * size ** 3, moved=8 * size ** 2,
+    )(two, third, fourth)
     other = lax.ppermute(own, "tm", pairs[1:])
-    locals_, own_term, mean = call(
-        local_kernel, (steps, rows, row), [V] * 6, flops=128 * size ** 2, moved=8 * size ** 2
-    )(drive, begin, second, third, fourth, own)
-    mean = lax.ppermute(mean, "tm", pairs[:1])
+    locals_, own_term = call(
+        local_kernel, (steps, rows), [V] * 4, flops=96 * size ** 2, moved=6 * size ** 2
+    )(drive, second, third, fourth)
     other_term = lax.ppermute(own_term, "tm", pairs[1:])
 
     def hop(value, turn):
@@ -339,14 +349,13 @@
     turned, term = call(
         pair_kernel, (matrix, row), [V] * 5, flops=2 * size ** 3, moved=6 * size ** 2
     )(own, own_term, other, other_term, value)
+    other0, other0_term = lax.ppermute(after((own, own_term), turned), "tm", pairs[:1])
     for turn in range(2, chips - 1):
         begin, value = call(
             functools.partial(hop_kernel, turn), (row, row), [V] * 4,
             flops=32 * size ** 2, moved=2 * size ** 2,
         )(begin, came, turned, term)
         came = hop(value, turn)
-        if turn == 2:
-            other0, other0_term = lax.ppermute(after((own, own_term), value), "tm", pairs[:1])
         if turn == 3:
             maps, terms = call(
                 ready_kernel,

time: 163 us -> 167 us (1.025)
  waiting for transfers between devices: 93.6 us -> 108 us
  local copies, waits for them, and re-layouts: 6.06 us -> 1.45 us
  Pallas kernels: 17.8 us -> 14.2 us
    ppermute x7, waiting for transfers between devices: 26.8 us -> 37.9 us  [ring_rounds(): pieces[count - r] = lax.ppermute(left, axis, forward)]
    ppermute x1, waiting for transfers between devices: 42.7 us -> 47.7 us  [shards(): last = lax.ppermute(came, 'tm', [(b, a) for a, b in pairs[-1:]])]
    pallas_call x1, Pallas kernels: 5.22 us -> 1.58 us  [shards(): call(drive_kernel, jax.ShapeDtypeStruct((half * width + 16, size), BF16),...]
    unnamed x10 -> x12, local copies, waits for them, and re-layouts: 2.96 us -> 0.03 us
    ppermute x7, waiting for transfers between devices: 24 us -> 22.1 us  [ring_rounds(): pieces[r] = lax.ppermute(right, axis, backward)]
    reshape x2 -> x0, local copies, waits for them, and re-layouts: 1.93 us -> none  [the longest x1 0.97 us: shards(): observations.reshape(pieces)]
    pallas_call x3 -> x4, Pallas kernels: 10.8 us -> 10.9 us  [the longest x1 5.07 us: shards(): call(four_kernel, (matrix, slab, slab), [V] * 3, [whole], flops=4 * size...]
  transfers between devices with their start and end apart: 36 -> 36, of which waited for: 10 -> 11; matrix products, arithmetic and copies ran while one was open for 1% -> 0% of each run, Pallas kernels for 7% -> 4%
where the time goes in v5:
time: 167 us
  waiting for transfers between devices  108 us (65%)
  starting transfers between devices  42.4 us (25%)
  Pallas kernels  14.2 us (9%)
    ppermute x1, waiting for transfers between devices, shards(): last = lax.ppermute(came, 'tm', [(b, a) for a, b in pairs[-1:]])  47.7 us
    ppermute x7, waiting for transfers between devices, ring_rounds(): pieces[count - r] = lax.ppermute(left, axis, forward)  37.9 us
    ppermute x7, waiting for transfers between devices, ring_rounds(): pieces[r] = lax.ppermute(right, axis, backward)  22.1 us
    ppermute x7, starting transfers between devices, ring_rounds(): pieces[r] = lax.ppermute(right, axis, backward)  20.3 us
    ppermute x15, starting transfers between devices, hop(): return lax.ppermute(value, 'tm', [(2 * turn + 1, 2 * turn + 3)])  9.92 us
    ppermute x7, starting transfers between devices, ring_rounds(): pieces[count - r] = lax.ppermute(left, axis, forward)  5.4 us
    pallas_call x1, Pallas kernels, shards(): call(four_kernel, (matrix, slab, slab), [V] * 3, [whole], flops=4 * size...  5.07 us
  transfers between devices with their start and end apart: 36, of which 11 were waited for; matrix products, arithmetic and copies ran while one was open for 0% of the time, Pallas kernels for 4%

profile of v5, /device:TPU:30, one launch (start us, length us, event | category | flops | bytes accessed | tf_op | source)
XLA Modules:
  0.0 166.5 jit_solution(17568697023021148901)
XLA Ops:
  0.0 1.4 fusion
  1.5 2.0 %collective-permute-start.1 = (bf16[256,1024]{1,0:T(8,128)(2,1)S(1)}, bf16[256,1024]{1,0:T(8,128)(2,1)S(1)}, u32[]{:S(2)}, u32[]{:S(2)}) collective-permute-start(bf16[256,1024]{1,0:T(8,128)(2,1)S(1)} %bitcast.2), channel_id=1, source_target_pairs={{0,1},{1,2},{2,3},{3,4},{4,5},{5,6},{6,7},{7,0},{8,9},{9,10},{10,1... | collective-permute-start | bytes 1572872 | tf_op jit(solution)/shard_map/ppermute | solution.py:281
  3.4 4.0 %collective-permute-start = (bf16[256,1024]{1,0:T(8,128)(2,1)S(1)}, bf16[256,1024]{1,0:T(8,128)(2,1)S(1)}, u32[]{:S(2)}, u32[]{:S(2)}) collective-permute-start(bf16[256,1024]{1,0:T(8,128)(2,1)S(1)} %bitcast.3), channel_id=1, source_target_pairs={{1,0},{2,1},{3,2},{4,3},{5,4},{6,5},{7,6},{0,7},{9,8},{10,9},{11,1... | collective-permute-start | bytes 1572872 | tf_op jit(solution)/shard_map/ppermute | solution.py:283
  7.5 1.6 shard_map.73.refs_0_
  9.1 2.0 %collective-permute-start.7 = (bf16[272,1024]{1,0:T(8,128)(2,1)S(1)}, bf16[272,1024]{1,0:T(8,128)(2,1)S(1)}, u32[]{:S(2)}, u32[]{:S(2)}) collective-permute-start(bf16[272,1024]{1,0:T(8,128)(2,1)S(1)} %shard_map.73.refs_0_), channel_id=1, source_target_pairs={{1,0},{2,1},{3,2},{4,3},{5,4},{6,5},{7,6},{0,7},{9,8},{10,9},{11,1... | collective-permute-start | bytes 1671176 | tf_op jit(solution)/shard_map/ppermute | solution.py:283
  11.1 8.2 %collective-permute-done.1.refs_7_ = bf16[256,1024]{1,0:T(8,128)(2,1)S(1)} collective-permute-done((bf16[256,1024]{1,0:T(8,128)(2,1)S(1)}, bf16[256,1024]{1,0:T(8,128)(2,1)S(1)}, u32[]{:S(2)}, u32[]{:S(2)}) %collective-permute-start.1) | collective-permute-done | bytes 524320 | tf_op jit(solution)/shard_map/ppermute | solution.py:281
  20.2 3.0 %collective-permute-start.11 = (bf16[272,1024]{1,0:T(8,128)(2,1)S(1)}, bf16[272,1024]{1,0:T(8,128)(2,1)S(1)}, u32[]{:S(2)}, u32[]{:S(2)}) collective-permute-start(bf16[272,1024]{1,0:T(8,128)(2,1)S(1)} %shard_map.73.refs_0_), channel_id=1, source_target_pairs={{0,1},{1,2},{2,3},{3,4},{4,5},{5,6},{6,7},{7,0},{8,9},{9,10},{10,1... | collective-permute-start | bytes 1671176 | tf_op jit(solution)/shard_map/ppermute | solution.py:281
  23.2 7.4 %collective-permute-done.7.refs_1_ = bf16[272,1024]{1,0:T(8,128)(2,1)S(1)} collective-permute-done((bf16[272,1024]{1,0:T(8,128)(2,1)S(1)}, bf16[272,1024]{1,0:T(8,128)(2,1)S(1)}, u32[]{:S(2)}, u32[]{:S(2)}) %collective-permute-start.7) | collective-permute-done | bytes 557088 | tf_op jit(solution)/shard_map/ppermute | solution.py:283
  30.6 3.7 %collective-permute-start.8 = (bf16[272,1024]{1,0:T(8,128)(2,1)S(1)}, bf16[272,1024]{1,0:T(8,128)(2,1)S(1)}, u32[]{:S(2)}, u32[]{:S(2)}) collective-permute-start(bf16[272,1024]{1,0:T(8,128)(2,1)S(1)} %collective-permute-done.7.refs_1_), channel_id=1, source_target_pairs={{1,0},{2,1},{3,2},{4,3},{5,4},{6,5},{7,6},{0,7},{9,8},{10,9},{11,1... | collective-permute-start | bytes 1671176 | tf_op jit(solution)/shard_map/ppermute | solution.py:283
  34.7 1.6 collective-permute-done.4.refs_6_
  36.3 11.9 %collective-permute-done.11.refs_7_ = bf16[272,1024]{1,0:T(8,128)(2,1)S(1)} collective-permute-done((bf16[272,1024]{1,0:T(8,128)(2,1)S(1)}, bf16[272,1024]{1,0:T(8,128)(2,1)S(1)}, u32[]{:S(2)}, u32[]{:S(2)}) %collective-permute-start.11) | collective-permute-done | bytes 557088 | tf_op jit(solution)/shard_map/ppermute | solution.py:281
  48.3 3.2 %collective-permute-start.9 = (bf16[272,1024]{1,0:T(8,128)(2,1)S(1)}, bf16[272,1024]{1,0:T(8,128)(2,1)S(1)}, u32[]{:S(2)}, u32[]{:S(2)}) collective-permute-start(bf16[272,1024]{1,0:T(8,128)(2,1)S(1)} %collective-permute-done.8.refs_2_), channel_id=1, source_target_pairs={{1,0},{2,1},{3,2},{4,3},{5,4},{6,5},{7,6},{0,7},{9,8},{10,9},{11,1... | collective-permute-start | bytes 1671176 | tf_op jit(solution)/shard_map/ppermute | solution.py:283
  51.5 7.1 %collective-permute-done.2.refs_2_ = bf16[256,1024]{1,0:T(8,128)(2,1)S(1)} collective-permute-done((bf16[256,1024]{1,0:T(8,128)(2,1)S(1)}, bf16[256,1024]{1,0:T(8,128)(2,1)S(1)}, u32[]{:S(2)}, u32[]{:S(2)}) %collective-permute-start.2) | collective-permute-done | bytes 524320 | tf_op jit(solution)/shard_map/ppermute | solution.py:283
  58.6 3.7 %collective-permute-start.3 = (bf16[256,1024]{1,0:T(8,128)(2,1)S(1)}, bf16[256,1024]{1,0:T(8,128)(2,1)S(1)}, u32[]{:S(2)}, u32[]{:S(2)}) collective-permute-start(bf16[256,1024]{1,0:T(8,128)(2,1)S(1)} %collective-permute-done.2.refs_2_), channel_id=1, source_target_pairs={{1,0},{2,1},{3,2},{4,3},{5,4},{6,5},{7,6},{0,7},{9,8},{10,9},{11,1... | collective-permute-start | bytes 1572872 | tf_op jit(solution)/shard_map/ppermute | solution.py:283
  62.3 9.1 %collective-permute-done.12.refs_6_ = bf16[272,1024]{1,0:T(8,128)(2,1)S(1)} collective-permute-done((bf16[272,1024]{1,0:T(8,128)(2,1)S(1)}, bf16[272,1024]{1,0:T(8,128)(2,1)S(1)}, u32[]{:S(2)}, u32[]{:S(2)}) %collective-permute-start.12) | collective-permute-done | bytes 557088 | tf_op jit(solution)/shard_map/ppermute | solution.py:281
  71.5 3.2 %collective-permute-start.10 = (bf16[272,1024]{1,0:T(8,128)(2,1)S(1)}, bf16[272,1024]{1,0:T(8,128)(2,1)S(1)}, u32[]{:S(2)}, u32[]{:S(2)}) collective-permute-start(bf16[272,1024]{1,0:T(8,128)(2,1)S(1)} %collective-permute-done.9.refs_3_), channel_id=1, source_target_pairs={{1,0},{2,1},{3,2},{4,3},{5,4},{6,5},{7,6},{0,7},{9,8},{10,9},{11,1... | collective-permute-start | bytes 1671176 | tf_op jit(solution)/shard_map/ppermute | solution.py:283
  74.7 7.1 %collective-permute-done.3.refs_3_ = bf16[256,1024]{1,0:T(8,128)(2,1)S(1)} collective-permute-done((bf16[256,1024]{1,0:T(8,128)(2,1)S(1)}, bf16[256,1024]{1,0:T(8,128)(2,1)S(1)}, u32[]{:S(2)}, u32[]{:S(2)}) %collective-permute-start.3) | collective-permute-done | bytes 524320 | tf_op jit(solution)/shard_map/ppermute | solution.py:283
  81.8 0.9 collective-permute-done.6.refs_4_
  82.7 3.1 %shard_map.74 = (bf16[1024,1024]{1,0:T(8,128)(2,1)S(1)}, bf16[128,1024]{1,0:T(8,128)(2,1)S(1)}, bf16[1024,1024]{1,0:T(8,128)(2,1)S(1)}, bf16[1024,1024]{1,0:T(8,128)(2,1)S(1)}) custom-call(bf16[256,1024]{1,0:T(8,128)(2,1)S(1)} %bitcast.4, bf16[256,1024]{1,0:T(8,128)(2,1)S(1)} %collective-permute-done.refs_1_, ...), custom_call_target="tpu_custom_call" | custom-call | flops 2147483648 | bytes 6291456 | tf_op jit(solution)/shard_map/pallas_call | solution.py:317
  85.7 6.2 %collective-permute-done.13.refs_5_ = bf16[272,1024]{1,0:T(8,128)(2,1)S(1)} collective-permute-done((bf16[272,1024]{1,0:T(8,128)(2,1)S(1)}, bf16[272,1024]{1,0:T(8,128)(2,1)S(1)}, u32[]{:S(2)}, u32[]{:S(2)}) %collective-permute-start.13) | collective-permute-done | bytes 557088 | tf_op jit(solution)/shard_map/ppermute | solution.py:281
  91.9 1.0 shard_map.75
  92.9 5.1 %shard_map.76 = (bf16[1024,1024]{1,0:T(8,128)(2,1)S(1)}, bf16[128,1024]{1,0:T(8,128)(2,1)S(1)}, bf16[128,1024]{1,0:T(8,128)(2,1)S(1)}) custom-call(bf16[1024,1024]{1,0:T(8,128)(2,1)S(1)} %get-tuple-element.60.two_ref, bf16[1024,1024]{1,0:T(8,128)(2,1)S(1)} %get-tuple-element.61.third_ref, bf16[1024,1024]{1,0:T(8,128)(2,1)S(1)} %get-tuple-element.62.fourth_ref), custom_call_target="tpu_custom_call" | custom-call | flops 4294967296 | bytes 8388608 | tf_op jit(solution)/shard_map/pallas_call | solution.py:330
  98.0 1.4 collective-permute-start.16
  99.4 1.8 %shard_map.77 = (f32[4,1024]{1,0:T(4,128)S(1)}, bf16[16,1024]{1,0:T(8,128)(2,1)S(1)}) custom-call(f32[16,1024]{1,0:T(8,128)S(1)} %get-tuple-element.64.drive_ref, bf16[1024,1024]{1,0:T(8,128)(2,1)S(1)} %get-tuple-element.58.second_ref, bf16[1024,1024]{1,0:T(8,128)(2,1)S(1)} %get-tuple-element.61.third_ref, bf16[1024,1024]{1,0:T(8,128)(2,1)S(1)} %get-tuple-element.62.fourth_ref), custom_call_target="tpu_custom_call" | custom-call | flops 100663296 | bytes 6291456 | tf_op jit(solution)/shard_map/pallas_call | solution.py:334
  101.2 1.3 collective-permute-start.17
  102.5 0.7 collective-permute-start.14
  103.2 0.7 collective-permute-start.15
  103.9 0.8 collective-permute-start.22
  104.8 0.7 collective-permute-start.23
  116.6 1.3 collective-permute-start.35
  117.9 47.7 %collective-permute-done.35.last_ref = f32[1,1024]{1,0:T(1,128)S(1)} collective-permute-done((f32[1,1024]{1,0:T(1,128)S(1)}, f32[1,1024]{1,0:T(1,128)S(1)}, u32[]{:S(2)}, u32[]{:S(2)}) %collective-permute-start.35) | collective-permute-done | bytes 4128 | tf_op jit(solution)/shard_map/ppermute | solution.py:368
  165.7 0.8 shard_map.95
  (77 shorter events, 12.3 us)
Async XLA Ops:
  1.5 17.9 %collective-permute-start.1 = (bf16[256,1024]{1,0:T(8,128)(2,1)S(1)}, bf16[256,1024]{1,0:T(8,128)(2,1)S(1)}, u32[]{:S(2)}, u32[]{:S(2)}) collective-permute-start(bf16[256,1024]{1,0:T(8,128)(2,1)S(1)} %bitcast.2), channel_id=1, source_target_pairs={{0,1},{1,2},{2,3},{3,4},{4,5},{5,6},{6,7},{7,0},{8,9},{9,10},{10,1... | collective-permute-start | bytes 1572872 | tf_op jit(solution)/shard_map/ppermute | solution.py:281
  3.4 16.4 %collective-permute-start = (bf16[256,1024]{1,0:T(8,128)(2,1)S(1)}, bf16[256,1024]{1,0:T(8,128)(2,1)S(1)}, u32[]{:S(2)}, u32[]{:S(2)}) collective-permute-start(bf16[256,1024]{1,0:T(8,128)(2,1)S(1)} %bitcast.3), channel_id=1, source_target_pairs={{1,0},{2,1},{3,2},{4,3},{5,4},{6,5},{7,6},{0,7},{9,8},{10,9},{11,1... | collective-permute-start | bytes 1572872 | tf_op jit(solution)/shard_map/ppermute | solution.py:283
  9.1 21.5 %collective-permute-start.7 = (bf16[272,1024]{1,0:T(8,128)(2,1)S(1)}, bf16[272,1024]{1,0:T(8,128)(2,1)S(1)}, u32[]{:S(2)}, u32[]{:S(2)}) collective-permute-start(bf16[272,1024]{1,0:T(8,128)(2,1)S(1)} %shard_map.73.refs_0_), channel_id=1, source_target_pairs={{1,0},{2,1},{3,2},{4,3},{5,4},{6,5},{7,6},{0,7},{9,8},{10,9},{11,1... | collective-permute-start | bytes 1671176 | tf_op jit(solution)/shard_map/ppermute | solution.py:283
  19.8 16.5 %collective-permute-start.4 = (bf16[256,1024]{1,0:T(8,128)(2,1)S(1)}, bf16[256,1024]{1,0:T(8,128)(2,1)S(1)}, u32[]{:S(2)}, u32[]{:S(2)}) collective-permute-start(bf16[256,1024]{1,0:T(8,128)(2,1)S(1)} %collective-permute-done.1.refs_7_), channel_id=1, source_target_pairs={{0,1},{1,2},{2,3},{3,4},{4,5},{5,6},{6,7},{7,0},{8,9},{9,10},{10,1... | collective-permute-start | bytes 1572872 | tf_op jit(solution)/shard_map/ppermute | solution.py:281
  20.2 28.1 %collective-permute-start.11 = (bf16[272,1024]{1,0:T(8,128)(2,1)S(1)}, bf16[272,1024]{1,0:T(8,128)(2,1)S(1)}, u32[]{:S(2)}, u32[]{:S(2)}) collective-permute-start(bf16[272,1024]{1,0:T(8,128)(2,1)S(1)} %shard_map.73.refs_0_), channel_id=1, source_target_pairs={{0,1},{1,2},{2,3},{3,4},{4,5},{5,6},{6,7},{7,0},{8,9},{9,10},{10,1... | collective-permute-start | bytes 1671176 | tf_op jit(solution)/shard_map/ppermute | solution.py:281
  30.6 17.7 %collective-permute-start.8 = (bf16[272,1024]{1,0:T(8,128)(2,1)S(1)}, bf16[272,1024]{1,0:T(8,128)(2,1)S(1)}, u32[]{:S(2)}, u32[]{:S(2)}) collective-permute-start(bf16[272,1024]{1,0:T(8,128)(2,1)S(1)} %collective-permute-done.7.refs_1_), channel_id=1, source_target_pairs={{1,0},{2,1},{3,2},{4,3},{5,4},{6,5},{7,6},{0,7},{9,8},{10,9},{11,1... | collective-permute-start | bytes 1671176 | tf_op jit(solution)/shard_map/ppermute | solution.py:283
  34.3 24.3 %collective-permute-start.2 = (bf16[256,1024]{1,0:T(8,128)(2,1)S(1)}, bf16[256,1024]{1,0:T(8,128)(2,1)S(1)}, u32[]{:S(2)}, u32[]{:S(2)}) collective-permute-start(bf16[256,1024]{1,0:T(8,128)(2,1)S(1)} %collective-permute-done.refs_1_), channel_id=1, source_target_pairs={{1,0},{2,1},{3,2},{4,3},{5,4},{6,5},{7,6},{0,7},{9,8},{10,9},{11,1... | collective-permute-start | bytes 1572872 | tf_op jit(solution)/shard_map/ppermute | solution.py:283
  36.3 26.0 %collective-permute-start.5 = (bf16[256,1024]{1,0:T(8,128)(2,1)S(1)}, bf16[256,1024]{1,0:T(8,128)(2,1)S(1)}, u32[]{:S(2)}, u32[]{:S(2)}) collective-permute-start(bf16[256,1024]{1,0:T(8,128)(2,1)S(1)} %collective-permute-done.4.refs_6_), channel_id=1, source_target_pairs={{0,1},{1,2},{2,3},{3,4},{4,5},{5,6},{6,7},{7,0},{8,9},{9,10},{10,1... | collective-permute-start | bytes 1572872 | tf_op jit(solution)/shard_map/ppermute | solution.py:281
  48.3 23.2 %collective-permute-start.12 = (bf16[272,1024]{1,0:T(8,128)(2,1)S(1)}, bf16[272,1024]{1,0:T(8,128)(2,1)S(1)}, u32[]{:S(2)}, u32[]{:S(2)}) collective-permute-start(bf16[272,1024]{1,0:T(8,128)(2,1)S(1)} %collective-permute-done.11.refs_7_), channel_id=1, source_target_pairs={{0,1},{1,2},{2,3},{3,4},{4,5},{5,6},{6,7},{7,0},{8,9},{9,10},{10,1... | collective-permute-start | bytes 1671176 | tf_op jit(solution)/shard_map/ppermute | solution.py:281
  48.3 23.2 %collective-permute-start.9 = (bf16[272,1024]{1,0:T(8,128)(2,1)S(1)}, bf16[272,1024]{1,0:T(8,128)(2,1)S(1)}, u32[]{:S(2)}, u32[]{:S(2)}) collective-permute-start(bf16[272,1024]{1,0:T(8,128)(2,1)S(1)} %collective-permute-done.8.refs_2_), channel_id=1, source_target_pairs={{1,0},{2,1},{3,2},{4,3},{5,4},{6,5},{7,6},{0,7},{9,8},{10,9},{11,1... | collective-permute-start | bytes 1671176 | tf_op jit(solution)/shard_map/ppermute | solution.py:283
  58.6 23.2 %collective-permute-start.3 = (bf16[256,1024]{1,0:T(8,128)(2,1)S(1)}, bf16[256,1024]{1,0:T(8,128)(2,1)S(1)}, u32[]{:S(2)}, u32[]{:S(2)}) collective-permute-start(bf16[256,1024]{1,0:T(8,128)(2,1)S(1)} %collective-permute-done.2.refs_2_), channel_id=1, source_target_pairs={{1,0},{2,1},{3,2},{4,3},{5,4},{6,5},{7,6},{0,7},{9,8},{10,9},{11,1... | collective-permute-start | bytes 1572872 | tf_op jit(solution)/shard_map/ppermute | solution.py:283
  62.3 20.4 %collective-permute-start.6 = (bf16[256,1024]{1,0:T(8,128)(2,1)S(1)}, bf16[256,1024]{1,0:T(8,128)(2,1)S(1)}, u32[]{:S(2)}, u32[]{:S(2)}) collective-permute-start(bf16[256,1024]{1,0:T(8,128)(2,1)S(1)} %collective-permute-done.5.refs_5_), channel_id=1, source_target_pairs={{0,1},{1,2},{2,3},{3,4},{4,5},{5,6},{6,7},{7,0},{8,9},{9,10},{10,1... | collective-permute-start | bytes 1572872 | tf_op jit(solution)/shard_map/ppermute | solution.py:281
  71.4 20.5 %collective-permute-start.13 = (bf16[272,1024]{1,0:T(8,128)(2,1)S(1)}, bf16[272,1024]{1,0:T(8,128)(2,1)S(1)}, u32[]{:S(2)}, u32[]{:S(2)}) collective-permute-start(bf16[272,1024]{1,0:T(8,128)(2,1)S(1)} %collective-permute-done.12.refs_6_), channel_id=1, source_target_pairs={{0,1},{1,2},{2,3},{3,4},{4,5},{5,6},{6,7},{7,0},{8,9},{9,10},{10,1... | collective-permute-start | bytes 1671176 | tf_op jit(solution)/shard_map/ppermute | solution.py:281
  71.5 20.5 %collective-permute-start.10 = (bf16[272,1024]{1,0:T(8,128)(2,1)S(1)}, bf16[272,1024]{1,0:T(8,128)(2,1)S(1)}, u32[]{:S(2)}, u32[]{:S(2)}) collective-permute-start(bf16[272,1024]{1,0:T(8,128)(2,1)S(1)} %collective-permute-done.9.refs_3_), channel_id=1, source_target_pairs={{1,0},{2,1},{3,2},{4,3},{5,4},{6,5},{7,6},{0,7},{9,8},{10,9},{11,1... | collective-permute-start | bytes 1671176 | tf_op jit(solution)/shard_map/ppermute | solution.py:283
  98.0 5.9 %collective-permute-start.16 = (bf16[1024,1024]{1,0:T(8,128)(2,1)S(1)}, bf16[1024,1024]{1,0:T(8,128)(2,1)S(1)}, u32[]{:S(2)}, u32[]{:S(2)}) collective-permute-start(bf16[1024,1024]{1,0:T(8,128)(2,1)S(1)} %get-tuple-element.76.own_ref), channel_id=1, source_target_pairs={{16,24},{32,40},{48,56},{64,72},{80,88},{96,104},{112,120},{128,13... | collective-permute-start | bytes 6291464 | tf_op jit(solution)/shard_map/ppermute | solution.py:333
  101.2 2.7 %collective-permute-start.17 = (bf16[16,1024]{1,0:T(8,128)(2,1)S(1)}, bf16[16,1024]{1,0:T(8,128)(2,1)S(1)}, u32[]{:S(2)}, u32[]{:S(2)}) collective-permute-start(bf16[16,1024]{1,0:T(8,128)(2,1)S(1)} %get-tuple-element.77.term_ref.own_term_ref), channel_id=1, source_target_pairs={{16,24},{32,40},{48,56},{64,72},{80,88},{96,104},{112,120},{128,13... | collective-permute-start | bytes 98312 | tf_op jit(solution)/shard_map/ppermute | solution.py:337
  102.5 0.7 collective-permute-start.14
  103.2 0.7 collective-permute-start.15
  103.9 4.3 %collective-permute-start.22 = (bf16[1024,1024]{1,0:T(8,128)(2,1)S(1)}, bf16[1024,1024]{1,0:T(8,128)(2,1)S(1)}, u32[]{:S(2)}, u32[]{:S(2)}) collective-permute-start(bf16[1024,1024]{1,0:T(8,128)(2,1)S(1)} %get-tuple-element.76.own_ref), channel_id=1, source_target_pairs={{0,8},{1,9},{2,10},{3,11},{4,12},{5,13},{6,14},{7,15}} | collective-permute-start | bytes 6291464 | tf_op jit(solution)/shard_map/ppermute | solution.py:352
  104.8 3.5 %collective-permute-start.23 = (bf16[16,1024]{1,0:T(8,128)(2,1)S(1)}, bf16[16,1024]{1,0:T(8,128)(2,1)S(1)}, u32[]{:S(2)}, u32[]{:S(2)}) collective-permute-start(bf16[16,1024]{1,0:T(8,128)(2,1)S(1)} %get-tuple-element.77.term_ref.own_term_ref), channel_id=1, source_target_pairs={{0,8},{1,9},{2,10},{3,11},{4,12},{5,13},{6,14},{7,15}} | collective-permute-start | bytes 98312 | tf_op jit(solution)/shard_map/ppermute | solution.py:352
  105.4 0.7 collective-permute-start.18
  106.1 0.7 collective-permute-start.19
  106.8 0.7 collective-permute-start.20
  107.6 1.3 collective-permute-start.21
  111.7 0.7 collective-permute-start.28
  112.4 0.7 collective-permute-start.29
  113.2 0.7 collective-permute-start.30
  113.9 0.7 collective-permute-start.31
  114.6 0.7 collective-permute-start.32
  115.3 1.3 collective-permute-start.33
  116.0 2.0 %collective-permute-start.34 = (f32[1,1024]{1,0:T(1,128)S(1)}, f32[1,1024]{1,0:T(1,128)S(1)}, u32[]{:S(2)}, u32[]{:S(2)}) collective-permute-start(f32[1,1024]{1,0:T(1,128)S(1)} %get-tuple-element.102.begin_ref), channel_id=1, source_target_pairs={{8,0},{24,16},{40,32},{56,48},{72,64},{88,80},{104,96},{120,112},{... | collective-permute-start | bytes 12296 | tf_op jit(solution)/shard_map/ppermute | solution.py:367
  116.6 49.0 %collective-permute-start.35 = (f32[1,1024]{1,0:T(1,128)S(1)}, f32[1,1024]{1,0:T(1,128)S(1)}, u32[]{:S(2)}, u32[]{:S(2)}) collective-permute-start(f32[1,1024]{1,0:T(1,128)S(1)} %collective-permute-done.33.came_ref), channel_id=1, source_target_pairs={{248,240},{249,241},{250,242},{251,243},{252,244},{253,245},{254,2... | collective-permute-start | bytes 12296 | tf_op jit(solution)/shard_map/ppermute | solution.py:368
  (10 other events, 123.0 us)

commit v6 on v5

--- a/solution.py
+++ b/solution.py
@@ -108,7 +108,7 @@
 
 
 def two_kernel(count, *refs):
-    pieces, (two_ref, slab_ref, one_ref, next_ref, sems) = refs[:count], refs[count:]
+    pieces, (two_ref, slab_ref, next_ref, one_ref, sems) = refs[:count], refs[count:]
     width = slab_ref.shape[0]
     place = lax.axis_index("state")
     ones = fetched(count, place, pieces, 0, one_ref, sems, 0)
@@ -119,37 +119,29 @@
     slab_ref[...] = two_ref[pl.ds(pl.multiple_of(place * width, width), width), :]
 
 
-def gather_kernel(count, prior_ref, first_ref, second_ref, *refs):
+def four_kernel(count, two_ref, *refs):
     pieces = refs[:count]
-    third_ref, fourth_ref, drive_ref, mean_ref, parts_ref, sems = refs[count:]
-    width = third_ref.shape[0] // count
+    four_ref, slab3_ref, slab4_ref, third_ref, fourth_ref, drive_ref, three_ref, parts_ref, sems = refs[count:]
+    width = slab3_ref.shape[0]
     place = lax.axis_index("state")
-    copies = fetched(count, place, pieces, 0, third_ref, sems, 0)
-    copies += fetched(count, place, pieces, 1, fourth_ref, sems, count)
+    thirds = fetched(count, place, pieces, 0, third_ref, sems, 0)
+    fourths = fetched(count, place, pieces, 1, fourth_ref, sems, count)
     parts = []
     for r in range(count):
         parts.append(pltpu.make_async_copy(pieces[r].at[pl.ds(2 * width, 16), :], parts_ref.at[r], sems.at[2 * count + r]))
         parts[r].start()
-    for copy in copies + parts:
+    mine = pl.ds(pl.multiple_of(place * width, width), width)
+    for copy in thirds:
+        copy.wait()
+    matmul(third_ref, two_ref, three_ref)
+    slab3_ref[...] = three_ref[mine, :]
+    for copy in fourths:
+        copy.wait()
+    matmul(fourth_ref, three_ref, four_ref)
+    slab4_ref[...] = four_ref[mine, :]
+    for copy in parts:
         copy.wait()
     drive_ref[...] = jnp.sum(parts_ref[...].astype(F32), axis=0)
-    mean_ref[...] = prior_ref[...]
-
-    @pl.when(lax.axis_index("tm") == 0)
-    def _():
-        mean = prior_ref[...]
-        for j, map_ref in enumerate((first_ref, second_ref, third_ref, fourth_ref)):
-            mean = times_t(mean, map_ref[...]) + joined(drive_ref[3 * j:3 * j + 3, :])
-        mean_ref[...] = mean
-
-
-def four_kernel(two_ref, third_ref, fourth_ref, four_ref, slab3_ref, slab4_ref, three_ref):
-    width = slab3_ref.shape[0]
-    mine = pl.ds(pl.multiple_of(lax.axis_index("state") * width, width), width)
-    matmul(third_ref, two_ref, three_ref)
-    slab3_ref[...] = three_ref[mine, :]
-    matmul(fourth_ref, three_ref, four_ref)
-    slab4_ref[...] = four_ref[mine, :]
 
 
 def local_kernel(drive_ref, second_ref, third_ref, fourth_ref, locals_ref, term_ref):
@@ -161,32 +153,35 @@
     term_ref[...] = split_rows(local)
 
 
-def pair_kernel(own_ref, own_term_ref, other_ref, other_term_ref, after_ref, qt_ref, q_ref):
-    @pl.when(core_here() != 0)
+DIRECT = 3
+
+
+def pair_kernel(own_ref, own_term_ref, other_ref, other_term_ref, turned_ref):
+    size = own_ref.shape[0]
+
+    @pl.when(jnp.logical_and(core_here() != 0, chip_here() >= DIRECT))
     def _():
         def block(i, carry):
             at = pl.ds(pl.multiple_of(i * ROWS, ROWS), ROWS)
             out = jnp.dot(own_ref[at, :], other_ref[...], preferred_element_type=F32)
-            qt_ref[:, at] = out.T.astype(BF16)
+            turned_ref[:size, at] = out.T.astype(BF16)
             return carry
 
-        lax.fori_loop(0, own_ref.shape[0] // ROWS, block, 0)
-        q_ref[...] = times_t(joined(other_term_ref[...]), own_ref[...]) + joined(own_term_ref[...])
-
-
-def first_hop_kernel(mean_ref, own_ref, term_ref, value_ref):
-    value_ref[...] = mean_ref[...]
-
-    @pl.when(lax.axis_index("tm") == 1)
-    def _():
-        value_ref[...] = times_t(mean_ref[...], own_ref[...]) + joined(term_ref[...])
-
-
-def second_hop_kernel(begin_ref, came_ref, own_ref, own_term_ref, other_ref, other_term_ref, held_ref, value_ref):
+        lax.fori_loop(0, size // ROWS, block, 0)
+        term = times_t(joined(other_term_ref[...]), own_ref[...]) + joined(own_term_ref[...])
+        turned_ref[size:, :] = split_rows(term)
+
+
+def applied(x, turned_ref):
+    size = x.shape[1]
+    return times(x, turned_ref[:size, :]) + joined(turned_ref[size:, :])
+
+
+def direct_kernel(turn, begin_ref, came_ref, own_ref, own_term_ref, other_ref, other_term_ref, held_ref, value_ref):
     held_ref[...] = begin_ref[...]
     value_ref[...] = begin_ref[...]
 
-    @pl.when(lax.axis_index("tm") == 3)
+    @pl.when(lax.axis_index("tm") == 2 * turn + 1)
     def _():
         begin = came_ref[...]
         held_ref[...] = begin
@@ -194,14 +189,14 @@
         value_ref[...] = times_t(between, own_ref[...]) + joined(own_term_ref[...])
 
 
-def hop_kernel(turn, begin_ref, came_ref, qt_ref, q_ref, held_ref, value_ref):
-    here = jnp.logical_and(chip_here() == turn, core_here() != 0)
+def hop_kernel(turn, begin_ref, came_ref, turned_ref, held_ref, value_ref):
+    here = lax.axis_index("tm") == 2 * turn + 1
 
     @pl.when(here)
     def _():
         begin = came_ref[...]
         held_ref[...] = begin
-        value_ref[...] = times(begin, qt_ref[...]) + q_ref[...]
+        value_ref[...] = applied(begin, turned_ref)
 
     @pl.when(jnp.logical_not(here))
     def _():
@@ -209,41 +204,63 @@
         value_ref[...] = begin_ref[...]
 
 
-def ready_kernel(other_ref, other_term_ref, other0_ref, other0_term_ref, locals_ref, after_ref, *refs):
+def double_kernel(firsts, came_ref, turned_ref, double_ref):
+    size = turned_ref.shape[1]
+    chip = chip_here()
+
+    @pl.when((core_here() != 0) & (chip > firsts) & (lax.rem(chip, 2) == 1) & (chip < 2 * firsts - 1))
+    def _():
+        matmul(came_ref.at[:size, :], turned_ref.at[:size, :], double_ref)
+        double_ref[size:, :] = split_rows(applied(joined(came_ref[size:, :]), turned_ref))
+
+
+def far_kernel(chip, last, begin_ref, came_ref, before_ref, map_ref, double_ref, held_ref, value_ref):
+    here = lax.axis_index("tm") == 2 * chip + 1
+
+    @pl.when(here)
+    def _():
+        if last:
+            value_ref[...] = before_ref[...]
+        else:
+            value_ref[...] = applied(came_ref[...], double_ref)
+        held_ref[...] = applied(came_ref[...], map_ref)
+
+    @pl.when(jnp.logical_not(here))
+    def _():
+        held_ref[...] = begin_ref[...]
+        value_ref[...] = before_ref[...]
+
+
+def final_kernel(firsts, held_ref, handed_ref, begin_ref):
+    chip = chip_here()
+    handed = jnp.logical_and(chip >= firsts, lax.rem(chip, 2) == 0)
+    begin_ref[...] = jnp.where(handed, handed_ref[...], held_ref[...])
+
+
+def ready_kernel(other_ref, other_term_ref, locals_ref, after_ref, *refs):
     slabs, (maps_ref, terms_ref) = refs[:-2], refs[-2:]
     width, size = slabs[1].shape
     mine = pl.ds(pl.multiple_of(lax.axis_index("state") * width, width), width)
 
-    def write(whole_ref, term_ref):
-        for j, slab_ref in enumerate(slabs):
-            at = slice(j * width, (j + 1) * width)
-            out = jnp.dot(slab_ref[:width, :], whole_ref[...], preferred_element_type=F32)
-            maps_ref[:, at] = out.T.astype(BF16)
-            term = times_t(joined(term_ref[...]), slab_ref[:width, :])
-            terms_ref[j:j + 1, :] = term + locals_ref[j:j + 1, mine]
-
     @pl.when(core_here() == 0)
     def _():
         for j, slab_ref in enumerate(slabs):
             maps_ref[:, j * width:(j + 1) * width] = slab_ref[:width, :].astype(F32).T.astype(BF16)
             terms_ref[j:j + 1, :] = locals_ref[j:j + 1, mine]
 
-    @pl.when(lax.axis_index("tm") == 1)
-    def _():
-        write(other0_ref, other0_term_ref)
-
-    @pl.when(jnp.logical_and(core_here() != 0, lax.axis_index("tm") != 1))
-    def _():
-        write(other_ref, other_term_ref)
-
-
-def out_kernel(last, begin_ref, came_ref, got_ref, last_ref, maps_ref, terms_ref, out_ref):
+    @pl.when(core_here() != 0)
+    def _():
+        for j, slab_ref in enumerate(slabs):
+            at = slice(j * width, (j + 1) * width)
+            out = jnp.dot(slab_ref[:width, :], other_ref[...], preferred_element_type=F32)
+            maps_ref[:, at] = out.T.astype(BF16)
+            term = times_t(joined(other_term_ref[...]), slab_ref[:width, :])
+            terms_ref[j:j + 1, :] = term + locals_ref[j:j + 1, mine]
+
+
+def out_kernel(begin_ref, got_ref, maps_ref, terms_ref, out_ref):
     steps, width = out_ref.shape
-    first, second = (got_ref[...], last_ref[...]), (begin_ref[...], came_ref[...])
-    at_last = chip_here() == last
-    begin = jnp.where(
-        core_here() == 0, jnp.where(at_last, first[1], first[0]), jnp.where(at_last, second[1], second[0])
-    )
+    begin = jnp.where(core_here() == 0, got_ref[...], begin_ref[...])
     row = times(begin, maps_ref[...])
     for j in range(steps):
         out_ref[j:j + 1, :] = row[:, j * width:(j + 1) * width] + terms_ref[j:j + 1, :]
@@ -313,63 +330,71 @@
         [transition[:half].reshape(half * width, size), packed], "state",
         lambda r, i, found: (packed,) if (r, i) == (2, 0) else (),
     )
-    begin = prior.reshape(1, size)
-    two, slab2, first, second = call(
-        functools.partial(two_kernel, count), (matrix, slab, matrix, matrix), [A] * count,
-        [pltpu.SemaphoreType.DMA((2 * count,))], flops=2 * size ** 3, moved=6 * size ** 2,
+    two, slab2, second = call(
+        functools.partial(two_kernel, count), (matrix, slab, matrix), [A] * count,
+        [whole, pltpu.SemaphoreType.DMA((2 * count,))], flops=2 * size ** 3, moved=6 * size ** 2,
     )(*early)
-    third, fourth, drive, mean = call(
-        functools.partial(gather_kernel, count),
-        (matrix, matrix, jax.ShapeDtypeStruct((16, size), F32), row),
-        [V] * 3 + [A] * count,
-        [pltpu.VMEM((count, 16, size), BF16), pltpu.SemaphoreType.DMA((3 * count,))],
-        flops=128 * size ** 2, moved=8 * size ** 2,
-    )(begin, first, second, *late)
+    own, slab3, slab4, third, fourth, drive = call(
+        functools.partial(four_kernel, count),
+        (matrix, slab, slab, matrix, matrix, jax.ShapeDtypeStruct((16, size), F32)),
+        [V] + [A] * count,
+        [whole, pltpu.VMEM((count, 16, size), BF16), pltpu.SemaphoreType.DMA((3 * count,))],
+        flops=4 * size ** 3, moved=8 * size ** 2,
+    )(two, *late)
     pairs = [(i, i + 1) for i in range(0, blocks_of_time, 2)]
-    mean = lax.ppermute(mean, "tm", pairs[:1])
-    own, slab3, slab4 = call(
-        four_kernel, (matrix, slab, slab), [V] * 3, [whole], flops=4 * size ** 3, moved=8 * size ** 2,
-    )(two, third, fourth)
-    other = lax.ppermute(own, "tm", pairs[1:])
+    other = lax.ppermute(own, "tm", pairs)
     locals_, own_term = call(
         local_kernel, (steps, rows), [V] * 4, flops=96 * size ** 2, moved=6 * size ** 2
     )(drive, second, third, fourth)
-    other_term = lax.ppermute(own_term, "tm", pairs[1:])
-
-    def hop(value, turn):
-        return lax.ppermute(value, "tm", [(2 * turn + 1, 2 * turn + 3)])
+    other_term = lax.ppermute(own_term, "tm", pairs)
 
     chips = blocks_of_time // 2
-    value = call(first_hop_kernel, row, [V] * 3, flops=32 * size ** 2, moved=2 * size ** 2)(mean, own, own_term)
-    came = hop(value, 0)
-    begin, value = call(
-        second_hop_kernel, (row, row), [V] * 6, flops=64 * size ** 2, moved=4 * size ** 2
-    )(begin, came, own, own_term, other, other_term)
-    came = hop(value, 1)
-    turned, term = call(
-        pair_kernel, (matrix, row), [V] * 5, flops=2 * size ** 3, moved=6 * size ** 2
-    )(own, own_term, other, other_term, value)
-    other0, other0_term = lax.ppermute(after((own, own_term), turned), "tm", pairs[:1])
-    for turn in range(2, chips - 1):
-        begin, value = call(
-            functools.partial(hop_kernel, turn), (row, row), [V] * 4,
-            flops=32 * size ** 2, moved=2 * size ** 2,
-        )(begin, came, turned, term)
-        came = hop(value, turn)
-        if turn == 3:
+    firsts = chips // 2
+    longer = jax.ShapeDtypeStruct((size + 16, size), BF16)
+    turned = call(
+        pair_kernel, longer, [V] * 4, flops=2 * size ** 3, moved=6 * size ** 2
+    )(own, own_term, other, other_term)
+    before = lax.ppermute(turned, "tm", [(2 * c + 1, 2 * c + 3) for c in range(firsts, chips, 2)])
+
+    begin = after(prior.reshape(1, size), turned)
+    came = begin
+    for turn in range(firsts):
+        if turn < DIRECT:
+            begin, value = call(
+                functools.partial(direct_kernel, turn), (row, row), [V] * 6,
+                flops=64 * size ** 2, moved=4 * size ** 2,
+            )(begin, came, own, own_term, other, other_term)
+        else:
+            begin, value = call(
+                functools.partial(hop_kernel, turn), (row, row), [V] * 3,
+                flops=32 * size ** 2, moved=2 * size ** 2,
+            )(begin, came, turned)
+        came = lax.ppermute(value, "tm", [(2 * turn + 1, 2 * turn + (3 if turn + 1 < firsts else 5))])
+        if turn == DIRECT:
             maps, terms = call(
                 ready_kernel,
                 (jax.ShapeDtypeStruct((size, steps_here * width), BF16), jax.ShapeDtypeStruct((steps_here, width), F32)),
-                [V] * 10, flops=size ** 3, moved=4 * size ** 2,
-            )(other, other_term, other0, other0_term, locals_, value, early[0], slab2, slab3, slab4)
-        if turn == 4:
+                [V] * 8, flops=size ** 3, moved=4 * size ** 2,
+            )(other, other_term, locals_, value, early[0], slab2, slab3, slab4)
+        if turn == DIRECT + 1:
             came = after(came, maps)
-    got = lax.ppermute(begin, "tm", [(b, a) for a, b in pairs[:-1]])
-    last = lax.ppermute(came, "tm", [(b, a) for a, b in pairs[-1:]])
+    double = call(
+        functools.partial(double_kernel, firsts), longer, [V, V], flops=2 * size ** 3, moved=6 * size ** 2
+    )(before, turned)
+    for chip in range(firsts + 1, chips, 2):
+        begin, value = call(
+            functools.partial(far_kernel, chip, chip == chips - 1), (row, row), [V] * 5,
+            flops=64 * size ** 2, moved=4 * size ** 2,
+        )(begin, came, value, before, double)
+        if chip < chips - 1:
+            came = lax.ppermute(value, "tm", [(2 * chip + 1, 2 * chip + 5)])
+    handed = lax.ppermute(value, "tm", [(2 * c - 1, 2 * c + 1) for c in range(firsts, chips, 2)])
+    begin = call(functools.partial(final_kernel, firsts), row, [V, V])(begin, handed)
+    got = lax.ppermute(begin, "tm", [(b, a) for a, b in pairs])
     return call(
-        functools.partial(out_kernel, chips - 1), jax.ShapeDtypeStruct((steps_here, width), F32), [V] * 6,
+        out_kernel, jax.ShapeDtypeStruct((steps_here, width), F32), [V] * 4,
         flops=16 * size ** 2, moved=size ** 2,
-    )(begin, came, got, last, maps, terms)
+    )(begin, got, maps, terms)
 
 
 def solution(mesh):

time: 167 us -> 157 us (0.940)
  waiting for transfers between devices: 108 us -> 101 us
  starting transfers between devices: 42.4 us -> 38.5 us
    ppermute x22 -> x16, waiting for transfers between devices: 47.8 us -> 41.4 us  [the longest x1 40.6 us: shards(): got = lax.ppermute(begin, 'tm', [(b, a) for a, b in pairs])]
    ppermute x22 -> x16, starting transfers between devices: 16.7 us -> 12.7 us  [the longest x8 5.29 us: shards(): lax.ppermute(value, 'tm', [(2 * turn + 1, 2 * turn + (3 if turn + 1 < fir...]
    pallas_call x20 -> x18, Pallas kernels: 10.3 us -> 10.4 us  [the longest x1 6.03 us: shards(): call(functools.partial(four_kernel, count), (matrix, slab, slab, matrix,...]
  transfers between devices with their start and end apart: 36 -> 30, of which waited for: 11 -> 12; matrix products, arithmetic and copies ran while one was open for 0% -> 0% of each run, Pallas kernels for 4% -> 5%
where the time goes in v6:
time: 157 us; the launch traced here: 156 us
  waiting for transfers between devices  101 us (64%)
  starting transfers between devices  38.5 us (25%)
  Pallas kernels  14.1 us (9%)
    ppermute x1, waiting for transfers between devices, shards(): got = lax.ppermute(begin, 'tm', [(b, a) for a, b in pairs])  40.6 us
    ppermute x7, waiting for transfers between devices, ring_rounds(): pieces[count - r] = lax.ppermute(left, axis, forward)  38 us
    ppermute x7, waiting for transfers between devices, ring_rounds(): pieces[r] = lax.ppermute(right, axis, backward)  22.1 us
    ppermute x7, starting transfers between devices, ring_rounds(): pieces[r] = lax.ppermute(right, axis, backward)  20.3 us
    pallas_call x1, Pallas kernels, shards(): call(functools.partial(four_kernel, count), (matrix, slab, slab, matrix,...  6.03 us
    ppermute x7, starting transfers between devices, ring_rounds(): pieces[count - r] = lax.ppermute(left, axis, forward)  5.4 us
    ppermute x8, starting transfers between devices, shards(): lax.ppermute(value, 'tm', [(2 * turn + 1, 2 * turn + (3 if turn + 1 < fir...  5.29 us
  transfers between devices with their start and end apart: 30, of which 12 were waited for; matrix products, arithmetic and copies ran while one was open for 0% of the time, Pallas kernels for 5%

profile of v6, /device:TPU:30, one launch (start us, length us, event | category | flops | bytes accessed | tf_op | source)
XLA Modules:
  0.0 156.0 jit_solution(15303809127289016625)
XLA Ops:
  0.0 1.4 fusion
  1.5 2.0 %collective-permute-start.1 = (bf16[256,1024]{1,0:T(8,128)(2,1)S(1)}, bf16[256,1024]{1,0:T(8,128)(2,1)S(1)}, u32[]{:S(2)}, u32[]{:S(2)}) collective-permute-start(bf16[256,1024]{1,0:T(8,128)(2,1)S(1)} %bitcast.2), channel_id=1, source_target_pairs={{0,1},{1,2},{2,3},{3,4},{4,5},{5,6},{6,7},{7,0},{8,9},{9,10},{10,1... | collective-permute-start | bytes 1572872 | tf_op jit(solution)/shard_map/ppermute | solution.py:298
  3.4 4.0 %collective-permute-start = (bf16[256,1024]{1,0:T(8,128)(2,1)S(1)}, bf16[256,1024]{1,0:T(8,128)(2,1)S(1)}, u32[]{:S(2)}, u32[]{:S(2)}) collective-permute-start(bf16[256,1024]{1,0:T(8,128)(2,1)S(1)} %bitcast.3), channel_id=1, source_target_pairs={{1,0},{2,1},{3,2},{4,3},{5,4},{6,5},{7,6},{0,7},{9,8},{10,9},{11,1... | collective-permute-start | bytes 1572872 | tf_op jit(solution)/shard_map/ppermute | solution.py:300
  7.5 1.6 %shard_map.73.refs_0_ = bf16[272,1024]{1,0:T(8,128)(2,1)S(1)} custom-call(s32[4,32]{1,0:T(4,128)S(1)} %copy-done.2, s32[4,32]{1,0:T(4,128)S(1)} %copy-done.3, bf16[4,4096]{1,0:T(4,128)(2,1)S(1)} %multiply_convert_fusion.values_ref, bf16[4,32,64,64]{3,2,1,0:T(8,128)(2,1)S(1)} %copy-done, bf16[2,128,1024]{2,1,0:T(8,128)(2,1)S(1)} %get-tuple-element.87.maps_ref), custom_call_target="tpu_custom_call" | custom-call | flops 10000000 | bytes 2097152 | tf_op jit(solution)/shard_map/pallas_call | solution.py:320
  9.1 2.0 %collective-permute-start.7 = (bf16[272,1024]{1,0:T(8,128)(2,1)S(1)}, bf16[272,1024]{1,0:T(8,128)(2,1)S(1)}, u32[]{:S(2)}, u32[]{:S(2)}) collective-permute-start(bf16[272,1024]{1,0:T(8,128)(2,1)S(1)} %shard_map.73.refs_0_), channel_id=1, source_target_pairs={{1,0},{2,1},{3,2},{4,3},{5,4},{6,5},{7,6},{0,7},{9,8},{10,9},{11,1... | collective-permute-start | bytes 1671176 | tf_op jit(solution)/shard_map/ppermute | solution.py:300
  11.1 8.2 %collective-permute-done.1.refs_7_ = bf16[256,1024]{1,0:T(8,128)(2,1)S(1)} collective-permute-done((bf16[256,1024]{1,0:T(8,128)(2,1)S(1)}, bf16[256,1024]{1,0:T(8,128)(2,1)S(1)}, u32[]{:S(2)}, u32[]{:S(2)}) %collective-permute-start.1) | collective-permute-done | bytes 524320 | tf_op jit(solution)/shard_map/ppermute | solution.py:298
  20.2 3.0 %collective-permute-start.11 = (bf16[272,1024]{1,0:T(8,128)(2,1)S(1)}, bf16[272,1024]{1,0:T(8,128)(2,1)S(1)}, u32[]{:S(2)}, u32[]{:S(2)}) collective-permute-start(bf16[272,1024]{1,0:T(8,128)(2,1)S(1)} %shard_map.73.refs_0_), channel_id=1, source_target_pairs={{0,1},{1,2},{2,3},{3,4},{4,5},{5,6},{6,7},{7,0},{8,9},{9,10},{10,1... | collective-permute-start | bytes 1671176 | tf_op jit(solution)/shard_map/ppermute | solution.py:298
  23.2 7.4 %collective-permute-done.7.refs_1_ = bf16[272,1024]{1,0:T(8,128)(2,1)S(1)} collective-permute-done((bf16[272,1024]{1,0:T(8,128)(2,1)S(1)}, bf16[272,1024]{1,0:T(8,128)(2,1)S(1)}, u32[]{:S(2)}, u32[]{:S(2)}) %collective-permute-start.7) | collective-permute-done | bytes 557088 | tf_op jit(solution)/shard_map/ppermute | solution.py:300
  30.6 3.7 %collective-permute-start.8 = (bf16[272,1024]{1,0:T(8,128)(2,1)S(1)}, bf16[272,1024]{1,0:T(8,128)(2,1)S(1)}, u32[]{:S(2)}, u32[]{:S(2)}) collective-permute-start(bf16[272,1024]{1,0:T(8,128)(2,1)S(1)} %collective-permute-done.7.refs_1_), channel_id=1, source_target_pairs={{1,0},{2,1},{3,2},{4,3},{5,4},{6,5},{7,6},{0,7},{9,8},{10,9},{11,1... | collective-permute-start | bytes 1671176 | tf_op jit(solution)/shard_map/ppermute | solution.py:300
  34.7 1.6 %collective-permute-done.4.refs_6_ = bf16[256,1024]{1,0:T(8,128)(2,1)S(1)} collective-permute-done((bf16[256,1024]{1,0:T(8,128)(2,1)S(1)}, bf16[256,1024]{1,0:T(8,128)(2,1)S(1)}, u32[]{:S(2)}, u32[]{:S(2)}) %collective-permute-start.4) | collective-permute-done | bytes 524320 | tf_op jit(solution)/shard_map/ppermute | solution.py:298
  36.3 11.9 %collective-permute-done.11.refs_7_ = bf16[272,1024]{1,0:T(8,128)(2,1)S(1)} collective-permute-done((bf16[272,1024]{1,0:T(8,128)(2,1)S(1)}, bf16[272,1024]{1,0:T(8,128)(2,1)S(1)}, u32[]{:S(2)}, u32[]{:S(2)}) %collective-permute-start.11) | collective-permute-done | bytes 557088 | tf_op jit(solution)/shard_map/ppermute | solution.py:298
  48.3 3.2 %collective-permute-start.9 = (bf16[272,1024]{1,0:T(8,128)(2,1)S(1)}, bf16[272,1024]{1,0:T(8,128)(2,1)S(1)}, u32[]{:S(2)}, u32[]{:S(2)}) collective-permute-start(bf16[272,1024]{1,0:T(8,128)(2,1)S(1)} %collective-permute-done.8.refs_2_), channel_id=1, source_target_pairs={{1,0},{2,1},{3,2},{4,3},{5,4},{6,5},{7,6},{0,7},{9,8},{10,9},{11,1... | collective-permute-start | bytes 1671176 | tf_op jit(solution)/shard_map/ppermute | solution.py:300
  51.5 7.1 %collective-permute-done.2.refs_2_ = bf16[256,1024]{1,0:T(8,128)(2,1)S(1)} collective-permute-done((bf16[256,1024]{1,0:T(8,128)(2,1)S(1)}, bf16[256,1024]{1,0:T(8,128)(2,1)S(1)}, u32[]{:S(2)}, u32[]{:S(2)}) %collective-permute-start.2) | collective-permute-done | bytes 524320 | tf_op jit(solution)/shard_map/ppermute | solution.py:300
  58.6 3.7 %collective-permute-start.3 = (bf16[256,1024]{1,0:T(8,128)(2,1)S(1)}, bf16[256,1024]{1,0:T(8,128)(2,1)S(1)}, u32[]{:S(2)}, u32[]{:S(2)}) collective-permute-start(bf16[256,1024]{1,0:T(8,128)(2,1)S(1)} %collective-permute-done.2.refs_2_), channel_id=1, source_target_pairs={{1,0},{2,1},{3,2},{4,3},{5,4},{6,5},{7,6},{0,7},{9,8},{10,9},{11,1... | collective-permute-start | bytes 1572872 | tf_op jit(solution)/shard_map/ppermute | solution.py:300
  62.3 9.1 %collective-permute-done.12.refs_6_ = bf16[272,1024]{1,0:T(8,128)(2,1)S(1)} collective-permute-done((bf16[272,1024]{1,0:T(8,128)(2,1)S(1)}, bf16[272,1024]{1,0:T(8,128)(2,1)S(1)}, u32[]{:S(2)}, u32[]{:S(2)}) %collective-permute-start.12) | collective-permute-done | bytes 557088 | tf_op jit(solution)/shard_map/ppermute | solution.py:298
  71.5 3.2 %collective-permute-start.10 = (bf16[272,1024]{1,0:T(8,128)(2,1)S(1)}, bf16[272,1024]{1,0:T(8,128)(2,1)S(1)}, u32[]{:S(2)}, u32[]{:S(2)}) collective-permute-start(bf16[272,1024]{1,0:T(8,128)(2,1)S(1)} %collective-permute-done.9.refs_3_), channel_id=1, source_target_pairs={{1,0},{2,1},{3,2},{4,3},{5,4},{6,5},{7,6},{0,7},{9,8},{10,9},{11,1... | collective-permute-start | bytes 1671176 | tf_op jit(solution)/shard_map/ppermute | solution.py:300
  74.7 7.1 %collective-permute-done.3.refs_3_ = bf16[256,1024]{1,0:T(8,128)(2,1)S(1)} collective-permute-done((bf16[256,1024]{1,0:T(8,128)(2,1)S(1)}, bf16[256,1024]{1,0:T(8,128)(2,1)S(1)}, u32[]{:S(2)}, u32[]{:S(2)}) %collective-permute-start.3) | collective-permute-done | bytes 524320 | tf_op jit(solution)/shard_map/ppermute | solution.py:300
  81.8 0.9 collective-permute-done.6.refs_4_
  82.7 3.0 %shard_map.74 = (bf16[1024,1024]{1,0:T(8,128)(2,1)S(1)}, bf16[128,1024]{1,0:T(8,128)(2,1)S(1)}, bf16[1024,1024]{1,0:T(8,128)(2,1)S(1)}) custom-call(bf16[256,1024]{1,0:T(8,128)(2,1)S(1)} %bitcast.4, bf16[256,1024]{1,0:T(8,128)(2,1)S(1)} %collective-permute-done.refs_1_, bf16[256,1024]{1,0:T(8,128)(2,1)S(1)} %collective-permute-done.2.refs_2_, ...), custom_call_target="tpu_custom_call" | custom-call | flops 2147483648 | bytes 6291456 | tf_op jit(solution)/shard_map/pallas_call | solution.py:333
  85.7 6.2 %collective-permute-done.13.refs_5_ = bf16[272,1024]{1,0:T(8,128)(2,1)S(1)} collective-permute-done((bf16[272,1024]{1,0:T(8,128)(2,1)S(1)}, bf16[272,1024]{1,0:T(8,128)(2,1)S(1)}, u32[]{:S(2)}, u32[]{:S(2)}) %collective-permute-start.13) | collective-permute-done | bytes 557088 | tf_op jit(solution)/shard_map/ppermute | solution.py:298
  91.9 6.0 %shard_map.75 = (bf16[1024,1024]{1,0:T(8,128)(2,1)S(1)}, bf16[128,1024]{1,0:T(8,128)(2,1)S(1)}, bf16[128,1024]{1,0:T(8,128)(2,1)S(1)}, bf16[1024,1024]{1,0:T(8,1...) custom-call(bf16[1024,1024]{1,0:T(8,128)(2,1)S(1)} %get-tuple-element.48.two_ref, ...), custom_call_target="tpu_custom_call" | custom-call | flops 4294967296 | bytes 8388608 | tf_op jit(solution)/shard_map/pallas_call | solution.py:337
  98.0 1.4 collective-permute-start.14
  99.4 1.8 %shard_map.76 = (f32[4,1024]{1,0:T(4,128)S(1)}, bf16[16,1024]{1,0:T(8,128)(2,1)S(1)}) custom-call(f32[16,1024]{1,0:T(8,128)S(1)} %get-tuple-element.50.drive_ref, bf16[1024,1024]{1,0:T(8,128)(2,1)S(1)} %get-tuple-element.51.second_ref, bf16[1024,1024]{1,0:T(8,128)(2,1)S(1)} %get-tuple-element.52.third_ref, bf16[1024,1024]{1,0:T(8,128)(2,1)S(1)} %get-tuple-element.53.fourth_ref), custom_call_target="tpu_custom_call" | custom-call | flops 100663296 | bytes 6291456 | tf_op jit(solution)/shard_map/pallas_call | solution.py:346
  101.2 1.3 collective-permute-start.15
  102.5 0.8 collective-permute-done.15.other_term_ref
  103.3 0.8 collective-permute-start.24
  104.1 0.7 collective-permute-start.16
  104.9 0.7 collective-permute-start.17
  105.6 0.7 collective-permute-start.18
  113.3 1.3 collective-permute-start.29
  114.6 40.6 %collective-permute-done.29.got_ref = f32[1,1024]{1,0:T(1,128)S(1)} collective-permute-done((f32[1,1024]{1,0:T(1,128)S(1)}, f32[1,1024]{1,0:T(1,128)S(1)}, u32[]{:S(2)}, u32[]{:S(2)}) %collective-permute-start.29) | collective-permute-done | bytes 4128 | tf_op jit(solution)/shard_map/ppermute | solution.py:393
  155.1 0.8 shard_map.93
  (63 shorter events, 8.3 us)
Async XLA Ops:
  0.0 7.5 %copy-start.2 = (s32[4,32]{1,0:T(4,128)S(1)}, s32[4,32]{1,0:T(4,128)}, u32[]{:S(2)}) copy-start(s32[4,32]{1,0:T(4,128)} %rows_ref.1) | copy-start | bytes 1540
  0.0 7.5 %copy-start = (bf16[4,32,64,64]{3,2,1,0:T(8,128)(2,1)S(1)}, bf16[4,32,64,64]{3,2,1,0:T(8,128)(2,1)}, u32[]{:S(2)}) copy-start(bf16[4,32,64,64]{3,2,1,0:T(8,128)(2,1)} %blocks_ref.1) | copy-start | bytes 3145732
  1.5 17.9 %collective-permute-start.1 = (bf16[256,1024]{1,0:T(8,128)(2,1)S(1)}, bf16[256,1024]{1,0:T(8,128)(2,1)S(1)}, u32[]{:S(2)}, u32[]{:S(2)}) collective-permute-start(bf16[256,1024]{1,0:T(8,128)(2,1)S(1)} %bitcast.2), channel_id=1, source_target_pairs={{0,1},{1,2},{2,3},{3,4},{4,5},{5,6},{6,7},{7,0},{8,9},{9,10},{10,1... | collective-permute-start | bytes 1572872 | tf_op jit(solution)/shard_map/ppermute | solution.py:298
  3.4 16.4 %collective-permute-start = (bf16[256,1024]{1,0:T(8,128)(2,1)S(1)}, bf16[256,1024]{1,0:T(8,128)(2,1)S(1)}, u32[]{:S(2)}, u32[]{:S(2)}) collective-permute-start(bf16[256,1024]{1,0:T(8,128)(2,1)S(1)} %bitcast.3), channel_id=1, source_target_pairs={{1,0},{2,1},{3,2},{4,3},{5,4},{6,5},{7,6},{0,7},{9,8},{10,9},{11,1... | collective-permute-start | bytes 1572872 | tf_op jit(solution)/shard_map/ppermute | solution.py:300
  9.1 21.5 %collective-permute-start.7 = (bf16[272,1024]{1,0:T(8,128)(2,1)S(1)}, bf16[272,1024]{1,0:T(8,128)(2,1)S(1)}, u32[]{:S(2)}, u32[]{:S(2)}) collective-permute-start(bf16[272,1024]{1,0:T(8,128)(2,1)S(1)} %shard_map.73.refs_0_), channel_id=1, source_target_pairs={{1,0},{2,1},{3,2},{4,3},{5,4},{6,5},{7,6},{0,7},{9,8},{10,9},{11,1... | collective-permute-start | bytes 1671176 | tf_op jit(solution)/shard_map/ppermute | solution.py:300
  19.8 16.5 %collective-permute-start.4 = (bf16[256,1024]{1,0:T(8,128)(2,1)S(1)}, bf16[256,1024]{1,0:T(8,128)(2,1)S(1)}, u32[]{:S(2)}, u32[]{:S(2)}) collective-permute-start(bf16[256,1024]{1,0:T(8,128)(2,1)S(1)} %collective-permute-done.1.refs_7_), channel_id=1, source_target_pairs={{0,1},{1,2},{2,3},{3,4},{4,5},{5,6},{6,7},{7,0},{8,9},{9,10},{10,1... | collective-permute-start | bytes 1572872 | tf_op jit(solution)/shard_map/ppermute | solution.py:298
  20.2 28.1 %collective-permute-start.11 = (bf16[272,1024]{1,0:T(8,128)(2,1)S(1)}, bf16[272,1024]{1,0:T(8,128)(2,1)S(1)}, u32[]{:S(2)}, u32[]{:S(2)}) collective-permute-start(bf16[272,1024]{1,0:T(8,128)(2,1)S(1)} %shard_map.73.refs_0_), channel_id=1, source_target_pairs={{0,1},{1,2},{2,3},{3,4},{4,5},{5,6},{6,7},{7,0},{8,9},{9,10},{10,1... | collective-permute-start | bytes 1671176 | tf_op jit(solution)/shard_map/ppermute | solution.py:298
  30.6 17.7 %collective-permute-start.8 = (bf16[272,1024]{1,0:T(8,128)(2,1)S(1)}, bf16[272,1024]{1,0:T(8,128)(2,1)S(1)}, u32[]{:S(2)}, u32[]{:S(2)}) collective-permute-start(bf16[272,1024]{1,0:T(8,128)(2,1)S(1)} %collective-permute-done.7.refs_1_), channel_id=1, source_target_pairs={{1,0},{2,1},{3,2},{4,3},{5,4},{6,5},{7,6},{0,7},{9,8},{10,9},{11,1... | collective-permute-start | bytes 1671176 | tf_op jit(solution)/shard_map/ppermute | solution.py:300
  34.3 24.3 %collective-permute-start.2 = (bf16[256,1024]{1,0:T(8,128)(2,1)S(1)}, bf16[256,1024]{1,0:T(8,128)(2,1)S(1)}, u32[]{:S(2)}, u32[]{:S(2)}) collective-permute-start(bf16[256,1024]{1,0:T(8,128)(2,1)S(1)} %collective-permute-done.refs_1_), channel_id=1, source_target_pairs={{1,0},{2,1},{3,2},{4,3},{5,4},{6,5},{7,6},{0,7},{9,8},{10,9},{11,1... | collective-permute-start | bytes 1572872 | tf_op jit(solution)/shard_map/ppermute | solution.py:300
  36.3 26.0 %collective-permute-start.5 = (bf16[256,1024]{1,0:T(8,128)(2,1)S(1)}, bf16[256,1024]{1,0:T(8,128)(2,1)S(1)}, u32[]{:S(2)}, u32[]{:S(2)}) collective-permute-start(bf16[256,1024]{1,0:T(8,128)(2,1)S(1)} %collective-permute-done.4.refs_6_), channel_id=1, source_target_pairs={{0,1},{1,2},{2,3},{3,4},{4,5},{5,6},{6,7},{7,0},{8,9},{9,10},{10,1... | collective-permute-start | bytes 1572872 | tf_op jit(solution)/shard_map/ppermute | solution.py:298
  48.3 23.2 %collective-permute-start.12 = (bf16[272,1024]{1,0:T(8,128)(2,1)S(1)}, bf16[272,1024]{1,0:T(8,128)(2,1)S(1)}, u32[]{:S(2)}, u32[]{:S(2)}) collective-permute-start(bf16[272,1024]{1,0:T(8,128)(2,1)S(1)} %collective-permute-done.11.refs_7_), channel_id=1, source_target_pairs={{0,1},{1,2},{2,3},{3,4},{4,5},{5,6},{6,7},{7,0},{8,9},{9,10},{10,1... | collective-permute-start | bytes 1671176 | tf_op jit(solution)/shard_map/ppermute | solution.py:298
  48.3 23.2 %collective-permute-start.9 = (bf16[272,1024]{1,0:T(8,128)(2,1)S(1)}, bf16[272,1024]{1,0:T(8,128)(2,1)S(1)}, u32[]{:S(2)}, u32[]{:S(2)}) collective-permute-start(bf16[272,1024]{1,0:T(8,128)(2,1)S(1)} %collective-permute-done.8.refs_2_), channel_id=1, source_target_pairs={{1,0},{2,1},{3,2},{4,3},{5,4},{6,5},{7,6},{0,7},{9,8},{10,9},{11,1... | collective-permute-start | bytes 1671176 | tf_op jit(solution)/shard_map/ppermute | solution.py:300
  58.6 23.2 %collective-permute-start.3 = (bf16[256,1024]{1,0:T(8,128)(2,1)S(1)}, bf16[256,1024]{1,0:T(8,128)(2,1)S(1)}, u32[]{:S(2)}, u32[]{:S(2)}) collective-permute-start(bf16[256,1024]{1,0:T(8,128)(2,1)S(1)} %collective-permute-done.2.refs_2_), channel_id=1, source_target_pairs={{1,0},{2,1},{3,2},{4,3},{5,4},{6,5},{7,6},{0,7},{9,8},{10,9},{11,1... | collective-permute-start | bytes 1572872 | tf_op jit(solution)/shard_map/ppermute | solution.py:300
  62.3 20.4 %collective-permute-start.6 = (bf16[256,1024]{1,0:T(8,128)(2,1)S(1)}, bf16[256,1024]{1,0:T(8,128)(2,1)S(1)}, u32[]{:S(2)}, u32[]{:S(2)}) collective-permute-start(bf16[256,1024]{1,0:T(8,128)(2,1)S(1)} %collective-permute-done.5.refs_5_), channel_id=1, source_target_pairs={{0,1},{1,2},{2,3},{3,4},{4,5},{5,6},{6,7},{7,0},{8,9},{9,10},{10,1... | collective-permute-start | bytes 1572872 | tf_op jit(solution)/shard_map/ppermute | solution.py:298
  71.4 20.5 %collective-permute-start.13 = (bf16[272,1024]{1,0:T(8,128)(2,1)S(1)}, bf16[272,1024]{1,0:T(8,128)(2,1)S(1)}, u32[]{:S(2)}, u32[]{:S(2)}) collective-permute-start(bf16[272,1024]{1,0:T(8,128)(2,1)S(1)} %collective-permute-done.12.refs_6_), channel_id=1, source_target_pairs={{0,1},{1,2},{2,3},{3,4},{4,5},{5,6},{6,7},{7,0},{8,9},{9,10},{10,1... | collective-permute-start | bytes 1671176 | tf_op jit(solution)/shard_map/ppermute | solution.py:298
  71.5 20.5 %collective-permute-start.10 = (bf16[272,1024]{1,0:T(8,128)(2,1)S(1)}, bf16[272,1024]{1,0:T(8,128)(2,1)S(1)}, u32[]{:S(2)}, u32[]{:S(2)}) collective-permute-start(bf16[272,1024]{1,0:T(8,128)(2,1)S(1)} %collective-permute-done.9.refs_3_), channel_id=1, source_target_pairs={{1,0},{2,1},{3,2},{4,3},{5,4},{6,5},{7,6},{0,7},{9,8},{10,9},{11,1... | collective-permute-start | bytes 1671176 | tf_op jit(solution)/shard_map/ppermute | solution.py:300
  98.0 5.4 %collective-permute-start.14 = (bf16[1024,1024]{1,0:T(8,128)(2,1)S(1)}, bf16[1024,1024]{1,0:T(8,128)(2,1)S(1)}, u32[]{:S(2)}, u32[]{:S(2)}) collective-permute-start(bf16[1024,1024]{1,0:T(8,128)(2,1)S(1)} %get-tuple-element.49.own_ref), channel_id=1, source_target_pairs={{0,8},{16,24},{32,40},{48,56},{64,72},{80,88},{96,104},{112,120},{... | collective-permute-start | bytes 6291464 | tf_op jit(solution)/shard_map/ppermute | solution.py:345
  101.2 2.1 %collective-permute-start.15 = (bf16[16,1024]{1,0:T(8,128)(2,1)S(1)}, bf16[16,1024]{1,0:T(8,128)(2,1)S(1)}, u32[]{:S(2)}, u32[]{:S(2)}) collective-permute-start(bf16[16,1024]{1,0:T(8,128)(2,1)S(1)} %get-tuple-element.54.own_term_ref), channel_id=1, source_target_pairs={{0,8},{16,24},{32,40},{48,56},{64,72},{80,88},{96,104},{112,120},{... | collective-permute-start | bytes 98312 | tf_op jit(solution)/shard_map/ppermute | solution.py:349
  103.3 7.0 %collective-permute-start.24 = (bf16[1040,1024]{1,0:T(8,128)(2,1)S(1)}, bf16[1040,1024]{1,0:T(8,128)(2,1)S(1)}, u32[]{:S(2)}, u32[]{:S(2)}) collective-permute-start(bf16[1040,1024]{1,0:T(8,128)(2,1)S(1)} %shard_map.77.turned_ref), channel_id=1, source_target_pairs={{136,152},{168,184},{200,216},{232,248},{137,153},{169,185},{201,2... | collective-permute-start | bytes 6389768 | tf_op jit(solution)/shard_map/ppermute | solution.py:357
  104.1 0.7 collective-permute-start.16
  104.9 0.7 collective-permute-start.17
  105.6 0.7 collective-permute-start.18
  106.3 0.7 collective-permute-start.19
  107.0 1.0 collective-permute-start.20
  108.3 0.7 collective-permute-start.21
  109.0 0.7 collective-permute-start.22
  109.7 0.7 collective-permute-start.23
  110.4 0.7 collective-permute-start.25
  111.2 0.7 collective-permute-start.26
  111.9 0.7 collective-permute-start.27
  112.6 0.7 collective-permute-start.28
  113.3 41.9 %collective-permute-start.29 = (f32[1,1024]{1,0:T(1,128)S(1)}, f32[1,1024]{1,0:T(1,128)S(1)}, u32[]{:S(2)}, u32[]{:S(2)}) collective-permute-start(f32[1,1024]{1,0:T(1,128)S(1)} %shard_map.92.begin_ref), channel_id=1, source_target_pairs={{8,0},{24,16},{40,32},{56,48},{72,64},{88,80},{104,96},{120,112},{... | collective-permute-start | bytes 12296 | tf_op jit(solution)/shard_map/ppermute | solution.py:393
  (4 other events, 25.4 us)

commit v7 on v6

--- a/solution.py
+++ b/solution.py
@@ -31,13 +31,25 @@
     return jnp.sum(rows.astype(F32), axis=0, keepdims=True)
 
 
-def times_t(x, matrix):
-    out = lax.dot_general(split_rows(x), matrix, (((1,), (1,)), ((), ())), preferred_element_type=F32)
-    return joined(out)
-
-
-def times(x, matrix):
-    return joined(jnp.dot(split_rows(x), matrix, preferred_element_type=F32))
+def times_t(x, *parts):
+    left = split_rows(x)
+    out = [
+        joined(lax.dot_general(left, part, (((1,), (1,)), ((), ())), preferred_element_type=F32)) for part in parts
+    ]
+    return out[0] if len(out) == 1 else jnp.concatenate(out, axis=1)
+
+
+def times(x, *parts):
+    left = split_rows(x)
+    return joined(product(left, *parts))
+
+
+def product(left, *parts):
+    rows = parts[0].shape[0]
+    out = [
+        jnp.dot(left[:, i * rows:(i + 1) * rows], part, preferred_element_type=F32) for i, part in enumerate(parts)
+    ]
+    return sum(out[1:], out[0])
 
 
 def matmul(left_ref, right_ref, out_ref):
@@ -97,10 +109,10 @@
 def fetched(count, place, pieces, j, whole_ref, sems, first):
     width = whole_ref.shape[0] // count
     copies = []
-    for r in range(count):
+    for i, (r, piece) in enumerate(pieces):
         at = pl.multiple_of(lax.rem(place + r, count) * width, width)
         copy = pltpu.make_async_copy(
-            pieces[r].at[pl.ds(j * width, width), :], whole_ref.at[pl.ds(at, width), :], sems.at[first + r]
+            piece.at[pl.ds(j * width, width), :], whole_ref.at[pl.ds(at, width), :], sems.at[first + i]
         )
         copy.start()
         copies.append(copy)
@@ -108,7 +120,7 @@
 
 
 def two_kernel(count, *refs):
-    pieces, (two_ref, slab_ref, next_ref, one_ref, sems) = refs[:count], refs[count:]
+    pieces, (two_ref, slab_ref, next_ref, one_ref, sems) = list(enumerate(refs[:count])), refs[count:]
     width = slab_ref.shape[0]
     place = lax.axis_index("state")
     ones = fetched(count, place, pieces, 0, one_ref, sems, 0)
@@ -119,25 +131,42 @@
     slab_ref[...] = two_ref[pl.ds(pl.multiple_of(place * width, width), width), :]
 
 
-def four_kernel(count, two_ref, *refs):
-    pieces = refs[:count]
-    four_ref, slab3_ref, slab4_ref, third_ref, fourth_ref, drive_ref, three_ref, parts_ref, sems = refs[count:]
+def three_kernel(count, have, two_ref, *refs):
+    pieces = list(zip(have, refs[:len(have)]))
+    three_ref, third_ref, fourth_ref, sems = refs[len(have):]
+    width = third_ref.shape[0] // count
+    place = lax.axis_index("state")
+    copies = fetched(count, place, pieces, 0, third_ref, sems, 0)
+    copies += fetched(count, place, pieces, 1, fourth_ref, sems, len(have))
+    for copy in copies:
+        copy.wait()
+    for r in have:
+        at = pl.ds(pl.multiple_of(lax.rem(place + r, count) * width, width), width)
+        three_ref[at, :] = jnp.dot(third_ref[at, :], two_ref[...], preferred_element_type=F32).astype(BF16)
+
+
+def four_kernel(count, have, two_ref, threes_ref, thirds_ref, fourths_ref, *refs):
+    missing = [(r, refs[r]) for r in range(count) if r not in have]
+    four_ref, slab3_ref, slab4_ref, three_ref, third_ref, fourth_ref, drive_ref, parts_ref, sems = refs[count:]
     width = slab3_ref.shape[0]
     place = lax.axis_index("state")
-    thirds = fetched(count, place, pieces, 0, third_ref, sems, 0)
-    fourths = fetched(count, place, pieces, 1, fourth_ref, sems, count)
+    thirds = fetched(count, place, missing, 0, third_ref, sems, 0)
+    fourths = fetched(count, place, missing, 1, fourth_ref, sems, len(missing))
     parts = []
     for r in range(count):
-        parts.append(pltpu.make_async_copy(pieces[r].at[pl.ds(2 * width, 16), :], parts_ref.at[r], sems.at[2 * count + r]))
+        at = 2 * len(missing) + r
+        parts.append(pltpu.make_async_copy(refs[r].at[pl.ds(2 * width, 16), :], parts_ref.at[r], sems.at[at]))
         parts[r].start()
+    for copy in thirds:
+        copy.wait()
+    for r, _ in missing:
+        at = pl.ds(pl.multiple_of(lax.rem(place + r, count) * width, width), width)
+        three_ref[at, :] = jnp.dot(third_ref[at, :], two_ref[...], preferred_element_type=F32).astype(BF16)
+    for copy in fourths:
+        copy.wait()
+    matmul(fourth_ref, three_ref, four_ref)
     mine = pl.ds(pl.multiple_of(place * width, width), width)
-    for copy in thirds:
-        copy.wait()
-    matmul(third_ref, two_ref, three_ref)
     slab3_ref[...] = three_ref[mine, :]
-    for copy in fourths:
-        copy.wait()
-    matmul(fourth_ref, three_ref, four_ref)
     slab4_ref[...] = four_ref[mine, :]
     for copy in parts:
         copy.wait()
@@ -156,25 +185,23 @@
 DIRECT = 3
 
 
-def pair_kernel(own_ref, own_term_ref, other_ref, other_term_ref, turned_ref):
-    size = own_ref.shape[0]
+def pair_kernel(half, own_ref, own_term_ref, other_ref, other_term_ref, turned_ref):
+    rows = own_ref.shape[0] // 2
+    at = slice(half * rows, (half + 1) * rows)
 
     @pl.when(jnp.logical_and(core_here() != 0, chip_here() >= DIRECT))
     def _():
-        def block(i, carry):
-            at = pl.ds(pl.multiple_of(i * ROWS, ROWS), ROWS)
-            out = jnp.dot(own_ref[at, :], other_ref[...], preferred_element_type=F32)
-            turned_ref[:size, at] = out.T.astype(BF16)
-            return carry
-
-        lax.fori_loop(0, size // ROWS, block, 0)
-        term = times_t(joined(other_term_ref[...]), own_ref[...]) + joined(own_term_ref[...])
-        turned_ref[size:, :] = split_rows(term)
-
-
-def applied(x, turned_ref):
-    size = x.shape[1]
-    return times(x, turned_ref[:size, :]) + joined(turned_ref[size:, :])
+        for i in range(2):
+            out = jnp.dot(own_ref[i * rows:(i + 1) * rows, :], other_ref[:, at], preferred_element_type=F32)
+            turned_ref[:rows, i * rows:(i + 1) * rows] = out.T.astype(BF16)
+        if half == 1:
+            term = times_t(joined(other_term_ref[...]), own_ref[...]) + joined(own_term_ref[...])
+            turned_ref[rows:, :] = split_rows(term)
+
+
+def applied(x, turned0_ref, turned1_ref):
+    rows = turned0_ref.shape[0]
+    return times(x, turned0_ref[...], turned1_ref[:rows, :]) + joined(turned1_ref[rows:, :])
 
 
 def direct_kernel(turn, begin_ref, came_ref, own_ref, own_term_ref, other_ref, other_term_ref, held_ref, value_ref):
@@ -189,14 +216,14 @@
         value_ref[...] = times_t(between, own_ref[...]) + joined(own_term_ref[...])
 
 
-def hop_kernel(turn, begin_ref, came_ref, turned_ref, held_ref, value_ref):
+def hop_kernel(turn, begin_ref, came_ref, turned0_ref, turned1_ref, held_ref, value_ref):
     here = lax.axis_index("tm") == 2 * turn + 1
 
     @pl.when(here)
     def _():
         begin = came_ref[...]
         held_ref[...] = begin
-        value_ref[...] = applied(begin, turned_ref)
+        value_ref[...] = applied(begin, turned0_ref, turned1_ref)
 
     @pl.when(jnp.logical_not(here))
     def _():
@@ -204,17 +231,20 @@
         value_ref[...] = begin_ref[...]
 
 
-def double_kernel(firsts, came_ref, turned_ref, double_ref):
-    size = turned_ref.shape[1]
+def double_kernel(half, firsts, came_ref, turned0_ref, turned1_ref, double_ref):
+    rows = turned0_ref.shape[0]
     chip = chip_here()
 
     @pl.when((core_here() != 0) & (chip > firsts) & (lax.rem(chip, 2) == 1) & (chip < 2 * firsts - 1))
     def _():
-        matmul(came_ref.at[:size, :], turned_ref.at[:size, :], double_ref)
-        double_ref[size:, :] = split_rows(applied(joined(came_ref[size:, :]), turned_ref))
-
-
-def far_kernel(chip, last, begin_ref, came_ref, before_ref, map_ref, double_ref, held_ref, value_ref):
+        double_ref[:rows, :] = product(came_ref[:rows, :], turned0_ref[...], turned1_ref[:rows, :]).astype(BF16)
+        if half == 1:
+            double_ref[rows:, :] = split_rows(applied(joined(came_ref[rows:, :]), turned0_ref, turned1_ref))
+
+
+def far_kernel(
+    chip, last, begin_ref, came_ref, before_ref, map0_ref, map1_ref, double0_ref, double1_ref, held_ref, value_ref
+):
     here = lax.axis_index("tm") == 2 * chip + 1
 
     @pl.when(here)
@@ -222,8 +252,8 @@
         if last:
             value_ref[...] = before_ref[...]
         else:
-            value_ref[...] = applied(came_ref[...], double_ref)
-        held_ref[...] = applied(came_ref[...], map_ref)
+            value_ref[...] = applied(came_ref[...], double0_ref, double1_ref)
+        held_ref[...] = applied(came_ref[...], map0_ref, map1_ref)
 
     @pl.when(jnp.logical_not(here))
     def _():
@@ -266,13 +296,14 @@
         out_ref[j:j + 1, :] = row[:, j * width:(j + 1) * width] + terms_ref[j:j + 1, :]
 
 
-def call(kernel, out_shape, spaces, scratch=(), flops=0, moved=0):
+def call(kernel, out_shape, spaces, scratch=(), flops=0, moved=0, aliases={}):
     return pl.pallas_call(
         kernel,
         out_shape=out_shape,
         in_specs=[pl.BlockSpec(memory_space=s) for s in spaces],
         out_specs=jax.tree.map(lambda _: pl.BlockSpec(memory_space=pltpu.VMEM), out_shape),
         scratch_shapes=list(scratch),
+        input_output_aliases=aliases,
         compiler_params=pltpu.CompilerParams(vmem_limit_bytes=VMEM_LIMIT),
         cost_estimate=pl.CostEstimate(flops=flops, bytes_accessed=moved, transcendentals=0),
     )
@@ -334,13 +365,18 @@
         functools.partial(two_kernel, count), (matrix, slab, matrix), [A] * count,
         [whole, pltpu.SemaphoreType.DMA((2 * count,))], flops=2 * size ** 3, moved=6 * size ** 2,
     )(*early)
-    own, slab3, slab4, third, fourth, drive = call(
-        functools.partial(four_kernel, count),
-        (matrix, slab, slab, matrix, matrix, jax.ShapeDtypeStruct((16, size), F32)),
-        [V] + [A] * count,
-        [whole, pltpu.VMEM((count, 16, size), BF16), pltpu.SemaphoreType.DMA((3 * count,))],
-        flops=4 * size ** 3, moved=8 * size ** 2,
-    )(two, *late)
+    have = [r for r in range(count) if r not in (count // 2, count // 2 + 1)]
+    three, third, fourth = call(
+        functools.partial(three_kernel, count, have), (matrix, matrix, matrix), [V] + [A] * len(have),
+        [pltpu.SemaphoreType.DMA((2 * len(have),))], flops=2 * size ** 3, moved=6 * size ** 2,
+    )(two, *[late[r] for r in have])
+    own, slab3, slab4, _, third, fourth, drive = call(
+        functools.partial(four_kernel, count, have),
+        (matrix, slab, slab, matrix, matrix, matrix, jax.ShapeDtypeStruct((16, size), F32)),
+        [V] * 4 + [A] * count,
+        [pltpu.VMEM((count, 16, size), BF16), pltpu.SemaphoreType.DMA((3 * count,))],
+        flops=2 * size ** 3, moved=6 * size ** 2, aliases={1: 3, 2: 4, 3: 5},
+    )(two, three, third, fourth, *late)
     pairs = [(i, i + 1) for i in range(0, blocks_of_time, 2)]
     other = lax.ppermute(own, "tm", pairs)
     locals_, own_term = call(
@@ -350,25 +386,29 @@
 
     chips = blocks_of_time // 2
     firsts = chips // 2
-    longer = jax.ShapeDtypeStruct((size + 16, size), BF16)
-    turned = call(
-        pair_kernel, longer, [V] * 4, flops=2 * size ** 3, moved=6 * size ** 2
-    )(own, own_term, other, other_term)
-    before = lax.ppermute(turned, "tm", [(2 * c + 1, 2 * c + 3) for c in range(firsts, chips, 2)])
-
-    begin = after(prior.reshape(1, size), turned)
+    part = jax.ShapeDtypeStruct((size // 2, size), BF16)
+    longer = jax.ShapeDtypeStruct((size // 2 + 16, size), BF16)
+    blocks_here = (own, own_term, other, other_term)
+    onward = [(2 * c + 1, 2 * c + 3) for c in range(firsts, chips, 2)]
+    half_cost = dict(flops=size ** 3, moved=6 * size ** 2)
+    turned0 = call(functools.partial(pair_kernel, 0), part, [V] * 4, **half_cost)(*blocks_here)
+    before0 = lax.ppermute(turned0, "tm", onward)
+    turned1 = call(functools.partial(pair_kernel, 1), longer, [V] * 4, **half_cost)(*blocks_here)
+    before1 = lax.ppermute(turned1, "tm", onward)
+
+    begin = after(prior.reshape(1, size), turned1)
     came = begin
     for turn in range(firsts):
         if turn < DIRECT:
             begin, value = call(
                 functools.partial(direct_kernel, turn), (row, row), [V] * 6,
                 flops=64 * size ** 2, moved=4 * size ** 2,
-            )(begin, came, own, own_term, other, other_term)
+            )(begin, came, *blocks_here)
         else:
             begin, value = call(
-                functools.partial(hop_kernel, turn), (row, row), [V] * 3,
+                functools.partial(hop_kernel, turn), (row, row), [V] * 4,
                 flops=32 * size ** 2, moved=2 * size ** 2,
-            )(begin, came, turned)
+            )(begin, came, turned0, turned1)
         came = lax.ppermute(value, "tm", [(2 * turn + 1, 2 * turn + (3 if turn + 1 < firsts else 5))])
         if turn == DIRECT:
             maps, terms = call(
@@ -378,14 +418,13 @@
             )(other, other_term, locals_, value, early[0], slab2, slab3, slab4)
         if turn == DIRECT + 1:
             came = after(came, maps)
-    double = call(
-        functools.partial(double_kernel, firsts), longer, [V, V], flops=2 * size ** 3, moved=6 * size ** 2
-    )(before, turned)
+    double0 = call(functools.partial(double_kernel, 0, firsts), part, [V] * 3, **half_cost)(before0, turned0, turned1)
+    double1 = call(functools.partial(double_kernel, 1, firsts), longer, [V] * 3, **half_cost)(before1, turned0, turned1)
     for chip in range(firsts + 1, chips, 2):
         begin, value = call(
-            functools.partial(far_kernel, chip, chip == chips - 1), (row, row), [V] * 5,
+            functools.partial(far_kernel, chip, chip == chips - 1), (row, row), [V] * 7,
             flops=64 * size ** 2, moved=4 * size ** 2,
-        )(begin, came, value, before, double)
+        )(begin, came, value, before0, before1, double0, double1)
         if chip < chips - 1:
             came = lax.ppermute(value, "tm", [(2 * chip + 1, 2 * chip + 5)])
     handed = lax.ppermute(value, "tm", [(2 * c - 1, 2 * c + 1) for c in range(firsts, chips, 2)])

time: 157 us -> 152 us (0.968)
  waiting for transfers between devices: 101 us -> 95.5 us
    ppermute x1, waiting for transfers between devices: 40.6 us -> 36.8 us  [shards(): got = lax.ppermute(begin, 'tm', [(b, a) for a, b in pairs])]
    ppermute x7, waiting for transfers between devices: 38 us -> 35.8 us  [ring_rounds(): pieces[count - r] = lax.ppermute(left, axis, forward)]
    pallas_call x8 -> x11, Pallas kernels: 6.39 us -> 6.56 us  [the longest x1 3.96 us: shards(): call(functools.partial(four_kernel, count, have), (matrix, slab, slab, ma...]
  transfers between devices with their start and end apart: 30 -> 31, of which waited for: 12 -> 12; matrix products, arithmetic and copies ran while one was open for 0% -> 0% of each run, Pallas kernels for 5% -> 6%
where the time goes in v7:
time: 152 us; the launch traced here: 151 us
  waiting for transfers between devices  95.5 us (63%)
  starting transfers between devices  39.3 us (26%)
  Pallas kernels  14.3 us (9%)
    ppermute x1, waiting for transfers between devices, shards(): got = lax.ppermute(begin, 'tm', [(b, a) for a, b in pairs])  36.8 us
    ppermute x7, waiting for transfers between devices, ring_rounds(): pieces[count - r] = lax.ppermute(left, axis, forward)  35.8 us
    ppermute x7, waiting for transfers between devices, ring_rounds(): pieces[r] = lax.ppermute(right, axis, backward)  22.1 us
    ppermute x7, starting transfers between devices, ring_rounds(): pieces[r] = lax.ppermute(right, axis, backward)  20.3 us
    ppermute x7, starting transfers between devices, ring_rounds(): pieces[count - r] = lax.ppermute(left, axis, forward)  5.4 us
    ppermute x8, starting transfers between devices, shards(): lax.ppermute(value, 'tm', [(2 * turn + 1, 2 * turn + (3 if turn + 1 < fir...  5.29 us
    pallas_call x1, Pallas kernels, shards(): call(functools.partial(four_kernel, count, have), (matrix, slab, slab, ma...  3.96 us
  transfers between devices with their start and end apart: 31, of which 12 were waited for; matrix products, arithmetic and copies ran while one was open for 0% of the time, Pallas kernels for 6%

profile of v7, /device:TPU:30, one launch (start us, length us, event | category | flops | bytes accessed | tf_op | source)
XLA Modules:
  0.0 151.0 jit_solution(18177282781790839427)
XLA Ops:
  0.0 1.4 fusion
  1.5 2.0 %collective-permute-start.1 = (bf16[256,1024]{1,0:T(8,128)(2,1)S(1)}, bf16[256,1024]{1,0:T(8,128)(2,1)S(1)}, u32[]{:S(2)}, u32[]{:S(2)}) collective-permute-start(bf16[256,1024]{1,0:T(8,128)(2,1)S(1)} %bitcast.2), channel_id=1, source_target_pairs={{0,1},{1,2},{2,3},{3,4},{4,5},{5,6},{6,7},{7,0},{8,9},{9,10},{10,1... | collective-permute-start | bytes 1572872 | tf_op jit(solution)/shard_map/ppermute | solution.py:329
  3.4 4.0 %collective-permute-start = (bf16[256,1024]{1,0:T(8,128)(2,1)S(1)}, bf16[256,1024]{1,0:T(8,128)(2,1)S(1)}, u32[]{:S(2)}, u32[]{:S(2)}) collective-permute-start(bf16[256,1024]{1,0:T(8,128)(2,1)S(1)} %bitcast.3), channel_id=1, source_target_pairs={{1,0},{2,1},{3,2},{4,3},{5,4},{6,5},{7,6},{0,7},{9,8},{10,9},{11,1... | collective-permute-start | bytes 1572872 | tf_op jit(solution)/shard_map/ppermute | solution.py:331
  7.5 1.6 %shard_map.73.refs_0_ = bf16[272,1024]{1,0:T(8,128)(2,1)S(1)} custom-call(s32[4,32]{1,0:T(4,128)S(1)} %copy-done.2, s32[4,32]{1,0:T(4,128)S(1)} %copy-done.3, bf16[4,4096]{1,0:T(4,128)(2,1)S(1)} %multiply_convert_fusion.values_ref, bf16[4,32,64,64]{3,2,1,0:T(8,128)(2,1)S(1)} %copy-done, bf16[2,128,1024]{2,1,0:T(8,128)(2,1)S(1)} %get-tuple-element.93.maps_ref), custom_call_target="tpu_custom_call" | custom-call | flops 10000000 | bytes 2097152 | tf_op jit(solution)/shard_map/pallas_call | solution.py:351
  9.1 2.0 %collective-permute-start.7 = (bf16[272,1024]{1,0:T(8,128)(2,1)S(1)}, bf16[272,1024]{1,0:T(8,128)(2,1)S(1)}, u32[]{:S(2)}, u32[]{:S(2)}) collective-permute-start(bf16[272,1024]{1,0:T(8,128)(2,1)S(1)} %shard_map.73.refs_0_), channel_id=1, source_target_pairs={{1,0},{2,1},{3,2},{4,3},{5,4},{6,5},{7,6},{0,7},{9,8},{10,9},{11,1... | collective-permute-start | bytes 1671176 | tf_op jit(solution)/shard_map/ppermute | solution.py:331
  11.1 8.2 %collective-permute-done.1.refs_7_ = bf16[256,1024]{1,0:T(8,128)(2,1)S(1)} collective-permute-done((bf16[256,1024]{1,0:T(8,128)(2,1)S(1)}, bf16[256,1024]{1,0:T(8,128)(2,1)S(1)}, u32[]{:S(2)}, u32[]{:S(2)}) %collective-permute-start.1) | collective-permute-done | bytes 524320 | tf_op jit(solution)/shard_map/ppermute | solution.py:329
  20.2 3.0 %collective-permute-start.10 = (bf16[272,1024]{1,0:T(8,128)(2,1)S(1)}, bf16[272,1024]{1,0:T(8,128)(2,1)S(1)}, u32[]{:S(2)}, u32[]{:S(2)}) collective-permute-start(bf16[272,1024]{1,0:T(8,128)(2,1)S(1)} %shard_map.73.refs_0_), channel_id=1, source_target_pairs={{0,1},{1,2},{2,3},{3,4},{4,5},{5,6},{6,7},{7,0},{8,9},{9,10},{10,1... | collective-permute-start | bytes 1671176 | tf_op jit(solution)/shard_map/ppermute | solution.py:329
  23.2 7.4 %collective-permute-done.7.refs_1_ = bf16[272,1024]{1,0:T(8,128)(2,1)S(1)} collective-permute-done((bf16[272,1024]{1,0:T(8,128)(2,1)S(1)}, bf16[272,1024]{1,0:T(8,128)(2,1)S(1)}, u32[]{:S(2)}, u32[]{:S(2)}) %collective-permute-start.7) | collective-permute-done | bytes 557088 | tf_op jit(solution)/shard_map/ppermute | solution.py:331
  30.6 3.7 %collective-permute-start.8 = (bf16[272,1024]{1,0:T(8,128)(2,1)S(1)}, bf16[272,1024]{1,0:T(8,128)(2,1)S(1)}, u32[]{:S(2)}, u32[]{:S(2)}) collective-permute-start(bf16[272,1024]{1,0:T(8,128)(2,1)S(1)} %collective-permute-done.7.refs_1_), channel_id=1, source_target_pairs={{1,0},{2,1},{3,2},{4,3},{5,4},{6,5},{7,6},{0,7},{9,8},{10,9},{11,1... | collective-permute-start | bytes 1671176 | tf_op jit(solution)/shard_map/ppermute | solution.py:331
  34.7 1.6 %collective-permute-done.4.refs_6_ = bf16[256,1024]{1,0:T(8,128)(2,1)S(1)} collective-permute-done((bf16[256,1024]{1,0:T(8,128)(2,1)S(1)}, bf16[256,1024]{1,0:T(8,128)(2,1)S(1)}, u32[]{:S(2)}, u32[]{:S(2)}) %collective-permute-start.4) | collective-permute-done | bytes 524320 | tf_op jit(solution)/shard_map/ppermute | solution.py:329
  36.3 11.9 %collective-permute-done.10.refs_5_.refs_7_ = bf16[272,1024]{1,0:T(8,128)(2,1)S(1)} collective-permute-done((bf16[272,1024]{1,0:T(8,128)(2,1)S(1)}, bf16[272,1024]{1,0:T(8,128)(2,1)S(1)}, u32[]{:S(2)}, u32[]{:S(2)}) %collective-permute-start.10) | collective-permute-done | bytes 557088 | tf_op jit(solution)/shard_map/ppermute | solution.py:329
  48.3 3.2 %collective-permute-start.9 = (bf16[272,1024]{1,0:T(8,128)(2,1)S(1)}, bf16[272,1024]{1,0:T(8,128)(2,1)S(1)}, u32[]{:S(2)}, u32[]{:S(2)}) collective-permute-start(bf16[272,1024]{1,0:T(8,128)(2,1)S(1)} %collective-permute-done.8.refs_2_), channel_id=1, source_target_pairs={{1,0},{2,1},{3,2},{4,3},{5,4},{6,5},{7,6},{0,7},{9,8},{10,9},{11,1... | collective-permute-start | bytes 1671176 | tf_op jit(solution)/shard_map/ppermute | solution.py:331
  51.5 7.1 %collective-permute-done.2.refs_2_ = bf16[256,1024]{1,0:T(8,128)(2,1)S(1)} collective-permute-done((bf16[256,1024]{1,0:T(8,128)(2,1)S(1)}, bf16[256,1024]{1,0:T(8,128)(2,1)S(1)}, u32[]{:S(2)}, u32[]{:S(2)}) %collective-permute-start.2) | collective-permute-done | bytes 524320 | tf_op jit(solution)/shard_map/ppermute | solution.py:331
  58.6 3.7 %collective-permute-start.3 = (bf16[256,1024]{1,0:T(8,128)(2,1)S(1)}, bf16[256,1024]{1,0:T(8,128)(2,1)S(1)}, u32[]{:S(2)}, u32[]{:S(2)}) collective-permute-start(bf16[256,1024]{1,0:T(8,128)(2,1)S(1)} %collective-permute-done.2.refs_2_), channel_id=1, source_target_pairs={{1,0},{2,1},{3,2},{4,3},{5,4},{6,5},{7,6},{0,7},{9,8},{10,9},{11,1... | collective-permute-start | bytes 1572872 | tf_op jit(solution)/shard_map/ppermute | solution.py:331
  62.3 9.1 %collective-permute-done.11.refs_4_.refs_6_ = bf16[272,1024]{1,0:T(8,128)(2,1)S(1)} collective-permute-done((bf16[272,1024]{1,0:T(8,128)(2,1)S(1)}, bf16[272,1024]{1,0:T(8,128)(2,1)S(1)}, u32[]{:S(2)}, u32[]{:S(2)}) %collective-permute-start.11) | collective-permute-done | bytes 557088 | tf_op jit(solution)/shard_map/ppermute | solution.py:329
  71.5 3.2 %collective-permute-start.12 = (bf16[272,1024]{1,0:T(8,128)(2,1)S(1)}, bf16[272,1024]{1,0:T(8,128)(2,1)S(1)}, u32[]{:S(2)}, u32[]{:S(2)}) collective-permute-start(bf16[272,1024]{1,0:T(8,128)(2,1)S(1)} %collective-permute-done.9.refs_3_), channel_id=1, source_target_pairs={{1,0},{2,1},{3,2},{4,3},{5,4},{6,5},{7,6},{0,7},{9,8},{10,9},{11,1... | collective-permute-start | bytes 1671176 | tf_op jit(solution)/shard_map/ppermute | solution.py:331
  74.7 7.1 %collective-permute-done.3.refs_3_ = bf16[256,1024]{1,0:T(8,128)(2,1)S(1)} collective-permute-done((bf16[256,1024]{1,0:T(8,128)(2,1)S(1)}, bf16[256,1024]{1,0:T(8,128)(2,1)S(1)}, u32[]{:S(2)}, u32[]{:S(2)}) %collective-permute-start.3) | collective-permute-done | bytes 524320 | tf_op jit(solution)/shard_map/ppermute | solution.py:331
  81.8 0.9 collective-permute-done.6.refs_4_
  82.7 3.0 %shard_map.74 = (bf16[1024,1024]{1,0:T(8,128)(2,1)S(1)}, bf16[128,1024]{1,0:T(8,128)(2,1)S(1)}, bf16[1024,1024]{1,0:T(8,128)(2,1)S(1)}) custom-call(bf16[256,1024]{1,0:T(8,128)(2,1)S(1)} %bitcast.4, bf16[256,1024]{1,0:T(8,128)(2,1)S(1)} %collective-permute-done.refs_1_, bf16[256,1024]{1,0:T(8,128)(2,1)S(1)} %collective-permute-done.2.refs_2_, ...), custom_call_target="tpu_custom_call" | custom-call | flops 2147483648 | bytes 6291456 | tf_op jit(solution)/shard_map/pallas_call | solution.py:364
  85.7 2.2 %shard_map.75 = (bf16[1024,1024]{1,0:T(8,128)(2,1)S(1)}, bf16[1024,1024]{1,0:T(8,128)(2,1)S(1)}, bf16[1024,1024]{1,0:T(8,128)(2,1)S(1)}) custom-call(bf16[1024,1024]{1,0:T(8,128)(2,1)S(1)} %get-tuple-element.51.two_ref, bf16[272,1024]{1,0:T(8,128)(2,1)S(1)} %shard_map.73.refs_0_, bf16[272,1024]{1,0:T(8,128)(2,1)S(1)} %collective-permute-done.7.refs_1_, ...), custom_call_target="tpu_custom_call" | custom-call | flops 2147483648 | bytes 6291456 | tf_op jit(solution)/shard_map/pallas_call | solution.py:369
  87.9 4.0 %collective-permute-done.13.refs_5_ = bf16[272,1024]{1,0:T(8,128)(2,1)S(1)} collective-permute-done((bf16[272,1024]{1,0:T(8,128)(2,1)S(1)}, bf16[272,1024]{1,0:T(8,128)(2,1)S(1)}, u32[]{:S(2)}, u32[]{:S(2)}) %collective-permute-start.13) | collective-permute-done | bytes 557088 | tf_op jit(solution)/shard_map/ppermute | solution.py:329
  91.9 4.0 %shard_map.76 = (bf16[1024,1024]{1,0:T(8,128)(2,1)S(1)}, bf16[128,1024]{1,0:T(8,128)(2,1)S(1)}, bf16[128,1024]{1,0:T(8,128)(2,1)S(1)}, bf16[1024,1024]{1,0:T(8,1...) custom-call(bf16[1024,1024]{1,0:T(8,128)(2,1)S(1)} %get-tuple-elemen, ...), custom_call_target="tpu_custom_call", output_to_operand_aliasing={{3}: (1, {}), {4}: (2, {}), {5}: (3, {})} | custom-call | flops 2147483648 | bytes 6291456 | tf_op jit(solution)/shard_map/pallas_call | solution.py:373
  95.9 1.4 collective-permute-start.14
  97.3 1.8 %shard_map.77 = (f32[4,1024]{1,0:T(4,128)S(1)}, bf16[16,1024]{1,0:T(8,128)(2,1)S(1)}) custom-call(f32[16,1024]{1,0:T(8,128)S(1)} %get-tuple-element.56.drive_ref, bf16[1024,1024]{1,0:T(8,128)(2,1)S(1)} %get-tuple-element.57.second_ref, bf16[1024,1024]{1,0:T(8,128)(2,1)S(1)} %get-tuple-element.58.third_ref, bf16[1024,1024]{1,0:T(8,128)(2,1)S(1)} %get-tuple-element.59.fourth_ref), custom_call_target="tpu_custom_call" | custom-call | flops 100663296 | bytes 6291456 | tf_op jit(solution)/shard_map/pallas_call | solution.py:382
  99.1 1.3 collective-permute-start.15
  100.4 0.8 collective-permute-done.15.other_term_ref
  101.2 0.8 collective-permute-start.24
  102.1 0.7 collective-permute-start.25
  102.9 0.7 collective-permute-start.16
  112.1 1.3 collective-permute-start.30
  113.4 36.8 %collective-permute-done.30.got_ref = f32[1,1024]{1,0:T(1,128)S(1)} collective-permute-done((f32[1,1024]{1,0:T(1,128)S(1)}, f32[1,1024]{1,0:T(1,128)S(1)}, u32[]{:S(2)}, u32[]{:S(2)}) %collective-permute-start.30) | collective-permute-done | bytes 4128 | tf_op jit(solution)/shard_map/ppermute | solution.py:432
  150.2 0.8 shard_map.96
  (68 shorter events, 9.6 us)
Async XLA Ops:
  0.0 7.5 %copy-start.2 = (s32[4,32]{1,0:T(4,128)S(1)}, s32[4,32]{1,0:T(4,128)}, u32[]{:S(2)}) copy-start(s32[4,32]{1,0:T(4,128)} %rows_ref.1) | copy-start | bytes 1540
  1.5 17.9 %collective-permute-start.1 = (bf16[256,1024]{1,0:T(8,128)(2,1)S(1)}, bf16[256,1024]{1,0:T(8,128)(2,1)S(1)}, u32[]{:S(2)}, u32[]{:S(2)}) collective-permute-start(bf16[256,1024]{1,0:T(8,128)(2,1)S(1)} %bitcast.2), channel_id=1, source_target_pairs={{0,1},{1,2},{2,3},{3,4},{4,5},{5,6},{6,7},{7,0},{8,9},{9,10},{10,1... | collective-permute-start | bytes 1572872 | tf_op jit(solution)/shard_map/ppermute | solution.py:329
  3.4 16.4 %collective-permute-start = (bf16[256,1024]{1,0:T(8,128)(2,1)S(1)}, bf16[256,1024]{1,0:T(8,128)(2,1)S(1)}, u32[]{:S(2)}, u32[]{:S(2)}) collective-permute-start(bf16[256,1024]{1,0:T(8,128)(2,1)S(1)} %bitcast.3), channel_id=1, source_target_pairs={{1,0},{2,1},{3,2},{4,3},{5,4},{6,5},{7,6},{0,7},{9,8},{10,9},{11,1... | collective-permute-start | bytes 1572872 | tf_op jit(solution)/shard_map/ppermute | solution.py:331
  9.1 21.5 %collective-permute-start.7 = (bf16[272,1024]{1,0:T(8,128)(2,1)S(1)}, bf16[272,1024]{1,0:T(8,128)(2,1)S(1)}, u32[]{:S(2)}, u32[]{:S(2)}) collective-permute-start(bf16[272,1024]{1,0:T(8,128)(2,1)S(1)} %shard_map.73.refs_0_), channel_id=1, source_target_pairs={{1,0},{2,1},{3,2},{4,3},{5,4},{6,5},{7,6},{0,7},{9,8},{10,9},{11,1... | collective-permute-start | bytes 1671176 | tf_op jit(solution)/shard_map/ppermute | solution.py:331
  19.8 16.5 %collective-permute-start.4 = (bf16[256,1024]{1,0:T(8,128)(2,1)S(1)}, bf16[256,1024]{1,0:T(8,128)(2,1)S(1)}, u32[]{:S(2)}, u32[]{:S(2)}) collective-permute-start(bf16[256,1024]{1,0:T(8,128)(2,1)S(1)} %collective-permute-done.1.refs_7_), channel_id=1, source_target_pairs={{0,1},{1,2},{2,3},{3,4},{4,5},{5,6},{6,7},{7,0},{8,9},{9,10},{10,1... | collective-permute-start | bytes 1572872 | tf_op jit(solution)/shard_map/ppermute | solution.py:329
  20.2 28.1 %collective-permute-start.10 = (bf16[272,1024]{1,0:T(8,128)(2,1)S(1)}, bf16[272,1024]{1,0:T(8,128)(2,1)S(1)}, u32[]{:S(2)}, u32[]{:S(2)}) collective-permute-start(bf16[272,1024]{1,0:T(8,128)(2,1)S(1)} %shard_map.73.refs_0_), channel_id=1, source_target_pairs={{0,1},{1,2},{2,3},{3,4},{4,5},{5,6},{6,7},{7,0},{8,9},{9,10},{10,1... | collective-permute-start | bytes 1671176 | tf_op jit(solution)/shard_map/ppermute | solution.py:329
  30.6 17.7 %collective-permute-start.8 = (bf16[272,1024]{1,0:T(8,128)(2,1)S(1)}, bf16[272,1024]{1,0:T(8,128)(2,1)S(1)}, u32[]{:S(2)}, u32[]{:S(2)}) collective-permute-start(bf16[272,1024]{1,0:T(8,128)(2,1)S(1)} %collective-permute-done.7.refs_1_), channel_id=1, source_target_pairs={{1,0},{2,1},{3,2},{4,3},{5,4},{6,5},{7,6},{0,7},{9,8},{10,9},{11,1... | collective-permute-start | bytes 1671176 | tf_op jit(solution)/shard_map/ppermute | solution.py:331
  34.3 24.3 %collective-permute-start.2 = (bf16[256,1024]{1,0:T(8,128)(2,1)S(1)}, bf16[256,1024]{1,0:T(8,128)(2,1)S(1)}, u32[]{:S(2)}, u32[]{:S(2)}) collective-permute-start(bf16[256,1024]{1,0:T(8,128)(2,1)S(1)} %collective-permute-done.refs_1_), channel_id=1, source_target_pairs={{1,0},{2,1},{3,2},{4,3},{5,4},{6,5},{7,6},{0,7},{9,8},{10,9},{11,1... | collective-permute-start | bytes 1572872 | tf_op jit(solution)/shard_map/ppermute | solution.py:331
  36.3 26.0 %collective-permute-start.5 = (bf16[256,1024]{1,0:T(8,128)(2,1)S(1)}, bf16[256,1024]{1,0:T(8,128)(2,1)S(1)}, u32[]{:S(2)}, u32[]{:S(2)}) collective-permute-start(bf16[256,1024]{1,0:T(8,128)(2,1)S(1)} %collective-permute-done.4.refs_6_), channel_id=1, source_target_pairs={{0,1},{1,2},{2,3},{3,4},{4,5},{5,6},{6,7},{7,0},{8,9},{9,10},{10,1... | collective-permute-start | bytes 1572872 | tf_op jit(solution)/shard_map/ppermute | solution.py:329
  48.3 23.2 %collective-permute-start.11 = (bf16[272,1024]{1,0:T(8,128)(2,1)S(1)}, bf16[272,1024]{1,0:T(8,128)(2,1)S(1)}, u32[]{:S(2)}, u32[]{:S(2)}) collective-permute-start(bf16[272,1024]{1,0:T(8,128)(2,1)S(1)} %collective-permute-done.10.refs_5_.refs_7_), channel_id=1, source_target_pairs={{0,1},{1,2},{2,3},{3,4},{4,5},{5,6},{6,7},{7,0},{8,9},{9,10},{10,1... | collective-permute-start | bytes 1671176 | tf_op jit(solution)/shard_map/ppermute | solution.py:329
  48.3 23.2 %collective-permute-start.9 = (bf16[272,1024]{1,0:T(8,128)(2,1)S(1)}, bf16[272,1024]{1,0:T(8,128)(2,1)S(1)}, u32[]{:S(2)}, u32[]{:S(2)}) collective-permute-start(bf16[272,1024]{1,0:T(8,128)(2,1)S(1)} %collective-permute-done.8.refs_2_), channel_id=1, source_target_pairs={{1,0},{2,1},{3,2},{4,3},{5,4},{6,5},{7,6},{0,7},{9,8},{10,9},{11,1... | collective-permute-start | bytes 1671176 | tf_op jit(solution)/shard_map/ppermute | solution.py:331
  58.6 23.2 %collective-permute-start.3 = (bf16[256,1024]{1,0:T(8,128)(2,1)S(1)}, bf16[256,1024]{1,0:T(8,128)(2,1)S(1)}, u32[]{:S(2)}, u32[]{:S(2)}) collective-permute-start(bf16[256,1024]{1,0:T(8,128)(2,1)S(1)} %collective-permute-done.2.refs_2_), channel_id=1, source_target_pairs={{1,0},{2,1},{3,2},{4,3},{5,4},{6,5},{7,6},{0,7},{9,8},{10,9},{11,1... | collective-permute-start | bytes 1572872 | tf_op jit(solution)/shard_map/ppermute | solution.py:331
  62.3 20.4 %collective-permute-start.6 = (bf16[256,1024]{1,0:T(8,128)(2,1)S(1)}, bf16[256,1024]{1,0:T(8,128)(2,1)S(1)}, u32[]{:S(2)}, u32[]{:S(2)}) collective-permute-start(bf16[256,1024]{1,0:T(8,128)(2,1)S(1)} %collective-permute-done.5.refs_5_), channel_id=1, source_target_pairs={{0,1},{1,2},{2,3},{3,4},{4,5},{5,6},{6,7},{7,0},{8,9},{9,10},{10,1... | collective-permute-start | bytes 1572872 | tf_op jit(solution)/shard_map/ppermute | solution.py:329
  71.4 20.5 %collective-permute-start.13 = (bf16[272,1024]{1,0:T(8,128)(2,1)S(1)}, bf16[272,1024]{1,0:T(8,128)(2,1)S(1)}, u32[]{:S(2)}, u32[]{:S(2)}) collective-permute-start(bf16[272,1024]{1,0:T(8,128)(2,1)S(1)} %collective-permute-done.11.refs_4_.refs_6_), channel_id=1, source_target_pairs={{0,1},{1,2},{2,3},{3,4},{4,5},{5,6},{6,7},{7,0},{8,9},{9,10},{10,1... | collective-permute-start | bytes 1671176 | tf_op jit(solution)/shard_map/ppermute | solution.py:329
  71.5 20.5 %collective-permute-start.12 = (bf16[272,1024]{1,0:T(8,128)(2,1)S(1)}, bf16[272,1024]{1,0:T(8,128)(2,1)S(1)}, u32[]{:S(2)}, u32[]{:S(2)}) collective-permute-start(bf16[272,1024]{1,0:T(8,128)(2,1)S(1)} %collective-permute-done.9.refs_3_), channel_id=1, source_target_pairs={{1,0},{2,1},{3,2},{4,3},{5,4},{6,5},{7,6},{0,7},{9,8},{10,9},{11,1... | collective-permute-start | bytes 1671176 | tf_op jit(solution)/shard_map/ppermute | solution.py:331
  95.9 5.3 %collective-permute-start.14 = (bf16[1024,1024]{1,0:T(8,128)(2,1)S(1)}, bf16[1024,1024]{1,0:T(8,128)(2,1)S(1)}, u32[]{:S(2)}, u32[]{:S(2)}) collective-permute-start(bf16[1024,1024]{1,0:T(8,128)(2,1)S(1)} %get-tuple-element.55.own_ref), channel_id=1, source_target_pairs={{0,8},{16,24},{32,40},{48,56},{64,72},{80,88},{96,104},{112,120},{... | collective-permute-start | bytes 6291464 | tf_op jit(solution)/shard_map/ppermute | solution.py:381
  99.1 2.1 %collective-permute-start.15 = (bf16[16,1024]{1,0:T(8,128)(2,1)S(1)}, bf16[16,1024]{1,0:T(8,128)(2,1)S(1)}, u32[]{:S(2)}, u32[]{:S(2)}) collective-permute-start(bf16[16,1024]{1,0:T(8,128)(2,1)S(1)} %get-tuple-element.60.own_term_ref), channel_id=1, source_target_pairs={{0,8},{16,24},{32,40},{48,56},{64,72},{80,88},{96,104},{112,120},{... | collective-permute-start | bytes 98312 | tf_op jit(solution)/shard_map/ppermute | solution.py:385
  101.2 7.9 %collective-permute-start.24 = (bf16[512,1024]{1,0:T(8,128)(2,1)S(1)}, bf16[512,1024]{1,0:T(8,128)(2,1)S(1)}, u32[]{:S(2)}, u32[]{:S(2)}) collective-permute-start(bf16[512,1024]{1,0:T(8,128)(2,1)S(1)} %shard_map.82.turned0_ref), channel_id=1, source_target_pairs={{136,152},{168,184},{200,216},{232,248},{137,153},{169,185},{201,2... | collective-permute-start | bytes 3145736 | tf_op jit(solution)/shard_map/ppermute | solution.py:395
  102.1 7.0 %collective-permute-start.25 = (bf16[528,1024]{1,0:T(8,128)(2,1)S(1)}, bf16[528,1024]{1,0:T(8,128)(2,1)S(1)}, u32[]{:S(2)}, u32[]{:S(2)}) collective-permute-start(bf16[528,1024]{1,0:T(8,128)(2,1)S(1)} %shard_map.78.turned1_ref), channel_id=1, source_target_pairs={{136,152},{168,184},{200,216},{232,248},{137,153},{169,185},{201,2... | collective-permute-start | bytes 3244040 | tf_op jit(solution)/shard_map/ppermute | solution.py:397
  102.9 0.7 collective-permute-start.16
  103.6 0.7 collective-permute-start.17
  104.3 0.7 collective-permute-start.18
  105.0 0.7 collective-permute-start.19
  105.9 1.0 collective-permute-start.20
  107.0 0.7 collective-permute-start.21
  107.7 0.7 collective-permute-start.22
  108.4 0.8 collective-permute-start.23
  109.2 0.7 collective-permute-start.26
  109.9 0.7 collective-permute-start.27
  110.7 0.7 collective-permute-start.28
  111.4 0.7 collective-permute-start.29
  112.1 38.1 %collective-permute-start.30 = (f32[1,1024]{1,0:T(1,128)S(1)}, f32[1,1024]{1,0:T(1,128)S(1)}, u32[]{:S(2)}, u32[]{:S(2)}) collective-permute-start(f32[1,1024]{1,0:T(1,128)S(1)} %shard_map.95.begin_ref), channel_id=1, source_target_pairs={{8,0},{24,16},{40,32},{56,48},{72,64},{88,80},{104,96},{120,112},{... | collective-permute-start | bytes 12296 | tf_op jit(solution)/shard_map/ppermute | solution.py:432
  (5 other events, 31.6 us)

commit v8 on v7

--- a/solution.py
+++ b/solution.py
@@ -173,13 +173,26 @@
     drive_ref[...] = jnp.sum(parts_ref[...].astype(F32), axis=0)
 
 
-def local_kernel(drive_ref, second_ref, third_ref, fourth_ref, locals_ref, term_ref):
+def local_kernel(drive_ref, prior_ref, second_ref, third_ref, fourth_ref, four_ref, locals_ref, term_ref, mean_ref):
     local = joined(drive_ref[0:3, :])
     locals_ref[0:1, :] = local
     for j, map_ref in enumerate((second_ref, third_ref, fourth_ref)):
         local = times_t(local, map_ref[...]) + joined(drive_ref[3 * j + 3:3 * j + 6, :])
         locals_ref[j + 1:j + 2, :] = local
     term_ref[...] = split_rows(local)
+    mean_ref[...] = local
+
+    @pl.when(lax.axis_index("tm") == 0)
+    def _():
+        mean_ref[...] = times_t(prior_ref[...], four_ref[...]) + local
+
+
+def first_kernel(mean_ref, own_ref, term_ref, value_ref):
+    value_ref[...] = mean_ref[...]
+
+    @pl.when(lax.axis_index("tm") == 1)
+    def _():
+        value_ref[...] = times_t(mean_ref[...], own_ref[...]) + joined(term_ref[...])
 
 
 DIRECT = 3
@@ -231,29 +244,16 @@
         value_ref[...] = begin_ref[...]
 
 
-def double_kernel(half, firsts, came_ref, turned0_ref, turned1_ref, double_ref):
-    rows = turned0_ref.shape[0]
-    chip = chip_here()
-
-    @pl.when((core_here() != 0) & (chip > firsts) & (lax.rem(chip, 2) == 1) & (chip < 2 * firsts - 1))
-    def _():
-        double_ref[:rows, :] = product(came_ref[:rows, :], turned0_ref[...], turned1_ref[:rows, :]).astype(BF16)
-        if half == 1:
-            double_ref[rows:, :] = split_rows(applied(joined(came_ref[rows:, :]), turned0_ref, turned1_ref))
-
-
 def far_kernel(
-    chip, last, begin_ref, came_ref, before_ref, map0_ref, map1_ref, double0_ref, double1_ref, held_ref, value_ref
+    chip, begin_ref, came_ref, before_ref, map0_ref, map1_ref, turned0_ref, turned1_ref, held_ref, value_ref
 ):
     here = lax.axis_index("tm") == 2 * chip + 1
 
     @pl.when(here)
     def _():
-        if last:
-            value_ref[...] = before_ref[...]
-        else:
-            value_ref[...] = applied(came_ref[...], double0_ref, double1_ref)
-        held_ref[...] = applied(came_ref[...], map0_ref, map1_ref)
+        begin = applied(came_ref[...], map0_ref, map1_ref)
+        held_ref[...] = begin
+        value_ref[...] = applied(begin, turned0_ref, turned1_ref)
 
     @pl.when(jnp.logical_not(here))
     def _():
@@ -272,13 +272,15 @@
     width, size = slabs[1].shape
     mine = pl.ds(pl.multiple_of(lax.axis_index("state") * width, width), width)
 
-    @pl.when(core_here() == 0)
+    plain = jnp.logical_or(core_here() == 0, chip_here() == 0)
+
+    @pl.when(plain)
     def _():
         for j, slab_ref in enumerate(slabs):
             maps_ref[:, j * width:(j + 1) * width] = slab_ref[:width, :].astype(F32).T.astype(BF16)
             terms_ref[j:j + 1, :] = locals_ref[j:j + 1, mine]
 
-    @pl.when(core_here() != 0)
+    @pl.when(jnp.logical_not(plain))
     def _():
         for j, slab_ref in enumerate(slabs):
             at = slice(j * width, (j + 1) * width)
@@ -288,9 +290,11 @@
             terms_ref[j:j + 1, :] = term + locals_ref[j:j + 1, mine]
 
 
-def out_kernel(begin_ref, got_ref, maps_ref, terms_ref, out_ref):
+def out_kernel(prior_ref, mean_ref, begin_ref, got_ref, maps_ref, terms_ref, out_ref):
     steps, width = out_ref.shape
+    first = jnp.where(core_here() == 0, prior_ref[...], mean_ref[...])
     begin = jnp.where(core_here() == 0, got_ref[...], begin_ref[...])
+    begin = jnp.where(chip_here() == 0, first, begin)
     row = times(begin, maps_ref[...])
     for j in range(steps):
         out_ref[j:j + 1, :] = row[:, j * width:(j + 1) * width] + terms_ref[j:j + 1, :]
@@ -378,27 +382,31 @@
         flops=2 * size ** 3, moved=6 * size ** 2, aliases={1: 3, 2: 4, 3: 5},
     )(two, three, third, fourth, *late)
     pairs = [(i, i + 1) for i in range(0, blocks_of_time, 2)]
-    other = lax.ppermute(own, "tm", pairs)
-    locals_, own_term = call(
-        local_kernel, (steps, rows), [V] * 4, flops=96 * size ** 2, moved=6 * size ** 2
-    )(drive, second, third, fourth)
-    other_term = lax.ppermute(own_term, "tm", pairs)
+    other = lax.ppermute(own, "tm", pairs[1:])
+    start = prior.reshape(1, size)
+    locals_, own_term, mean = call(
+        local_kernel, (steps, rows, row), [V] * 6, flops=128 * size ** 2, moved=8 * size ** 2
+    )(drive, start, second, third, fourth, own)
+    mean = lax.ppermute(mean, "tm", pairs[:1])
+    other_term = lax.ppermute(own_term, "tm", pairs[1:])
+    value = call(first_kernel, row, [V] * 3, flops=32 * size ** 2, moved=2 * size ** 2)(mean, own, own_term)
+    came = lax.ppermute(value, "tm", [(1, 3)])
 
     chips = blocks_of_time // 2
     firsts = chips // 2
     part = jax.ShapeDtypeStruct((size // 2, size), BF16)
     longer = jax.ShapeDtypeStruct((size // 2 + 16, size), BF16)
     blocks_here = (own, own_term, other, other_term)
+    pair_blocks = after(blocks_here, value)
     onward = [(2 * c + 1, 2 * c + 3) for c in range(firsts, chips, 2)]
     half_cost = dict(flops=size ** 3, moved=6 * size ** 2)
-    turned0 = call(functools.partial(pair_kernel, 0), part, [V] * 4, **half_cost)(*blocks_here)
+    turned0 = call(functools.partial(pair_kernel, 0), part, [V] * 4, **half_cost)(*pair_blocks)
     before0 = lax.ppermute(turned0, "tm", onward)
-    turned1 = call(functools.partial(pair_kernel, 1), longer, [V] * 4, **half_cost)(*blocks_here)
+    turned1 = call(functools.partial(pair_kernel, 1), longer, [V] * 4, **half_cost)(*pair_blocks)
     before1 = lax.ppermute(turned1, "tm", onward)
 
-    begin = after(prior.reshape(1, size), turned1)
-    came = begin
-    for turn in range(firsts):
+    begin = start
+    for turn in range(1, firsts):
         if turn < DIRECT:
             begin, value = call(
                 functools.partial(direct_kernel, turn), (row, row), [V] * 6,
@@ -418,22 +426,20 @@
             )(other, other_term, locals_, value, early[0], slab2, slab3, slab4)
         if turn == DIRECT + 1:
             came = after(came, maps)
-    double0 = call(functools.partial(double_kernel, 0, firsts), part, [V] * 3, **half_cost)(before0, turned0, turned1)
-    double1 = call(functools.partial(double_kernel, 1, firsts), longer, [V] * 3, **half_cost)(before1, turned0, turned1)
     for chip in range(firsts + 1, chips, 2):
         begin, value = call(
-            functools.partial(far_kernel, chip, chip == chips - 1), (row, row), [V] * 7,
+            functools.partial(far_kernel, chip), (row, row), [V] * 7,
             flops=64 * size ** 2, moved=4 * size ** 2,
-        )(begin, came, value, before0, before1, double0, double1)
+        )(begin, came, value, before0, before1, turned0, turned1)
         if chip < chips - 1:
             came = lax.ppermute(value, "tm", [(2 * chip + 1, 2 * chip + 5)])
     handed = lax.ppermute(value, "tm", [(2 * c - 1, 2 * c + 1) for c in range(firsts, chips, 2)])
     begin = call(functools.partial(final_kernel, firsts), row, [V, V])(begin, handed)
     got = lax.ppermute(begin, "tm", [(b, a) for a, b in pairs])
     return call(
-        out_kernel, jax.ShapeDtypeStruct((steps_here, width), F32), [V] * 4,
+        out_kernel, jax.ShapeDtypeStruct((steps_here, width), F32), [V] * 6,
         flops=16 * size ** 2, moved=size ** 2,
-    )(begin, got, maps, terms)
+    )(start, mean, begin, got, maps, terms)
 
 
 def solution(mesh):

time: 152 us -> 152 us (level)
    ppermute x2 -> x4, starting transfers between devices: 2.72 us -> 4.04 us  [the longest x1 1.42 us: shards(): other = lax.ppermute(own, 'tm', pairs[1:])]
    ppermute x8 -> x7, starting transfers between devices: 5.29 us -> 4.63 us  [shards(): lax.ppermute(value, 'tm', [(2 * turn + 1, 2 * turn + (3 if turn + 1 < fir...]
  transfers between devices with their start and end apart: 31 -> 32, of which waited for: 12 -> 12; matrix products, arithmetic and copies ran while one was open for 0% -> 0% of each run, Pallas kernels for 6% -> 6%
where the time goes in v8:
time: 152 us
  waiting for transfers between devices  95.6 us (63%)
  starting transfers between devices  39.8 us (26%)
  Pallas kernels  14.2 us (9%)
    ppermute x1, waiting for transfers between devices, shards(): got = lax.ppermute(begin, 'tm', [(b, a) for a, b in pairs])  37.6 us
    ppermute x7, waiting for transfers between devices, ring_rounds(): pieces[count - r] = lax.ppermute(left, axis, forward)  35.8 us
    ppermute x7, waiting for transfers between devices, ring_rounds(): pieces[r] = lax.ppermute(right, axis, backward)  22.1 us
    ppermute x7, starting transfers between devices, ring_rounds(): pieces[r] = lax.ppermute(right, axis, backward)  20.3 us
    ppermute x7, starting transfers between devices, ring_rounds(): pieces[count - r] = lax.ppermute(left, axis, forward)  5.4 us
    ppermute x7, starting transfers between devices, shards(): lax.ppermute(value, 'tm', [(2 * turn + 1, 2 * turn + (3 if turn + 1 < fir...  4.63 us
    pallas_call x1, Pallas kernels, shards(): call(functools.partial(four_kernel, count, have), (matrix, slab, slab, ma...  3.95 us
  transfers between devices with their start and end apart: 32, of which 12 were waited for; matrix products, arithmetic and copies ran while one was open for 0% of the time, Pallas kernels for 6%

profile of v8, /device:TPU:30, one launch (start us, length us, event | category | flops | bytes accessed | tf_op | source)
XLA Modules:
  0.0 151.6 jit_solution(13575150322392084718)
XLA Ops:
  0.0 1.4 fusion
  1.5 2.0 %collective-permute-start.1 = (bf16[256,1024]{1,0:T(8,128)(2,1)S(1)}, bf16[256,1024]{1,0:T(8,128)(2,1)S(1)}, u32[]{:S(2)}, u32[]{:S(2)}) collective-permute-start(bf16[256,1024]{1,0:T(8,128)(2,1)S(1)} %bitcast.2), channel_id=1, source_target_pairs={{0,1},{1,2},{2,3},{3,4},{4,5},{5,6},{6,7},{7,0},{8,9},{9,10},{10,1... | collective-permute-start | bytes 1572872 | tf_op jit(solution)/shard_map/ppermute | solution.py:333
  3.4 4.0 %collective-permute-start = (bf16[256,1024]{1,0:T(8,128)(2,1)S(1)}, bf16[256,1024]{1,0:T(8,128)(2,1)S(1)}, u32[]{:S(2)}, u32[]{:S(2)}) collective-permute-start(bf16[256,1024]{1,0:T(8,128)(2,1)S(1)} %bitcast.3), channel_id=1, source_target_pairs={{1,0},{2,1},{3,2},{4,3},{5,4},{6,5},{7,6},{0,7},{9,8},{10,9},{11,1... | collective-permute-start | bytes 1572872 | tf_op jit(solution)/shard_map/ppermute | solution.py:335
  7.5 1.6 %shard_map.73.refs_0_ = bf16[272,1024]{1,0:T(8,128)(2,1)S(1)} custom-call(s32[4,32]{1,0:T(4,128)S(1)} %copy-done.2, s32[4,32]{1,0:T(4,128)S(1)} %copy-done.3, bf16[4,4096]{1,0:T(4,128)(2,1)S(1)} %multiply_convert_fusion.values_ref, bf16[4,32,64,64]{3,2,1,0:T(8,128)(2,1)S(1)} %copy-done, bf16[2,128,1024]{2,1,0:T(8,128)(2,1)S(1)} %get-tuple-element.97.maps_ref), custom_call_target="tpu_custom_call" | custom-call | flops 10000000 | bytes 2097152 | tf_op jit(solution)/shard_map/pallas_call | solution.py:355
  9.1 2.0 %collective-permute-start.7 = (bf16[272,1024]{1,0:T(8,128)(2,1)S(1)}, bf16[272,1024]{1,0:T(8,128)(2,1)S(1)}, u32[]{:S(2)}, u32[]{:S(2)}) collective-permute-start(bf16[272,1024]{1,0:T(8,128)(2,1)S(1)} %shard_map.73.refs_0_), channel_id=1, source_target_pairs={{1,0},{2,1},{3,2},{4,3},{5,4},{6,5},{7,6},{0,7},{9,8},{10,9},{11,1... | collective-permute-start | bytes 1671176 | tf_op jit(solution)/shard_map/ppermute | solution.py:335
  11.1 8.2 %collective-permute-done.1.refs_7_ = bf16[256,1024]{1,0:T(8,128)(2,1)S(1)} collective-permute-done((bf16[256,1024]{1,0:T(8,128)(2,1)S(1)}, bf16[256,1024]{1,0:T(8,128)(2,1)S(1)}, u32[]{:S(2)}, u32[]{:S(2)}) %collective-permute-start.1) | collective-permute-done | bytes 524320 | tf_op jit(solution)/shard_map/ppermute | solution.py:333
  20.2 3.0 %collective-permute-start.10 = (bf16[272,1024]{1,0:T(8,128)(2,1)S(1)}, bf16[272,1024]{1,0:T(8,128)(2,1)S(1)}, u32[]{:S(2)}, u32[]{:S(2)}) collective-permute-start(bf16[272,1024]{1,0:T(8,128)(2,1)S(1)} %shard_map.73.refs_0_), channel_id=1, source_target_pairs={{0,1},{1,2},{2,3},{3,4},{4,5},{5,6},{6,7},{7,0},{8,9},{9,10},{10,1... | collective-permute-start | bytes 1671176 | tf_op jit(solution)/shard_map/ppermute | solution.py:333
  23.2 7.4 %collective-permute-done.7.refs_1_ = bf16[272,1024]{1,0:T(8,128)(2,1)S(1)} collective-permute-done((bf16[272,1024]{1,0:T(8,128)(2,1)S(1)}, bf16[272,1024]{1,0:T(8,128)(2,1)S(1)}, u32[]{:S(2)}, u32[]{:S(2)}) %collective-permute-start.7) | collective-permute-done | bytes 557088 | tf_op jit(solution)/shard_map/ppermute | solution.py:335
  30.6 3.7 %collective-permute-start.8 = (bf16[272,1024]{1,0:T(8,128)(2,1)S(1)}, bf16[272,1024]{1,0:T(8,128)(2,1)S(1)}, u32[]{:S(2)}, u32[]{:S(2)}) collective-permute-start(bf16[272,1024]{1,0:T(8,128)(2,1)S(1)} %collective-permute-done.7.refs_1_), channel_id=1, source_target_pairs={{1,0},{2,1},{3,2},{4,3},{5,4},{6,5},{7,6},{0,7},{9,8},{10,9},{11,1... | collective-permute-start | bytes 1671176 | tf_op jit(solution)/shard_map/ppermute | solution.py:335
  34.7 1.6 %collective-permute-done.4.refs_6_ = bf16[256,1024]{1,0:T(8,128)(2,1)S(1)} collective-permute-done((bf16[256,1024]{1,0:T(8,128)(2,1)S(1)}, bf16[256,1024]{1,0:T(8,128)(2,1)S(1)}, u32[]{:S(2)}, u32[]{:S(2)}) %collective-permute-start.4) | collective-permute-done | bytes 524320 | tf_op jit(solution)/shard_map/ppermute | solution.py:333
  36.3 11.9 %collective-permute-done.10.refs_5_.refs_7_ = bf16[272,1024]{1,0:T(8,128)(2,1)S(1)} collective-permute-done((bf16[272,1024]{1,0:T(8,128)(2,1)S(1)}, bf16[272,1024]{1,0:T(8,128)(2,1)S(1)}, u32[]{:S(2)}, u32[]{:S(2)}) %collective-permute-start.10) | collective-permute-done | bytes 557088 | tf_op jit(solution)/shard_map/ppermute | solution.py:333
  48.3 3.2 %collective-permute-start.9 = (bf16[272,1024]{1,0:T(8,128)(2,1)S(1)}, bf16[272,1024]{1,0:T(8,128)(2,1)S(1)}, u32[]{:S(2)}, u32[]{:S(2)}) collective-permute-start(bf16[272,1024]{1,0:T(8,128)(2,1)S(1)} %collective-permute-done.8.refs_2_), channel_id=1, source_target_pairs={{1,0},{2,1},{3,2},{4,3},{5,4},{6,5},{7,6},{0,7},{9,8},{10,9},{11,1... | collective-permute-start | bytes 1671176 | tf_op jit(solution)/shard_map/ppermute | solution.py:335
  51.5 7.1 %collective-permute-done.2.refs_2_ = bf16[256,1024]{1,0:T(8,128)(2,1)S(1)} collective-permute-done((bf16[256,1024]{1,0:T(8,128)(2,1)S(1)}, bf16[256,1024]{1,0:T(8,128)(2,1)S(1)}, u32[]{:S(2)}, u32[]{:S(2)}) %collective-permute-start.2) | collective-permute-done | bytes 524320 | tf_op jit(solution)/shard_map/ppermute | solution.py:335
  58.6 3.7 %collective-permute-start.3 = (bf16[256,1024]{1,0:T(8,128)(2,1)S(1)}, bf16[256,1024]{1,0:T(8,128)(2,1)S(1)}, u32[]{:S(2)}, u32[]{:S(2)}) collective-permute-start(bf16[256,1024]{1,0:T(8,128)(2,1)S(1)} %collective-permute-done.2.refs_2_), channel_id=1, source_target_pairs={{1,0},{2,1},{3,2},{4,3},{5,4},{6,5},{7,6},{0,7},{9,8},{10,9},{11,1... | collective-permute-start | bytes 1572872 | tf_op jit(solution)/shard_map/ppermute | solution.py:335
  62.3 9.1 %collective-permute-done.11.refs_4_.refs_6_ = bf16[272,1024]{1,0:T(8,128)(2,1)S(1)} collective-permute-done((bf16[272,1024]{1,0:T(8,128)(2,1)S(1)}, bf16[272,1024]{1,0:T(8,128)(2,1)S(1)}, u32[]{:S(2)}, u32[]{:S(2)}) %collective-permute-start.11) | collective-permute-done | bytes 557088 | tf_op jit(solution)/shard_map/ppermute | solution.py:333
  71.5 3.2 %collective-permute-start.12 = (bf16[272,1024]{1,0:T(8,128)(2,1)S(1)}, bf16[272,1024]{1,0:T(8,128)(2,1)S(1)}, u32[]{:S(2)}, u32[]{:S(2)}) collective-permute-start(bf16[272,1024]{1,0:T(8,128)(2,1)S(1)} %collective-permute-done.9.refs_3_), channel_id=1, source_target_pairs={{1,0},{2,1},{3,2},{4,3},{5,4},{6,5},{7,6},{0,7},{9,8},{10,9},{11,1... | collective-permute-start | bytes 1671176 | tf_op jit(solution)/shard_map/ppermute | solution.py:335
  74.7 7.1 %collective-permute-done.3.refs_3_ = bf16[256,1024]{1,0:T(8,128)(2,1)S(1)} collective-permute-done((bf16[256,1024]{1,0:T(8,128)(2,1)S(1)}, bf16[256,1024]{1,0:T(8,128)(2,1)S(1)}, u32[]{:S(2)}, u32[]{:S(2)}) %collective-permute-start.3) | collective-permute-done | bytes 524320 | tf_op jit(solution)/shard_map/ppermute | solution.py:335
  81.8 0.9 collective-permute-done.6.refs_4_
  82.7 3.0 %shard_map.74 = (bf16[1024,1024]{1,0:T(8,128)(2,1)S(1)}, bf16[128,1024]{1,0:T(8,128)(2,1)S(1)}, bf16[1024,1024]{1,0:T(8,128)(2,1)S(1)}) custom-call(bf16[256,1024]{1,0:T(8,128)(2,1)S(1)} %bitcast.4, bf16[256,1024]{1,0:T(8,128)(2,1)S(1)} %collective-permute-done.refs_1_, bf16[256,1024]{1,0:T(8,128)(2,1)S(1)} %collective-permute-done.2.refs_2_, ...), custom_call_target="tpu_custom_call" | custom-call | flops 2147483648 | bytes 6291456 | tf_op jit(solution)/shard_map/pallas_call | solution.py:368
  85.7 2.2 %shard_map.75 = (bf16[1024,1024]{1,0:T(8,128)(2,1)S(1)}, bf16[1024,1024]{1,0:T(8,128)(2,1)S(1)}, bf16[1024,1024]{1,0:T(8,128)(2,1)S(1)}) custom-call(bf16[1024,1024]{1,0:T(8,128)(2,1)S(1)} %get-tuple-element.53.two_ref, bf16[272,1024]{1,0:T(8,128)(2,1)S(1)} %shard_map.73.refs_0_, bf16[272,1024]{1,0:T(8,128)(2,1)S(1)} %collective-permute-done.7.refs_1_, ...), custom_call_target="tpu_custom_call" | custom-call | flops 2147483648 | bytes 6291456 | tf_op jit(solution)/shard_map/pallas_call | solution.py:373
  87.9 4.0 %collective-permute-done.13.refs_5_ = bf16[272,1024]{1,0:T(8,128)(2,1)S(1)} collective-permute-done((bf16[272,1024]{1,0:T(8,128)(2,1)S(1)}, bf16[272,1024]{1,0:T(8,128)(2,1)S(1)}, u32[]{:S(2)}, u32[]{:S(2)}) %collective-permute-start.13) | collective-permute-done | bytes 557088 | tf_op jit(solution)/shard_map/ppermute | solution.py:333
  91.9 4.0 %shard_map.76 = (bf16[1024,1024]{1,0:T(8,128)(2,1)S(1)}, bf16[128,1024]{1,0:T(8,128)(2,1)S(1)}, bf16[128,1024]{1,0:T(8,128)(2,1)S(1)}, bf16[1024,1024]{1,0:T(8,1...) custom-call(bf16[1024,1024]{1,0:T(8,128)(2,1)S(1)} %get-tuple-elemen, ...), custom_call_target="tpu_custom_call", output_to_operand_aliasing={{3}: (1, {}), {4}: (2, {}), {5}: (3, {})} | custom-call | flops 2147483648 | bytes 6291456 | tf_op jit(solution)/shard_map/pallas_call | solution.py:377
  95.9 1.4 collective-permute-start.16
  97.3 1.8 %shard_map.77 = (f32[4,1024]{1,0:T(4,128)S(1)}, bf16[16,1024]{1,0:T(8,128)(2,1)S(1)}, f32[1,1024]{1,0:T(1,128)S(1)}) custom-call(f32[16,1024]{1,0:T(8,128)S(1)} %get-tuple-element.57.drive_ref, f32[1,1024]{1,0:T(1,128)S(1)} %bitcast.6, bf16[1024,1024]{1,0:T(8,128)(2,1)S(1)} %get-tuple-element.58.second_ref, ...), custom_call_target="tpu_custom_call" | custom-call | flops 134217728 | bytes 8388608 | tf_op jit(solution)/shard_map/pallas_call | solution.py:387
  99.1 1.3 collective-permute-start.17
  100.4 0.7 collective-permute-start.14
  101.2 0.7 collective-permute-start.26
  102.0 0.7 collective-permute-start.25
  102.7 0.7 collective-permute-start.15
  111.8 1.3 collective-permute-start.31
  113.1 37.6 %collective-permute-done.31.got_ref = f32[1,1024]{1,0:T(1,128)S(1)} collective-permute-done((f32[1,1024]{1,0:T(1,128)S(1)}, f32[1,1024]{1,0:T(1,128)S(1)}, u32[]{:S(2)}, u32[]{:S(2)}) %collective-permute-start.31) | collective-permute-done | bytes 4128 | tf_op jit(solution)/shard_map/ppermute | solution.py:438
  150.7 0.8 shard_map.94
  (68 shorter events, 9.7 us)
Async XLA Ops:
  1.5 17.9 %collective-permute-start.1 = (bf16[256,1024]{1,0:T(8,128)(2,1)S(1)}, bf16[256,1024]{1,0:T(8,128)(2,1)S(1)}, u32[]{:S(2)}, u32[]{:S(2)}) collective-permute-start(bf16[256,1024]{1,0:T(8,128)(2,1)S(1)} %bitcast.2), channel_id=1, source_target_pairs={{0,1},{1,2},{2,3},{3,4},{4,5},{5,6},{6,7},{7,0},{8,9},{9,10},{10,1... | collective-permute-start | bytes 1572872 | tf_op jit(solution)/shard_map/ppermute | solution.py:333
  3.4 16.4 %collective-permute-start = (bf16[256,1024]{1,0:T(8,128)(2,1)S(1)}, bf16[256,1024]{1,0:T(8,128)(2,1)S(1)}, u32[]{:S(2)}, u32[]{:S(2)}) collective-permute-start(bf16[256,1024]{1,0:T(8,128)(2,1)S(1)} %bitcast.3), channel_id=1, source_target_pairs={{1,0},{2,1},{3,2},{4,3},{5,4},{6,5},{7,6},{0,7},{9,8},{10,9},{11,1... | collective-permute-start | bytes 1572872 | tf_op jit(solution)/shard_map/ppermute | solution.py:335
  9.1 21.5 %collective-permute-start.7 = (bf16[272,1024]{1,0:T(8,128)(2,1)S(1)}, bf16[272,1024]{1,0:T(8,128)(2,1)S(1)}, u32[]{:S(2)}, u32[]{:S(2)}) collective-permute-start(bf16[272,1024]{1,0:T(8,128)(2,1)S(1)} %shard_map.73.refs_0_), channel_id=1, source_target_pairs={{1,0},{2,1},{3,2},{4,3},{5,4},{6,5},{7,6},{0,7},{9,8},{10,9},{11,1... | collective-permute-start | bytes 1671176 | tf_op jit(solution)/shard_map/ppermute | solution.py:335
  19.8 16.5 %collective-permute-start.4 = (bf16[256,1024]{1,0:T(8,128)(2,1)S(1)}, bf16[256,1024]{1,0:T(8,128)(2,1)S(1)}, u32[]{:S(2)}, u32[]{:S(2)}) collective-permute-start(bf16[256,1024]{1,0:T(8,128)(2,1)S(1)} %collective-permute-done.1.refs_7_), channel_id=1, source_target_pairs={{0,1},{1,2},{2,3},{3,4},{4,5},{5,6},{6,7},{7,0},{8,9},{9,10},{10,1... | collective-permute-start | bytes 1572872 | tf_op jit(solution)/shard_map/ppermute | solution.py:333
  20.2 28.1 %collective-permute-start.10 = (bf16[272,1024]{1,0:T(8,128)(2,1)S(1)}, bf16[272,1024]{1,0:T(8,128)(2,1)S(1)}, u32[]{:S(2)}, u32[]{:S(2)}) collective-permute-start(bf16[272,1024]{1,0:T(8,128)(2,1)S(1)} %shard_map.73.refs_0_), channel_id=1, source_target_pairs={{0,1},{1,2},{2,3},{3,4},{4,5},{5,6},{6,7},{7,0},{8,9},{9,10},{10,1... | collective-permute-start | bytes 1671176 | tf_op jit(solution)/shard_map/ppermute | solution.py:333
  30.6 17.7 %collective-permute-start.8 = (bf16[272,1024]{1,0:T(8,128)(2,1)S(1)}, bf16[272,1024]{1,0:T(8,128)(2,1)S(1)}, u32[]{:S(2)}, u32[]{:S(2)}) collective-permute-start(bf16[272,1024]{1,0:T(8,128)(2,1)S(1)} %collective-permute-done.7.refs_1_), channel_id=1, source_target_pairs={{1,0},{2,1},{3,2},{4,3},{5,4},{6,5},{7,6},{0,7},{9,8},{10,9},{11,1... | collective-permute-start | bytes 1671176 | tf_op jit(solution)/shard_map/ppermute | solution.py:335
  34.3 24.3 %collective-permute-start.2 = (bf16[256,1024]{1,0:T(8,128)(2,1)S(1)}, bf16[256,1024]{1,0:T(8,128)(2,1)S(1)}, u32[]{:S(2)}, u32[]{:S(2)}) collective-permute-start(bf16[256,1024]{1,0:T(8,128)(2,1)S(1)} %collective-permute-done.refs_1_), channel_id=1, source_target_pairs={{1,0},{2,1},{3,2},{4,3},{5,4},{6,5},{7,6},{0,7},{9,8},{10,9},{11,1... | collective-permute-start | bytes 1572872 | tf_op jit(solution)/shard_map/ppermute | solution.py:335
  36.3 26.0 %collective-permute-start.5 = (bf16[256,1024]{1,0:T(8,128)(2,1)S(1)}, bf16[256,1024]{1,0:T(8,128)(2,1)S(1)}, u32[]{:S(2)}, u32[]{:S(2)}) collective-permute-start(bf16[256,1024]{1,0:T(8,128)(2,1)S(1)} %collective-permute-done.4.refs_6_), channel_id=1, source_target_pairs={{0,1},{1,2},{2,3},{3,4},{4,5},{5,6},{6,7},{7,0},{8,9},{9,10},{10,1... | collective-permute-start | bytes 1572872 | tf_op jit(solution)/shard_map/ppermute | solution.py:333
  48.3 23.2 %collective-permute-start.11 = (bf16[272,1024]{1,0:T(8,128)(2,1)S(1)}, bf16[272,1024]{1,0:T(8,128)(2,1)S(1)}, u32[]{:S(2)}, u32[]{:S(2)}) collective-permute-start(bf16[272,1024]{1,0:T(8,128)(2,1)S(1)} %collective-permute-done.10.refs_5_.refs_7_), channel_id=1, source_target_pairs={{0,1},{1,2},{2,3},{3,4},{4,5},{5,6},{6,7},{7,0},{8,9},{9,10},{10,1... | collective-permute-start | bytes 1671176 | tf_op jit(solution)/shard_map/ppermute | solution.py:333
  48.3 23.2 %collective-permute-start.9 = (bf16[272,1024]{1,0:T(8,128)(2,1)S(1)}, bf16[272,1024]{1,0:T(8,128)(2,1)S(1)}, u32[]{:S(2)}, u32[]{:S(2)}) collective-permute-start(bf16[272,1024]{1,0:T(8,128)(2,1)S(1)} %collective-permute-done.8.refs_2_), channel_id=1, source_target_pairs={{1,0},{2,1},{3,2},{4,3},{5,4},{6,5},{7,6},{0,7},{9,8},{10,9},{11,1... | collective-permute-start | bytes 1671176 | tf_op jit(solution)/shard_map/ppermute | solution.py:335
  58.6 23.2 %collective-permute-start.3 = (bf16[256,1024]{1,0:T(8,128)(2,1)S(1)}, bf16[256,1024]{1,0:T(8,128)(2,1)S(1)}, u32[]{:S(2)}, u32[]{:S(2)}) collective-permute-start(bf16[256,1024]{1,0:T(8,128)(2,1)S(1)} %collective-permute-done.2.refs_2_), channel_id=1, source_target_pairs={{1,0},{2,1},{3,2},{4,3},{5,4},{6,5},{7,6},{0,7},{9,8},{10,9},{11,1... | collective-permute-start | bytes 1572872 | tf_op jit(solution)/shard_map/ppermute | solution.py:335
  62.3 20.4 %collective-permute-start.6 = (bf16[256,1024]{1,0:T(8,128)(2,1)S(1)}, bf16[256,1024]{1,0:T(8,128)(2,1)S(1)}, u32[]{:S(2)}, u32[]{:S(2)}) collective-permute-start(bf16[256,1024]{1,0:T(8,128)(2,1)S(1)} %collective-permute-done.5.refs_5_), channel_id=1, source_target_pairs={{0,1},{1,2},{2,3},{3,4},{4,5},{5,6},{6,7},{7,0},{8,9},{9,10},{10,1... | collective-permute-start | bytes 1572872 | tf_op jit(solution)/shard_map/ppermute | solution.py:333
  71.4 20.5 %collective-permute-start.13 = (bf16[272,1024]{1,0:T(8,128)(2,1)S(1)}, bf16[272,1024]{1,0:T(8,128)(2,1)S(1)}, u32[]{:S(2)}, u32[]{:S(2)}) collective-permute-start(bf16[272,1024]{1,0:T(8,128)(2,1)S(1)} %collective-permute-done.11.refs_4_.refs_6_), channel_id=1, source_target_pairs={{0,1},{1,2},{2,3},{3,4},{4,5},{5,6},{6,7},{7,0},{8,9},{9,10},{10,1... | collective-permute-start | bytes 1671176 | tf_op jit(solution)/shard_map/ppermute | solution.py:333
  71.5 20.5 %collective-permute-start.12 = (bf16[272,1024]{1,0:T(8,128)(2,1)S(1)}, bf16[272,1024]{1,0:T(8,128)(2,1)S(1)}, u32[]{:S(2)}, u32[]{:S(2)}) collective-permute-start(bf16[272,1024]{1,0:T(8,128)(2,1)S(1)} %collective-permute-done.9.refs_3_), channel_id=1, source_target_pairs={{1,0},{2,1},{3,2},{4,3},{5,4},{6,5},{7,6},{0,7},{9,8},{10,9},{11,1... | collective-permute-start | bytes 1671176 | tf_op jit(solution)/shard_map/ppermute | solution.py:335
  95.9 5.4 %collective-permute-start.16 = (bf16[1024,1024]{1,0:T(8,128)(2,1)S(1)}, bf16[1024,1024]{1,0:T(8,128)(2,1)S(1)}, u32[]{:S(2)}, u32[]{:S(2)}) collective-permute-start(bf16[1024,1024]{1,0:T(8,128)(2,1)S(1)} %get-tuple-element.68.four_ref.own_ref), channel_id=1, source_target_pairs={{16,24},{32,40},{48,56},{64,72},{80,88},{96,104},{112,120},{128,13... | collective-permute-start | bytes 6291464 | tf_op jit(solution)/shard_map/ppermute | solution.py:385
  99.1 2.1 %collective-permute-start.17 = (bf16[16,1024]{1,0:T(8,128)(2,1)S(1)}, bf16[16,1024]{1,0:T(8,128)(2,1)S(1)}, u32[]{:S(2)}, u32[]{:S(2)}) collective-permute-start(bf16[16,1024]{1,0:T(8,128)(2,1)S(1)} %get-tuple-element.69.term_ref.own_term_ref), channel_id=1, source_target_pairs={{16,24},{32,40},{48,56},{64,72},{80,88},{96,104},{112,120},{128,13... | collective-permute-start | bytes 98312 | tf_op jit(solution)/shard_map/ppermute | solution.py:391
  100.4 0.7 collective-permute-start.14
  101.2 7.7 %collective-permute-start.26 = (bf16[528,1024]{1,0:T(8,128)(2,1)S(1)}, bf16[528,1024]{1,0:T(8,128)(2,1)S(1)}, u32[]{:S(2)}, u32[]{:S(2)}) collective-permute-start(bf16[528,1024]{1,0:T(8,128)(2,1)S(1)} %shard_map.82.turned1_ref), channel_id=1, source_target_pairs={{136,152},{168,184},{200,216},{232,248},{137,153},{169,185},{201,2... | collective-permute-start | bytes 3244040 | tf_op jit(solution)/shard_map/ppermute | solution.py:406
  102.0 7.0 %collective-permute-start.25 = (bf16[512,1024]{1,0:T(8,128)(2,1)S(1)}, bf16[512,1024]{1,0:T(8,128)(2,1)S(1)}, u32[]{:S(2)}, u32[]{:S(2)}) collective-permute-start(bf16[512,1024]{1,0:T(8,128)(2,1)S(1)} %shard_map.81.turned0_ref), channel_id=1, source_target_pairs={{136,152},{168,184},{200,216},{232,248},{137,153},{169,185},{201,2... | collective-permute-start | bytes 3145736 | tf_op jit(solution)/shard_map/ppermute | solution.py:404
  102.7 0.7 collective-permute-start.15
  103.4 0.7 collective-permute-start.18
  104.1 0.7 collective-permute-start.19
  104.9 0.7 collective-permute-start.20
  105.8 1.0 collective-permute-start.21
  106.9 0.7 collective-permute-start.22
  107.6 0.7 collective-permute-start.23
  108.3 0.7 collective-permute-start.24
  109.0 0.7 collective-permute-start.27
  109.7 0.7 collective-permute-start.28
  110.4 0.7 collective-permute-start.29
  111.1 0.7 collective-permute-start.30
  111.8 38.9 %collective-permute-start.31 = (f32[1,1024]{1,0:T(1,128)S(1)}, f32[1,1024]{1,0:T(1,128)S(1)}, u32[]{:S(2)}, u32[]{:S(2)}) collective-permute-start(f32[1,1024]{1,0:T(1,128)S(1)} %shard_map.93.begin_ref), channel_id=1, source_target_pairs={{8,0},{24,16},{40,32},{56,48},{72,64},{88,80},{104,96},{120,112},{... | collective-permute-start | bytes 12296 | tf_op jit(solution)/shard_map/ppermute | solution.py:438
  (6 other events, 42.9 us)

commit v9 on v7

--- a/solution.py
+++ b/solution.py
@@ -182,7 +182,7 @@
     term_ref[...] = split_rows(local)
 
 
-DIRECT = 3
+DIRECT = 2
 
 
 def pair_kernel(half, own_ref, own_term_ref, other_ref, other_term_ref, turned_ref):
@@ -242,29 +242,27 @@
             double_ref[rows:, :] = split_rows(applied(joined(came_ref[rows:, :]), turned0_ref, turned1_ref))
 
 
-def far_kernel(
-    chip, last, begin_ref, came_ref, before_ref, map0_ref, map1_ref, double0_ref, double1_ref, held_ref, value_ref
-):
+def far_kernel(chip, came_ref, before_ref, double0_ref, double1_ref, value_ref):
     here = lax.axis_index("tm") == 2 * chip + 1
 
     @pl.when(here)
     def _():
-        if last:
-            value_ref[...] = before_ref[...]
-        else:
-            value_ref[...] = applied(came_ref[...], double0_ref, double1_ref)
-        held_ref[...] = applied(came_ref[...], map0_ref, map1_ref)
+        value_ref[...] = applied(came_ref[...], double0_ref, double1_ref)
 
     @pl.when(jnp.logical_not(here))
     def _():
-        held_ref[...] = begin_ref[...]
         value_ref[...] = before_ref[...]
 
 
-def final_kernel(firsts, held_ref, handed_ref, begin_ref):
+def final_kernel(firsts, held_ref, handed_ref, map0_ref, map1_ref, *refs):
+    cames, begin_ref = refs[:-1], refs[-1]
     chip = chip_here()
     handed = jnp.logical_and(chip >= firsts, lax.rem(chip, 2) == 0)
     begin_ref[...] = jnp.where(handed, handed_ref[...], held_ref[...])
+    for i, came_ref in enumerate(cames):
+        @pl.when(lax.axis_index("tm") == 2 * (firsts + 1 + 2 * i) + 1)
+        def _():
+            begin_ref[...] = applied(came_ref[...], map0_ref, map1_ref)
 
 
 def ready_kernel(other_ref, other_term_ref, locals_ref, after_ref, *refs):
@@ -410,25 +408,27 @@
                 flops=32 * size ** 2, moved=2 * size ** 2,
             )(begin, came, turned0, turned1)
         came = lax.ppermute(value, "tm", [(2 * turn + 1, 2 * turn + (3 if turn + 1 < firsts else 5))])
-        if turn == DIRECT:
+        if turn == 3:
             maps, terms = call(
                 ready_kernel,
                 (jax.ShapeDtypeStruct((size, steps_here * width), BF16), jax.ShapeDtypeStruct((steps_here, width), F32)),
                 [V] * 8, flops=size ** 3, moved=4 * size ** 2,
             )(other, other_term, locals_, value, early[0], slab2, slab3, slab4)
-        if turn == DIRECT + 1:
+        if turn == 4:
             came = after(came, maps)
     double0 = call(functools.partial(double_kernel, 0, firsts), part, [V] * 3, **half_cost)(before0, turned0, turned1)
     double1 = call(functools.partial(double_kernel, 1, firsts), longer, [V] * 3, **half_cost)(before1, turned0, turned1)
-    for chip in range(firsts + 1, chips, 2):
-        begin, value = call(
-            functools.partial(far_kernel, chip, chip == chips - 1), (row, row), [V] * 7,
-            flops=64 * size ** 2, moved=4 * size ** 2,
-        )(begin, came, value, before0, before1, double0, double1)
-        if chip < chips - 1:
-            came = lax.ppermute(value, "tm", [(2 * chip + 1, 2 * chip + 5)])
+    cames = [came]
+    for chip in range(firsts + 1, chips - 1, 2):
+        value = call(
+            functools.partial(far_kernel, chip), row, [V] * 4, flops=32 * size ** 2, moved=2 * size ** 2
+        )(came, value, double0, double1)
+        came = lax.ppermute(value, "tm", [(2 * chip + 1, 2 * chip + 5)])
+        cames.append(came)
     handed = lax.ppermute(value, "tm", [(2 * c - 1, 2 * c + 1) for c in range(firsts, chips, 2)])
-    begin = call(functools.partial(final_kernel, firsts), row, [V, V])(begin, handed)
+    begin = call(
+        functools.partial(final_kernel, firsts), row, [V] * (4 + len(cames)), flops=32 * size ** 2, moved=2 * size ** 2
+    )(begin, handed, before0, before1, *cames)
     got = lax.ppermute(begin, "tm", [(b, a) for a, b in pairs])
     return call(
         out_kernel, jax.ShapeDtypeStruct((steps_here, width), F32), [V] * 4,

time: 152 us -> 150 us (0.987)
  waiting for transfers between devices: 95.5 us -> 93.8 us
    ppermute x1, waiting for transfers between devices: 36.8 us -> 35.1 us  [shards(): got = lax.ppermute(begin, 'tm', [(b, a) for a, b in pairs])]
where the time goes in v9:
time: 150 us; the launch traced here: 149 us
  waiting for transfers between devices  93.8 us (63%)
  starting transfers between devices  39.3 us (26%)
  Pallas kernels  14.3 us (10%)
    ppermute x7, waiting for transfers between devices, ring_rounds(): pieces[count - r] = lax.ppermute(left, axis, forward)  35.8 us
    ppermute x1, waiting for transfers between devices, shards(): got = lax.ppermute(begin, 'tm', [(b, a) for a, b in pairs])  35.1 us
    ppermute x7, waiting for transfers between devices, ring_rounds(): pieces[r] = lax.ppermute(right, axis, backward)  22.1 us
    ppermute x7, starting transfers between devices, ring_rounds(): pieces[r] = lax.ppermute(right, axis, backward)  20.3 us
    ppermute x7, starting transfers between devices, ring_rounds(): pieces[count - r] = lax.ppermute(left, axis, forward)  5.4 us
    ppermute x8, starting transfers between devices, shards(): lax.ppermute(value, 'tm', [(2 * turn + 1, 2 * turn + (3 if turn + 1 < fir...  5.29 us
    pallas_call x1, Pallas kernels, shards(): call(functools.partial(four_kernel, count, have), (matrix, slab, slab, ma...  3.96 us
    pallas_call x1, Pallas kernels, shards(): call(functools.partial(two_kernel, count), (matrix, slab, matrix), [A] *...  3.02 us
  transfers between devices with their start and end apart: 31, of which 12 were waited for; matrix products, arithmetic and copies ran while one was open for 0% of the time, Pallas kernels for 6%

profile of v9, /device:TPU:30, one launch (start us, length us, event | category | flops | bytes accessed | tf_op | source)
XLA Modules:
  0.0 149.3 jit_solution(17514952157582822591)
XLA Ops:
  0.0 1.4 fusion
  1.5 2.0 %collective-permute-start.1 = (bf16[256,1024]{1,0:T(8,128)(2,1)S(1)}, bf16[256,1024]{1,0:T(8,128)(2,1)S(1)}, u32[]{:S(2)}, u32[]{:S(2)}) collective-permute-start(bf16[256,1024]{1,0:T(8,128)(2,1)S(1)} %bitcast.2), channel_id=1, source_target_pairs={{0,1},{1,2},{2,3},{3,4},{4,5},{5,6},{6,7},{7,0},{8,9},{9,10},{10,1... | collective-permute-start | bytes 1572872 | tf_op jit(solution)/shard_map/ppermute | solution.py:327
  3.4 4.0 %collective-permute-start = (bf16[256,1024]{1,0:T(8,128)(2,1)S(1)}, bf16[256,1024]{1,0:T(8,128)(2,1)S(1)}, u32[]{:S(2)}, u32[]{:S(2)}) collective-permute-start(bf16[256,1024]{1,0:T(8,128)(2,1)S(1)} %bitcast.3), channel_id=1, source_target_pairs={{1,0},{2,1},{3,2},{4,3},{5,4},{6,5},{7,6},{0,7},{9,8},{10,9},{11,1... | collective-permute-start | bytes 1572872 | tf_op jit(solution)/shard_map/ppermute | solution.py:329
  7.5 1.6 %shard_map.73.refs_0_ = bf16[272,1024]{1,0:T(8,128)(2,1)S(1)} custom-call(s32[4,32]{1,0:T(4,128)S(1)} %copy-done.2, s32[4,32]{1,0:T(4,128)S(1)} %copy-done.3, bf16[4,4096]{1,0:T(4,128)(2,1)S(1)} %multiply_convert_fusion.values_ref, bf16[4,32,64,64]{3,2,1,0:T(8,128)(2,1)S(1)} %copy-done, bf16[2,128,1024]{2,1,0:T(8,128)(2,1)S(1)} %get-tuple-element.77.maps_ref), custom_call_target="tpu_custom_call" | custom-call | flops 10000000 | bytes 2097152 | tf_op jit(solution)/shard_map/pallas_call | solution.py:349
  9.1 2.0 %collective-permute-start.7 = (bf16[272,1024]{1,0:T(8,128)(2,1)S(1)}, bf16[272,1024]{1,0:T(8,128)(2,1)S(1)}, u32[]{:S(2)}, u32[]{:S(2)}) collective-permute-start(bf16[272,1024]{1,0:T(8,128)(2,1)S(1)} %shard_map.73.refs_0_), channel_id=1, source_target_pairs={{1,0},{2,1},{3,2},{4,3},{5,4},{6,5},{7,6},{0,7},{9,8},{10,9},{11,1... | collective-permute-start | bytes 1671176 | tf_op jit(solution)/shard_map/ppermute | solution.py:329
  11.1 8.2 %collective-permute-done.1.refs_7_ = bf16[256,1024]{1,0:T(8,128)(2,1)S(1)} collective-permute-done((bf16[256,1024]{1,0:T(8,128)(2,1)S(1)}, bf16[256,1024]{1,0:T(8,128)(2,1)S(1)}, u32[]{:S(2)}, u32[]{:S(2)}) %collective-permute-start.1) | collective-permute-done | bytes 524320 | tf_op jit(solution)/shard_map/ppermute | solution.py:327
  20.2 3.0 %collective-permute-start.10 = (bf16[272,1024]{1,0:T(8,128)(2,1)S(1)}, bf16[272,1024]{1,0:T(8,128)(2,1)S(1)}, u32[]{:S(2)}, u32[]{:S(2)}) collective-permute-start(bf16[272,1024]{1,0:T(8,128)(2,1)S(1)} %shard_map.73.refs_0_), channel_id=1, source_target_pairs={{0,1},{1,2},{2,3},{3,4},{4,5},{5,6},{6,7},{7,0},{8,9},{9,10},{10,1... | collective-permute-start | bytes 1671176 | tf_op jit(solution)/shard_map/ppermute | solution.py:327
  23.2 7.4 %collective-permute-done.7.refs_1_ = bf16[272,1024]{1,0:T(8,128)(2,1)S(1)} collective-permute-done((bf16[272,1024]{1,0:T(8,128)(2,1)S(1)}, bf16[272,1024]{1,0:T(8,128)(2,1)S(1)}, u32[]{:S(2)}, u32[]{:S(2)}) %collective-permute-start.7) | collective-permute-done | bytes 557088 | tf_op jit(solution)/shard_map/ppermute | solution.py:329
  30.6 3.7 %collective-permute-start.8 = (bf16[272,1024]{1,0:T(8,128)(2,1)S(1)}, bf16[272,1024]{1,0:T(8,128)(2,1)S(1)}, u32[]{:S(2)}, u32[]{:S(2)}) collective-permute-start(bf16[272,1024]{1,0:T(8,128)(2,1)S(1)} %collective-permute-done.7.refs_1_), channel_id=1, source_target_pairs={{1,0},{2,1},{3,2},{4,3},{5,4},{6,5},{7,6},{0,7},{9,8},{10,9},{11,1... | collective-permute-start | bytes 1671176 | tf_op jit(solution)/shard_map/ppermute | solution.py:329
  34.7 1.6 %collective-permute-done.4.refs_6_ = bf16[256,1024]{1,0:T(8,128)(2,1)S(1)} collective-permute-done((bf16[256,1024]{1,0:T(8,128)(2,1)S(1)}, bf16[256,1024]{1,0:T(8,128)(2,1)S(1)}, u32[]{:S(2)}, u32[]{:S(2)}) %collective-permute-start.4) | collective-permute-done | bytes 524320 | tf_op jit(solution)/shard_map/ppermute | solution.py:327
  36.3 11.9 %collective-permute-done.10.refs_5_.refs_7_ = bf16[272,1024]{1,0:T(8,128)(2,1)S(1)} collective-permute-done((bf16[272,1024]{1,0:T(8,128)(2,1)S(1)}, bf16[272,1024]{1,0:T(8,128)(2,1)S(1)}, u32[]{:S(2)}, u32[]{:S(2)}) %collective-permute-start.10) | collective-permute-done | bytes 557088 | tf_op jit(solution)/shard_map/ppermute | solution.py:327
  48.3 3.2 %collective-permute-start.9 = (bf16[272,1024]{1,0:T(8,128)(2,1)S(1)}, bf16[272,1024]{1,0:T(8,128)(2,1)S(1)}, u32[]{:S(2)}, u32[]{:S(2)}) collective-permute-start(bf16[272,1024]{1,0:T(8,128)(2,1)S(1)} %collective-permute-done.8.refs_2_), channel_id=1, source_target_pairs={{1,0},{2,1},{3,2},{4,3},{5,4},{6,5},{7,6},{0,7},{9,8},{10,9},{11,1... | collective-permute-start | bytes 1671176 | tf_op jit(solution)/shard_map/ppermute | solution.py:329
  51.5 7.1 %collective-permute-done.2.refs_2_ = bf16[256,1024]{1,0:T(8,128)(2,1)S(1)} collective-permute-done((bf16[256,1024]{1,0:T(8,128)(2,1)S(1)}, bf16[256,1024]{1,0:T(8,128)(2,1)S(1)}, u32[]{:S(2)}, u32[]{:S(2)}) %collective-permute-start.2) | collective-permute-done | bytes 524320 | tf_op jit(solution)/shard_map/ppermute | solution.py:329
  58.6 3.7 %collective-permute-start.3 = (bf16[256,1024]{1,0:T(8,128)(2,1)S(1)}, bf16[256,1024]{1,0:T(8,128)(2,1)S(1)}, u32[]{:S(2)}, u32[]{:S(2)}) collective-permute-start(bf16[256,1024]{1,0:T(8,128)(2,1)S(1)} %collective-permute-done.2.refs_2_), channel_id=1, source_target_pairs={{1,0},{2,1},{3,2},{4,3},{5,4},{6,5},{7,6},{0,7},{9,8},{10,9},{11,1... | collective-permute-start | bytes 1572872 | tf_op jit(solution)/shard_map/ppermute | solution.py:329
  62.3 9.1 %collective-permute-done.11.refs_4_.refs_6_ = bf16[272,1024]{1,0:T(8,128)(2,1)S(1)} collective-permute-done((bf16[272,1024]{1,0:T(8,128)(2,1)S(1)}, bf16[272,1024]{1,0:T(8,128)(2,1)S(1)}, u32[]{:S(2)}, u32[]{:S(2)}) %collective-permute-start.11) | collective-permute-done | bytes 557088 | tf_op jit(solution)/shard_map/ppermute | solution.py:327
  71.5 3.2 %collective-permute-start.12 = (bf16[272,1024]{1,0:T(8,128)(2,1)S(1)}, bf16[272,1024]{1,0:T(8,128)(2,1)S(1)}, u32[]{:S(2)}, u32[]{:S(2)}) collective-permute-start(bf16[272,1024]{1,0:T(8,128)(2,1)S(1)} %collective-permute-done.9.refs_3_), channel_id=1, source_target_pairs={{1,0},{2,1},{3,2},{4,3},{5,4},{6,5},{7,6},{0,7},{9,8},{10,9},{11,1... | collective-permute-start | bytes 1671176 | tf_op jit(solution)/shard_map/ppermute | solution.py:329
  74.7 7.1 %collective-permute-done.3.refs_3_ = bf16[256,1024]{1,0:T(8,128)(2,1)S(1)} collective-permute-done((bf16[256,1024]{1,0:T(8,128)(2,1)S(1)}, bf16[256,1024]{1,0:T(8,128)(2,1)S(1)}, u32[]{:S(2)}, u32[]{:S(2)}) %collective-permute-start.3) | collective-permute-done | bytes 524320 | tf_op jit(solution)/shard_map/ppermute | solution.py:329
  81.8 0.9 collective-permute-done.6.refs_4_
  82.7 3.0 %shard_map.74 = (bf16[1024,1024]{1,0:T(8,128)(2,1)S(1)}, bf16[128,1024]{1,0:T(8,128)(2,1)S(1)}, bf16[1024,1024]{1,0:T(8,128)(2,1)S(1)}) custom-call(bf16[256,1024]{1,0:T(8,128)(2,1)S(1)} %bitcast.4, bf16[256,1024]{1,0:T(8,128)(2,1)S(1)} %collective-permute-done.refs_1_, bf16[256,1024]{1,0:T(8,128)(2,1)S(1)} %collective-permute-done.2.refs_2_, ...), custom_call_target="tpu_custom_call" | custom-call | flops 2147483648 | bytes 6291456 | tf_op jit(solution)/shard_map/pallas_call | solution.py:362
  85.7 2.2 %shard_map.75 = (bf16[1024,1024]{1,0:T(8,128)(2,1)S(1)}, bf16[1024,1024]{1,0:T(8,128)(2,1)S(1)}, bf16[1024,1024]{1,0:T(8,128)(2,1)S(1)}) custom-call(bf16[1024,1024]{1,0:T(8,128)(2,1)S(1)} %get-tuple-element.43.two_ref, bf16[272,1024]{1,0:T(8,128)(2,1)S(1)} %shard_map.73.refs_0_, bf16[272,1024]{1,0:T(8,128)(2,1)S(1)} %collective-permute-done.7.refs_1_, ...), custom_call_target="tpu_custom_call" | custom-call | flops 2147483648 | bytes 6291456 | tf_op jit(solution)/shard_map/pallas_call | solution.py:367
  87.9 4.0 %collective-permute-done.13.refs_5_ = bf16[272,1024]{1,0:T(8,128)(2,1)S(1)} collective-permute-done((bf16[272,1024]{1,0:T(8,128)(2,1)S(1)}, bf16[272,1024]{1,0:T(8,128)(2,1)S(1)}, u32[]{:S(2)}, u32[]{:S(2)}) %collective-permute-start.13) | collective-permute-done | bytes 557088 | tf_op jit(solution)/shard_map/ppermute | solution.py:327
  91.9 4.0 %shard_map.76 = (bf16[1024,1024]{1,0:T(8,128)(2,1)S(1)}, bf16[128,1024]{1,0:T(8,128)(2,1)S(1)}, bf16[128,1024]{1,0:T(8,128)(2,1)S(1)}, bf16[1024,1024]{1,0:T(8,1...) custom-call(bf16[1024,1024]{1,0:T(8,128)(2,1)S(1)} %get-tuple-elemen, ...), custom_call_target="tpu_custom_call", output_to_operand_aliasing={{3}: (1, {}), {4}: (2, {}), {5}: (3, {})} | custom-call | flops 2147483648 | bytes 6291456 | tf_op jit(solution)/shard_map/pallas_call | solution.py:371
  95.9 1.4 collective-permute-start.14
  97.3 1.8 %shard_map.77 = (f32[4,1024]{1,0:T(4,128)S(1)}, bf16[16,1024]{1,0:T(8,128)(2,1)S(1)}) custom-call(f32[16,1024]{1,0:T(8,128)S(1)} %get-tuple-element.48.drive_ref, bf16[1024,1024]{1,0:T(8,128)(2,1)S(1)} %get-tuple-element.49.second_ref, bf16[1024,1024]{1,0:T(8,128)(2,1)S(1)} %get-tuple-element.50.third_ref, bf16[1024,1024]{1,0:T(8,128)(2,1)S(1)} %get-tuple-element.51.fourth_ref), custom_call_target="tpu_custom_call" | custom-call | flops 100663296 | bytes 6291456 | tf_op jit(solution)/shard_map/pallas_call | solution.py:380
  99.1 1.3 collective-permute-start.15
  100.4 0.8 collective-permute-done.15.other_term_ref
  101.2 0.8 collective-permute-start.24
  102.1 0.7 collective-permute-start.25
  102.9 0.7 collective-permute-start.16
  112.1 1.3 collective-permute-start.30
  113.4 35.1 %collective-permute-done.30.got_ref = f32[1,1024]{1,0:T(1,128)S(1)} collective-permute-done((f32[1,1024]{1,0:T(1,128)S(1)}, f32[1,1024]{1,0:T(1,128)S(1)}, u32[]{:S(2)}, u32[]{:S(2)}) %collective-permute-start.30) | collective-permute-done | bytes 4128 | tf_op jit(solution)/shard_map/ppermute | solution.py:432
  148.4 0.8 shard_map.95
  (67 shorter events, 9.6 us)
Async XLA Ops:
  0.0 7.5 %copy-start.2 = (s32[4,32]{1,0:T(4,128)S(1)}, s32[4,32]{1,0:T(4,128)}, u32[]{:S(2)}) copy-start(s32[4,32]{1,0:T(4,128)} %rows_ref.1) | copy-start | bytes 1540
  1.5 17.9 %collective-permute-start.1 = (bf16[256,1024]{1,0:T(8,128)(2,1)S(1)}, bf16[256,1024]{1,0:T(8,128)(2,1)S(1)}, u32[]{:S(2)}, u32[]{:S(2)}) collective-permute-start(bf16[256,1024]{1,0:T(8,128)(2,1)S(1)} %bitcast.2), channel_id=1, source_target_pairs={{0,1},{1,2},{2,3},{3,4},{4,5},{5,6},{6,7},{7,0},{8,9},{9,10},{10,1... | collective-permute-start | bytes 1572872 | tf_op jit(solution)/shard_map/ppermute | solution.py:327
  3.4 16.4 %collective-permute-start = (bf16[256,1024]{1,0:T(8,128)(2,1)S(1)}, bf16[256,1024]{1,0:T(8,128)(2,1)S(1)}, u32[]{:S(2)}, u32[]{:S(2)}) collective-permute-start(bf16[256,1024]{1,0:T(8,128)(2,1)S(1)} %bitcast.3), channel_id=1, source_target_pairs={{1,0},{2,1},{3,2},{4,3},{5,4},{6,5},{7,6},{0,7},{9,8},{10,9},{11,1... | collective-permute-start | bytes 1572872 | tf_op jit(solution)/shard_map/ppermute | solution.py:329
  9.1 21.5 %collective-permute-start.7 = (bf16[272,1024]{1,0:T(8,128)(2,1)S(1)}, bf16[272,1024]{1,0:T(8,128)(2,1)S(1)}, u32[]{:S(2)}, u32[]{:S(2)}) collective-permute-start(bf16[272,1024]{1,0:T(8,128)(2,1)S(1)} %shard_map.73.refs_0_), channel_id=1, source_target_pairs={{1,0},{2,1},{3,2},{4,3},{5,4},{6,5},{7,6},{0,7},{9,8},{10,9},{11,1... | collective-permute-start | bytes 1671176 | tf_op jit(solution)/shard_map/ppermute | solution.py:329
  19.8 16.5 %collective-permute-start.4 = (bf16[256,1024]{1,0:T(8,128)(2,1)S(1)}, bf16[256,1024]{1,0:T(8,128)(2,1)S(1)}, u32[]{:S(2)}, u32[]{:S(2)}) collective-permute-start(bf16[256,1024]{1,0:T(8,128)(2,1)S(1)} %collective-permute-done.1.refs_7_), channel_id=1, source_target_pairs={{0,1},{1,2},{2,3},{3,4},{4,5},{5,6},{6,7},{7,0},{8,9},{9,10},{10,1... | collective-permute-start | bytes 1572872 | tf_op jit(solution)/shard_map/ppermute | solution.py:327
  20.2 28.1 %collective-permute-start.10 = (bf16[272,1024]{1,0:T(8,128)(2,1)S(1)}, bf16[272,1024]{1,0:T(8,128)(2,1)S(1)}, u32[]{:S(2)}, u32[]{:S(2)}) collective-permute-start(bf16[272,1024]{1,0:T(8,128)(2,1)S(1)} %shard_map.73.refs_0_), channel_id=1, source_target_pairs={{0,1},{1,2},{2,3},{3,4},{4,5},{5,6},{6,7},{7,0},{8,9},{9,10},{10,1... | collective-permute-start | bytes 1671176 | tf_op jit(solution)/shard_map/ppermute | solution.py:327
  30.6 17.7 %collective-permute-start.8 = (bf16[272,1024]{1,0:T(8,128)(2,1)S(1)}, bf16[272,1024]{1,0:T(8,128)(2,1)S(1)}, u32[]{:S(2)}, u32[]{:S(2)}) collective-permute-start(bf16[272,1024]{1,0:T(8,128)(2,1)S(1)} %collective-permute-done.7.refs_1_), channel_id=1, source_target_pairs={{1,0},{2,1},{3,2},{4,3},{5,4},{6,5},{7,6},{0,7},{9,8},{10,9},{11,1... | collective-permute-start | bytes 1671176 | tf_op jit(solution)/shard_map/ppermute | solution.py:329
  34.3 24.3 %collective-permute-start.2 = (bf16[256,1024]{1,0:T(8,128)(2,1)S(1)}, bf16[256,1024]{1,0:T(8,128)(2,1)S(1)}, u32[]{:S(2)}, u32[]{:S(2)}) collective-permute-start(bf16[256,1024]{1,0:T(8,128)(2,1)S(1)} %collective-permute-done.refs_1_), channel_id=1, source_target_pairs={{1,0},{2,1},{3,2},{4,3},{5,4},{6,5},{7,6},{0,7},{9,8},{10,9},{11,1... | collective-permute-start | bytes 1572872 | tf_op jit(solution)/shard_map/ppermute | solution.py:329
  36.3 26.0 %collective-permute-start.5 = (bf16[256,1024]{1,0:T(8,128)(2,1)S(1)}, bf16[256,1024]{1,0:T(8,128)(2,1)S(1)}, u32[]{:S(2)}, u32[]{:S(2)}) collective-permute-start(bf16[256,1024]{1,0:T(8,128)(2,1)S(1)} %collective-permute-done.4.refs_6_), channel_id=1, source_target_pairs={{0,1},{1,2},{2,3},{3,4},{4,5},{5,6},{6,7},{7,0},{8,9},{9,10},{10,1... | collective-permute-start | bytes 1572872 | tf_op jit(solution)/shard_map/ppermute | solution.py:327
  48.3 23.2 %collective-permute-start.11 = (bf16[272,1024]{1,0:T(8,128)(2,1)S(1)}, bf16[272,1024]{1,0:T(8,128)(2,1)S(1)}, u32[]{:S(2)}, u32[]{:S(2)}) collective-permute-start(bf16[272,1024]{1,0:T(8,128)(2,1)S(1)} %collective-permute-done.10.refs_5_.refs_7_), channel_id=1, source_target_pairs={{0,1},{1,2},{2,3},{3,4},{4,5},{5,6},{6,7},{7,0},{8,9},{9,10},{10,1... | collective-permute-start | bytes 1671176 | tf_op jit(solution)/shard_map/ppermute | solution.py:327
  48.3 23.2 %collective-permute-start.9 = (bf16[272,1024]{1,0:T(8,128)(2,1)S(1)}, bf16[272,1024]{1,0:T(8,128)(2,1)S(1)}, u32[]{:S(2)}, u32[]{:S(2)}) collective-permute-start(bf16[272,1024]{1,0:T(8,128)(2,1)S(1)} %collective-permute-done.8.refs_2_), channel_id=1, source_target_pairs={{1,0},{2,1},{3,2},{4,3},{5,4},{6,5},{7,6},{0,7},{9,8},{10,9},{11,1... | collective-permute-start | bytes 1671176 | tf_op jit(solution)/shard_map/ppermute | solution.py:329
  58.6 23.2 %collective-permute-start.3 = (bf16[256,1024]{1,0:T(8,128)(2,1)S(1)}, bf16[256,1024]{1,0:T(8,128)(2,1)S(1)}, u32[]{:S(2)}, u32[]{:S(2)}) collective-permute-start(bf16[256,1024]{1,0:T(8,128)(2,1)S(1)} %collective-permute-done.2.refs_2_), channel_id=1, source_target_pairs={{1,0},{2,1},{3,2},{4,3},{5,4},{6,5},{7,6},{0,7},{9,8},{10,9},{11,1... | collective-permute-start | bytes 1572872 | tf_op jit(solution)/shard_map/ppermute | solution.py:329
  62.3 20.4 %collective-permute-start.6 = (bf16[256,1024]{1,0:T(8,128)(2,1)S(1)}, bf16[256,1024]{1,0:T(8,128)(2,1)S(1)}, u32[]{:S(2)}, u32[]{:S(2)}) collective-permute-start(bf16[256,1024]{1,0:T(8,128)(2,1)S(1)} %collective-permute-done.5.refs_5_), channel_id=1, source_target_pairs={{0,1},{1,2},{2,3},{3,4},{4,5},{5,6},{6,7},{7,0},{8,9},{9,10},{10,1... | collective-permute-start | bytes 1572872 | tf_op jit(solution)/shard_map/ppermute | solution.py:327
  71.4 20.5 %collective-permute-start.13 = (bf16[272,1024]{1,0:T(8,128)(2,1)S(1)}, bf16[272,1024]{1,0:T(8,128)(2,1)S(1)}, u32[]{:S(2)}, u32[]{:S(2)}) collective-permute-start(bf16[272,1024]{1,0:T(8,128)(2,1)S(1)} %collective-permute-done.11.refs_4_.refs_6_), channel_id=1, source_target_pairs={{0,1},{1,2},{2,3},{3,4},{4,5},{5,6},{6,7},{7,0},{8,9},{9,10},{10,1... | collective-permute-start | bytes 1671176 | tf_op jit(solution)/shard_map/ppermute | solution.py:327
  71.5 20.5 %collective-permute-start.12 = (bf16[272,1024]{1,0:T(8,128)(2,1)S(1)}, bf16[272,1024]{1,0:T(8,128)(2,1)S(1)}, u32[]{:S(2)}, u32[]{:S(2)}) collective-permute-start(bf16[272,1024]{1,0:T(8,128)(2,1)S(1)} %collective-permute-done.9.refs_3_), channel_id=1, source_target_pairs={{1,0},{2,1},{3,2},{4,3},{5,4},{6,5},{7,6},{0,7},{9,8},{10,9},{11,1... | collective-permute-start | bytes 1671176 | tf_op jit(solution)/shard_map/ppermute | solution.py:329
  95.9 5.3 %collective-permute-start.14 = (bf16[1024,1024]{1,0:T(8,128)(2,1)S(1)}, bf16[1024,1024]{1,0:T(8,128)(2,1)S(1)}, u32[]{:S(2)}, u32[]{:S(2)}) collective-permute-start(bf16[1024,1024]{1,0:T(8,128)(2,1)S(1)} %get-tuple-element.47.own_ref), channel_id=1, source_target_pairs={{0,8},{16,24},{32,40},{48,56},{64,72},{80,88},{96,104},{112,120},{... | collective-permute-start | bytes 6291464 | tf_op jit(solution)/shard_map/ppermute | solution.py:379
  99.1 2.1 %collective-permute-start.15 = (bf16[16,1024]{1,0:T(8,128)(2,1)S(1)}, bf16[16,1024]{1,0:T(8,128)(2,1)S(1)}, u32[]{:S(2)}, u32[]{:S(2)}) collective-permute-start(bf16[16,1024]{1,0:T(8,128)(2,1)S(1)} %get-tuple-element.52.own_term_ref), channel_id=1, source_target_pairs={{0,8},{16,24},{32,40},{48,56},{64,72},{80,88},{96,104},{112,120},{... | collective-permute-start | bytes 98312 | tf_op jit(solution)/shard_map/ppermute | solution.py:383
  101.2 7.9 %collective-permute-start.24 = (bf16[512,1024]{1,0:T(8,128)(2,1)S(1)}, bf16[512,1024]{1,0:T(8,128)(2,1)S(1)}, u32[]{:S(2)}, u32[]{:S(2)}) collective-permute-start(bf16[512,1024]{1,0:T(8,128)(2,1)S(1)} %shard_map.81.turned0_ref), channel_id=1, source_target_pairs={{136,152},{168,184},{200,216},{232,248},{137,153},{169,185},{201,2... | collective-permute-start | bytes 3145736 | tf_op jit(solution)/shard_map/ppermute | solution.py:393
  102.1 7.0 %collective-permute-start.25 = (bf16[528,1024]{1,0:T(8,128)(2,1)S(1)}, bf16[528,1024]{1,0:T(8,128)(2,1)S(1)}, u32[]{:S(2)}, u32[]{:S(2)}) collective-permute-start(bf16[528,1024]{1,0:T(8,128)(2,1)S(1)} %shard_map.78.turned1_ref), channel_id=1, source_target_pairs={{136,152},{168,184},{200,216},{232,248},{137,153},{169,185},{201,2... | collective-permute-start | bytes 3244040 | tf_op jit(solution)/shard_map/ppermute | solution.py:395
  102.9 0.7 collective-permute-start.16
  103.6 0.7 collective-permute-start.17
  104.3 0.7 collective-permute-start.18
  105.0 0.7 collective-permute-start.19
  105.7 1.3 collective-permute-start.20
  107.0 0.7 collective-permute-start.21
  107.7 0.7 collective-permute-start.22
  108.4 0.8 collective-permute-start.23
  109.2 0.7 collective-permute-start.26
  109.9 0.7 collective-permute-start.27
  110.7 1.3 collective-permute-start.29
  111.3 0.7 collective-permute-start.28
  112.1 36.4 %collective-permute-start.30 = (f32[1,1024]{1,0:T(1,128)S(1)}, f32[1,1024]{1,0:T(1,128)S(1)}, u32[]{:S(2)}, u32[]{:S(2)}) collective-permute-start(f32[1,1024]{1,0:T(1,128)S(1)} %shard_map.94.begin_ref), channel_id=1, source_target_pairs={{8,0},{24,16},{40,32},{56,48},{72,64},{88,80},{104,96},{120,112},{... | collective-permute-start | bytes 12296 | tf_op jit(solution)/shard_map/ppermute | solution.py:432
  (5 other events, 31.6 us)

commit v10 on v9

--- a/solution.py
+++ b/solution.py
@@ -120,7 +120,7 @@
 
 
 def two_kernel(count, *refs):
-    pieces, (two_ref, slab_ref, next_ref, one_ref, sems) = list(enumerate(refs[:count])), refs[count:]
+    pieces, (two_ref, slab_ref, one_ref, next_ref, sems) = list(enumerate(refs[:count])), refs[count:]
     width = slab_ref.shape[0]
     place = lax.axis_index("state")
     ones = fetched(count, place, pieces, 0, one_ref, sems, 0)
@@ -145,63 +145,94 @@
         three_ref[at, :] = jnp.dot(third_ref[at, :], two_ref[...], preferred_element_type=F32).astype(BF16)
 
 
-def four_kernel(count, have, two_ref, threes_ref, thirds_ref, fourths_ref, *refs):
+def stepped(x, drive_ref, *map_refs):
+    for j, map_ref in enumerate(map_refs):
+        x = times_t(x, map_ref[...]) + joined(drive_ref[3 * j:3 * j + 3, :])
+    return x
+
+
+def gather_kernel(count, have, prior_ref, first_ref, second_ref, thirds_ref, fourths_ref, *refs):
     missing = [(r, refs[r]) for r in range(count) if r not in have]
-    four_ref, slab3_ref, slab4_ref, three_ref, third_ref, fourth_ref, drive_ref, parts_ref, sems = refs[count:]
+    third_ref, fourth_ref, drive_ref, mean_ref, parts_ref, sems = refs[count:]
+    width = third_ref.shape[0] // count
+    place = lax.axis_index("state")
+    copies = fetched(count, place, missing, 0, third_ref, sems, 0)
+    copies += fetched(count, place, missing, 1, fourth_ref, sems, len(missing))
+    for r in range(count):
+        at = 2 * len(missing) + r
+        copies.append(pltpu.make_async_copy(refs[r].at[pl.ds(2 * width, 16), :], parts_ref.at[r], sems.at[at]))
+        copies[at].start()
+    for copy in copies:
+        copy.wait()
+    drive_ref[...] = jnp.sum(parts_ref[...].astype(F32), axis=0)
+    mean_ref[...] = prior_ref[...]
+
+    @pl.when(lax.axis_index("tm") == 0)
+    def _():
+        mean_ref[...] = stepped(prior_ref[...], drive_ref, first_ref, second_ref, third_ref, fourth_ref)
+
+
+def first_kernel(mean_ref, drive_ref, first_ref, second_ref, third_ref, fourth_ref, value_ref):
+    value_ref[...] = mean_ref[...]
+
+    @pl.when(lax.axis_index("tm") == 1)
+    def _():
+        value_ref[...] = stepped(mean_ref[...], drive_ref, first_ref, second_ref, third_ref, fourth_ref)
+
+
+def four_kernel(count, have, after_ref, two_ref, threes_ref, third_ref, fourth_ref, four_ref, slab3_ref, slab4_ref, three_ref):
     width = slab3_ref.shape[0]
     place = lax.axis_index("state")
-    thirds = fetched(count, place, missing, 0, third_ref, sems, 0)
-    fourths = fetched(count, place, missing, 1, fourth_ref, sems, len(missing))
-    parts = []
     for r in range(count):
-        at = 2 * len(missing) + r
-        parts.append(pltpu.make_async_copy(refs[r].at[pl.ds(2 * width, 16), :], parts_ref.at[r], sems.at[at]))
-        parts[r].start()
-    for copy in thirds:
-        copy.wait()
-    for r, _ in missing:
-        at = pl.ds(pl.multiple_of(lax.rem(place + r, count) * width, width), width)
-        three_ref[at, :] = jnp.dot(third_ref[at, :], two_ref[...], preferred_element_type=F32).astype(BF16)
-    for copy in fourths:
-        copy.wait()
-    matmul(fourth_ref, three_ref, four_ref)
+        if r not in have:
+            at = pl.ds(pl.multiple_of(lax.rem(place + r, count) * width, width), width)
+            three_ref[at, :] = jnp.dot(third_ref[at, :], two_ref[...], preferred_element_type=F32).astype(BF16)
     mine = pl.ds(pl.multiple_of(place * width, width), width)
     slab3_ref[...] = three_ref[mine, :]
-    slab4_ref[...] = four_ref[mine, :]
-    for copy in parts:
-        copy.wait()
-    drive_ref[...] = jnp.sum(parts_ref[...].astype(F32), axis=0)
-
-
-def local_kernel(drive_ref, second_ref, third_ref, fourth_ref, locals_ref, term_ref):
-    local = joined(drive_ref[0:3, :])
-    locals_ref[0:1, :] = local
-    for j, map_ref in enumerate((second_ref, third_ref, fourth_ref)):
-        local = times_t(local, map_ref[...]) + joined(drive_ref[3 * j + 3:3 * j + 6, :])
-        locals_ref[j + 1:j + 2, :] = local
-    term_ref[...] = split_rows(local)
+
+    @pl.when(chip_here() == 0)
+    def _():
+        slab4_ref[...] = jnp.dot(fourth_ref[mine, :], three_ref[...], preferred_element_type=F32).astype(BF16)
+
+    @pl.when(chip_here() != 0)
+    def _():
+        matmul(fourth_ref, three_ref, four_ref)
+        slab4_ref[...] = four_ref[mine, :]
+
+
+def local_kernel(late, drive_ref, after_ref, second_ref, third_ref, fourth_ref, locals_ref, term_ref):
+    @pl.when((chip_here() == 0) == late)
+    def _():
+        local = joined(drive_ref[0:3, :])
+        locals_ref[0:1, :] = local
+        for j, map_ref in enumerate((second_ref, third_ref, fourth_ref)):
+            local = times_t(local, map_ref[...]) + joined(drive_ref[3 * j + 3:3 * j + 6, :])
+            locals_ref[j + 1:j + 2, :] = local
+        term_ref[...] = split_rows(local)
 
 
 DIRECT = 2
 
 
-def pair_kernel(half, own_ref, own_term_ref, other_ref, other_term_ref, turned_ref):
-    rows = own_ref.shape[0] // 2
-    at = slice(half * rows, (half + 1) * rows)
+def pair_kernel(own_ref, own_term_ref, other_ref, other_term_ref, turned_ref):
+    size = own_ref.shape[0]
 
     @pl.when(jnp.logical_and(core_here() != 0, chip_here() >= DIRECT))
     def _():
-        for i in range(2):
-            out = jnp.dot(own_ref[i * rows:(i + 1) * rows, :], other_ref[:, at], preferred_element_type=F32)
-            turned_ref[:rows, i * rows:(i + 1) * rows] = out.T.astype(BF16)
-        if half == 1:
-            term = times_t(joined(other_term_ref[...]), own_ref[...]) + joined(own_term_ref[...])
-            turned_ref[rows:, :] = split_rows(term)
-
-
-def applied(x, turned0_ref, turned1_ref):
-    rows = turned0_ref.shape[0]
-    return times(x, turned0_ref[...], turned1_ref[:rows, :]) + joined(turned1_ref[rows:, :])
+        def block(i, carry):
+            at = pl.ds(pl.multiple_of(i * ROWS, ROWS), ROWS)
+            out = jnp.dot(own_ref[at, :], other_ref[...], preferred_element_type=F32)
+            turned_ref[:size, at] = out.T.astype(BF16)
+            return carry
+
+        lax.fori_loop(0, size // ROWS, block, 0)
+        term = times_t(joined(other_term_ref[...]), own_ref[...]) + joined(own_term_ref[...])
+        turned_ref[size:, :] = split_rows(term)
+
+
+def applied(x, turned_ref):
+    size = x.shape[1]
+    return times(x, turned_ref[:size, :]) + joined(turned_ref[size:, :])
 
 
 def direct_kernel(turn, begin_ref, came_ref, own_ref, own_term_ref, other_ref, other_term_ref, held_ref, value_ref):
@@ -216,14 +247,14 @@
         value_ref[...] = times_t(between, own_ref[...]) + joined(own_term_ref[...])
 
 
-def hop_kernel(turn, begin_ref, came_ref, turned0_ref, turned1_ref, held_ref, value_ref):
+def hop_kernel(turn, begin_ref, came_ref, turned_ref, held_ref, value_ref):
     here = lax.axis_index("tm") == 2 * turn + 1
 
     @pl.when(here)
     def _():
         begin = came_ref[...]
         held_ref[...] = begin
-        value_ref[...] = applied(begin, turned0_ref, turned1_ref)
+        value_ref[...] = applied(begin, turned_ref)
 
     @pl.when(jnp.logical_not(here))
     def _():
@@ -231,30 +262,29 @@
         value_ref[...] = begin_ref[...]
 
 
-def double_kernel(half, firsts, came_ref, turned0_ref, turned1_ref, double_ref):
-    rows = turned0_ref.shape[0]
+def double_kernel(firsts, came_ref, turned_ref, double_ref):
+    size = turned_ref.shape[1]
     chip = chip_here()
 
     @pl.when((core_here() != 0) & (chip > firsts) & (lax.rem(chip, 2) == 1) & (chip < 2 * firsts - 1))
     def _():
-        double_ref[:rows, :] = product(came_ref[:rows, :], turned0_ref[...], turned1_ref[:rows, :]).astype(BF16)
-        if half == 1:
-            double_ref[rows:, :] = split_rows(applied(joined(came_ref[rows:, :]), turned0_ref, turned1_ref))
-
-
-def far_kernel(chip, came_ref, before_ref, double0_ref, double1_ref, value_ref):
+        matmul(came_ref.at[:size, :], turned_ref.at[:size, :], double_ref)
+        double_ref[size:, :] = split_rows(applied(joined(came_ref[size:, :]), turned_ref))
+
+
+def far_kernel(chip, came_ref, before_ref, double_ref, value_ref):
     here = lax.axis_index("tm") == 2 * chip + 1
 
     @pl.when(here)
     def _():
-        value_ref[...] = applied(came_ref[...], double0_ref, double1_ref)
+        value_ref[...] = applied(came_ref[...], double_ref)
 
     @pl.when(jnp.logical_not(here))
     def _():
         value_ref[...] = before_ref[...]
 
 
-def final_kernel(firsts, held_ref, handed_ref, map0_ref, map1_ref, *refs):
+def final_kernel(firsts, held_ref, handed_ref, map_ref, *refs):
     cames, begin_ref = refs[:-1], refs[-1]
     chip = chip_here()
     handed = jnp.logical_and(chip >= firsts, lax.rem(chip, 2) == 0)
@@ -262,33 +292,35 @@
     for i, came_ref in enumerate(cames):
         @pl.when(lax.axis_index("tm") == 2 * (firsts + 1 + 2 * i) + 1)
         def _():
-            begin_ref[...] = applied(came_ref[...], map0_ref, map1_ref)
-
-
-def ready_kernel(other_ref, other_term_ref, locals_ref, after_ref, *refs):
+            begin_ref[...] = applied(came_ref[...], map_ref)
+
+
+def ready_kernel(other_ref, other_term_ref, locals_ref, lates_ref, after_ref, *refs):
     slabs, (maps_ref, terms_ref) = refs[:-2], refs[-2:]
     width, size = slabs[1].shape
     mine = pl.ds(pl.multiple_of(lax.axis_index("state") * width, width), width)
-
-    @pl.when(core_here() == 0)
+    plain = jnp.logical_or(core_here() == 0, chip_here() == 0)
+    terms_ref[...] = jnp.where(chip_here() == 0, lates_ref[:, mine], locals_ref[:, mine])
+
+    @pl.when(plain)
     def _():
         for j, slab_ref in enumerate(slabs):
             maps_ref[:, j * width:(j + 1) * width] = slab_ref[:width, :].astype(F32).T.astype(BF16)
-            terms_ref[j:j + 1, :] = locals_ref[j:j + 1, mine]
-
-    @pl.when(core_here() != 0)
+
+    @pl.when(jnp.logical_not(plain))
     def _():
         for j, slab_ref in enumerate(slabs):
             at = slice(j * width, (j + 1) * width)
             out = jnp.dot(slab_ref[:width, :], other_ref[...], preferred_element_type=F32)
             maps_ref[:, at] = out.T.astype(BF16)
-            term = times_t(joined(other_term_ref[...]), slab_ref[:width, :])
-            terms_ref[j:j + 1, :] = term + locals_ref[j:j + 1, mine]
-
-
-def out_kernel(begin_ref, got_ref, maps_ref, terms_ref, out_ref):
+            terms_ref[j:j + 1, :] += times_t(joined(other_term_ref[...]), slab_ref[:width, :])
+
+
+def out_kernel(prior_ref, mean_ref, begin_ref, got_ref, maps_ref, terms_ref, out_ref):
     steps, width = out_ref.shape
+    first = jnp.where(core_here() == 0, prior_ref[...], mean_ref[...])
     begin = jnp.where(core_here() == 0, got_ref[...], begin_ref[...])
+    begin = jnp.where(chip_here() == 0, first, begin)
     row = times(begin, maps_ref[...])
     for j in range(steps):
         out_ref[j:j + 1, :] = row[:, j * width:(j + 1) * width] + terms_ref[j:j + 1, :]
@@ -359,44 +391,54 @@
         [transition[:half].reshape(half * width, size), packed], "state",
         lambda r, i, found: (packed,) if (r, i) == (2, 0) else (),
     )
-    two, slab2, second = call(
-        functools.partial(two_kernel, count), (matrix, slab, matrix), [A] * count,
-        [whole, pltpu.SemaphoreType.DMA((2 * count,))], flops=2 * size ** 3, moved=6 * size ** 2,
+    two, slab2, first, second = call(
+        functools.partial(two_kernel, count), (matrix, slab, matrix, matrix), [A] * count,
+        [pltpu.SemaphoreType.DMA((2 * count,))], flops=2 * size ** 3, moved=6 * size ** 2,
     )(*early)
     have = [r for r in range(count) if r not in (count // 2, count // 2 + 1)]
     three, third, fourth = call(
         functools.partial(three_kernel, count, have), (matrix, matrix, matrix), [V] + [A] * len(have),
         [pltpu.SemaphoreType.DMA((2 * len(have),))], flops=2 * size ** 3, moved=6 * size ** 2,
     )(two, *[late[r] for r in have])
-    own, slab3, slab4, _, third, fourth, drive = call(
-        functools.partial(four_kernel, count, have),
-        (matrix, slab, slab, matrix, matrix, matrix, jax.ShapeDtypeStruct((16, size), F32)),
-        [V] * 4 + [A] * count,
+    start = prior.reshape(1, size)
+    third, fourth, drive, mean = call(
+        functools.partial(gather_kernel, count, have),
+        (matrix, matrix, jax.ShapeDtypeStruct((16, size), F32), row),
+        [V] * 5 + [A] * count,
         [pltpu.VMEM((count, 16, size), BF16), pltpu.SemaphoreType.DMA((3 * count,))],
-        flops=2 * size ** 3, moved=6 * size ** 2, aliases={1: 3, 2: 4, 3: 5},
-    )(two, three, third, fourth, *late)
+        flops=128 * size ** 2, moved=2 * size ** 2, aliases={3: 0, 4: 1},
+    )(start, first, second, third, fourth, *late)
     pairs = [(i, i + 1) for i in range(0, blocks_of_time, 2)]
-    other = lax.ppermute(own, "tm", pairs)
-    locals_, own_term = call(
-        local_kernel, (steps, rows), [V] * 4, flops=96 * size ** 2, moved=6 * size ** 2
-    )(drive, second, third, fourth)
-    other_term = lax.ppermute(own_term, "tm", pairs)
+    mean = lax.ppermute(mean, "tm", pairs[:1])
+    value = call(first_kernel, row, [V] * 6, flops=128 * size ** 2, moved=8 * size ** 2)(
+        mean, drive, first, second, third, fourth
+    )
+    came = lax.ppermute(value, "tm", [(1, 3)])
+    own, slab3, slab4, _ = call(
+        functools.partial(four_kernel, count, have), (matrix, slab, slab, matrix), [V] * 5,
+        flops=2 * size ** 3, moved=6 * size ** 2, aliases={2: 3},
+    )(value, two, three, third, fourth)
+    other = lax.ppermute(own, "tm", pairs[1:])
+
+    def locals_of(is_late, needed):
+        return call(
+            functools.partial(local_kernel, is_late), (steps, rows), [V] * 5, flops=96 * size ** 2, moved=6 * size ** 2
+        )(drive, needed, second, third, fourth)
+
+    locals_, own_term = locals_of(False, value)
+    other_term = lax.ppermute(own_term, "tm", pairs[1:])
 
     chips = blocks_of_time // 2
     firsts = chips // 2
     part = jax.ShapeDtypeStruct((size // 2, size), BF16)
-    longer = jax.ShapeDtypeStruct((size // 2 + 16, size), BF16)
+    longer = jax.ShapeDtypeStruct((size + 16, size), BF16)
     blocks_here = (own, own_term, other, other_term)
     onward = [(2 * c + 1, 2 * c + 3) for c in range(firsts, chips, 2)]
-    half_cost = dict(flops=size ** 3, moved=6 * size ** 2)
-    turned0 = call(functools.partial(pair_kernel, 0), part, [V] * 4, **half_cost)(*blocks_here)
-    before0 = lax.ppermute(turned0, "tm", onward)
-    turned1 = call(functools.partial(pair_kernel, 1), longer, [V] * 4, **half_cost)(*blocks_here)
-    before1 = lax.ppermute(turned1, "tm", onward)
-
-    begin = after(prior.reshape(1, size), turned1)
-    came = begin
-    for turn in range(firsts):
+    turned = call(pair_kernel, longer, [V] * 4, flops=2 * size ** 3, moved=6 * size ** 2)(*blocks_here)
+    before = lax.ppermute(turned, "tm", onward)
+
+    begin = after(start, turned)
+    for turn in range(1, firsts):
         if turn < DIRECT:
             begin, value = call(
                 functools.partial(direct_kernel, turn), (row, row), [V] * 6,
@@ -404,36 +446,38 @@
             )(begin, came, *blocks_here)
         else:
             begin, value = call(
-                functools.partial(hop_kernel, turn), (row, row), [V] * 4,
+                functools.partial(hop_kernel, turn), (row, row), [V] * 3,
                 flops=32 * size ** 2, moved=2 * size ** 2,
-            )(begin, came, turned0, turned1)
+            )(begin, came, turned)
         came = lax.ppermute(value, "tm", [(2 * turn + 1, 2 * turn + (3 if turn + 1 < firsts else 5))])
         if turn == 3:
+            lates, _ = locals_of(True, value)
             maps, terms = call(
                 ready_kernel,
                 (jax.ShapeDtypeStruct((size, steps_here * width), BF16), jax.ShapeDtypeStruct((steps_here, width), F32)),
-                [V] * 8, flops=size ** 3, moved=4 * size ** 2,
-            )(other, other_term, locals_, value, early[0], slab2, slab3, slab4)
+                [V] * 9, flops=size ** 3, moved=4 * size ** 2,
+            )(other, other_term, locals_, lates, value, early[0], slab2, slab3, slab4)
         if turn == 4:
             came = after(came, maps)
-    double0 = call(functools.partial(double_kernel, 0, firsts), part, [V] * 3, **half_cost)(before0, turned0, turned1)
-    double1 = call(functools.partial(double_kernel, 1, firsts), longer, [V] * 3, **half_cost)(before1, turned0, turned1)
+    double = call(
+        functools.partial(double_kernel, firsts), longer, [V, V], flops=2 * size ** 3, moved=6 * size ** 2
+    )(before, turned)
     cames = [came]
     for chip in range(firsts + 1, chips - 1, 2):
         value = call(
-            functools.partial(far_kernel, chip), row, [V] * 4, flops=32 * size ** 2, moved=2 * size ** 2
-        )(came, value, double0, double1)
+            functools.partial(far_kernel, chip), row, [V] * 3, flops=32 * size ** 2, moved=2 * size ** 2
+        )(came, value, double)
         came = lax.ppermute(value, "tm", [(2 * chip + 1, 2 * chip + 5)])
         cames.append(came)
     handed = lax.ppermute(value, "tm", [(2 * c - 1, 2 * c + 1) for c in range(firsts, chips, 2)])
     begin = call(
-        functools.partial(final_kernel, firsts), row, [V] * (4 + len(cames)), flops=32 * size ** 2, moved=2 * size ** 2
-    )(begin, handed, before0, before1, *cames)
+        functools.partial(final_kernel, firsts), row, [V] * (3 + len(cames)), flops=32 * size ** 2, moved=2 * size ** 2
+    )(begin, handed, before, *cames)
     got = lax.ppermute(begin, "tm", [(b, a) for a, b in pairs])
     return call(
-        out_kernel, jax.ShapeDtypeStruct((steps_here, width), F32), [V] * 4,
+        out_kernel, jax.ShapeDtypeStruct((steps_here, width), F32), [V] * 6,
         flops=16 * size ** 2, moved=size ** 2,
-    )(begin, got, maps, terms)
+    )(start, mean, begin, got, maps, terms)
 
 
 def solution(mesh):

time: 150 us -> 154 us (1.027)
  waiting for transfers between devices: 93.8 us -> 97.5 us
    ppermute x1, waiting for transfers between devices: 35.1 us -> 38.8 us  [shards(): got = lax.ppermute(begin, 'tm', [(b, a) for a, b in pairs])]
    pallas_call x17 -> x18, Pallas kernels: 5.93 us -> 7.21 us  [the longest x1 3.04 us: shards(): call(functools.partial(two_kernel, count), (matrix, slab, matrix, matrix)...]
    ppermute x8 -> x7, starting transfers between devices: 5.29 us -> 4.62 us  [shards(): lax.ppermute(value, 'tm', [(2 * turn + 1, 2 * turn + (3 if turn + 1 < fir...]
    ppermute x4 -> x5, starting transfers between devices: 4.29 us -> 4.83 us  [the longest x1 1.42 us: shards(): other = lax.ppermute(own, 'tm', pairs[1:])]
where the time goes in v10:
time: 154 us; the launch traced here: 153 us
  waiting for transfers between devices  97.5 us (63%)
  starting transfers between devices  39.1 us (25%)
  Pallas kernels  14.9 us (10%)
    ppermute x1, waiting for transfers between devices, shards(): got = lax.ppermute(begin, 'tm', [(b, a) for a, b in pairs])  38.8 us
    ppermute x7, waiting for transfers between devices, ring_rounds(): pieces[count - r] = lax.ppermute(left, axis, forward)  35.7 us
    ppermute x7, waiting for transfers between devices, ring_rounds(): pieces[r] = lax.ppermute(right, axis, backward)  22.1 us
    ppermute x7, starting transfers between devices, ring_rounds(): pieces[r] = lax.ppermute(right, axis, backward)  20.3 us
    ppermute x7, starting transfers between devices, ring_rounds(): pieces[count - r] = lax.ppermute(left, axis, forward)  5.4 us
    ppermute x7, starting transfers between devices, shards(): lax.ppermute(value, 'tm', [(2 * turn + 1, 2 * turn + (3 if turn + 1 < fir...  4.62 us
    pallas_call x1, Pallas kernels, shards(): call(functools.partial(four_kernel, count, have), (matrix, slab, slab, ma...  3.28 us
  transfers between devices with their start and end apart: 31, of which 12 were waited for; matrix products, arithmetic and copies ran while one was open for 0% of the time, Pallas kernels for 6%

profile of v10, /device:TPU:30, one launch (start us, length us, event | category | flops | bytes accessed | tf_op | source)
XLA Modules:
  0.0 153.4 jit_solution(13390354989106587046)
XLA Ops:
  0.0 1.4 fusion
  1.5 2.0 %collective-permute-start.1 = (bf16[256,1024]{1,0:T(8,128)(2,1)S(1)}, bf16[256,1024]{1,0:T(8,128)(2,1)S(1)}, u32[]{:S(2)}, u32[]{:S(2)}) collective-permute-start(bf16[256,1024]{1,0:T(8,128)(2,1)S(1)} %bitcast.2), channel_id=1, source_target_pairs={{0,1},{1,2},{2,3},{3,4},{4,5},{5,6},{6,7},{7,0},{8,9},{9,10},{10,1... | collective-permute-start | bytes 1572872 | tf_op jit(solution)/shard_map/ppermute | solution.py:359
  3.4 4.0 %collective-permute-start = (bf16[256,1024]{1,0:T(8,128)(2,1)S(1)}, bf16[256,1024]{1,0:T(8,128)(2,1)S(1)}, u32[]{:S(2)}, u32[]{:S(2)}) collective-permute-start(bf16[256,1024]{1,0:T(8,128)(2,1)S(1)} %bitcast.3), channel_id=1, source_target_pairs={{1,0},{2,1},{3,2},{4,3},{5,4},{6,5},{7,6},{0,7},{9,8},{10,9},{11,1... | collective-permute-start | bytes 1572872 | tf_op jit(solution)/shard_map/ppermute | solution.py:361
  7.5 1.6 %shard_map.73.refs_0_ = bf16[272,1024]{1,0:T(8,128)(2,1)S(1)} custom-call(s32[4,32]{1,0:T(4,128)S(1)} %copy-done.2, s32[4,32]{1,0:T(4,128)S(1)} %copy-done.3, bf16[4,4096]{1,0:T(4,128)(2,1)S(1)} %multiply_convert_fusion.values_ref, bf16[4,32,64,64]{3,2,1,0:T(8,128)(2,1)S(1)} %copy-done, bf16[2,128,1024]{2,1,0:T(8,128)(2,1)S(1)} %get-tuple-element.79.maps_ref), custom_call_target="tpu_custom_call" | custom-call | flops 10000000 | bytes 2097152 | tf_op jit(solution)/shard_map/pallas_call | solution.py:381
  9.1 2.0 %collective-permute-start.7 = (bf16[272,1024]{1,0:T(8,128)(2,1)S(1)}, bf16[272,1024]{1,0:T(8,128)(2,1)S(1)}, u32[]{:S(2)}, u32[]{:S(2)}) collective-permute-start(bf16[272,1024]{1,0:T(8,128)(2,1)S(1)} %shard_map.73.refs_0_), channel_id=1, source_target_pairs={{1,0},{2,1},{3,2},{4,3},{5,4},{6,5},{7,6},{0,7},{9,8},{10,9},{11,1... | collective-permute-start | bytes 1671176 | tf_op jit(solution)/shard_map/ppermute | solution.py:361
  11.1 8.2 %collective-permute-done.1.refs_7_ = bf16[256,1024]{1,0:T(8,128)(2,1)S(1)} collective-permute-done((bf16[256,1024]{1,0:T(8,128)(2,1)S(1)}, bf16[256,1024]{1,0:T(8,128)(2,1)S(1)}, u32[]{:S(2)}, u32[]{:S(2)}) %collective-permute-start.1) | collective-permute-done | bytes 524320 | tf_op jit(solution)/shard_map/ppermute | solution.py:359
  20.2 3.0 %collective-permute-start.10 = (bf16[272,1024]{1,0:T(8,128)(2,1)S(1)}, bf16[272,1024]{1,0:T(8,128)(2,1)S(1)}, u32[]{:S(2)}, u32[]{:S(2)}) collective-permute-start(bf16[272,1024]{1,0:T(8,128)(2,1)S(1)} %shard_map.73.refs_0_), channel_id=1, source_target_pairs={{0,1},{1,2},{2,3},{3,4},{4,5},{5,6},{6,7},{7,0},{8,9},{9,10},{10,1... | collective-permute-start | bytes 1671176 | tf_op jit(solution)/shard_map/ppermute | solution.py:359
  23.2 7.4 %collective-permute-done.7.refs_1_ = bf16[272,1024]{1,0:T(8,128)(2,1)S(1)} collective-permute-done((bf16[272,1024]{1,0:T(8,128)(2,1)S(1)}, bf16[272,1024]{1,0:T(8,128)(2,1)S(1)}, u32[]{:S(2)}, u32[]{:S(2)}) %collective-permute-start.7) | collective-permute-done | bytes 557088 | tf_op jit(solution)/shard_map/ppermute | solution.py:361
  30.6 3.7 %collective-permute-start.8 = (bf16[272,1024]{1,0:T(8,128)(2,1)S(1)}, bf16[272,1024]{1,0:T(8,128)(2,1)S(1)}, u32[]{:S(2)}, u32[]{:S(2)}) collective-permute-start(bf16[272,1024]{1,0:T(8,128)(2,1)S(1)} %collective-permute-done.7.refs_1_), channel_id=1, source_target_pairs={{1,0},{2,1},{3,2},{4,3},{5,4},{6,5},{7,6},{0,7},{9,8},{10,9},{11,1... | collective-permute-start | bytes 1671176 | tf_op jit(solution)/shard_map/ppermute | solution.py:361
  34.7 1.6 %collective-permute-done.4.refs_6_ = bf16[256,1024]{1,0:T(8,128)(2,1)S(1)} collective-permute-done((bf16[256,1024]{1,0:T(8,128)(2,1)S(1)}, bf16[256,1024]{1,0:T(8,128)(2,1)S(1)}, u32[]{:S(2)}, u32[]{:S(2)}) %collective-permute-start.4) | collective-permute-done | bytes 524320 | tf_op jit(solution)/shard_map/ppermute | solution.py:359
  36.3 11.9 %collective-permute-done.10.refs_5_.refs_7_ = bf16[272,1024]{1,0:T(8,128)(2,1)S(1)} collective-permute-done((bf16[272,1024]{1,0:T(8,128)(2,1)S(1)}, bf16[272,1024]{1,0:T(8,128)(2,1)S(1)}, u32[]{:S(2)}, u32[]{:S(2)}) %collective-permute-start.10) | collective-permute-done | bytes 557088 | tf_op jit(solution)/shard_map/ppermute | solution.py:359
  48.3 3.2 %collective-permute-start.9 = (bf16[272,1024]{1,0:T(8,128)(2,1)S(1)}, bf16[272,1024]{1,0:T(8,128)(2,1)S(1)}, u32[]{:S(2)}, u32[]{:S(2)}) collective-permute-start(bf16[272,1024]{1,0:T(8,128)(2,1)S(1)} %collective-permute-done.8.refs_2_), channel_id=1, source_target_pairs={{1,0},{2,1},{3,2},{4,3},{5,4},{6,5},{7,6},{0,7},{9,8},{10,9},{11,1... | collective-permute-start | bytes 1671176 | tf_op jit(solution)/shard_map/ppermute | solution.py:361
  51.5 7.1 %collective-permute-done.2.refs_2_ = bf16[256,1024]{1,0:T(8,128)(2,1)S(1)} collective-permute-done((bf16[256,1024]{1,0:T(8,128)(2,1)S(1)}, bf16[256,1024]{1,0:T(8,128)(2,1)S(1)}, u32[]{:S(2)}, u32[]{:S(2)}) %collective-permute-start.2) | collective-permute-done | bytes 524320 | tf_op jit(solution)/shard_map/ppermute | solution.py:361
  58.6 3.7 %collective-permute-start.3 = (bf16[256,1024]{1,0:T(8,128)(2,1)S(1)}, bf16[256,1024]{1,0:T(8,128)(2,1)S(1)}, u32[]{:S(2)}, u32[]{:S(2)}) collective-permute-start(bf16[256,1024]{1,0:T(8,128)(2,1)S(1)} %collective-permute-done.2.refs_2_), channel_id=1, source_target_pairs={{1,0},{2,1},{3,2},{4,3},{5,4},{6,5},{7,6},{0,7},{9,8},{10,9},{11,1... | collective-permute-start | bytes 1572872 | tf_op jit(solution)/shard_map/ppermute | solution.py:361
  62.3 9.1 %collective-permute-done.11.refs_4_.refs_6_ = bf16[272,1024]{1,0:T(8,128)(2,1)S(1)} collective-permute-done((bf16[272,1024]{1,0:T(8,128)(2,1)S(1)}, bf16[272,1024]{1,0:T(8,128)(2,1)S(1)}, u32[]{:S(2)}, u32[]{:S(2)}) %collective-permute-start.11) | collective-permute-done | bytes 557088 | tf_op jit(solution)/shard_map/ppermute | solution.py:359
  71.5 3.2 %collective-permute-start.12 = (bf16[272,1024]{1,0:T(8,128)(2,1)S(1)}, bf16[272,1024]{1,0:T(8,128)(2,1)S(1)}, u32[]{:S(2)}, u32[]{:S(2)}) collective-permute-start(bf16[272,1024]{1,0:T(8,128)(2,1)S(1)} %collective-permute-done.9.refs_3_), channel_id=1, source_target_pairs={{1,0},{2,1},{3,2},{4,3},{5,4},{6,5},{7,6},{0,7},{9,8},{10,9},{11,1... | collective-permute-start | bytes 1671176 | tf_op jit(solution)/shard_map/ppermute | solution.py:361
  74.7 7.1 %collective-permute-done.3.refs_3_ = bf16[256,1024]{1,0:T(8,128)(2,1)S(1)} collective-permute-done((bf16[256,1024]{1,0:T(8,128)(2,1)S(1)}, bf16[256,1024]{1,0:T(8,128)(2,1)S(1)}, u32[]{:S(2)}, u32[]{:S(2)}) %collective-permute-start.3) | collective-permute-done | bytes 524320 | tf_op jit(solution)/shard_map/ppermute | solution.py:361
  81.8 0.9 collective-permute-done.6.refs_4_
  82.7 3.0 %shard_map.74 = (bf16[1024,1024]{1,0:T(8,128)(2,1)S(1)}, bf16[128,1024]{1,0:T(8,128)(2,1)S(1)}, bf16[1024,1024]{1,0:T(8,128)(2,1)S(1)}, bf16[1024,1024]{1,0:T(8,128)(2,1)S(1)}) custom-call(bf16[256,1024]{1,0:T(8,128)(2,1)S(1)} %bitcast.4, bf16[256,1024]{1,0:T(8,128)(2,1)S(1)} %collective-permute-done.refs_1_, ...), custom_call_target="tpu_custom_call" | custom-call | flops 2147483648 | bytes 6291456 | tf_op jit(solution)/shard_map/pallas_call | solution.py:394
  85.7 2.2 %shard_map.75 = (bf16[1024,1024]{1,0:T(8,128)(2,1)S(1)}, bf16[1024,1024]{1,0:T(8,128)(2,1)S(1)}, bf16[1024,1024]{1,0:T(8,128)(2,1)S(1)}) custom-call(bf16[1024,1024]{1,0:T(8,128)(2,1)S(1)} %get-tuple-element.46.two_ref, bf16[272,1024]{1,0:T(8,128)(2,1)S(1)} %shard_map.73.refs_0_, bf16[272,1024]{1,0:T(8,128)(2,1)S(1)} %collective-permute-done.7.refs_1_, ...), custom_call_target="tpu_custom_call" | custom-call | flops 2147483648 | bytes 6291456 | tf_op jit(solution)/shard_map/pallas_call | solution.py:399
  88.0 4.0 %collective-permute-done.13.refs_5_ = bf16[272,1024]{1,0:T(8,128)(2,1)S(1)} collective-permute-done((bf16[272,1024]{1,0:T(8,128)(2,1)S(1)}, bf16[272,1024]{1,0:T(8,128)(2,1)S(1)}, u32[]{:S(2)}, u32[]{:S(2)}) %collective-permute-start.13) | collective-permute-done | bytes 557088 | tf_op jit(solution)/shard_map/ppermute | solution.py:359
  91.9 0.7 shard_map.76
  92.6 0.7 collective-permute-start.14
  93.3 3.3 %shard_map.78 = (bf16[1024,1024]{1,0:T(8,128)(2,1)S(1)}, bf16[128,1024]{1,0:T(8,128)(2,1)S(1)}, bf16[128,1024]{1,0:T(8,128)(2,1)S(1)}, bf16[1024,1024]{1,0:T(8,128)(2,1)S(1)}) custom-call(f32[1,1024]{1,0:T(1,128)S(1)} %shard_map.77.after_ref, bf16[1024,1024]{1,0:T(8,128)(2,1)S(1)} %get-tuple-element.46.two_ref, ...), custom_call_target="tpu_custom_call", output_to_operand_aliasing={{3}: (2, {})} | custom-call | flops 2147483648 | bytes 6291456 | tf_op jit(solution)/shard_map/pallas_call | solution.py:417
  96.6 1.4 collective-permute-start.15
  98.0 1.8 %shard_map.79 = (f32[4,1024]{1,0:T(4,128)S(1)}, bf16[16,1024]{1,0:T(8,128)(2,1)S(1)}) custom-call(f32[16,1024]{1,0:T(8,128)S(1)} %get-tuple-element.50.drive_ref, f32[1,1024]{1,0:T(1,128)S(1)} %shard_map.77.after_ref, bf16[1024,1024]{1,0:T(8,128)(2,1)S(1)} %get-tuple-element.45.second_ref, bf16[1024,1024]{1,0:T(8,128)(2,1)S(1)} %get-tuple-element.51.third_ref, ...), custom_call_target="tpu_custom_call" | custom-call | flops 100663296 | bytes 6291456 | tf_op jit(solution)/shard_map/pallas_call | solution.py:424
  99.8 1.3 collective-permute-start.16
  101.1 0.8 collective-permute-done.16.other_term_ref
  102.0 0.8 collective-permute-start.25
  112.5 1.3 collective-permute-start.30
  113.8 38.8 %collective-permute-done.30.got_ref = f32[1,1024]{1,0:T(1,128)S(1)} collective-permute-done((f32[1,1024]{1,0:T(1,128)S(1)}, f32[1,1024]{1,0:T(1,128)S(1)}, u32[]{:S(2)}, u32[]{:S(2)}) %collective-permute-start.30) | collective-permute-done | bytes 4128 | tf_op jit(solution)/shard_map/ppermute | solution.py:476
  152.6 0.8 shard_map.95
  (67 shorter events, 10.8 us)
Async XLA Ops:
  0.0 7.5 %copy-start.2 = (s32[4,32]{1,0:T(4,128)S(1)}, s32[4,32]{1,0:T(4,128)}, u32[]{:S(2)}) copy-start(s32[4,32]{1,0:T(4,128)} %rows_ref.1) | copy-start | bytes 1540
  1.5 17.9 %collective-permute-start.1 = (bf16[256,1024]{1,0:T(8,128)(2,1)S(1)}, bf16[256,1024]{1,0:T(8,128)(2,1)S(1)}, u32[]{:S(2)}, u32[]{:S(2)}) collective-permute-start(bf16[256,1024]{1,0:T(8,128)(2,1)S(1)} %bitcast.2), channel_id=1, source_target_pairs={{0,1},{1,2},{2,3},{3,4},{4,5},{5,6},{6,7},{7,0},{8,9},{9,10},{10,1... | collective-permute-start | bytes 1572872 | tf_op jit(solution)/shard_map/ppermute | solution.py:359
  3.4 16.4 %collective-permute-start = (bf16[256,1024]{1,0:T(8,128)(2,1)S(1)}, bf16[256,1024]{1,0:T(8,128)(2,1)S(1)}, u32[]{:S(2)}, u32[]{:S(2)}) collective-permute-start(bf16[256,1024]{1,0:T(8,128)(2,1)S(1)} %bitcast.3), channel_id=1, source_target_pairs={{1,0},{2,1},{3,2},{4,3},{5,4},{6,5},{7,6},{0,7},{9,8},{10,9},{11,1... | collective-permute-start | bytes 1572872 | tf_op jit(solution)/shard_map/ppermute | solution.py:361
  9.1 21.5 %collective-permute-start.7 = (bf16[272,1024]{1,0:T(8,128)(2,1)S(1)}, bf16[272,1024]{1,0:T(8,128)(2,1)S(1)}, u32[]{:S(2)}, u32[]{:S(2)}) collective-permute-start(bf16[272,1024]{1,0:T(8,128)(2,1)S(1)} %shard_map.73.refs_0_), channel_id=1, source_target_pairs={{1,0},{2,1},{3,2},{4,3},{5,4},{6,5},{7,6},{0,7},{9,8},{10,9},{11,1... | collective-permute-start | bytes 1671176 | tf_op jit(solution)/shard_map/ppermute | solution.py:361
  19.8 16.5 %collective-permute-start.4 = (bf16[256,1024]{1,0:T(8,128)(2,1)S(1)}, bf16[256,1024]{1,0:T(8,128)(2,1)S(1)}, u32[]{:S(2)}, u32[]{:S(2)}) collective-permute-start(bf16[256,1024]{1,0:T(8,128)(2,1)S(1)} %collective-permute-done.1.refs_7_), channel_id=1, source_target_pairs={{0,1},{1,2},{2,3},{3,4},{4,5},{5,6},{6,7},{7,0},{8,9},{9,10},{10,1... | collective-permute-start | bytes 1572872 | tf_op jit(solution)/shard_map/ppermute | solution.py:359
  20.2 28.1 %collective-permute-start.10 = (bf16[272,1024]{1,0:T(8,128)(2,1)S(1)}, bf16[272,1024]{1,0:T(8,128)(2,1)S(1)}, u32[]{:S(2)}, u32[]{:S(2)}) collective-permute-start(bf16[272,1024]{1,0:T(8,128)(2,1)S(1)} %shard_map.73.refs_0_), channel_id=1, source_target_pairs={{0,1},{1,2},{2,3},{3,4},{4,5},{5,6},{6,7},{7,0},{8,9},{9,10},{10,1... | collective-permute-start | bytes 1671176 | tf_op jit(solution)/shard_map/ppermute | solution.py:359
  30.6 17.7 %collective-permute-start.8 = (bf16[272,1024]{1,0:T(8,128)(2,1)S(1)}, bf16[272,1024]{1,0:T(8,128)(2,1)S(1)}, u32[]{:S(2)}, u32[]{:S(2)}) collective-permute-start(bf16[272,1024]{1,0:T(8,128)(2,1)S(1)} %collective-permute-done.7.refs_1_), channel_id=1, source_target_pairs={{1,0},{2,1},{3,2},{4,3},{5,4},{6,5},{7,6},{0,7},{9,8},{10,9},{11,1... | collective-permute-start | bytes 1671176 | tf_op jit(solution)/shard_map/ppermute | solution.py:361
  34.3 24.3 %collective-permute-start.2 = (bf16[256,1024]{1,0:T(8,128)(2,1)S(1)}, bf16[256,1024]{1,0:T(8,128)(2,1)S(1)}, u32[]{:S(2)}, u32[]{:S(2)}) collective-permute-start(bf16[256,1024]{1,0:T(8,128)(2,1)S(1)} %collective-permute-done.refs_1_), channel_id=1, source_target_pairs={{1,0},{2,1},{3,2},{4,3},{5,4},{6,5},{7,6},{0,7},{9,8},{10,9},{11,1... | collective-permute-start | bytes 1572872 | tf_op jit(solution)/shard_map/ppermute | solution.py:361
  36.3 26.0 %collective-permute-start.5 = (bf16[256,1024]{1,0:T(8,128)(2,1)S(1)}, bf16[256,1024]{1,0:T(8,128)(2,1)S(1)}, u32[]{:S(2)}, u32[]{:S(2)}) collective-permute-start(bf16[256,1024]{1,0:T(8,128)(2,1)S(1)} %collective-permute-done.4.refs_6_), channel_id=1, source_target_pairs={{0,1},{1,2},{2,3},{3,4},{4,5},{5,6},{6,7},{7,0},{8,9},{9,10},{10,1... | collective-permute-start | bytes 1572872 | tf_op jit(solution)/shard_map/ppermute | solution.py:359
  48.3 23.2 %collective-permute-start.11 = (bf16[272,1024]{1,0:T(8,128)(2,1)S(1)}, bf16[272,1024]{1,0:T(8,128)(2,1)S(1)}, u32[]{:S(2)}, u32[]{:S(2)}) collective-permute-start(bf16[272,1024]{1,0:T(8,128)(2,1)S(1)} %collective-permute-done.10.refs_5_.refs_7_), channel_id=1, source_target_pairs={{0,1},{1,2},{2,3},{3,4},{4,5},{5,6},{6,7},{7,0},{8,9},{9,10},{10,1... | collective-permute-start | bytes 1671176 | tf_op jit(solution)/shard_map/ppermute | solution.py:359
  48.3 23.2 %collective-permute-start.9 = (bf16[272,1024]{1,0:T(8,128)(2,1)S(1)}, bf16[272,1024]{1,0:T(8,128)(2,1)S(1)}, u32[]{:S(2)}, u32[]{:S(2)}) collective-permute-start(bf16[272,1024]{1,0:T(8,128)(2,1)S(1)} %collective-permute-done.8.refs_2_), channel_id=1, source_target_pairs={{1,0},{2,1},{3,2},{4,3},{5,4},{6,5},{7,6},{0,7},{9,8},{10,9},{11,1... | collective-permute-start | bytes 1671176 | tf_op jit(solution)/shard_map/ppermute | solution.py:361
  58.6 23.2 %collective-permute-start.3 = (bf16[256,1024]{1,0:T(8,128)(2,1)S(1)}, bf16[256,1024]{1,0:T(8,128)(2,1)S(1)}, u32[]{:S(2)}, u32[]{:S(2)}) collective-permute-start(bf16[256,1024]{1,0:T(8,128)(2,1)S(1)} %collective-permute-done.2.refs_2_), channel_id=1, source_target_pairs={{1,0},{2,1},{3,2},{4,3},{5,4},{6,5},{7,6},{0,7},{9,8},{10,9},{11,1... | collective-permute-start | bytes 1572872 | tf_op jit(solution)/shard_map/ppermute | solution.py:361
  62.3 20.4 %collective-permute-start.6 = (bf16[256,1024]{1,0:T(8,128)(2,1)S(1)}, bf16[256,1024]{1,0:T(8,128)(2,1)S(1)}, u32[]{:S(2)}, u32[]{:S(2)}) collective-permute-start(bf16[256,1024]{1,0:T(8,128)(2,1)S(1)} %collective-permute-done.5.refs_5_), channel_id=1, source_target_pairs={{0,1},{1,2},{2,3},{3,4},{4,5},{5,6},{6,7},{7,0},{8,9},{9,10},{10,1... | collective-permute-start | bytes 1572872 | tf_op jit(solution)/shard_map/ppermute | solution.py:359
  71.4 20.5 %collective-permute-start.13 = (bf16[272,1024]{1,0:T(8,128)(2,1)S(1)}, bf16[272,1024]{1,0:T(8,128)(2,1)S(1)}, u32[]{:S(2)}, u32[]{:S(2)}) collective-permute-start(bf16[272,1024]{1,0:T(8,128)(2,1)S(1)} %collective-permute-done.11.refs_4_.refs_6_), channel_id=1, source_target_pairs={{0,1},{1,2},{2,3},{3,4},{4,5},{5,6},{6,7},{7,0},{8,9},{9,10},{10,1... | collective-permute-start | bytes 1671176 | tf_op jit(solution)/shard_map/ppermute | solution.py:359
  71.5 20.5 %collective-permute-start.12 = (bf16[272,1024]{1,0:T(8,128)(2,1)S(1)}, bf16[272,1024]{1,0:T(8,128)(2,1)S(1)}, u32[]{:S(2)}, u32[]{:S(2)}) collective-permute-start(bf16[272,1024]{1,0:T(8,128)(2,1)S(1)} %collective-permute-done.9.refs_3_), channel_id=1, source_target_pairs={{1,0},{2,1},{3,2},{4,3},{5,4},{6,5},{7,6},{0,7},{9,8},{10,9},{11,1... | collective-permute-start | bytes 1671176 | tf_op jit(solution)/shard_map/ppermute | solution.py:361
  92.6 0.7 collective-permute-start.14
  96.6 5.4 %collective-permute-start.15 = (bf16[1024,1024]{1,0:T(8,128)(2,1)S(1)}, bf16[1024,1024]{1,0:T(8,128)(2,1)S(1)}, u32[]{:S(2)}, u32[]{:S(2)}) collective-permute-start(bf16[1024,1024]{1,0:T(8,128)(2,1)S(1)} %get-tuple-element.54.own_ref), channel_id=1, source_target_pairs={{16,24},{32,40},{48,56},{64,72},{80,88},{96,104},{112,120},{128,13... | collective-permute-start | bytes 6291464 | tf_op jit(solution)/shard_map/ppermute | solution.py:421
  99.8 2.1 %collective-permute-start.16 = (bf16[16,1024]{1,0:T(8,128)(2,1)S(1)}, bf16[16,1024]{1,0:T(8,128)(2,1)S(1)}, u32[]{:S(2)}, u32[]{:S(2)}) collective-permute-start(bf16[16,1024]{1,0:T(8,128)(2,1)S(1)} %get-tuple-element.55.own_term_ref), channel_id=1, source_target_pairs={{16,24},{32,40},{48,56},{64,72},{80,88},{96,104},{112,120},{128,13... | collective-permute-start | bytes 98312 | tf_op jit(solution)/shard_map/ppermute | solution.py:429
  102.0 7.6 %collective-permute-start.25 = (bf16[1040,1024]{1,0:T(8,128)(2,1)S(1)}, bf16[1040,1024]{1,0:T(8,128)(2,1)S(1)}, u32[]{:S(2)}, u32[]{:S(2)}) collective-permute-start(bf16[1040,1024]{1,0:T(8,128)(2,1)S(1)} %shard_map.80.turned_ref), channel_id=1, source_target_pairs={{136,152},{168,184},{200,216},{232,248},{137,153},{169,185},{201,2... | collective-permute-start | bytes 6389768 | tf_op jit(solution)/shard_map/ppermute | solution.py:438
  102.8 0.7 collective-permute-start.17
  103.7 0.7 collective-permute-start.18
  104.4 0.7 collective-permute-start.19
  105.1 1.3 collective-permute-start.20
  106.4 1.0 collective-permute-start.21
  107.5 0.7 collective-permute-start.22
  108.2 0.7 collective-permute-start.23
  108.9 0.7 collective-permute-start.24
  109.6 0.7 collective-permute-start.26
  110.3 0.7 collective-permute-start.27
  111.1 1.3 collective-permute-start.29
  111.7 0.7 collective-permute-start.28
  112.5 40.1 %collective-permute-start.30 = (f32[1,1024]{1,0:T(1,128)S(1)}, f32[1,1024]{1,0:T(1,128)S(1)}, u32[]{:S(2)}, u32[]{:S(2)}) collective-permute-start(f32[1,1024]{1,0:T(1,128)S(1)} %shard_map.94.begin_ref), channel_id=1, source_target_pairs={{8,0},{24,16},{40,32},{56,48},{72,64},{88,80},{104,96},{120,112},{... | collective-permute-start | bytes 12296 | tf_op jit(solution)/shard_map/ppermute | solution.py:476
  (5 other events, 36.2 us)

commit v11 on v9

--- a/solution.py
+++ b/solution.py
@@ -106,13 +106,17 @@
         copy.wait()
 
 
-def fetched(count, place, pieces, j, whole_ref, sems, first):
+def rows_of(r, width, count):
+    owner = lax.rem(lax.axis_index("state") + r + core_here() * (count - 2 * r), count)
+    return pl.ds(pl.multiple_of(owner * width, width), width)
+
+
+def fetched(count, pieces, j, whole_ref, sems, first):
     width = whole_ref.shape[0] // count
     copies = []
     for i, (r, piece) in enumerate(pieces):
-        at = pl.multiple_of(lax.rem(place + r, count) * width, width)
         copy = pltpu.make_async_copy(
-            piece.at[pl.ds(j * width, width), :], whole_ref.at[pl.ds(at, width), :], sems.at[first + i]
+            piece.at[pl.ds(j * width, width), :], whole_ref.at[rows_of(r, width, count), :], sems.at[first + i]
         )
         copy.start()
         copies.append(copy)
@@ -123,8 +127,8 @@
     pieces, (two_ref, slab_ref, next_ref, one_ref, sems) = list(enumerate(refs[:count])), refs[count:]
     width = slab_ref.shape[0]
     place = lax.axis_index("state")
-    ones = fetched(count, place, pieces, 0, one_ref, sems, 0)
-    nexts = fetched(count, place, pieces, 1, next_ref, sems, count)
+    ones = fetched(count, pieces, 0, one_ref, sems, 0)
+    nexts = fetched(count, pieces, 1, next_ref, sems, count)
     for copy in ones + nexts:
         copy.wait()
     matmul(next_ref, one_ref, two_ref)
@@ -135,42 +139,38 @@
     pieces = list(zip(have, refs[:len(have)]))
     three_ref, third_ref, fourth_ref, sems = refs[len(have):]
     width = third_ref.shape[0] // count
-    place = lax.axis_index("state")
-    copies = fetched(count, place, pieces, 0, third_ref, sems, 0)
-    copies += fetched(count, place, pieces, 1, fourth_ref, sems, len(have))
+    copies = fetched(count, pieces, 0, third_ref, sems, 0)
+    copies += fetched(count, pieces, 1, fourth_ref, sems, len(have))
     for copy in copies:
         copy.wait()
     for r in have:
-        at = pl.ds(pl.multiple_of(lax.rem(place + r, count) * width, width), width)
+        at = rows_of(r, width, count)
         three_ref[at, :] = jnp.dot(third_ref[at, :], two_ref[...], preferred_element_type=F32).astype(BF16)
 
 
 def four_kernel(count, have, two_ref, threes_ref, thirds_ref, fourths_ref, *refs):
-    missing = [(r, refs[r]) for r in range(count) if r not in have]
+    pieces = refs[:count]
     four_ref, slab3_ref, slab4_ref, three_ref, third_ref, fourth_ref, drive_ref, parts_ref, sems = refs[count:]
     width = slab3_ref.shape[0]
-    place = lax.axis_index("state")
-    thirds = fetched(count, place, missing, 0, third_ref, sems, 0)
-    fourths = fetched(count, place, missing, 1, fourth_ref, sems, len(missing))
     parts = []
+    for i, r in enumerate(have):
+        parts.append(pltpu.make_async_copy(pieces[r].at[pl.ds(2 * width, 16), :], parts_ref.at[i], sems.at[i]))
+        parts[i].start()
+    drive = jnp.zeros(drive_ref.shape, F32)
     for r in range(count):
-        at = 2 * len(missing) + r
-        parts.append(pltpu.make_async_copy(refs[r].at[pl.ds(2 * width, 16), :], parts_ref.at[r], sems.at[at]))
-        parts[r].start()
-    for copy in thirds:
-        copy.wait()
-    for r, _ in missing:
-        at = pl.ds(pl.multiple_of(lax.rem(place + r, count) * width, width), width)
-        three_ref[at, :] = jnp.dot(third_ref[at, :], two_ref[...], preferred_element_type=F32).astype(BF16)
-    for copy in fourths:
-        copy.wait()
+        if r not in have:
+            at = rows_of(r, width, count)
+            third_ref[at, :] = pieces[r][:width, :]
+            fourth_ref[at, :] = pieces[r][width:2 * width, :]
+            three_ref[at, :] = jnp.dot(pieces[r][:width, :], two_ref[...], preferred_element_type=F32).astype(BF16)
+            drive += pieces[r][2 * width:, :].astype(F32)
     matmul(fourth_ref, three_ref, four_ref)
-    mine = pl.ds(pl.multiple_of(place * width, width), width)
+    mine = pl.ds(pl.multiple_of(lax.axis_index("state") * width, width), width)
     slab3_ref[...] = three_ref[mine, :]
     slab4_ref[...] = four_ref[mine, :]
     for copy in parts:
         copy.wait()
-    drive_ref[...] = jnp.sum(parts_ref[...].astype(F32), axis=0)
+    drive_ref[...] = drive + jnp.sum(parts_ref[...].astype(F32), axis=0)
 
 
 def local_kernel(drive_ref, second_ref, third_ref, fourth_ref, locals_ref, term_ref):
@@ -311,10 +311,10 @@
     return lax.optimization_barrier((value, needed))[0]
 
 
-def ring_rounds(parts, axis, needed):
-    count = lax.axis_size(axis)
-    forward = [(i, (i + 1) % count) for i in range(count)]
-    backward = [((i + 1) % count, i) for i in range(count)]
+def ring_rounds(parts, needed):
+    lines, count = lax.axis_size("tm"), lax.axis_size("state")
+    forward = [(b * count + i, b * count + (i + 1 - 2 * (b % 2)) % count) for b in range(lines) for i in range(count)]
+    backward = [(there, here) for here, there in forward]
     half = count // 2
     found = [{0: part} for part in parts]
     for r in range(1, half + 1):
@@ -324,9 +324,9 @@
             if more:
                 left, right = after((left, right), *more)
             if r < half or i % 2 == 0:
-                pieces[count - r] = lax.ppermute(left, axis, forward)
+                pieces[count - r] = lax.ppermute(left, ("tm", "state"), forward)
             if r < half or i % 2 == 1:
-                pieces[r] = lax.ppermute(right, axis, backward)
+                pieces[r] = lax.ppermute(right, ("tm", "state"), backward)
     return [[pieces[r] for r in range(count)] for pieces in found]
 
 
@@ -356,7 +356,7 @@
         flops=10 ** 7, moved=2 ** 21,
     )(block_rows, block_cols, (precisions * observations).astype(BF16), blocks, transition[half:])
     early, late = ring_rounds(
-        [transition[:half].reshape(half * width, size), packed], "state",
+        [transition[:half].reshape(half * width, size), packed],
         lambda r, i, found: (packed,) if (r, i) == (2, 0) else (),
     )
     two, slab2, second = call(
@@ -371,8 +371,8 @@
     own, slab3, slab4, _, third, fourth, drive = call(
         functools.partial(four_kernel, count, have),
         (matrix, slab, slab, matrix, matrix, matrix, jax.ShapeDtypeStruct((16, size), F32)),
-        [V] * 4 + [A] * count,
-        [pltpu.VMEM((count, 16, size), BF16), pltpu.SemaphoreType.DMA((3 * count,))],
+        [V] * 4 + [A if r in have else V for r in range(count)],
+        [pltpu.VMEM((len(have), 16, size), BF16), pltpu.SemaphoreType.DMA((len(have),))],
         flops=2 * size ** 3, moved=6 * size ** 2, aliases={1: 3, 2: 4, 3: 5},
     )(two, three, third, fourth, *late)
     pairs = [(i, i + 1) for i in range(0, blocks_of_time, 2)]
@@ -389,12 +389,7 @@
     blocks_here = (own, own_term, other, other_term)
     onward = [(2 * c + 1, 2 * c + 3) for c in range(firsts, chips, 2)]
     half_cost = dict(flops=size ** 3, moved=6 * size ** 2)
-    turned0 = call(functools.partial(pair_kernel, 0), part, [V] * 4, **half_cost)(*blocks_here)
-    before0 = lax.ppermute(turned0, "tm", onward)
-    turned1 = call(functools.partial(pair_kernel, 1), longer, [V] * 4, **half_cost)(*blocks_here)
-    before1 = lax.ppermute(turned1, "tm", onward)
-
-    begin = after(prior.reshape(1, size), turned1)
+    begin = prior.reshape(1, size)
     came = begin
     for turn in range(firsts):
         if turn < DIRECT:
@@ -408,6 +403,12 @@
                 flops=32 * size ** 2, moved=2 * size ** 2,
             )(begin, came, turned0, turned1)
         came = lax.ppermute(value, "tm", [(2 * turn + 1, 2 * turn + (3 if turn + 1 < firsts else 5))])
+        if turn == 1:
+            pair_blocks = after(blocks_here, value)
+            turned0 = call(functools.partial(pair_kernel, 0), part, [V] * 4, **half_cost)(*pair_blocks)
+            before0 = lax.ppermute(turned0, "tm", onward)
+            turned1 = call(functools.partial(pair_kernel, 1), longer, [V] * 4, **half_cost)(*pair_blocks)
+            before1 = lax.ppermute(turned1, "tm", onward)
         if turn == 3:
             maps, terms = call(
                 ready_kernel,

time: 150 us -> 149 us (level)
  waiting for transfers between devices: 93.8 us -> 92.1 us
    ppermute x14, waiting for transfers between devices: 57.8 us -> 55.3 us  [the longest x7 30.7 us: ring_rounds(): pieces[count - r] = lax.ppermute(left, ('tm', 'state'), forward)]
  transfers between devices with their start and end apart: 31 -> 31, of which waited for: 12 -> 13; matrix products, arithmetic and copies ran while one was open for 0% -> 0% of each run, Pallas kernels for 6% -> 6%
where the time goes in v11:
time: 149 us; the launch traced here: 148 us
  waiting for transfers between devices  92.1 us (62%)
  starting transfers between devices  40.2 us (27%)
  Pallas kernels  14 us (9%)
    ppermute x1, waiting for transfers between devices, shards(): got = lax.ppermute(begin, 'tm', [(b, a) for a, b in pairs])  35.9 us
    ppermute x7, waiting for transfers between devices, ring_rounds(): pieces[count - r] = lax.ppermute(left, ('tm', 'state'), forward)  30.7 us
    ppermute x7, waiting for transfers between devices, ring_rounds(): pieces[r] = lax.ppermute(right, ('tm', 'state'), backward)  24.6 us
    ppermute x7, starting transfers between devices, ring_rounds(): pieces[r] = lax.ppermute(right, ('tm', 'state'), backward)  20.8 us
    ppermute x8, starting transfers between devices, shards(): lax.ppermute(value, 'tm', [(2 * turn + 1, 2 * turn + (3 if turn + 1 < fir...  5.28 us
    ppermute x7, starting transfers between devices, ring_rounds(): pieces[count - r] = lax.ppermute(left, ('tm', 'state'), forward)  4.9 us
    pallas_call x1, Pallas kernels, shards(): call(functools.partial(four_kernel, count, have), (matrix, slab, slab, ma...  3.62 us
    pallas_call x1, Pallas kernels, shards(): call(functools.partial(two_kernel, count), (matrix, slab, matrix), [A] *...  3.03 us
  transfers between devices with their start and end apart: 31, of which 13 were waited for; matrix products, arithmetic and copies ran while one was open for 0% of the time, Pallas kernels for 6%

profile of v11, /device:TPU:30, one launch (start us, length us, event | category | flops | bytes accessed | tf_op | source)
XLA Modules:
  0.0 148.2 jit_solution(12807598335913517920)
XLA Ops:
  0.0 1.4 fusion
  1.5 2.0 %collective-permute-start.1 = (bf16[256,1024]{1,0:T(8,128)(2,1)S(1)}, bf16[256,1024]{1,0:T(8,128)(2,1)S(1)}, u32[]{:S(2)}, u32[]{:S(2)}) collective-permute-start(bf16[256,1024]{1,0:T(8,128)(2,1)S(1)} %bitcast.2), channel_id=1, source_target_pairs={{0,1},{1,2},{2,3},{3,4},{4,5},{5,6},{6,7},{7,0},{8,15},{9,8},{10,9... | collective-permute-start | bytes 1572872 | tf_op jit(solution)/shard_map/ppermute | solution.py:327
  3.4 4.0 %collective-permute-start = (bf16[256,1024]{1,0:T(8,128)(2,1)S(1)}, bf16[256,1024]{1,0:T(8,128)(2,1)S(1)}, u32[]{:S(2)}, u32[]{:S(2)}) collective-permute-start(bf16[256,1024]{1,0:T(8,128)(2,1)S(1)} %bitcast.3), channel_id=1, source_target_pairs={{1,0},{2,1},{3,2},{4,3},{5,4},{6,5},{7,6},{0,7},{15,8},{8,9},{9,10... | collective-permute-start | bytes 1572872 | tf_op jit(solution)/shard_map/ppermute | solution.py:329
  7.5 1.6 %shard_map.73.refs_0_ = bf16[272,1024]{1,0:T(8,128)(2,1)S(1)} custom-call(s32[4,32]{1,0:T(4,128)S(1)} %copy-done.2, s32[4,32]{1,0:T(4,128)S(1)} %copy-done.3, bf16[4,4096]{1,0:T(4,128)(2,1)S(1)} %multiply_convert_fusion.values_ref, bf16[4,32,64,64]{3,2,1,0:T(8,128)(2,1)S(1)} %copy-done, bf16[2,128,1024]{2,1,0:T(8,128)(2,1)S(1)} %get-tuple-element.83.maps_ref), custom_call_target="tpu_custom_call" | custom-call | flops 10000000 | bytes 2097152 | tf_op jit(solution)/shard_map/pallas_call | solution.py:349
  9.1 2.0 %collective-permute-start.7 = (bf16[272,1024]{1,0:T(8,128)(2,1)S(1)}, bf16[272,1024]{1,0:T(8,128)(2,1)S(1)}, u32[]{:S(2)}, u32[]{:S(2)}) collective-permute-start(bf16[272,1024]{1,0:T(8,128)(2,1)S(1)} %shard_map.73.refs_0_), channel_id=1, source_target_pairs={{1,0},{2,1},{3,2},{4,3},{5,4},{6,5},{7,6},{0,7},{15,8},{8,9},{9,10... | collective-permute-start | bytes 1671176 | tf_op jit(solution)/shard_map/ppermute | solution.py:329
  11.1 7.2 %collective-permute-done.1.refs_7_ = bf16[256,1024]{1,0:T(8,128)(2,1)S(1)} collective-permute-done((bf16[256,1024]{1,0:T(8,128)(2,1)S(1)}, bf16[256,1024]{1,0:T(8,128)(2,1)S(1)}, u32[]{:S(2)}, u32[]{:S(2)}) %collective-permute-start.1) | collective-permute-done | bytes 524320 | tf_op jit(solution)/shard_map/ppermute | solution.py:327
  18.6 1.6 %collective-permute-start.10 = (bf16[272,1024]{1,0:T(8,128)(2,1)S(1)}, bf16[272,1024]{1,0:T(8,128)(2,1)S(1)}, u32[]{:S(2)}, u32[]{:S(2)}) collective-permute-start(bf16[272,1024]{1,0:T(8,128)(2,1)S(1)} %shard_map.73.refs_0_), channel_id=1, source_target_pairs={{0,1},{1,2},{2,3},{3,4},{4,5},{5,6},{6,7},{7,0},{8,15},{9,8},{10,9... | collective-permute-start | bytes 1671176 | tf_op jit(solution)/shard_map/ppermute | solution.py:327
  20.2 7.2 %collective-permute-done.7.refs_1_ = bf16[272,1024]{1,0:T(8,128)(2,1)S(1)} collective-permute-done((bf16[272,1024]{1,0:T(8,128)(2,1)S(1)}, bf16[272,1024]{1,0:T(8,128)(2,1)S(1)}, u32[]{:S(2)}, u32[]{:S(2)}) %collective-permute-start.7) | collective-permute-done | bytes 557088 | tf_op jit(solution)/shard_map/ppermute | solution.py:329
  27.3 3.7 %collective-permute-start.8 = (bf16[272,1024]{1,0:T(8,128)(2,1)S(1)}, bf16[272,1024]{1,0:T(8,128)(2,1)S(1)}, u32[]{:S(2)}, u32[]{:S(2)}) collective-permute-start(bf16[272,1024]{1,0:T(8,128)(2,1)S(1)} %collective-permute-done.7.refs_1_), channel_id=1, source_target_pairs={{1,0},{2,1},{3,2},{4,3},{5,4},{6,5},{7,6},{0,7},{15,8},{8,9},{9,10... | collective-permute-start | bytes 1671176 | tf_op jit(solution)/shard_map/ppermute | solution.py:329
  31.8 1.3 collective-permute-start.5
  33.0 10.0 %collective-permute-done.10.refs_5_.refs_7_ = bf16[272,1024]{1,0:T(8,128)(2,1)S(1)} collective-permute-done((bf16[272,1024]{1,0:T(8,128)(2,1)S(1)}, bf16[272,1024]{1,0:T(8,128)(2,1)S(1)}, u32[]{:S(2)}, u32[]{:S(2)}) %collective-permute-start.10) | collective-permute-done | bytes 557088 | tf_op jit(solution)/shard_map/ppermute | solution.py:327
  43.1 1.0 collective-permute-done.8.refs_2_
  44.1 3.7 %collective-permute-start.9 = (bf16[272,1024]{1,0:T(8,128)(2,1)S(1)}, bf16[272,1024]{1,0:T(8,128)(2,1)S(1)}, u32[]{:S(2)}, u32[]{:S(2)}) collective-permute-start(bf16[272,1024]{1,0:T(8,128)(2,1)S(1)} %collective-permute-done.8.refs_2_), channel_id=1, source_target_pairs={{1,0},{2,1},{3,2},{4,3},{5,4},{6,5},{7,6},{0,7},{15,8},{8,9},{9,10... | collective-permute-start | bytes 1671176 | tf_op jit(solution)/shard_map/ppermute | solution.py:329
  47.8 7.5 %collective-permute-done.2.refs_2_ = bf16[256,1024]{1,0:T(8,128)(2,1)S(1)} collective-permute-done((bf16[256,1024]{1,0:T(8,128)(2,1)S(1)}, bf16[256,1024]{1,0:T(8,128)(2,1)S(1)}, u32[]{:S(2)}, u32[]{:S(2)}) %collective-permute-start.2) | collective-permute-done | bytes 524320 | tf_op jit(solution)/shard_map/ppermute | solution.py:329
  55.3 3.7 %collective-permute-start.3 = (bf16[256,1024]{1,0:T(8,128)(2,1)S(1)}, bf16[256,1024]{1,0:T(8,128)(2,1)S(1)}, u32[]{:S(2)}, u32[]{:S(2)}) collective-permute-start(bf16[256,1024]{1,0:T(8,128)(2,1)S(1)} %collective-permute-done.2.refs_2_), channel_id=1, source_target_pairs={{1,0},{2,1},{3,2},{4,3},{5,4},{6,5},{7,6},{0,7},{15,8},{8,9},{9,10... | collective-permute-start | bytes 1572872 | tf_op jit(solution)/shard_map/ppermute | solution.py:329
  59.0 7.2 %collective-permute-done.11.refs_4_.refs_6_ = bf16[272,1024]{1,0:T(8,128)(2,1)S(1)} collective-permute-done((bf16[272,1024]{1,0:T(8,128)(2,1)S(1)}, bf16[272,1024]{1,0:T(8,128)(2,1)S(1)}, u32[]{:S(2)}, u32[]{:S(2)}) %collective-permute-start.11) | collective-permute-done | bytes 557088 | tf_op jit(solution)/shard_map/ppermute | solution.py:327
  66.2 1.0 collective-permute-done.9.refs_3_
  67.3 3.7 %collective-permute-start.12 = (bf16[272,1024]{1,0:T(8,128)(2,1)S(1)}, bf16[272,1024]{1,0:T(8,128)(2,1)S(1)}, u32[]{:S(2)}, u32[]{:S(2)}) collective-permute-start(bf16[272,1024]{1,0:T(8,128)(2,1)S(1)} %collective-permute-done.9.refs_3_), channel_id=1, source_target_pairs={{1,0},{2,1},{3,2},{4,3},{5,4},{6,5},{7,6},{0,7},{15,8},{8,9},{9,10... | collective-permute-start | bytes 1671176 | tf_op jit(solution)/shard_map/ppermute | solution.py:329
  71.0 7.5 %collective-permute-done.3.refs_3_ = bf16[256,1024]{1,0:T(8,128)(2,1)S(1)} collective-permute-done((bf16[256,1024]{1,0:T(8,128)(2,1)S(1)}, bf16[256,1024]{1,0:T(8,128)(2,1)S(1)}, u32[]{:S(2)}, u32[]{:S(2)}) %collective-permute-start.3) | collective-permute-done | bytes 524320 | tf_op jit(solution)/shard_map/ppermute | solution.py:329
  78.5 3.0 %shard_map.74 = (bf16[1024,1024]{1,0:T(8,128)(2,1)S(1)}, bf16[128,1024]{1,0:T(8,128)(2,1)S(1)}, bf16[1024,1024]{1,0:T(8,128)(2,1)S(1)}) custom-call(bf16[256,1024]{1,0:T(8,128)(2,1)S(1)} %bitcast.4, bf16[256,1024]{1,0:T(8,128)(2,1)S(1)} %collective-permute-done.refs_1_, bf16[256,1024]{1,0:T(8,128)(2,1)S(1)} %collective-permute-done.2.refs_2_, ...), custom_call_target="tpu_custom_call" | custom-call | flops 2147483648 | bytes 6291456 | tf_op jit(solution)/shard_map/pallas_call | solution.py:362
  81.6 2.2 %shard_map.75 = (bf16[1024,1024]{1,0:T(8,128)(2,1)S(1)}, bf16[1024,1024]{1,0:T(8,128)(2,1)S(1)}, bf16[1024,1024]{1,0:T(8,128)(2,1)S(1)}) custom-call(bf16[1024,1024]{1,0:T(8,128)(2,1)S(1)} %get-tuple-element.46.two_ref, bf16[272,1024]{1,0:T(8,128)(2,1)S(1)} %shard_map.73.refs_0_, bf16[272,1024]{1,0:T(8,128)(2,1)S(1)} %collective-permute-done.7.refs_1_, ...), custom_call_target="tpu_custom_call" | custom-call | flops 2147483648 | bytes 6291456 | tf_op jit(solution)/shard_map/pallas_call | solution.py:367
  83.8 5.6 %collective-permute-done.13.refs_5_ = bf16[272,1024]{1,0:T(8,128)(2,1)S(1)} collective-permute-done((bf16[272,1024]{1,0:T(8,128)(2,1)S(1)}, bf16[272,1024]{1,0:T(8,128)(2,1)S(1)}, u32[]{:S(2)}, u32[]{:S(2)}) %collective-permute-start.13) | collective-permute-done | bytes 557088 | tf_op jit(solution)/shard_map/ppermute | solution.py:327
  89.4 3.6 %shard_map.76 = (bf16[1024,1024]{1,0:T(8,128)(2,1)S(1)}, bf16[128,1024]{1,0:T(8,128)(2,1)S(1)}, bf16[128,1024]{1,0:T(8,128)(2,1)S(1)}, bf16[1024,1024]{1,0:T(8,1...) custom-call(bf16[1024,1024]{1,0:T(8,128)(2,1)S(1)} %get-tuple-elemen, ...), custom_call_target="tpu_custom_call", output_to_operand_aliasing={{3}: (1, {}), {4}: (2, {}), {5}: (3, {})} | custom-call | flops 2147483648 | bytes 6291456 | tf_op jit(solution)/shard_map/pallas_call | solution.py:371
  93.0 2.5 %collective-permute-start.14 = (bf16[1024,1024]{1,0:T(8,128)(2,1)S(1)}, bf16[1024,1024]{1,0:T(8,128)(2,1)S(1)}, u32[]{:S(2)}, u32[]{:S(2)}) collective-permute-start(bf16[1024,1024]{1,0:T(8,128)(2,1)S(1)} %get-tuple-element.60.own_ref), channel_id=1, source_target_pairs={{0,8},{16,24},{32,40},{48,56},{64,72},{80,88},{96,104},{112,120},{... | collective-permute-start | bytes 6291464 | tf_op jit(solution)/shard_map/ppermute | solution.py:379
  95.5 1.8 %shard_map.77 = (f32[4,1024]{1,0:T(4,128)S(1)}, bf16[16,1024]{1,0:T(8,128)(2,1)S(1)}) custom-call(f32[16,1024]{1,0:T(8,128)S(1)} %get-tuple-element.51.drive_ref, bf16[1024,1024]{1,0:T(8,128)(2,1)S(1)} %get-tuple-element.52.second_ref, bf16[1024,1024]{1,0:T(8,128)(2,1)S(1)} %get-tuple-element.53.third_ref, bf16[1024,1024]{1,0:T(8,128)(2,1)S(1)} %get-tuple-element.54.fourth_ref), custom_call_target="tpu_custom_call" | custom-call | flops 100663296 | bytes 6291456 | tf_op jit(solution)/shard_map/pallas_call | solution.py:380
  97.3 1.3 collective-permute-start.15
  98.6 0.8 collective-permute-done.15.other_term_ref
  100.2 0.7 collective-permute-start.24
  100.9 0.7 collective-permute-start.25
  110.1 1.3 collective-permute-start.30
  111.4 35.9 %collective-permute-done.30.got_ref = f32[1,1024]{1,0:T(1,128)S(1)} collective-permute-done((f32[1,1024]{1,0:T(1,128)S(1)}, f32[1,1024]{1,0:T(1,128)S(1)}, u32[]{:S(2)}, u32[]{:S(2)}) %collective-permute-start.30) | collective-permute-done | bytes 4128 | tf_op jit(solution)/shard_map/ppermute | solution.py:433
  147.4 0.8 shard_map.95
  (67 shorter events, 10.0 us)
Async XLA Ops:
  0.0 7.5 %copy-start.2 = (s32[4,32]{1,0:T(4,128)S(1)}, s32[4,32]{1,0:T(4,128)}, u32[]{:S(2)}) copy-start(s32[4,32]{1,0:T(4,128)} %rows_ref.1) | copy-start | bytes 1540
  1.5 16.8 %collective-permute-start.1 = (bf16[256,1024]{1,0:T(8,128)(2,1)S(1)}, bf16[256,1024]{1,0:T(8,128)(2,1)S(1)}, u32[]{:S(2)}, u32[]{:S(2)}) collective-permute-start(bf16[256,1024]{1,0:T(8,128)(2,1)S(1)} %bitcast.2), channel_id=1, source_target_pairs={{0,1},{1,2},{2,3},{3,4},{4,5},{5,6},{6,7},{7,0},{8,15},{9,8},{10,9... | collective-permute-start | bytes 1572872 | tf_op jit(solution)/shard_map/ppermute | solution.py:327
  3.4 15.1 %collective-permute-start = (bf16[256,1024]{1,0:T(8,128)(2,1)S(1)}, bf16[256,1024]{1,0:T(8,128)(2,1)S(1)}, u32[]{:S(2)}, u32[]{:S(2)}) collective-permute-start(bf16[256,1024]{1,0:T(8,128)(2,1)S(1)} %bitcast.3), channel_id=1, source_target_pairs={{1,0},{2,1},{3,2},{4,3},{5,4},{6,5},{7,6},{0,7},{15,8},{8,9},{9,10... | collective-permute-start | bytes 1572872 | tf_op jit(solution)/shard_map/ppermute | solution.py:329
  9.1 18.2 %collective-permute-start.7 = (bf16[272,1024]{1,0:T(8,128)(2,1)S(1)}, bf16[272,1024]{1,0:T(8,128)(2,1)S(1)}, u32[]{:S(2)}, u32[]{:S(2)}) collective-permute-start(bf16[272,1024]{1,0:T(8,128)(2,1)S(1)} %shard_map.73.refs_0_), channel_id=1, source_target_pairs={{1,0},{2,1},{3,2},{4,3},{5,4},{6,5},{7,6},{0,7},{15,8},{8,9},{9,10... | collective-permute-start | bytes 1671176 | tf_op jit(solution)/shard_map/ppermute | solution.py:329
  18.6 13.2 %collective-permute-start.4 = (bf16[256,1024]{1,0:T(8,128)(2,1)S(1)}, bf16[256,1024]{1,0:T(8,128)(2,1)S(1)}, u32[]{:S(2)}, u32[]{:S(2)}) collective-permute-start(bf16[256,1024]{1,0:T(8,128)(2,1)S(1)} %collective-permute-done.1.refs_7_), channel_id=1, source_target_pairs={{0,1},{1,2},{2,3},{3,4},{4,5},{5,6},{6,7},{7,0},{8,15},{9,8},{10,9... | collective-permute-start | bytes 1572872 | tf_op jit(solution)/shard_map/ppermute | solution.py:327
  18.6 24.5 %collective-permute-start.10 = (bf16[272,1024]{1,0:T(8,128)(2,1)S(1)}, bf16[272,1024]{1,0:T(8,128)(2,1)S(1)}, u32[]{:S(2)}, u32[]{:S(2)}) collective-permute-start(bf16[272,1024]{1,0:T(8,128)(2,1)S(1)} %shard_map.73.refs_0_), channel_id=1, source_target_pairs={{0,1},{1,2},{2,3},{3,4},{4,5},{5,6},{6,7},{7,0},{8,15},{9,8},{10,9... | collective-permute-start | bytes 1671176 | tf_op jit(solution)/shard_map/ppermute | solution.py:327
  27.3 16.8 %collective-permute-start.8 = (bf16[272,1024]{1,0:T(8,128)(2,1)S(1)}, bf16[272,1024]{1,0:T(8,128)(2,1)S(1)}, u32[]{:S(2)}, u32[]{:S(2)}) collective-permute-start(bf16[272,1024]{1,0:T(8,128)(2,1)S(1)} %collective-permute-done.7.refs_1_), channel_id=1, source_target_pairs={{1,0},{2,1},{3,2},{4,3},{5,4},{6,5},{7,6},{0,7},{15,8},{8,9},{9,10... | collective-permute-start | bytes 1671176 | tf_op jit(solution)/shard_map/ppermute | solution.py:329
  31.0 24.3 %collective-permute-start.2 = (bf16[256,1024]{1,0:T(8,128)(2,1)S(1)}, bf16[256,1024]{1,0:T(8,128)(2,1)S(1)}, u32[]{:S(2)}, u32[]{:S(2)}) collective-permute-start(bf16[256,1024]{1,0:T(8,128)(2,1)S(1)} %collective-permute-done.refs_1_), channel_id=1, source_target_pairs={{1,0},{2,1},{3,2},{4,3},{5,4},{6,5},{7,6},{0,7},{15,8},{8,9},{9,10... | collective-permute-start | bytes 1572872 | tf_op jit(solution)/shard_map/ppermute | solution.py:329
  31.8 27.3 %collective-permute-start.5 = (bf16[256,1024]{1,0:T(8,128)(2,1)S(1)}, bf16[256,1024]{1,0:T(8,128)(2,1)S(1)}, u32[]{:S(2)}, u32[]{:S(2)}) collective-permute-start(bf16[256,1024]{1,0:T(8,128)(2,1)S(1)} %collective-permute-done.4.refs_6_), channel_id=1, source_target_pairs={{0,1},{1,2},{2,3},{3,4},{4,5},{5,6},{6,7},{7,0},{8,15},{9,8},{10,9... | collective-permute-start | bytes 1572872 | tf_op jit(solution)/shard_map/ppermute | solution.py:327
  43.1 23.2 %collective-permute-start.11 = (bf16[272,1024]{1,0:T(8,128)(2,1)S(1)}, bf16[272,1024]{1,0:T(8,128)(2,1)S(1)}, u32[]{:S(2)}, u32[]{:S(2)}) collective-permute-start(bf16[272,1024]{1,0:T(8,128)(2,1)S(1)} %collective-permute-done.10.refs_5_.refs_7_), channel_id=1, source_target_pairs={{0,1},{1,2},{2,3},{3,4},{4,5},{5,6},{6,7},{7,0},{8,15},{9,8},{10,9... | collective-permute-start | bytes 1671176 | tf_op jit(solution)/shard_map/ppermute | solution.py:327
  44.1 23.2 %collective-permute-start.9 = (bf16[272,1024]{1,0:T(8,128)(2,1)S(1)}, bf16[272,1024]{1,0:T(8,128)(2,1)S(1)}, u32[]{:S(2)}, u32[]{:S(2)}) collective-permute-start(bf16[272,1024]{1,0:T(8,128)(2,1)S(1)} %collective-permute-done.8.refs_2_), channel_id=1, source_target_pairs={{1,0},{2,1},{3,2},{4,3},{5,4},{6,5},{7,6},{0,7},{15,8},{8,9},{9,10... | collective-permute-start | bytes 1671176 | tf_op jit(solution)/shard_map/ppermute | solution.py:329
  55.3 23.2 %collective-permute-start.3 = (bf16[256,1024]{1,0:T(8,128)(2,1)S(1)}, bf16[256,1024]{1,0:T(8,128)(2,1)S(1)}, u32[]{:S(2)}, u32[]{:S(2)}) collective-permute-start(bf16[256,1024]{1,0:T(8,128)(2,1)S(1)} %collective-permute-done.2.refs_2_), channel_id=1, source_target_pairs={{1,0},{2,1},{3,2},{4,3},{5,4},{6,5},{7,6},{0,7},{15,8},{8,9},{9,10... | collective-permute-start | bytes 1572872 | tf_op jit(solution)/shard_map/ppermute | solution.py:329
  59.0 19.5 %collective-permute-start.6 = (bf16[256,1024]{1,0:T(8,128)(2,1)S(1)}, bf16[256,1024]{1,0:T(8,128)(2,1)S(1)}, u32[]{:S(2)}, u32[]{:S(2)}) collective-permute-start(bf16[256,1024]{1,0:T(8,128)(2,1)S(1)} %collective-permute-done.5.refs_5_), channel_id=1, source_target_pairs={{0,1},{1,2},{2,3},{3,4},{4,5},{5,6},{6,7},{7,0},{8,15},{9,8},{10,9... | collective-permute-start | bytes 1572872 | tf_op jit(solution)/shard_map/ppermute | solution.py:327
  66.2 23.2 %collective-permute-start.13 = (bf16[272,1024]{1,0:T(8,128)(2,1)S(1)}, bf16[272,1024]{1,0:T(8,128)(2,1)S(1)}, u32[]{:S(2)}, u32[]{:S(2)}) collective-permute-start(bf16[272,1024]{1,0:T(8,128)(2,1)S(1)} %collective-permute-done.11.refs_4_.refs_6_), channel_id=1, source_target_pairs={{0,1},{1,2},{2,3},{3,4},{4,5},{5,6},{6,7},{7,0},{8,15},{9,8},{10,9... | collective-permute-start | bytes 1671176 | tf_op jit(solution)/shard_map/ppermute | solution.py:327
  67.3 22.1 %collective-permute-start.12 = (bf16[272,1024]{1,0:T(8,128)(2,1)S(1)}, bf16[272,1024]{1,0:T(8,128)(2,1)S(1)}, u32[]{:S(2)}, u32[]{:S(2)}) collective-permute-start(bf16[272,1024]{1,0:T(8,128)(2,1)S(1)} %collective-permute-done.9.refs_3_), channel_id=1, source_target_pairs={{1,0},{2,1},{3,2},{4,3},{5,4},{6,5},{7,6},{0,7},{15,8},{8,9},{9,10... | collective-permute-start | bytes 1671176 | tf_op jit(solution)/shard_map/ppermute | solution.py:329
  93.0 6.4 %collective-permute-start.14 = (bf16[1024,1024]{1,0:T(8,128)(2,1)S(1)}, bf16[1024,1024]{1,0:T(8,128)(2,1)S(1)}, u32[]{:S(2)}, u32[]{:S(2)}) collective-permute-start(bf16[1024,1024]{1,0:T(8,128)(2,1)S(1)} %get-tuple-element.60.own_ref), channel_id=1, source_target_pairs={{0,8},{16,24},{32,40},{48,56},{64,72},{80,88},{96,104},{112,120},{... | collective-permute-start | bytes 6291464 | tf_op jit(solution)/shard_map/ppermute | solution.py:379
  97.3 2.1 %collective-permute-start.15 = (bf16[16,1024]{1,0:T(8,128)(2,1)S(1)}, bf16[16,1024]{1,0:T(8,128)(2,1)S(1)}, u32[]{:S(2)}, u32[]{:S(2)}) collective-permute-start(bf16[16,1024]{1,0:T(8,128)(2,1)S(1)} %get-tuple-element.61.own_term_ref), channel_id=1, source_target_pairs={{0,8},{16,24},{32,40},{48,56},{64,72},{80,88},{96,104},{112,120},{... | collective-permute-start | bytes 98312 | tf_op jit(solution)/shard_map/ppermute | solution.py:383
  99.4 0.7 collective-permute-start.16
  100.2 7.0 %collective-permute-start.24 = (bf16[512,1024]{1,0:T(8,128)(2,1)S(1)}, bf16[512,1024]{1,0:T(8,128)(2,1)S(1)}, u32[]{:S(2)}, u32[]{:S(2)}) collective-permute-start(bf16[512,1024]{1,0:T(8,128)(2,1)S(1)} %shard_map.80.turned0_ref), channel_id=1, source_target_pairs={{136,152},{168,184},{200,216},{232,248},{137,153},{169,185},{201,2... | collective-permute-start | bytes 3145736 | tf_op jit(solution)/shard_map/ppermute | solution.py:409
  100.9 6.3 %collective-permute-start.25 = (bf16[528,1024]{1,0:T(8,128)(2,1)S(1)}, bf16[528,1024]{1,0:T(8,128)(2,1)S(1)}, u32[]{:S(2)}, u32[]{:S(2)}) collective-permute-start(bf16[528,1024]{1,0:T(8,128)(2,1)S(1)} %shard_map.81.turned1_ref), channel_id=1, source_target_pairs={{136,152},{168,184},{200,216},{232,248},{137,153},{169,185},{201,2... | collective-permute-start | bytes 3244040 | tf_op jit(solution)/shard_map/ppermute | solution.py:411
  101.7 0.7 collective-permute-start.17
  102.4 0.7 collective-permute-start.18
  103.1 0.7 collective-permute-start.19
  103.8 1.3 collective-permute-start.20
  105.1 0.7 collective-permute-start.21
  105.8 0.7 collective-permute-start.22
  106.5 0.8 collective-permute-start.23
  107.3 0.7 collective-permute-start.26
  108.0 0.7 collective-permute-start.27
  108.7 1.3 collective-permute-start.29
  109.4 0.7 collective-permute-start.28
  110.1 37.2 %collective-permute-start.30 = (f32[1,1024]{1,0:T(1,128)S(1)}, f32[1,1024]{1,0:T(1,128)S(1)}, u32[]{:S(2)}, u32[]{:S(2)}) collective-permute-start(f32[1,1024]{1,0:T(1,128)S(1)} %shard_map.94.begin_ref), channel_id=1, source_target_pairs={{8,0},{24,16},{40,32},{56,48},{72,64},{88,80},{104,96},{120,112},{... | collective-permute-start | bytes 12296 | tf_op jit(solution)/shard_map/ppermute | solution.py:433
  (5 other events, 33.9 us)

commit v12 on v11

--- a/solution.py
+++ b/solution.py
@@ -389,7 +389,12 @@
     blocks_here = (own, own_term, other, other_term)
     onward = [(2 * c + 1, 2 * c + 3) for c in range(firsts, chips, 2)]
     half_cost = dict(flops=size ** 3, moved=6 * size ** 2)
-    begin = prior.reshape(1, size)
+    turned0 = call(functools.partial(pair_kernel, 0), part, [V] * 4, **half_cost)(*blocks_here)
+    before0 = lax.ppermute(turned0, "tm", onward)
+    turned1 = call(functools.partial(pair_kernel, 1), longer, [V] * 4, **half_cost)(*blocks_here)
+    before1 = lax.ppermute(turned1, "tm", onward)
+
+    begin = after(prior.reshape(1, size), turned1)
     came = begin
     for turn in range(firsts):
         if turn < DIRECT:
@@ -403,12 +408,6 @@
                 flops=32 * size ** 2, moved=2 * size ** 2,
             )(begin, came, turned0, turned1)
         came = lax.ppermute(value, "tm", [(2 * turn + 1, 2 * turn + (3 if turn + 1 < firsts else 5))])
-        if turn == 1:
-            pair_blocks = after(blocks_here, value)
-            turned0 = call(functools.partial(pair_kernel, 0), part, [V] * 4, **half_cost)(*pair_blocks)
-            before0 = lax.ppermute(turned0, "tm", onward)
-            turned1 = call(functools.partial(pair_kernel, 1), longer, [V] * 4, **half_cost)(*pair_blocks)
-            before1 = lax.ppermute(turned1, "tm", onward)
         if turn == 3:
             maps, terms = call(
                 ready_kernel,

time: 149 us -> 148 us (level)
  no operation moved by 1% of the time
where the time goes in v12:
time: 148 us; the launch traced here: 147 us
  waiting for transfers between devices  91.2 us (62%)
  starting transfers between devices  40.3 us (27%)
  Pallas kernels  14 us (9%)
    ppermute x1, waiting for transfers between devices, shards(): got = lax.ppermute(begin, 'tm', [(b, a) for a, b in pairs])  35.1 us
    ppermute x7, waiting for transfers between devices, ring_rounds(): pieces[count - r] = lax.ppermute(left, ('tm', 'state'), forward)  30.7 us
    ppermute x7, waiting for transfers between devices, ring_rounds(): pieces[r] = lax.ppermute(right, ('tm', 'state'), backward)  24.6 us
    ppermute x7, starting transfers between devices, ring_rounds(): pieces[r] = lax.ppermute(right, ('tm', 'state'), backward)  20.8 us
    ppermute x8, starting transfers between devices, shards(): lax.ppermute(value, 'tm', [(2 * turn + 1, 2 * turn + (3 if turn + 1 < fir...  5.29 us
    ppermute x7, starting transfers between devices, ring_rounds(): pieces[count - r] = lax.ppermute(left, ('tm', 'state'), forward)  4.9 us
    pallas_call x1, Pallas kernels, shards(): call(functools.partial(four_kernel, count, have), (matrix, slab, slab, ma...  3.62 us
    pallas_call x1, Pallas kernels, shards(): call(functools.partial(two_kernel, count), (matrix, slab, matrix), [A] *...  3.03 us
  transfers between devices with their start and end apart: 31, of which 13 were waited for; matrix products, arithmetic and copies ran while one was open for 0% of the time, Pallas kernels for 6%

profile of v12, /device:TPU:30, one launch (start us, length us, event | category | flops | bytes accessed | tf_op | source)
XLA Modules:
  0.0 147.5 jit_solution(16025940380641564314)
XLA Ops:
  0.0 1.4 fusion
  1.5 2.0 %collective-permute-start.1 = (bf16[256,1024]{1,0:T(8,128)(2,1)S(1)}, bf16[256,1024]{1,0:T(8,128)(2,1)S(1)}, u32[]{:S(2)}, u32[]{:S(2)}) collective-permute-start(bf16[256,1024]{1,0:T(8,128)(2,1)S(1)} %bitcast.2), channel_id=1, source_target_pairs={{0,1},{1,2},{2,3},{3,4},{4,5},{5,6},{6,7},{7,0},{8,15},{9,8},{10,9... | collective-permute-start | bytes 1572872 | tf_op jit(solution)/shard_map/ppermute | solution.py:327
  3.4 4.0 %collective-permute-start = (bf16[256,1024]{1,0:T(8,128)(2,1)S(1)}, bf16[256,1024]{1,0:T(8,128)(2,1)S(1)}, u32[]{:S(2)}, u32[]{:S(2)}) collective-permute-start(bf16[256,1024]{1,0:T(8,128)(2,1)S(1)} %bitcast.3), channel_id=1, source_target_pairs={{1,0},{2,1},{3,2},{4,3},{5,4},{6,5},{7,6},{0,7},{15,8},{8,9},{9,10... | collective-permute-start | bytes 1572872 | tf_op jit(solution)/shard_map/ppermute | solution.py:329
  7.5 1.6 %shard_map.73.refs_0_ = bf16[272,1024]{1,0:T(8,128)(2,1)S(1)} custom-call(s32[4,32]{1,0:T(4,128)S(1)} %copy-done.2, s32[4,32]{1,0:T(4,128)S(1)} %copy-done.3, bf16[4,4096]{1,0:T(4,128)(2,1)S(1)} %multiply_convert_fusion.values_ref, bf16[4,32,64,64]{3,2,1,0:T(8,128)(2,1)S(1)} %copy-done, bf16[2,128,1024]{2,1,0:T(8,128)(2,1)S(1)} %get-tuple-element.77.maps_ref), custom_call_target="tpu_custom_call" | custom-call | flops 10000000 | bytes 2097152 | tf_op jit(solution)/shard_map/pallas_call | solution.py:349
  9.1 2.0 %collective-permute-start.7 = (bf16[272,1024]{1,0:T(8,128)(2,1)S(1)}, bf16[272,1024]{1,0:T(8,128)(2,1)S(1)}, u32[]{:S(2)}, u32[]{:S(2)}) collective-permute-start(bf16[272,1024]{1,0:T(8,128)(2,1)S(1)} %shard_map.73.refs_0_), channel_id=1, source_target_pairs={{1,0},{2,1},{3,2},{4,3},{5,4},{6,5},{7,6},{0,7},{15,8},{8,9},{9,10... | collective-permute-start | bytes 1671176 | tf_op jit(solution)/shard_map/ppermute | solution.py:329
  11.1 7.2 %collective-permute-done.1.refs_7_ = bf16[256,1024]{1,0:T(8,128)(2,1)S(1)} collective-permute-done((bf16[256,1024]{1,0:T(8,128)(2,1)S(1)}, bf16[256,1024]{1,0:T(8,128)(2,1)S(1)}, u32[]{:S(2)}, u32[]{:S(2)}) %collective-permute-start.1) | collective-permute-done | bytes 524320 | tf_op jit(solution)/shard_map/ppermute | solution.py:327
  18.6 1.6 %collective-permute-start.10 = (bf16[272,1024]{1,0:T(8,128)(2,1)S(1)}, bf16[272,1024]{1,0:T(8,128)(2,1)S(1)}, u32[]{:S(2)}, u32[]{:S(2)}) collective-permute-start(bf16[272,1024]{1,0:T(8,128)(2,1)S(1)} %shard_map.73.refs_0_), channel_id=1, source_target_pairs={{0,1},{1,2},{2,3},{3,4},{4,5},{5,6},{6,7},{7,0},{8,15},{9,8},{10,9... | collective-permute-start | bytes 1671176 | tf_op jit(solution)/shard_map/ppermute | solution.py:327
  20.2 7.2 %collective-permute-done.7.refs_1_ = bf16[272,1024]{1,0:T(8,128)(2,1)S(1)} collective-permute-done((bf16[272,1024]{1,0:T(8,128)(2,1)S(1)}, bf16[272,1024]{1,0:T(8,128)(2,1)S(1)}, u32[]{:S(2)}, u32[]{:S(2)}) %collective-permute-start.7) | collective-permute-done | bytes 557088 | tf_op jit(solution)/shard_map/ppermute | solution.py:329
  27.3 3.7 %collective-permute-start.8 = (bf16[272,1024]{1,0:T(8,128)(2,1)S(1)}, bf16[272,1024]{1,0:T(8,128)(2,1)S(1)}, u32[]{:S(2)}, u32[]{:S(2)}) collective-permute-start(bf16[272,1024]{1,0:T(8,128)(2,1)S(1)} %collective-permute-done.7.refs_1_), channel_id=1, source_target_pairs={{1,0},{2,1},{3,2},{4,3},{5,4},{6,5},{7,6},{0,7},{15,8},{8,9},{9,10... | collective-permute-start | bytes 1671176 | tf_op jit(solution)/shard_map/ppermute | solution.py:329
  31.8 1.3 collective-permute-start.5
  33.0 10.0 %collective-permute-done.10.refs_5_.refs_7_ = bf16[272,1024]{1,0:T(8,128)(2,1)S(1)} collective-permute-done((bf16[272,1024]{1,0:T(8,128)(2,1)S(1)}, bf16[272,1024]{1,0:T(8,128)(2,1)S(1)}, u32[]{:S(2)}, u32[]{:S(2)}) %collective-permute-start.10) | collective-permute-done | bytes 557088 | tf_op jit(solution)/shard_map/ppermute | solution.py:327
  43.1 1.0 collective-permute-done.8.refs_2_
  44.1 3.7 %collective-permute-start.9 = (bf16[272,1024]{1,0:T(8,128)(2,1)S(1)}, bf16[272,1024]{1,0:T(8,128)(2,1)S(1)}, u32[]{:S(2)}, u32[]{:S(2)}) collective-permute-start(bf16[272,1024]{1,0:T(8,128)(2,1)S(1)} %collective-permute-done.8.refs_2_), channel_id=1, source_target_pairs={{1,0},{2,1},{3,2},{4,3},{5,4},{6,5},{7,6},{0,7},{15,8},{8,9},{9,10... | collective-permute-start | bytes 1671176 | tf_op jit(solution)/shard_map/ppermute | solution.py:329
  47.8 7.5 %collective-permute-done.2.refs_2_ = bf16[256,1024]{1,0:T(8,128)(2,1)S(1)} collective-permute-done((bf16[256,1024]{1,0:T(8,128)(2,1)S(1)}, bf16[256,1024]{1,0:T(8,128)(2,1)S(1)}, u32[]{:S(2)}, u32[]{:S(2)}) %collective-permute-start.2) | collective-permute-done | bytes 524320 | tf_op jit(solution)/shard_map/ppermute | solution.py:329
  55.3 3.7 %collective-permute-start.3 = (bf16[256,1024]{1,0:T(8,128)(2,1)S(1)}, bf16[256,1024]{1,0:T(8,128)(2,1)S(1)}, u32[]{:S(2)}, u32[]{:S(2)}) collective-permute-start(bf16[256,1024]{1,0:T(8,128)(2,1)S(1)} %collective-permute-done.2.refs_2_), channel_id=1, source_target_pairs={{1,0},{2,1},{3,2},{4,3},{5,4},{6,5},{7,6},{0,7},{15,8},{8,9},{9,10... | collective-permute-start | bytes 1572872 | tf_op jit(solution)/shard_map/ppermute | solution.py:329
  59.0 7.2 %collective-permute-done.11.refs_4_.refs_6_ = bf16[272,1024]{1,0:T(8,128)(2,1)S(1)} collective-permute-done((bf16[272,1024]{1,0:T(8,128)(2,1)S(1)}, bf16[272,1024]{1,0:T(8,128)(2,1)S(1)}, u32[]{:S(2)}, u32[]{:S(2)}) %collective-permute-start.11) | collective-permute-done | bytes 557088 | tf_op jit(solution)/shard_map/ppermute | solution.py:327
  66.2 1.0 collective-permute-done.9.refs_3_
  67.3 3.7 %collective-permute-start.12 = (bf16[272,1024]{1,0:T(8,128)(2,1)S(1)}, bf16[272,1024]{1,0:T(8,128)(2,1)S(1)}, u32[]{:S(2)}, u32[]{:S(2)}) collective-permute-start(bf16[272,1024]{1,0:T(8,128)(2,1)S(1)} %collective-permute-done.9.refs_3_), channel_id=1, source_target_pairs={{1,0},{2,1},{3,2},{4,3},{5,4},{6,5},{7,6},{0,7},{15,8},{8,9},{9,10... | collective-permute-start | bytes 1671176 | tf_op jit(solution)/shard_map/ppermute | solution.py:329
  71.0 7.5 %collective-permute-done.3.refs_3_ = bf16[256,1024]{1,0:T(8,128)(2,1)S(1)} collective-permute-done((bf16[256,1024]{1,0:T(8,128)(2,1)S(1)}, bf16[256,1024]{1,0:T(8,128)(2,1)S(1)}, u32[]{:S(2)}, u32[]{:S(2)}) %collective-permute-start.3) | collective-permute-done | bytes 524320 | tf_op jit(solution)/shard_map/ppermute | solution.py:329
  78.5 3.0 %shard_map.74 = (bf16[1024,1024]{1,0:T(8,128)(2,1)S(1)}, bf16[128,1024]{1,0:T(8,128)(2,1)S(1)}, bf16[1024,1024]{1,0:T(8,128)(2,1)S(1)}) custom-call(bf16[256,1024]{1,0:T(8,128)(2,1)S(1)} %bitcast.4, bf16[256,1024]{1,0:T(8,128)(2,1)S(1)} %collective-permute-done.refs_1_, bf16[256,1024]{1,0:T(8,128)(2,1)S(1)} %collective-permute-done.2.refs_2_, ...), custom_call_target="tpu_custom_call" | custom-call | flops 2147483648 | bytes 6291456 | tf_op jit(solution)/shard_map/pallas_call | solution.py:362
  81.6 2.2 %shard_map.75 = (bf16[1024,1024]{1,0:T(8,128)(2,1)S(1)}, bf16[1024,1024]{1,0:T(8,128)(2,1)S(1)}, bf16[1024,1024]{1,0:T(8,128)(2,1)S(1)}) custom-call(bf16[1024,1024]{1,0:T(8,128)(2,1)S(1)} %get-tuple-element.43.two_ref, bf16[272,1024]{1,0:T(8,128)(2,1)S(1)} %shard_map.73.refs_0_, bf16[272,1024]{1,0:T(8,128)(2,1)S(1)} %collective-permute-done.7.refs_1_, ...), custom_call_target="tpu_custom_call" | custom-call | flops 2147483648 | bytes 6291456 | tf_op jit(solution)/shard_map/pallas_call | solution.py:367
  83.8 5.6 %collective-permute-done.13.refs_5_ = bf16[272,1024]{1,0:T(8,128)(2,1)S(1)} collective-permute-done((bf16[272,1024]{1,0:T(8,128)(2,1)S(1)}, bf16[272,1024]{1,0:T(8,128)(2,1)S(1)}, u32[]{:S(2)}, u32[]{:S(2)}) %collective-permute-start.13) | collective-permute-done | bytes 557088 | tf_op jit(solution)/shard_map/ppermute | solution.py:327
  89.4 3.6 %shard_map.76 = (bf16[1024,1024]{1,0:T(8,128)(2,1)S(1)}, bf16[128,1024]{1,0:T(8,128)(2,1)S(1)}, bf16[128,1024]{1,0:T(8,128)(2,1)S(1)}, bf16[1024,1024]{1,0:T(8,1...) custom-call(bf16[1024,1024]{1,0:T(8,128)(2,1)S(1)} %get-tuple-elemen, ...), custom_call_target="tpu_custom_call", output_to_operand_aliasing={{3}: (1, {}), {4}: (2, {}), {5}: (3, {})} | custom-call | flops 2147483648 | bytes 6291456 | tf_op jit(solution)/shard_map/pallas_call | solution.py:371
  93.0 2.5 %collective-permute-start.14 = (bf16[1024,1024]{1,0:T(8,128)(2,1)S(1)}, bf16[1024,1024]{1,0:T(8,128)(2,1)S(1)}, u32[]{:S(2)}, u32[]{:S(2)}) collective-permute-start(bf16[1024,1024]{1,0:T(8,128)(2,1)S(1)} %get-tuple-element.47.own_ref), channel_id=1, source_target_pairs={{0,8},{16,24},{32,40},{48,56},{64,72},{80,88},{96,104},{112,120},{... | collective-permute-start | bytes 6291464 | tf_op jit(solution)/shard_map/ppermute | solution.py:379
  95.5 1.8 %shard_map.77 = (f32[4,1024]{1,0:T(4,128)S(1)}, bf16[16,1024]{1,0:T(8,128)(2,1)S(1)}) custom-call(f32[16,1024]{1,0:T(8,128)S(1)} %get-tuple-element.48.drive_ref, bf16[1024,1024]{1,0:T(8,128)(2,1)S(1)} %get-tuple-element.49.second_ref, bf16[1024,1024]{1,0:T(8,128)(2,1)S(1)} %get-tuple-element.50.third_ref, bf16[1024,1024]{1,0:T(8,128)(2,1)S(1)} %get-tuple-element.51.fourth_ref), custom_call_target="tpu_custom_call" | custom-call | flops 100663296 | bytes 6291456 | tf_op jit(solution)/shard_map/pallas_call | solution.py:380
  97.3 1.3 collective-permute-start.15
  98.6 0.8 collective-permute-done.15.other_term_ref
  99.4 0.8 collective-permute-start.24
  100.3 0.7 collective-permute-start.25
  110.3 1.3 collective-permute-start.30
  111.6 35.1 %collective-permute-done.30.got_ref = f32[1,1024]{1,0:T(1,128)S(1)} collective-permute-done((f32[1,1024]{1,0:T(1,128)S(1)}, f32[1,1024]{1,0:T(1,128)S(1)}, u32[]{:S(2)}, u32[]{:S(2)}) %collective-permute-start.30) | collective-permute-done | bytes 4128 | tf_op jit(solution)/shard_map/ppermute | solution.py:432
  146.6 0.8 shard_map.95
  (67 shorter events, 10.0 us)
Async XLA Ops:
  0.0 7.5 %copy-start.2 = (s32[4,32]{1,0:T(4,128)S(1)}, s32[4,32]{1,0:T(4,128)}, u32[]{:S(2)}) copy-start(s32[4,32]{1,0:T(4,128)} %rows_ref.1) | copy-start | bytes 1540
  1.5 16.8 %collective-permute-start.1 = (bf16[256,1024]{1,0:T(8,128)(2,1)S(1)}, bf16[256,1024]{1,0:T(8,128)(2,1)S(1)}, u32[]{:S(2)}, u32[]{:S(2)}) collective-permute-start(bf16[256,1024]{1,0:T(8,128)(2,1)S(1)} %bitcast.2), channel_id=1, source_target_pairs={{0,1},{1,2},{2,3},{3,4},{4,5},{5,6},{6,7},{7,0},{8,15},{9,8},{10,9... | collective-permute-start | bytes 1572872 | tf_op jit(solution)/shard_map/ppermute | solution.py:327
  3.4 15.1 %collective-permute-start = (bf16[256,1024]{1,0:T(8,128)(2,1)S(1)}, bf16[256,1024]{1,0:T(8,128)(2,1)S(1)}, u32[]{:S(2)}, u32[]{:S(2)}) collective-permute-start(bf16[256,1024]{1,0:T(8,128)(2,1)S(1)} %bitcast.3), channel_id=1, source_target_pairs={{1,0},{2,1},{3,2},{4,3},{5,4},{6,5},{7,6},{0,7},{15,8},{8,9},{9,10... | collective-permute-start | bytes 1572872 | tf_op jit(solution)/shard_map/ppermute | solution.py:329
  9.1 18.2 %collective-permute-start.7 = (bf16[272,1024]{1,0:T(8,128)(2,1)S(1)}, bf16[272,1024]{1,0:T(8,128)(2,1)S(1)}, u32[]{:S(2)}, u32[]{:S(2)}) collective-permute-start(bf16[272,1024]{1,0:T(8,128)(2,1)S(1)} %shard_map.73.refs_0_), channel_id=1, source_target_pairs={{1,0},{2,1},{3,2},{4,3},{5,4},{6,5},{7,6},{0,7},{15,8},{8,9},{9,10... | collective-permute-start | bytes 1671176 | tf_op jit(solution)/shard_map/ppermute | solution.py:329
  18.6 13.2 %collective-permute-start.4 = (bf16[256,1024]{1,0:T(8,128)(2,1)S(1)}, bf16[256,1024]{1,0:T(8,128)(2,1)S(1)}, u32[]{:S(2)}, u32[]{:S(2)}) collective-permute-start(bf16[256,1024]{1,0:T(8,128)(2,1)S(1)} %collective-permute-done.1.refs_7_), channel_id=1, source_target_pairs={{0,1},{1,2},{2,3},{3,4},{4,5},{5,6},{6,7},{7,0},{8,15},{9,8},{10,9... | collective-permute-start | bytes 1572872 | tf_op jit(solution)/shard_map/ppermute | solution.py:327
  18.6 24.5 %collective-permute-start.10 = (bf16[272,1024]{1,0:T(8,128)(2,1)S(1)}, bf16[272,1024]{1,0:T(8,128)(2,1)S(1)}, u32[]{:S(2)}, u32[]{:S(2)}) collective-permute-start(bf16[272,1024]{1,0:T(8,128)(2,1)S(1)} %shard_map.73.refs_0_), channel_id=1, source_target_pairs={{0,1},{1,2},{2,3},{3,4},{4,5},{5,6},{6,7},{7,0},{8,15},{9,8},{10,9... | collective-permute-start | bytes 1671176 | tf_op jit(solution)/shard_map/ppermute | solution.py:327
  27.3 16.8 %collective-permute-start.8 = (bf16[272,1024]{1,0:T(8,128)(2,1)S(1)}, bf16[272,1024]{1,0:T(8,128)(2,1)S(1)}, u32[]{:S(2)}, u32[]{:S(2)}) collective-permute-start(bf16[272,1024]{1,0:T(8,128)(2,1)S(1)} %collective-permute-done.7.refs_1_), channel_id=1, source_target_pairs={{1,0},{2,1},{3,2},{4,3},{5,4},{6,5},{7,6},{0,7},{15,8},{8,9},{9,10... | collective-permute-start | bytes 1671176 | tf_op jit(solution)/shard_map/ppermute | solution.py:329
  31.0 24.3 %collective-permute-start.2 = (bf16[256,1024]{1,0:T(8,128)(2,1)S(1)}, bf16[256,1024]{1,0:T(8,128)(2,1)S(1)}, u32[]{:S(2)}, u32[]{:S(2)}) collective-permute-start(bf16[256,1024]{1,0:T(8,128)(2,1)S(1)} %collective-permute-done.refs_1_), channel_id=1, source_target_pairs={{1,0},{2,1},{3,2},{4,3},{5,4},{6,5},{7,6},{0,7},{15,8},{8,9},{9,10... | collective-permute-start | bytes 1572872 | tf_op jit(solution)/shard_map/ppermute | solution.py:329
  31.8 27.3 %collective-permute-start.5 = (bf16[256,1024]{1,0:T(8,128)(2,1)S(1)}, bf16[256,1024]{1,0:T(8,128)(2,1)S(1)}, u32[]{:S(2)}, u32[]{:S(2)}) collective-permute-start(bf16[256,1024]{1,0:T(8,128)(2,1)S(1)} %collective-permute-done.4.refs_6_), channel_id=1, source_target_pairs={{0,1},{1,2},{2,3},{3,4},{4,5},{5,6},{6,7},{7,0},{8,15},{9,8},{10,9... | collective-permute-start | bytes 1572872 | tf_op jit(solution)/shard_map/ppermute | solution.py:327
  43.1 23.2 %collective-permute-start.11 = (bf16[272,1024]{1,0:T(8,128)(2,1)S(1)}, bf16[272,1024]{1,0:T(8,128)(2,1)S(1)}, u32[]{:S(2)}, u32[]{:S(2)}) collective-permute-start(bf16[272,1024]{1,0:T(8,128)(2,1)S(1)} %collective-permute-done.10.refs_5_.refs_7_), channel_id=1, source_target_pairs={{0,1},{1,2},{2,3},{3,4},{4,5},{5,6},{6,7},{7,0},{8,15},{9,8},{10,9... | collective-permute-start | bytes 1671176 | tf_op jit(solution)/shard_map/ppermute | solution.py:327
  44.1 23.2 %collective-permute-start.9 = (bf16[272,1024]{1,0:T(8,128)(2,1)S(1)}, bf16[272,1024]{1,0:T(8,128)(2,1)S(1)}, u32[]{:S(2)}, u32[]{:S(2)}) collective-permute-start(bf16[272,1024]{1,0:T(8,128)(2,1)S(1)} %collective-permute-done.8.refs_2_), channel_id=1, source_target_pairs={{1,0},{2,1},{3,2},{4,3},{5,4},{6,5},{7,6},{0,7},{15,8},{8,9},{9,10... | collective-permute-start | bytes 1671176 | tf_op jit(solution)/shard_map/ppermute | solution.py:329
  55.3 23.2 %collective-permute-start.3 = (bf16[256,1024]{1,0:T(8,128)(2,1)S(1)}, bf16[256,1024]{1,0:T(8,128)(2,1)S(1)}, u32[]{:S(2)}, u32[]{:S(2)}) collective-permute-start(bf16[256,1024]{1,0:T(8,128)(2,1)S(1)} %collective-permute-done.2.refs_2_), channel_id=1, source_target_pairs={{1,0},{2,1},{3,2},{4,3},{5,4},{6,5},{7,6},{0,7},{15,8},{8,9},{9,10... | collective-permute-start | bytes 1572872 | tf_op jit(solution)/shard_map/ppermute | solution.py:329
  59.0 19.5 %collective-permute-start.6 = (bf16[256,1024]{1,0:T(8,128)(2,1)S(1)}, bf16[256,1024]{1,0:T(8,128)(2,1)S(1)}, u32[]{:S(2)}, u32[]{:S(2)}) collective-permute-start(bf16[256,1024]{1,0:T(8,128)(2,1)S(1)} %collective-permute-done.5.refs_5_), channel_id=1, source_target_pairs={{0,1},{1,2},{2,3},{3,4},{4,5},{5,6},{6,7},{7,0},{8,15},{9,8},{10,9... | collective-permute-start | bytes 1572872 | tf_op jit(solution)/shard_map/ppermute | solution.py:327
  66.2 23.2 %collective-permute-start.13 = (bf16[272,1024]{1,0:T(8,128)(2,1)S(1)}, bf16[272,1024]{1,0:T(8,128)(2,1)S(1)}, u32[]{:S(2)}, u32[]{:S(2)}) collective-permute-start(bf16[272,1024]{1,0:T(8,128)(2,1)S(1)} %collective-permute-done.11.refs_4_.refs_6_), channel_id=1, source_target_pairs={{0,1},{1,2},{2,3},{3,4},{4,5},{5,6},{6,7},{7,0},{8,15},{9,8},{10,9... | collective-permute-start | bytes 1671176 | tf_op jit(solution)/shard_map/ppermute | solution.py:327
  67.3 22.1 %collective-permute-start.12 = (bf16[272,1024]{1,0:T(8,128)(2,1)S(1)}, bf16[272,1024]{1,0:T(8,128)(2,1)S(1)}, u32[]{:S(2)}, u32[]{:S(2)}) collective-permute-start(bf16[272,1024]{1,0:T(8,128)(2,1)S(1)} %collective-permute-done.9.refs_3_), channel_id=1, source_target_pairs={{1,0},{2,1},{3,2},{4,3},{5,4},{6,5},{7,6},{0,7},{15,8},{8,9},{9,10... | collective-permute-start | bytes 1671176 | tf_op jit(solution)/shard_map/ppermute | solution.py:329
  93.0 6.4 %collective-permute-start.14 = (bf16[1024,1024]{1,0:T(8,128)(2,1)S(1)}, bf16[1024,1024]{1,0:T(8,128)(2,1)S(1)}, u32[]{:S(2)}, u32[]{:S(2)}) collective-permute-start(bf16[1024,1024]{1,0:T(8,128)(2,1)S(1)} %get-tuple-element.47.own_ref), channel_id=1, source_target_pairs={{0,8},{16,24},{32,40},{48,56},{64,72},{80,88},{96,104},{112,120},{... | collective-permute-start | bytes 6291464 | tf_op jit(solution)/shard_map/ppermute | solution.py:379
  97.3 2.1 %collective-permute-start.15 = (bf16[16,1024]{1,0:T(8,128)(2,1)S(1)}, bf16[16,1024]{1,0:T(8,128)(2,1)S(1)}, u32[]{:S(2)}, u32[]{:S(2)}) collective-permute-start(bf16[16,1024]{1,0:T(8,128)(2,1)S(1)} %get-tuple-element.52.own_term_ref), channel_id=1, source_target_pairs={{0,8},{16,24},{32,40},{48,56},{64,72},{80,88},{96,104},{112,120},{... | collective-permute-start | bytes 98312 | tf_op jit(solution)/shard_map/ppermute | solution.py:383
  99.4 7.9 %collective-permute-start.24 = (bf16[512,1024]{1,0:T(8,128)(2,1)S(1)}, bf16[512,1024]{1,0:T(8,128)(2,1)S(1)}, u32[]{:S(2)}, u32[]{:S(2)}) collective-permute-start(bf16[512,1024]{1,0:T(8,128)(2,1)S(1)} %shard_map.81.turned0_ref), channel_id=1, source_target_pairs={{136,152},{168,184},{200,216},{232,248},{137,153},{169,185},{201,2... | collective-permute-start | bytes 3145736 | tf_op jit(solution)/shard_map/ppermute | solution.py:393
  100.3 7.0 %collective-permute-start.25 = (bf16[528,1024]{1,0:T(8,128)(2,1)S(1)}, bf16[528,1024]{1,0:T(8,128)(2,1)S(1)}, u32[]{:S(2)}, u32[]{:S(2)}) collective-permute-start(bf16[528,1024]{1,0:T(8,128)(2,1)S(1)} %shard_map.78.turned1_ref), channel_id=1, source_target_pairs={{136,152},{168,184},{200,216},{232,248},{137,153},{169,185},{201,2... | collective-permute-start | bytes 3244040 | tf_op jit(solution)/shard_map/ppermute | solution.py:395
  101.1 0.7 collective-permute-start.16
  101.8 0.7 collective-permute-start.17
  102.5 0.7 collective-permute-start.18
  103.2 0.7 collective-permute-start.19
  103.9 1.3 collective-permute-start.20
  105.2 0.7 collective-permute-start.21
  105.9 0.7 collective-permute-start.22
  106.6 0.8 collective-permute-start.23
  107.4 0.7 collective-permute-start.26
  108.1 0.7 collective-permute-start.27
  108.9 1.3 collective-permute-start.29
  109.5 0.7 collective-permute-start.28
  110.3 36.4 %collective-permute-start.30 = (f32[1,1024]{1,0:T(1,128)S(1)}, f32[1,1024]{1,0:T(1,128)S(1)}, u32[]{:S(2)}, u32[]{:S(2)}) collective-permute-start(f32[1,1024]{1,0:T(1,128)S(1)} %shard_map.94.begin_ref), channel_id=1, source_target_pairs={{8,0},{24,16},{40,32},{56,48},{72,64},{88,80},{104,96},{120,112},{... | collective-permute-start | bytes 12296 | tf_op jit(solution)/shard_map/ppermute | solution.py:432
  (5 other events, 31.6 us)

commit v13 on v12

--- a/solution.py
+++ b/solution.py
@@ -164,13 +164,26 @@
             fourth_ref[at, :] = pieces[r][width:2 * width, :]
             three_ref[at, :] = jnp.dot(pieces[r][:width, :], two_ref[...], preferred_element_type=F32).astype(BF16)
             drive += pieces[r][2 * width:, :].astype(F32)
-    matmul(fourth_ref, three_ref, four_ref)
     mine = pl.ds(pl.multiple_of(lax.axis_index("state") * width, width), width)
     slab3_ref[...] = three_ref[mine, :]
-    slab4_ref[...] = four_ref[mine, :]
+
+    @pl.when(core_here() == 0)
+    def _():
+        matmul(fourth_ref, three_ref, four_ref)
+        slab4_ref[...] = four_ref[mine, :]
+
     for copy in parts:
         copy.wait()
     drive_ref[...] = drive + jnp.sum(parts_ref[...].astype(F32), axis=0)
+
+
+def second_kernel(three_ref, fourth_ref, four_ref, slab4_ref):
+    width = slab4_ref.shape[0]
+
+    @pl.when(core_here() != 0)
+    def _():
+        matmul(fourth_ref, three_ref, four_ref)
+        slab4_ref[...] = four_ref[pl.ds(pl.multiple_of(lax.axis_index("state") * width, width), width), :]
 
 
 def local_kernel(drive_ref, second_ref, third_ref, fourth_ref, locals_ref, term_ref):
@@ -266,7 +279,7 @@
 
 
 def ready_kernel(other_ref, other_term_ref, locals_ref, after_ref, *refs):
-    slabs, (maps_ref, terms_ref) = refs[:-2], refs[-2:]
+    slabs, (second_ref, maps_ref, terms_ref) = refs[:-3], refs[-3:]
     width, size = slabs[1].shape
     mine = pl.ds(pl.multiple_of(lax.axis_index("state") * width, width), width)
 
@@ -278,7 +291,7 @@
 
     @pl.when(core_here() != 0)
     def _():
-        for j, slab_ref in enumerate(slabs):
+        for j, slab_ref in enumerate(slabs[:-1] + (second_ref,)):
             at = slice(j * width, (j + 1) * width)
             out = jnp.dot(slab_ref[:width, :], other_ref[...], preferred_element_type=F32)
             maps_ref[:, at] = out.T.astype(BF16)
@@ -368,7 +381,7 @@
         functools.partial(three_kernel, count, have), (matrix, matrix, matrix), [V] + [A] * len(have),
         [pltpu.SemaphoreType.DMA((2 * len(have),))], flops=2 * size ** 3, moved=6 * size ** 2,
     )(two, *[late[r] for r in have])
-    own, slab3, slab4, _, third, fourth, drive = call(
+    sent, slab3, slab4, three, third, fourth, drive = call(
         functools.partial(four_kernel, count, have),
         (matrix, slab, slab, matrix, matrix, matrix, jax.ShapeDtypeStruct((16, size), F32)),
         [V] * 4 + [A if r in have else V for r in range(count)],
@@ -376,7 +389,8 @@
         flops=2 * size ** 3, moved=6 * size ** 2, aliases={1: 3, 2: 4, 3: 5},
     )(two, three, third, fourth, *late)
     pairs = [(i, i + 1) for i in range(0, blocks_of_time, 2)]
-    other = lax.ppermute(own, "tm", pairs)
+    other = lax.ppermute(sent, "tm", pairs)
+    own, slab5 = call(second_kernel, (matrix, slab), [V] * 2, flops=2 * size ** 3, moved=6 * size ** 2)(three, fourth)
     locals_, own_term = call(
         local_kernel, (steps, rows), [V] * 4, flops=96 * size ** 2, moved=6 * size ** 2
     )(drive, second, third, fourth)
@@ -412,8 +426,8 @@
             maps, terms = call(
                 ready_kernel,
                 (jax.ShapeDtypeStruct((size, steps_here * width), BF16), jax.ShapeDtypeStruct((steps_here, width), F32)),
-                [V] * 8, flops=size ** 3, moved=4 * size ** 2,
-            )(other, other_term, locals_, value, early[0], slab2, slab3, slab4)
+                [V] * 9, flops=size ** 3, moved=4 * size ** 2,
+            )(other, other_term, locals_, value, early[0], slab2, slab3, slab4, slab5)
         if turn == 4:
             came = after(came, maps)
     double0 = call(functools.partial(double_kernel, 0, firsts), part, [V] * 3, **half_cost)(before0, turned0, turned1)

time: 148 us -> 147 us (level)
  no operation moved by 1% of the time
where the time goes in v13:
time: 147 us; the launch traced here: 146 us
  waiting for transfers between devices  91.2 us (62%)
  starting transfers between devices  39.5 us (27%)
  Pallas kernels  13.8 us (9%)
    ppermute x1, waiting for transfers between devices, shards(): got = lax.ppermute(begin, 'tm', [(b, a) for a, b in pairs])  35.1 us
    ppermute x7, waiting for transfers between devices, ring_rounds(): pieces[count - r] = lax.ppermute(left, ('tm', 'state'), forward)  30.7 us
    ppermute x7, waiting for transfers between devices, ring_rounds(): pieces[r] = lax.ppermute(right, ('tm', 'state'), backward)  24.6 us
    ppermute x7, starting transfers between devices, ring_rounds(): pieces[r] = lax.ppermute(right, ('tm', 'state'), backward)  20.8 us
    ppermute x8, starting transfers between devices, shards(): lax.ppermute(value, 'tm', [(2 * turn + 1, 2 * turn + (3 if turn + 1 < fir...  5.51 us
    ppermute x7, starting transfers between devices, ring_rounds(): pieces[count - r] = lax.ppermute(left, ('tm', 'state'), forward)  4.9 us
    pallas_call x1, Pallas kernels, shards(): call(functools.partial(four_kernel, count, have), (matrix, slab, slab, ma...  3.63 us
    pallas_call x1, Pallas kernels, shards(): call(functools.partial(two_kernel, count), (matrix, slab, matrix), [A] *...  3.03 us
  transfers between devices with their start and end apart: 31, of which 13 were waited for; matrix products, arithmetic and copies ran while one was open for 0% of the time, Pallas kernels for 6%

profile of v13, /device:TPU:30, one launch (start us, length us, event | category | flops | bytes accessed | tf_op | source)
XLA Modules:
  0.0 146.4 jit_solution(12956612838003376376)
XLA Ops:
  0.0 1.4 fusion
  1.5 2.0 %collective-permute-start.1 = (bf16[256,1024]{1,0:T(8,128)(2,1)S(1)}, bf16[256,1024]{1,0:T(8,128)(2,1)S(1)}, u32[]{:S(2)}, u32[]{:S(2)}) collective-permute-start(bf16[256,1024]{1,0:T(8,128)(2,1)S(1)} %bitcast.2), channel_id=1, source_target_pairs={{0,1},{1,2},{2,3},{3,4},{4,5},{5,6},{6,7},{7,0},{8,15},{9,8},{10,9... | collective-permute-start | bytes 1572872 | tf_op jit(solution)/shard_map/ppermute | solution.py:340
  3.4 4.0 %collective-permute-start = (bf16[256,1024]{1,0:T(8,128)(2,1)S(1)}, bf16[256,1024]{1,0:T(8,128)(2,1)S(1)}, u32[]{:S(2)}, u32[]{:S(2)}) collective-permute-start(bf16[256,1024]{1,0:T(8,128)(2,1)S(1)} %bitcast.3), channel_id=1, source_target_pairs={{1,0},{2,1},{3,2},{4,3},{5,4},{6,5},{7,6},{0,7},{15,8},{8,9},{9,10... | collective-permute-start | bytes 1572872 | tf_op jit(solution)/shard_map/ppermute | solution.py:342
  7.5 1.6 %shard_map.73.refs_0_ = bf16[272,1024]{1,0:T(8,128)(2,1)S(1)} custom-call(s32[4,32]{1,0:T(4,128)S(1)} %copy-done.2, s32[4,32]{1,0:T(4,128)S(1)} %copy-done.3, bf16[4,4096]{1,0:T(4,128)(2,1)S(1)} %multiply_convert_fusion.values_ref, bf16[4,32,64,64]{3,2,1,0:T(8,128)(2,1)S(1)} %copy-done, bf16[2,128,1024]{2,1,0:T(8,128)(2,1)S(1)} %get-tuple-element.83.maps_ref), custom_call_target="tpu_custom_call" | custom-call | flops 10000000 | bytes 2097152 | tf_op jit(solution)/shard_map/pallas_call | solution.py:362
  9.1 2.0 %collective-permute-start.7 = (bf16[272,1024]{1,0:T(8,128)(2,1)S(1)}, bf16[272,1024]{1,0:T(8,128)(2,1)S(1)}, u32[]{:S(2)}, u32[]{:S(2)}) collective-permute-start(bf16[272,1024]{1,0:T(8,128)(2,1)S(1)} %shard_map.73.refs_0_), channel_id=1, source_target_pairs={{1,0},{2,1},{3,2},{4,3},{5,4},{6,5},{7,6},{0,7},{15,8},{8,9},{9,10... | collective-permute-start | bytes 1671176 | tf_op jit(solution)/shard_map/ppermute | solution.py:342
  11.1 7.2 %collective-permute-done.1.refs_7_ = bf16[256,1024]{1,0:T(8,128)(2,1)S(1)} collective-permute-done((bf16[256,1024]{1,0:T(8,128)(2,1)S(1)}, bf16[256,1024]{1,0:T(8,128)(2,1)S(1)}, u32[]{:S(2)}, u32[]{:S(2)}) %collective-permute-start.1) | collective-permute-done | bytes 524320 | tf_op jit(solution)/shard_map/ppermute | solution.py:340
  18.6 1.6 %collective-permute-start.10 = (bf16[272,1024]{1,0:T(8,128)(2,1)S(1)}, bf16[272,1024]{1,0:T(8,128)(2,1)S(1)}, u32[]{:S(2)}, u32[]{:S(2)}) collective-permute-start(bf16[272,1024]{1,0:T(8,128)(2,1)S(1)} %shard_map.73.refs_0_), channel_id=1, source_target_pairs={{0,1},{1,2},{2,3},{3,4},{4,5},{5,6},{6,7},{7,0},{8,15},{9,8},{10,9... | collective-permute-start | bytes 1671176 | tf_op jit(solution)/shard_map/ppermute | solution.py:340
  20.2 7.2 %collective-permute-done.7.refs_1_ = bf16[272,1024]{1,0:T(8,128)(2,1)S(1)} collective-permute-done((bf16[272,1024]{1,0:T(8,128)(2,1)S(1)}, bf16[272,1024]{1,0:T(8,128)(2,1)S(1)}, u32[]{:S(2)}, u32[]{:S(2)}) %collective-permute-start.7) | collective-permute-done | bytes 557088 | tf_op jit(solution)/shard_map/ppermute | solution.py:342
  27.3 3.7 %collective-permute-start.8 = (bf16[272,1024]{1,0:T(8,128)(2,1)S(1)}, bf16[272,1024]{1,0:T(8,128)(2,1)S(1)}, u32[]{:S(2)}, u32[]{:S(2)}) collective-permute-start(bf16[272,1024]{1,0:T(8,128)(2,1)S(1)} %collective-permute-done.7.refs_1_), channel_id=1, source_target_pairs={{1,0},{2,1},{3,2},{4,3},{5,4},{6,5},{7,6},{0,7},{15,8},{8,9},{9,10... | collective-permute-start | bytes 1671176 | tf_op jit(solution)/shard_map/ppermute | solution.py:342
  31.8 1.3 collective-permute-start.5
  33.0 10.0 %collective-permute-done.10.refs_5_.refs_7_ = bf16[272,1024]{1,0:T(8,128)(2,1)S(1)} collective-permute-done((bf16[272,1024]{1,0:T(8,128)(2,1)S(1)}, bf16[272,1024]{1,0:T(8,128)(2,1)S(1)}, u32[]{:S(2)}, u32[]{:S(2)}) %collective-permute-start.10) | collective-permute-done | bytes 557088 | tf_op jit(solution)/shard_map/ppermute | solution.py:340
  43.1 1.0 collective-permute-done.8.refs_2_
  44.1 3.7 %collective-permute-start.9 = (bf16[272,1024]{1,0:T(8,128)(2,1)S(1)}, bf16[272,1024]{1,0:T(8,128)(2,1)S(1)}, u32[]{:S(2)}, u32[]{:S(2)}) collective-permute-start(bf16[272,1024]{1,0:T(8,128)(2,1)S(1)} %collective-permute-done.8.refs_2_), channel_id=1, source_target_pairs={{1,0},{2,1},{3,2},{4,3},{5,4},{6,5},{7,6},{0,7},{15,8},{8,9},{9,10... | collective-permute-start | bytes 1671176 | tf_op jit(solution)/shard_map/ppermute | solution.py:342
  47.8 7.5 %collective-permute-done.2.refs_2_ = bf16[256,1024]{1,0:T(8,128)(2,1)S(1)} collective-permute-done((bf16[256,1024]{1,0:T(8,128)(2,1)S(1)}, bf16[256,1024]{1,0:T(8,128)(2,1)S(1)}, u32[]{:S(2)}, u32[]{:S(2)}) %collective-permute-start.2) | collective-permute-done | bytes 524320 | tf_op jit(solution)/shard_map/ppermute | solution.py:342
  55.3 3.7 %collective-permute-start.3 = (bf16[256,1024]{1,0:T(8,128)(2,1)S(1)}, bf16[256,1024]{1,0:T(8,128)(2,1)S(1)}, u32[]{:S(2)}, u32[]{:S(2)}) collective-permute-start(bf16[256,1024]{1,0:T(8,128)(2,1)S(1)} %collective-permute-done.2.refs_2_), channel_id=1, source_target_pairs={{1,0},{2,1},{3,2},{4,3},{5,4},{6,5},{7,6},{0,7},{15,8},{8,9},{9,10... | collective-permute-start | bytes 1572872 | tf_op jit(solution)/shard_map/ppermute | solution.py:342
  59.0 7.2 %collective-permute-done.11.refs_4_.refs_6_ = bf16[272,1024]{1,0:T(8,128)(2,1)S(1)} collective-permute-done((bf16[272,1024]{1,0:T(8,128)(2,1)S(1)}, bf16[272,1024]{1,0:T(8,128)(2,1)S(1)}, u32[]{:S(2)}, u32[]{:S(2)}) %collective-permute-start.11) | collective-permute-done | bytes 557088 | tf_op jit(solution)/shard_map/ppermute | solution.py:340
  66.2 1.0 collective-permute-done.9.refs_3_
  67.3 3.7 %collective-permute-start.12 = (bf16[272,1024]{1,0:T(8,128)(2,1)S(1)}, bf16[272,1024]{1,0:T(8,128)(2,1)S(1)}, u32[]{:S(2)}, u32[]{:S(2)}) collective-permute-start(bf16[272,1024]{1,0:T(8,128)(2,1)S(1)} %collective-permute-done.9.refs_3_), channel_id=1, source_target_pairs={{1,0},{2,1},{3,2},{4,3},{5,4},{6,5},{7,6},{0,7},{15,8},{8,9},{9,10... | collective-permute-start | bytes 1671176 | tf_op jit(solution)/shard_map/ppermute | solution.py:342
  71.0 7.5 %collective-permute-done.3.refs_3_ = bf16[256,1024]{1,0:T(8,128)(2,1)S(1)} collective-permute-done((bf16[256,1024]{1,0:T(8,128)(2,1)S(1)}, bf16[256,1024]{1,0:T(8,128)(2,1)S(1)}, u32[]{:S(2)}, u32[]{:S(2)}) %collective-permute-start.3) | collective-permute-done | bytes 524320 | tf_op jit(solution)/shard_map/ppermute | solution.py:342
  78.5 3.0 %shard_map.74 = (bf16[1024,1024]{1,0:T(8,128)(2,1)S(1)}, bf16[128,1024]{1,0:T(8,128)(2,1)S(1)}, bf16[1024,1024]{1,0:T(8,128)(2,1)S(1)}) custom-call(bf16[256,1024]{1,0:T(8,128)(2,1)S(1)} %bitcast.4, bf16[256,1024]{1,0:T(8,128)(2,1)S(1)} %collective-permute-done.refs_1_, bf16[256,1024]{1,0:T(8,128)(2,1)S(1)} %collective-permute-done.2.refs_2_, ...), custom_call_target="tpu_custom_call" | custom-call | flops 2147483648 | bytes 6291456 | tf_op jit(solution)/shard_map/pallas_call | solution.py:375
  81.6 2.2 %shard_map.75 = (bf16[1024,1024]{1,0:T(8,128)(2,1)S(1)}, bf16[1024,1024]{1,0:T(8,128)(2,1)S(1)}, bf16[1024,1024]{1,0:T(8,128)(2,1)S(1)}) custom-call(bf16[1024,1024]{1,0:T(8,128)(2,1)S(1)} %get-tuple-element.46.two_ref, bf16[272,1024]{1,0:T(8,128)(2,1)S(1)} %shard_map.73.refs_0_, bf16[272,1024]{1,0:T(8,128)(2,1)S(1)} %collective-permute-done.7.refs_1_, ...), custom_call_target="tpu_custom_call" | custom-call | flops 2147483648 | bytes 6291456 | tf_op jit(solution)/shard_map/pallas_call | solution.py:380
  83.8 5.6 %collective-permute-done.13.refs_5_ = bf16[272,1024]{1,0:T(8,128)(2,1)S(1)} collective-permute-done((bf16[272,1024]{1,0:T(8,128)(2,1)S(1)}, bf16[272,1024]{1,0:T(8,128)(2,1)S(1)}, u32[]{:S(2)}, u32[]{:S(2)}) %collective-permute-start.13) | collective-permute-done | bytes 557088 | tf_op jit(solution)/shard_map/ppermute | solution.py:340
  89.4 3.6 %shard_map.76 = (bf16[1024,1024]{1,0:T(8,128)(2,1)S(1)}, bf16[128,1024]{1,0:T(8,128)(2,1)S(1)}, bf16[128,1024]{1,0:T(8,128)(2,1)S(1)}, bf16[1024,1024]{1,0:T(8,1...) custom-call(bf16[1024,1024]{1,0:T(8,128)(2,1)S(1)} %get-tuple-elemen, ...), custom_call_target="tpu_custom_call", output_to_operand_aliasing={{3}: (1, {}), {4}: (2, {}), {5}: (3, {})} | custom-call | flops 2147483648 | bytes 6291456 | tf_op jit(solution)/shard_map/pallas_call | solution.py:384
  93.0 1.4 collective-permute-start.14
  94.5 1.8 %shard_map.78 = (f32[4,1024]{1,0:T(4,128)S(1)}, bf16[16,1024]{1,0:T(8,128)(2,1)S(1)}) custom-call(f32[16,1024]{1,0:T(8,128)S(1)} %get-tuple-element.53.drive_ref, bf16[1024,1024]{1,0:T(8,128)(2,1)S(1)} %get-tuple-element.54.second_ref, bf16[1024,1024]{1,0:T(8,128)(2,1)S(1)} %get-tuple-element.55.third_ref, bf16[1024,1024]{1,0:T(8,128)(2,1)S(1)} %get-tuple-element.51.fourth_ref), custom_call_target="tpu_custom_call" | custom-call | flops 100663296 | bytes 6291456 | tf_op jit(solution)/shard_map/pallas_call | solution.py:394
  96.2 1.3 collective-permute-start.15
  97.6 0.8 collective-permute-done.15.other_term_ref
  98.4 0.8 collective-permute-start.24
  102.2 0.9 collective-permute-start.19
  109.2 1.3 collective-permute-start.30
  110.5 35.1 %collective-permute-done.30.got_ref = f32[1,1024]{1,0:T(1,128)S(1)} collective-permute-done((f32[1,1024]{1,0:T(1,128)S(1)}, f32[1,1024]{1,0:T(1,128)S(1)}, u32[]{:S(2)}, u32[]{:S(2)}) %collective-permute-start.30) | collective-permute-done | bytes 4128 | tf_op jit(solution)/shard_map/ppermute | solution.py:446
  145.6 0.8 shard_map.96
  (68 shorter events, 9.8 us)
Async XLA Ops:
  0.0 7.5 %copy-start.2 = (s32[4,32]{1,0:T(4,128)S(1)}, s32[4,32]{1,0:T(4,128)}, u32[]{:S(2)}) copy-start(s32[4,32]{1,0:T(4,128)} %rows_ref.1) | copy-start | bytes 1540
  1.5 16.8 %collective-permute-start.1 = (bf16[256,1024]{1,0:T(8,128)(2,1)S(1)}, bf16[256,1024]{1,0:T(8,128)(2,1)S(1)}, u32[]{:S(2)}, u32[]{:S(2)}) collective-permute-start(bf16[256,1024]{1,0:T(8,128)(2,1)S(1)} %bitcast.2), channel_id=1, source_target_pairs={{0,1},{1,2},{2,3},{3,4},{4,5},{5,6},{6,7},{7,0},{8,15},{9,8},{10,9... | collective-permute-start | bytes 1572872 | tf_op jit(solution)/shard_map/ppermute | solution.py:340
  3.4 15.1 %collective-permute-start = (bf16[256,1024]{1,0:T(8,128)(2,1)S(1)}, bf16[256,1024]{1,0:T(8,128)(2,1)S(1)}, u32[]{:S(2)}, u32[]{:S(2)}) collective-permute-start(bf16[256,1024]{1,0:T(8,128)(2,1)S(1)} %bitcast.3), channel_id=1, source_target_pairs={{1,0},{2,1},{3,2},{4,3},{5,4},{6,5},{7,6},{0,7},{15,8},{8,9},{9,10... | collective-permute-start | bytes 1572872 | tf_op jit(solution)/shard_map/ppermute | solution.py:342
  9.1 18.2 %collective-permute-start.7 = (bf16[272,1024]{1,0:T(8,128)(2,1)S(1)}, bf16[272,1024]{1,0:T(8,128)(2,1)S(1)}, u32[]{:S(2)}, u32[]{:S(2)}) collective-permute-start(bf16[272,1024]{1,0:T(8,128)(2,1)S(1)} %shard_map.73.refs_0_), channel_id=1, source_target_pairs={{1,0},{2,1},{3,2},{4,3},{5,4},{6,5},{7,6},{0,7},{15,8},{8,9},{9,10... | collective-permute-start | bytes 1671176 | tf_op jit(solution)/shard_map/ppermute | solution.py:342
  18.6 13.2 %collective-permute-start.4 = (bf16[256,1024]{1,0:T(8,128)(2,1)S(1)}, bf16[256,1024]{1,0:T(8,128)(2,1)S(1)}, u32[]{:S(2)}, u32[]{:S(2)}) collective-permute-start(bf16[256,1024]{1,0:T(8,128)(2,1)S(1)} %collective-permute-done.1.refs_7_), channel_id=1, source_target_pairs={{0,1},{1,2},{2,3},{3,4},{4,5},{5,6},{6,7},{7,0},{8,15},{9,8},{10,9... | collective-permute-start | bytes 1572872 | tf_op jit(solution)/shard_map/ppermute | solution.py:340
  18.6 24.5 %collective-permute-start.10 = (bf16[272,1024]{1,0:T(8,128)(2,1)S(1)}, bf16[272,1024]{1,0:T(8,128)(2,1)S(1)}, u32[]{:S(2)}, u32[]{:S(2)}) collective-permute-start(bf16[272,1024]{1,0:T(8,128)(2,1)S(1)} %shard_map.73.refs_0_), channel_id=1, source_target_pairs={{0,1},{1,2},{2,3},{3,4},{4,5},{5,6},{6,7},{7,0},{8,15},{9,8},{10,9... | collective-permute-start | bytes 1671176 | tf_op jit(solution)/shard_map/ppermute | solution.py:340
  27.3 16.8 %collective-permute-start.8 = (bf16[272,1024]{1,0:T(8,128)(2,1)S(1)}, bf16[272,1024]{1,0:T(8,128)(2,1)S(1)}, u32[]{:S(2)}, u32[]{:S(2)}) collective-permute-start(bf16[272,1024]{1,0:T(8,128)(2,1)S(1)} %collective-permute-done.7.refs_1_), channel_id=1, source_target_pairs={{1,0},{2,1},{3,2},{4,3},{5,4},{6,5},{7,6},{0,7},{15,8},{8,9},{9,10... | collective-permute-start | bytes 1671176 | tf_op jit(solution)/shard_map/ppermute | solution.py:342
  31.0 24.3 %collective-permute-start.2 = (bf16[256,1024]{1,0:T(8,128)(2,1)S(1)}, bf16[256,1024]{1,0:T(8,128)(2,1)S(1)}, u32[]{:S(2)}, u32[]{:S(2)}) collective-permute-start(bf16[256,1024]{1,0:T(8,128)(2,1)S(1)} %collective-permute-done.refs_1_), channel_id=1, source_target_pairs={{1,0},{2,1},{3,2},{4,3},{5,4},{6,5},{7,6},{0,7},{15,8},{8,9},{9,10... | collective-permute-start | bytes 1572872 | tf_op jit(solution)/shard_map/ppermute | solution.py:342
  31.8 27.3 %collective-permute-start.5 = (bf16[256,1024]{1,0:T(8,128)(2,1)S(1)}, bf16[256,1024]{1,0:T(8,128)(2,1)S(1)}, u32[]{:S(2)}, u32[]{:S(2)}) collective-permute-start(bf16[256,1024]{1,0:T(8,128)(2,1)S(1)} %collective-permute-done.4.refs_6_), channel_id=1, source_target_pairs={{0,1},{1,2},{2,3},{3,4},{4,5},{5,6},{6,7},{7,0},{8,15},{9,8},{10,9... | collective-permute-start | bytes 1572872 | tf_op jit(solution)/shard_map/ppermute | solution.py:340
  43.1 23.2 %collective-permute-start.11 = (bf16[272,1024]{1,0:T(8,128)(2,1)S(1)}, bf16[272,1024]{1,0:T(8,128)(2,1)S(1)}, u32[]{:S(2)}, u32[]{:S(2)}) collective-permute-start(bf16[272,1024]{1,0:T(8,128)(2,1)S(1)} %collective-permute-done.10.refs_5_.refs_7_), channel_id=1, source_target_pairs={{0,1},{1,2},{2,3},{3,4},{4,5},{5,6},{6,7},{7,0},{8,15},{9,8},{10,9... | collective-permute-start | bytes 1671176 | tf_op jit(solution)/shard_map/ppermute | solution.py:340
  44.1 23.2 %collective-permute-start.9 = (bf16[272,1024]{1,0:T(8,128)(2,1)S(1)}, bf16[272,1024]{1,0:T(8,128)(2,1)S(1)}, u32[]{:S(2)}, u32[]{:S(2)}) collective-permute-start(bf16[272,1024]{1,0:T(8,128)(2,1)S(1)} %collective-permute-done.8.refs_2_), channel_id=1, source_target_pairs={{1,0},{2,1},{3,2},{4,3},{5,4},{6,5},{7,6},{0,7},{15,8},{8,9},{9,10... | collective-permute-start | bytes 1671176 | tf_op jit(solution)/shard_map/ppermute | solution.py:342
  55.3 23.2 %collective-permute-start.3 = (bf16[256,1024]{1,0:T(8,128)(2,1)S(1)}, bf16[256,1024]{1,0:T(8,128)(2,1)S(1)}, u32[]{:S(2)}, u32[]{:S(2)}) collective-permute-start(bf16[256,1024]{1,0:T(8,128)(2,1)S(1)} %collective-permute-done.2.refs_2_), channel_id=1, source_target_pairs={{1,0},{2,1},{3,2},{4,3},{5,4},{6,5},{7,6},{0,7},{15,8},{8,9},{9,10... | collective-permute-start | bytes 1572872 | tf_op jit(solution)/shard_map/ppermute | solution.py:342
  59.0 19.5 %collective-permute-start.6 = (bf16[256,1024]{1,0:T(8,128)(2,1)S(1)}, bf16[256,1024]{1,0:T(8,128)(2,1)S(1)}, u32[]{:S(2)}, u32[]{:S(2)}) collective-permute-start(bf16[256,1024]{1,0:T(8,128)(2,1)S(1)} %collective-permute-done.5.refs_5_), channel_id=1, source_target_pairs={{0,1},{1,2},{2,3},{3,4},{4,5},{5,6},{6,7},{7,0},{8,15},{9,8},{10,9... | collective-permute-start | bytes 1572872 | tf_op jit(solution)/shard_map/ppermute | solution.py:340
  66.2 23.2 %collective-permute-start.13 = (bf16[272,1024]{1,0:T(8,128)(2,1)S(1)}, bf16[272,1024]{1,0:T(8,128)(2,1)S(1)}, u32[]{:S(2)}, u32[]{:S(2)}) collective-permute-start(bf16[272,1024]{1,0:T(8,128)(2,1)S(1)} %collective-permute-done.11.refs_4_.refs_6_), channel_id=1, source_target_pairs={{0,1},{1,2},{2,3},{3,4},{4,5},{5,6},{6,7},{7,0},{8,15},{9,8},{10,9... | collective-permute-start | bytes 1671176 | tf_op jit(solution)/shard_map/ppermute | solution.py:340
  67.3 22.1 %collective-permute-start.12 = (bf16[272,1024]{1,0:T(8,128)(2,1)S(1)}, bf16[272,1024]{1,0:T(8,128)(2,1)S(1)}, u32[]{:S(2)}, u32[]{:S(2)}) collective-permute-start(bf16[272,1024]{1,0:T(8,128)(2,1)S(1)} %collective-permute-done.9.refs_3_), channel_id=1, source_target_pairs={{1,0},{2,1},{3,2},{4,3},{5,4},{6,5},{7,6},{0,7},{15,8},{8,9},{9,10... | collective-permute-start | bytes 1671176 | tf_op jit(solution)/shard_map/ppermute | solution.py:342
  93.0 5.3 %collective-permute-start.14 = (bf16[1024,1024]{1,0:T(8,128)(2,1)S(1)}, bf16[1024,1024]{1,0:T(8,128)(2,1)S(1)}, u32[]{:S(2)}, u32[]{:S(2)}) collective-permute-start(bf16[1024,1024]{1,0:T(8,128)(2,1)S(1)} %get-tuple-element.57), channel_id=1, source_target_pairs={{0,8},{16,24},{32,40},{48,56},{64,72},{80,88},{96,104},{112,120},{... | collective-permute-start | bytes 6291464 | tf_op jit(solution)/shard_map/ppermute | solution.py:392
  96.2 2.1 %collective-permute-start.15 = (bf16[16,1024]{1,0:T(8,128)(2,1)S(1)}, bf16[16,1024]{1,0:T(8,128)(2,1)S(1)}, u32[]{:S(2)}, u32[]{:S(2)}) collective-permute-start(bf16[16,1024]{1,0:T(8,128)(2,1)S(1)} %get-tuple-element.56.own_term_ref), channel_id=1, source_target_pairs={{0,8},{16,24},{32,40},{48,56},{64,72},{80,88},{96,104},{112,120},{... | collective-permute-start | bytes 98312 | tf_op jit(solution)/shard_map/ppermute | solution.py:397
  98.4 7.9 %collective-permute-start.24 = (bf16[512,1024]{1,0:T(8,128)(2,1)S(1)}, bf16[512,1024]{1,0:T(8,128)(2,1)S(1)}, u32[]{:S(2)}, u32[]{:S(2)}) collective-permute-start(bf16[512,1024]{1,0:T(8,128)(2,1)S(1)} %shard_map.82.turned0_ref), channel_id=1, source_target_pairs={{136,152},{168,184},{200,216},{232,248},{137,153},{169,185},{201,2... | collective-permute-start | bytes 3145736 | tf_op jit(solution)/shard_map/ppermute | solution.py:407
  99.3 7.0 %collective-permute-start.25 = (bf16[528,1024]{1,0:T(8,128)(2,1)S(1)}, bf16[528,1024]{1,0:T(8,128)(2,1)S(1)}, u32[]{:S(2)}, u32[]{:S(2)}) collective-permute-start(bf16[528,1024]{1,0:T(8,128)(2,1)S(1)} %shard_map.79.turned1_ref), channel_id=1, source_target_pairs={{136,152},{168,184},{200,216},{232,248},{137,153},{169,185},{201,2... | collective-permute-start | bytes 3244040 | tf_op jit(solution)/shard_map/ppermute | solution.py:409
  100.0 0.7 collective-permute-start.16
  100.7 0.7 collective-permute-start.17
  101.5 0.7 collective-permute-start.18
  102.2 0.9 collective-permute-start.19
  103.1 1.0 collective-permute-start.20
  104.2 0.7 collective-permute-start.21
  104.9 0.7 collective-permute-start.22
  105.6 0.8 collective-permute-start.23
  106.4 0.7 collective-permute-start.26
  107.1 0.7 collective-permute-start.27
  107.8 1.3 collective-permute-start.29
  108.5 0.7 collective-permute-start.28
  109.2 36.4 %collective-permute-start.30 = (f32[1,1024]{1,0:T(1,128)S(1)}, f32[1,1024]{1,0:T(1,128)S(1)}, u32[]{:S(2)}, u32[]{:S(2)}) collective-permute-start(f32[1,1024]{1,0:T(1,128)S(1)} %shard_map.95.begin_ref), channel_id=1, source_target_pairs={{8,0},{24,16},{40,32},{56,48},{72,64},{88,80},{104,96},{120,112},{... | collective-permute-start | bytes 12296 | tf_op jit(solution)/shard_map/ppermute | solution.py:446
  (5 other events, 31.6 us)

commit v14 on v13

--- a/solution.py
+++ b/solution.py
@@ -178,12 +178,25 @@
 
 
 def second_kernel(three_ref, fourth_ref, four_ref, slab4_ref):
-    width = slab4_ref.shape[0]
-
-    @pl.when(core_here() != 0)
+    width, size = slab4_ref.shape
+    mine = pl.ds(pl.multiple_of(lax.axis_index("state") * width, width), width)
+    turned = chip_here() < DIRECT
+
+    @pl.when(jnp.logical_and(core_here() != 0, turned))
+    def _():
+        def block(i, carry):
+            at = pl.ds(pl.multiple_of(i * ROWS, ROWS), ROWS)
+            out = jnp.dot(fourth_ref[at, :], three_ref[...], preferred_element_type=F32)
+            four_ref[:, at] = out.T.astype(BF16)
+            return carry
+
+        lax.fori_loop(0, size // ROWS, block, 0)
+        slab4_ref[...] = four_ref[:, mine].astype(F32).T.astype(BF16)
+
+    @pl.when(jnp.logical_and(core_here() != 0, jnp.logical_not(turned)))
     def _():
         matmul(fourth_ref, three_ref, four_ref)
-        slab4_ref[...] = four_ref[pl.ds(pl.multiple_of(lax.axis_index("state") * width, width), width), :]
+        slab4_ref[...] = four_ref[mine, :]
 
 
 def local_kernel(drive_ref, second_ref, third_ref, fourth_ref, locals_ref, term_ref):
@@ -226,7 +239,7 @@
         begin = came_ref[...]
         held_ref[...] = begin
         between = times_t(begin, other_ref[...]) + joined(other_term_ref[...])
-        value_ref[...] = times_t(between, own_ref[...]) + joined(own_term_ref[...])
+        value_ref[...] = times(between, own_ref[...]) + joined(own_term_ref[...])
 
 
 def hop_kernel(turn, begin_ref, came_ref, turned0_ref, turned1_ref, held_ref, value_ref):

time: 147 us -> 147 us (level)
  no operation moved by 1% of the time
where the time goes in v14:
time: 147 us; the launch traced here: 146 us
  waiting for transfers between devices  91.2 us (62%)
  starting transfers between devices  39.3 us (27%)
  Pallas kernels  14 us (10%)
    ppermute x1, waiting for transfers between devices, shards(): got = lax.ppermute(begin, 'tm', [(b, a) for a, b in pairs])  35.1 us
    ppermute x7, waiting for transfers between devices, ring_rounds(): pieces[count - r] = lax.ppermute(left, ('tm', 'state'), forward)  30.7 us
    ppermute x7, waiting for transfers between devices, ring_rounds(): pieces[r] = lax.ppermute(right, ('tm', 'state'), backward)  24.6 us
    ppermute x7, starting transfers between devices, ring_rounds(): pieces[r] = lax.ppermute(right, ('tm', 'state'), backward)  20.8 us
    ppermute x8, starting transfers between devices, shards(): lax.ppermute(value, 'tm', [(2 * turn + 1, 2 * turn + (3 if turn + 1 < fir...  5.29 us
    ppermute x7, starting transfers between devices, ring_rounds(): pieces[count - r] = lax.ppermute(left, ('tm', 'state'), forward)  4.9 us
    pallas_call x1, Pallas kernels, shards(): call(functools.partial(four_kernel, count, have), (matrix, slab, slab, ma...  3.63 us
    pallas_call x1, Pallas kernels, shards(): call(functools.partial(two_kernel, count), (matrix, slab, matrix), [A] *...  3.03 us
  transfers between devices with their start and end apart: 31, of which 13 were waited for; matrix products, arithmetic and copies ran while one was open for 0% of the time, Pallas kernels for 6%

profile of v14, /device:TPU:30, one launch (start us, length us, event | category | flops | bytes accessed | tf_op | source)
XLA Modules:
  0.0 146.4 jit_solution(14721329601528707661)
XLA Ops:
  0.0 1.4 fusion
  1.5 2.0 %collective-permute-start.1 = (bf16[256,1024]{1,0:T(8,128)(2,1)S(1)}, bf16[256,1024]{1,0:T(8,128)(2,1)S(1)}, u32[]{:S(2)}, u32[]{:S(2)}) collective-permute-start(bf16[256,1024]{1,0:T(8,128)(2,1)S(1)} %bitcast.2), channel_id=1, source_target_pairs={{0,1},{1,2},{2,3},{3,4},{4,5},{5,6},{6,7},{7,0},{8,15},{9,8},{10,9... | collective-permute-start | bytes 1572872 | tf_op jit(solution)/shard_map/ppermute | solution.py:353
  3.4 4.0 %collective-permute-start = (bf16[256,1024]{1,0:T(8,128)(2,1)S(1)}, bf16[256,1024]{1,0:T(8,128)(2,1)S(1)}, u32[]{:S(2)}, u32[]{:S(2)}) collective-permute-start(bf16[256,1024]{1,0:T(8,128)(2,1)S(1)} %bitcast.3), channel_id=1, source_target_pairs={{1,0},{2,1},{3,2},{4,3},{5,4},{6,5},{7,6},{0,7},{15,8},{8,9},{9,10... | collective-permute-start | bytes 1572872 | tf_op jit(solution)/shard_map/ppermute | solution.py:355
  7.5 1.6 %shard_map.73.refs_0_ = bf16[272,1024]{1,0:T(8,128)(2,1)S(1)} custom-call(s32[4,32]{1,0:T(4,128)S(1)} %copy-done.2, s32[4,32]{1,0:T(4,128)S(1)} %copy-done.3, bf16[4,4096]{1,0:T(4,128)(2,1)S(1)} %multiply_convert_fusion.values_ref, bf16[4,32,64,64]{3,2,1,0:T(8,128)(2,1)S(1)} %copy-done, bf16[2,128,1024]{2,1,0:T(8,128)(2,1)S(1)} %get-tuple-element.83.maps_ref), custom_call_target="tpu_custom_call" | custom-call | flops 10000000 | bytes 2097152 | tf_op jit(solution)/shard_map/pallas_call | solution.py:375
  9.1 2.0 %collective-permute-start.7 = (bf16[272,1024]{1,0:T(8,128)(2,1)S(1)}, bf16[272,1024]{1,0:T(8,128)(2,1)S(1)}, u32[]{:S(2)}, u32[]{:S(2)}) collective-permute-start(bf16[272,1024]{1,0:T(8,128)(2,1)S(1)} %shard_map.73.refs_0_), channel_id=1, source_target_pairs={{1,0},{2,1},{3,2},{4,3},{5,4},{6,5},{7,6},{0,7},{15,8},{8,9},{9,10... | collective-permute-start | bytes 1671176 | tf_op jit(solution)/shard_map/ppermute | solution.py:355
  11.1 7.2 %collective-permute-done.1.refs_7_ = bf16[256,1024]{1,0:T(8,128)(2,1)S(1)} collective-permute-done((bf16[256,1024]{1,0:T(8,128)(2,1)S(1)}, bf16[256,1024]{1,0:T(8,128)(2,1)S(1)}, u32[]{:S(2)}, u32[]{:S(2)}) %collective-permute-start.1) | collective-permute-done | bytes 524320 | tf_op jit(solution)/shard_map/ppermute | solution.py:353
  18.6 1.6 %collective-permute-start.10 = (bf16[272,1024]{1,0:T(8,128)(2,1)S(1)}, bf16[272,1024]{1,0:T(8,128)(2,1)S(1)}, u32[]{:S(2)}, u32[]{:S(2)}) collective-permute-start(bf16[272,1024]{1,0:T(8,128)(2,1)S(1)} %shard_map.73.refs_0_), channel_id=1, source_target_pairs={{0,1},{1,2},{2,3},{3,4},{4,5},{5,6},{6,7},{7,0},{8,15},{9,8},{10,9... | collective-permute-start | bytes 1671176 | tf_op jit(solution)/shard_map/ppermute | solution.py:353
  20.2 7.2 %collective-permute-done.7.refs_1_ = bf16[272,1024]{1,0:T(8,128)(2,1)S(1)} collective-permute-done((bf16[272,1024]{1,0:T(8,128)(2,1)S(1)}, bf16[272,1024]{1,0:T(8,128)(2,1)S(1)}, u32[]{:S(2)}, u32[]{:S(2)}) %collective-permute-start.7) | collective-permute-done | bytes 557088 | tf_op jit(solution)/shard_map/ppermute | solution.py:355
  27.3 3.7 %collective-permute-start.8 = (bf16[272,1024]{1,0:T(8,128)(2,1)S(1)}, bf16[272,1024]{1,0:T(8,128)(2,1)S(1)}, u32[]{:S(2)}, u32[]{:S(2)}) collective-permute-start(bf16[272,1024]{1,0:T(8,128)(2,1)S(1)} %collective-permute-done.7.refs_1_), channel_id=1, source_target_pairs={{1,0},{2,1},{3,2},{4,3},{5,4},{6,5},{7,6},{0,7},{15,8},{8,9},{9,10... | collective-permute-start | bytes 1671176 | tf_op jit(solution)/shard_map/ppermute | solution.py:355
  31.8 1.3 collective-permute-start.5
  33.0 10.0 %collective-permute-done.10.refs_5_.refs_7_ = bf16[272,1024]{1,0:T(8,128)(2,1)S(1)} collective-permute-done((bf16[272,1024]{1,0:T(8,128)(2,1)S(1)}, bf16[272,1024]{1,0:T(8,128)(2,1)S(1)}, u32[]{:S(2)}, u32[]{:S(2)}) %collective-permute-start.10) | collective-permute-done | bytes 557088 | tf_op jit(solution)/shard_map/ppermute | solution.py:353
  43.1 1.0 collective-permute-done.8.refs_2_
  44.1 3.7 %collective-permute-start.9 = (bf16[272,1024]{1,0:T(8,128)(2,1)S(1)}, bf16[272,1024]{1,0:T(8,128)(2,1)S(1)}, u32[]{:S(2)}, u32[]{:S(2)}) collective-permute-start(bf16[272,1024]{1,0:T(8,128)(2,1)S(1)} %collective-permute-done.8.refs_2_), channel_id=1, source_target_pairs={{1,0},{2,1},{3,2},{4,3},{5,4},{6,5},{7,6},{0,7},{15,8},{8,9},{9,10... | collective-permute-start | bytes 1671176 | tf_op jit(solution)/shard_map/ppermute | solution.py:355
  47.8 7.5 %collective-permute-done.2.refs_2_ = bf16[256,1024]{1,0:T(8,128)(2,1)S(1)} collective-permute-done((bf16[256,1024]{1,0:T(8,128)(2,1)S(1)}, bf16[256,1024]{1,0:T(8,128)(2,1)S(1)}, u32[]{:S(2)}, u32[]{:S(2)}) %collective-permute-start.2) | collective-permute-done | bytes 524320 | tf_op jit(solution)/shard_map/ppermute | solution.py:355
  55.3 3.7 %collective-permute-start.3 = (bf16[256,1024]{1,0:T(8,128)(2,1)S(1)}, bf16[256,1024]{1,0:T(8,128)(2,1)S(1)}, u32[]{:S(2)}, u32[]{:S(2)}) collective-permute-start(bf16[256,1024]{1,0:T(8,128)(2,1)S(1)} %collective-permute-done.2.refs_2_), channel_id=1, source_target_pairs={{1,0},{2,1},{3,2},{4,3},{5,4},{6,5},{7,6},{0,7},{15,8},{8,9},{9,10... | collective-permute-start | bytes 1572872 | tf_op jit(solution)/shard_map/ppermute | solution.py:355
  59.0 7.2 %collective-permute-done.11.refs_4_.refs_6_ = bf16[272,1024]{1,0:T(8,128)(2,1)S(1)} collective-permute-done((bf16[272,1024]{1,0:T(8,128)(2,1)S(1)}, bf16[272,1024]{1,0:T(8,128)(2,1)S(1)}, u32[]{:S(2)}, u32[]{:S(2)}) %collective-permute-start.11) | collective-permute-done | bytes 557088 | tf_op jit(solution)/shard_map/ppermute | solution.py:353
  66.2 1.0 collective-permute-done.9.refs_3_
  67.3 3.7 %collective-permute-start.12 = (bf16[272,1024]{1,0:T(8,128)(2,1)S(1)}, bf16[272,1024]{1,0:T(8,128)(2,1)S(1)}, u32[]{:S(2)}, u32[]{:S(2)}) collective-permute-start(bf16[272,1024]{1,0:T(8,128)(2,1)S(1)} %collective-permute-done.9.refs_3_), channel_id=1, source_target_pairs={{1,0},{2,1},{3,2},{4,3},{5,4},{6,5},{7,6},{0,7},{15,8},{8,9},{9,10... | collective-permute-start | bytes 1671176 | tf_op jit(solution)/shard_map/ppermute | solution.py:355
  71.0 7.5 %collective-permute-done.3.refs_3_ = bf16[256,1024]{1,0:T(8,128)(2,1)S(1)} collective-permute-done((bf16[256,1024]{1,0:T(8,128)(2,1)S(1)}, bf16[256,1024]{1,0:T(8,128)(2,1)S(1)}, u32[]{:S(2)}, u32[]{:S(2)}) %collective-permute-start.3) | collective-permute-done | bytes 524320 | tf_op jit(solution)/shard_map/ppermute | solution.py:355
  78.5 3.0 %shard_map.74 = (bf16[1024,1024]{1,0:T(8,128)(2,1)S(1)}, bf16[128,1024]{1,0:T(8,128)(2,1)S(1)}, bf16[1024,1024]{1,0:T(8,128)(2,1)S(1)}) custom-call(bf16[256,1024]{1,0:T(8,128)(2,1)S(1)} %bitcast.4, bf16[256,1024]{1,0:T(8,128)(2,1)S(1)} %collective-permute-done.refs_1_, bf16[256,1024]{1,0:T(8,128)(2,1)S(1)} %collective-permute-done.2.refs_2_, ...), custom_call_target="tpu_custom_call" | custom-call | flops 2147483648 | bytes 6291456 | tf_op jit(solution)/shard_map/pallas_call | solution.py:388
  81.6 2.2 %shard_map.75 = (bf16[1024,1024]{1,0:T(8,128)(2,1)S(1)}, bf16[1024,1024]{1,0:T(8,128)(2,1)S(1)}, bf16[1024,1024]{1,0:T(8,128)(2,1)S(1)}) custom-call(bf16[1024,1024]{1,0:T(8,128)(2,1)S(1)} %get-tuple-element.46.two_ref, bf16[272,1024]{1,0:T(8,128)(2,1)S(1)} %shard_map.73.refs_0_, bf16[272,1024]{1,0:T(8,128)(2,1)S(1)} %collective-permute-done.7.refs_1_, ...), custom_call_target="tpu_custom_call" | custom-call | flops 2147483648 | bytes 6291456 | tf_op jit(solution)/shard_map/pallas_call | solution.py:393
  83.8 5.6 %collective-permute-done.13.refs_5_ = bf16[272,1024]{1,0:T(8,128)(2,1)S(1)} collective-permute-done((bf16[272,1024]{1,0:T(8,128)(2,1)S(1)}, bf16[272,1024]{1,0:T(8,128)(2,1)S(1)}, u32[]{:S(2)}, u32[]{:S(2)}) %collective-permute-start.13) | collective-permute-done | bytes 557088 | tf_op jit(solution)/shard_map/ppermute | solution.py:353
  89.4 3.6 %shard_map.76 = (bf16[1024,1024]{1,0:T(8,128)(2,1)S(1)}, bf16[128,1024]{1,0:T(8,128)(2,1)S(1)}, bf16[128,1024]{1,0:T(8,128)(2,1)S(1)}, bf16[1024,1024]{1,0:T(8,1...) custom-call(bf16[1024,1024]{1,0:T(8,128)(2,1)S(1)} %get-tuple-elemen, ...), custom_call_target="tpu_custom_call", output_to_operand_aliasing={{3}: (1, {}), {4}: (2, {}), {5}: (3, {})} | custom-call | flops 2147483648 | bytes 6291456 | tf_op jit(solution)/shard_map/pallas_call | solution.py:397
  93.0 1.4 collective-permute-start.14
  94.5 1.8 %shard_map.78 = (f32[4,1024]{1,0:T(4,128)S(1)}, bf16[16,1024]{1,0:T(8,128)(2,1)S(1)}) custom-call(f32[16,1024]{1,0:T(8,128)S(1)} %get-tuple-element.53.drive_ref, bf16[1024,1024]{1,0:T(8,128)(2,1)S(1)} %get-tuple-element.54.second_ref, bf16[1024,1024]{1,0:T(8,128)(2,1)S(1)} %get-tuple-element.55.third_ref, bf16[1024,1024]{1,0:T(8,128)(2,1)S(1)} %get-tuple-element.51.fourth_ref), custom_call_target="tpu_custom_call" | custom-call | flops 100663296 | bytes 6291456 | tf_op jit(solution)/shard_map/pallas_call | solution.py:407
  96.2 1.3 collective-permute-start.15
  97.6 0.8 collective-permute-done.15.other_term_ref
  98.4 0.8 collective-permute-start.24
  99.3 0.7 collective-permute-start.25
  109.2 1.3 collective-permute-start.30
  110.5 35.1 %collective-permute-done.30.got_ref = f32[1,1024]{1,0:T(1,128)S(1)} collective-permute-done((f32[1,1024]{1,0:T(1,128)S(1)}, f32[1,1024]{1,0:T(1,128)S(1)}, u32[]{:S(2)}, u32[]{:S(2)}) %collective-permute-start.30) | collective-permute-done | bytes 4128 | tf_op jit(solution)/shard_map/ppermute | solution.py:459
  145.6 0.8 shard_map.96
  (68 shorter events, 10.0 us)
Async XLA Ops:
  0.0 7.5 %copy-start.2 = (s32[4,32]{1,0:T(4,128)S(1)}, s32[4,32]{1,0:T(4,128)}, u32[]{:S(2)}) copy-start(s32[4,32]{1,0:T(4,128)} %rows_ref.1) | copy-start | bytes 1540
  1.5 16.8 %collective-permute-start.1 = (bf16[256,1024]{1,0:T(8,128)(2,1)S(1)}, bf16[256,1024]{1,0:T(8,128)(2,1)S(1)}, u32[]{:S(2)}, u32[]{:S(2)}) collective-permute-start(bf16[256,1024]{1,0:T(8,128)(2,1)S(1)} %bitcast.2), channel_id=1, source_target_pairs={{0,1},{1,2},{2,3},{3,4},{4,5},{5,6},{6,7},{7,0},{8,15},{9,8},{10,9... | collective-permute-start | bytes 1572872 | tf_op jit(solution)/shard_map/ppermute | solution.py:353
  3.4 15.1 %collective-permute-start = (bf16[256,1024]{1,0:T(8,128)(2,1)S(1)}, bf16[256,1024]{1,0:T(8,128)(2,1)S(1)}, u32[]{:S(2)}, u32[]{:S(2)}) collective-permute-start(bf16[256,1024]{1,0:T(8,128)(2,1)S(1)} %bitcast.3), channel_id=1, source_target_pairs={{1,0},{2,1},{3,2},{4,3},{5,4},{6,5},{7,6},{0,7},{15,8},{8,9},{9,10... | collective-permute-start | bytes 1572872 | tf_op jit(solution)/shard_map/ppermute | solution.py:355
  9.1 18.2 %collective-permute-start.7 = (bf16[272,1024]{1,0:T(8,128)(2,1)S(1)}, bf16[272,1024]{1,0:T(8,128)(2,1)S(1)}, u32[]{:S(2)}, u32[]{:S(2)}) collective-permute-start(bf16[272,1024]{1,0:T(8,128)(2,1)S(1)} %shard_map.73.refs_0_), channel_id=1, source_target_pairs={{1,0},{2,1},{3,2},{4,3},{5,4},{6,5},{7,6},{0,7},{15,8},{8,9},{9,10... | collective-permute-start | bytes 1671176 | tf_op jit(solution)/shard_map/ppermute | solution.py:355
  18.6 13.2 %collective-permute-start.4 = (bf16[256,1024]{1,0:T(8,128)(2,1)S(1)}, bf16[256,1024]{1,0:T(8,128)(2,1)S(1)}, u32[]{:S(2)}, u32[]{:S(2)}) collective-permute-start(bf16[256,1024]{1,0:T(8,128)(2,1)S(1)} %collective-permute-done.1.refs_7_), channel_id=1, source_target_pairs={{0,1},{1,2},{2,3},{3,4},{4,5},{5,6},{6,7},{7,0},{8,15},{9,8},{10,9... | collective-permute-start | bytes 1572872 | tf_op jit(solution)/shard_map/ppermute | solution.py:353
  18.6 24.5 %collective-permute-start.10 = (bf16[272,1024]{1,0:T(8,128)(2,1)S(1)}, bf16[272,1024]{1,0:T(8,128)(2,1)S(1)}, u32[]{:S(2)}, u32[]{:S(2)}) collective-permute-start(bf16[272,1024]{1,0:T(8,128)(2,1)S(1)} %shard_map.73.refs_0_), channel_id=1, source_target_pairs={{0,1},{1,2},{2,3},{3,4},{4,5},{5,6},{6,7},{7,0},{8,15},{9,8},{10,9... | collective-permute-start | bytes 1671176 | tf_op jit(solution)/shard_map/ppermute | solution.py:353
  27.3 16.8 %collective-permute-start.8 = (bf16[272,1024]{1,0:T(8,128)(2,1)S(1)}, bf16[272,1024]{1,0:T(8,128)(2,1)S(1)}, u32[]{:S(2)}, u32[]{:S(2)}) collective-permute-start(bf16[272,1024]{1,0:T(8,128)(2,1)S(1)} %collective-permute-done.7.refs_1_), channel_id=1, source_target_pairs={{1,0},{2,1},{3,2},{4,3},{5,4},{6,5},{7,6},{0,7},{15,8},{8,9},{9,10... | collective-permute-start | bytes 1671176 | tf_op jit(solution)/shard_map/ppermute | solution.py:355
  31.0 24.3 %collective-permute-start.2 = (bf16[256,1024]{1,0:T(8,128)(2,1)S(1)}, bf16[256,1024]{1,0:T(8,128)(2,1)S(1)}, u32[]{:S(2)}, u32[]{:S(2)}) collective-permute-start(bf16[256,1024]{1,0:T(8,128)(2,1)S(1)} %collective-permute-done.refs_1_), channel_id=1, source_target_pairs={{1,0},{2,1},{3,2},{4,3},{5,4},{6,5},{7,6},{0,7},{15,8},{8,9},{9,10... | collective-permute-start | bytes 1572872 | tf_op jit(solution)/shard_map/ppermute | solution.py:355
  31.8 27.3 %collective-permute-start.5 = (bf16[256,1024]{1,0:T(8,128)(2,1)S(1)}, bf16[256,1024]{1,0:T(8,128)(2,1)S(1)}, u32[]{:S(2)}, u32[]{:S(2)}) collective-permute-start(bf16[256,1024]{1,0:T(8,128)(2,1)S(1)} %collective-permute-done.4.refs_6_), channel_id=1, source_target_pairs={{0,1},{1,2},{2,3},{3,4},{4,5},{5,6},{6,7},{7,0},{8,15},{9,8},{10,9... | collective-permute-start | bytes 1572872 | tf_op jit(solution)/shard_map/ppermute | solution.py:353
  43.1 23.2 %collective-permute-start.11 = (bf16[272,1024]{1,0:T(8,128)(2,1)S(1)}, bf16[272,1024]{1,0:T(8,128)(2,1)S(1)}, u32[]{:S(2)}, u32[]{:S(2)}) collective-permute-start(bf16[272,1024]{1,0:T(8,128)(2,1)S(1)} %collective-permute-done.10.refs_5_.refs_7_), channel_id=1, source_target_pairs={{0,1},{1,2},{2,3},{3,4},{4,5},{5,6},{6,7},{7,0},{8,15},{9,8},{10,9... | collective-permute-start | bytes 1671176 | tf_op jit(solution)/shard_map/ppermute | solution.py:353
  44.1 23.2 %collective-permute-start.9 = (bf16[272,1024]{1,0:T(8,128)(2,1)S(1)}, bf16[272,1024]{1,0:T(8,128)(2,1)S(1)}, u32[]{:S(2)}, u32[]{:S(2)}) collective-permute-start(bf16[272,1024]{1,0:T(8,128)(2,1)S(1)} %collective-permute-done.8.refs_2_), channel_id=1, source_target_pairs={{1,0},{2,1},{3,2},{4,3},{5,4},{6,5},{7,6},{0,7},{15,8},{8,9},{9,10... | collective-permute-start | bytes 1671176 | tf_op jit(solution)/shard_map/ppermute | solution.py:355
  55.3 23.2 %collective-permute-start.3 = (bf16[256,1024]{1,0:T(8,128)(2,1)S(1)}, bf16[256,1024]{1,0:T(8,128)(2,1)S(1)}, u32[]{:S(2)}, u32[]{:S(2)}) collective-permute-start(bf16[256,1024]{1,0:T(8,128)(2,1)S(1)} %collective-permute-done.2.refs_2_), channel_id=1, source_target_pairs={{1,0},{2,1},{3,2},{4,3},{5,4},{6,5},{7,6},{0,7},{15,8},{8,9},{9,10... | collective-permute-start | bytes 1572872 | tf_op jit(solution)/shard_map/ppermute | solution.py:355
  59.0 19.5 %collective-permute-start.6 = (bf16[256,1024]{1,0:T(8,128)(2,1)S(1)}, bf16[256,1024]{1,0:T(8,128)(2,1)S(1)}, u32[]{:S(2)}, u32[]{:S(2)}) collective-permute-start(bf16[256,1024]{1,0:T(8,128)(2,1)S(1)} %collective-permute-done.5.refs_5_), channel_id=1, source_target_pairs={{0,1},{1,2},{2,3},{3,4},{4,5},{5,6},{6,7},{7,0},{8,15},{9,8},{10,9... | collective-permute-start | bytes 1572872 | tf_op jit(solution)/shard_map/ppermute | solution.py:353
  66.2 23.2 %collective-permute-start.13 = (bf16[272,1024]{1,0:T(8,128)(2,1)S(1)}, bf16[272,1024]{1,0:T(8,128)(2,1)S(1)}, u32[]{:S(2)}, u32[]{:S(2)}) collective-permute-start(bf16[272,1024]{1,0:T(8,128)(2,1)S(1)} %collective-permute-done.11.refs_4_.refs_6_), channel_id=1, source_target_pairs={{0,1},{1,2},{2,3},{3,4},{4,5},{5,6},{6,7},{7,0},{8,15},{9,8},{10,9... | collective-permute-start | bytes 1671176 | tf_op jit(solution)/shard_map/ppermute | solution.py:353
  67.3 22.1 %collective-permute-start.12 = (bf16[272,1024]{1,0:T(8,128)(2,1)S(1)}, bf16[272,1024]{1,0:T(8,128)(2,1)S(1)}, u32[]{:S(2)}, u32[]{:S(2)}) collective-permute-start(bf16[272,1024]{1,0:T(8,128)(2,1)S(1)} %collective-permute-done.9.refs_3_), channel_id=1, source_target_pairs={{1,0},{2,1},{3,2},{4,3},{5,4},{6,5},{7,6},{0,7},{15,8},{8,9},{9,10... | collective-permute-start | bytes 1671176 | tf_op jit(solution)/shard_map/ppermute | solution.py:355
  93.0 5.3 %collective-permute-start.14 = (bf16[1024,1024]{1,0:T(8,128)(2,1)S(1)}, bf16[1024,1024]{1,0:T(8,128)(2,1)S(1)}, u32[]{:S(2)}, u32[]{:S(2)}) collective-permute-start(bf16[1024,1024]{1,0:T(8,128)(2,1)S(1)} %get-tuple-element.57), channel_id=1, source_target_pairs={{0,8},{16,24},{32,40},{48,56},{64,72},{80,88},{96,104},{112,120},{... | collective-permute-start | bytes 6291464 | tf_op jit(solution)/shard_map/ppermute | solution.py:405
  96.2 2.1 %collective-permute-start.15 = (bf16[16,1024]{1,0:T(8,128)(2,1)S(1)}, bf16[16,1024]{1,0:T(8,128)(2,1)S(1)}, u32[]{:S(2)}, u32[]{:S(2)}) collective-permute-start(bf16[16,1024]{1,0:T(8,128)(2,1)S(1)} %get-tuple-element.56.own_term_ref), channel_id=1, source_target_pairs={{0,8},{16,24},{32,40},{48,56},{64,72},{80,88},{96,104},{112,120},{... | collective-permute-start | bytes 98312 | tf_op jit(solution)/shard_map/ppermute | solution.py:410
  98.4 7.9 %collective-permute-start.24 = (bf16[512,1024]{1,0:T(8,128)(2,1)S(1)}, bf16[512,1024]{1,0:T(8,128)(2,1)S(1)}, u32[]{:S(2)}, u32[]{:S(2)}) collective-permute-start(bf16[512,1024]{1,0:T(8,128)(2,1)S(1)} %shard_map.82.turned0_ref), channel_id=1, source_target_pairs={{136,152},{168,184},{200,216},{232,248},{137,153},{169,185},{201,2... | collective-permute-start | bytes 3145736 | tf_op jit(solution)/shard_map/ppermute | solution.py:420
  99.3 7.0 %collective-permute-start.25 = (bf16[528,1024]{1,0:T(8,128)(2,1)S(1)}, bf16[528,1024]{1,0:T(8,128)(2,1)S(1)}, u32[]{:S(2)}, u32[]{:S(2)}) collective-permute-start(bf16[528,1024]{1,0:T(8,128)(2,1)S(1)} %shard_map.79.turned1_ref), channel_id=1, source_target_pairs={{136,152},{168,184},{200,216},{232,248},{137,153},{169,185},{201,2... | collective-permute-start | bytes 3244040 | tf_op jit(solution)/shard_map/ppermute | solution.py:422
  100.0 0.7 collective-permute-start.16
  101.0 0.7 collective-permute-start.17
  101.7 0.7 collective-permute-start.18
  102.4 0.7 collective-permute-start.19
  103.1 1.0 collective-permute-start.20
  104.2 0.7 collective-permute-start.21
  104.9 0.7 collective-permute-start.22
  105.6 0.8 collective-permute-start.23
  106.4 0.7 collective-permute-start.26
  107.1 0.7 collective-permute-start.27
  107.8 1.3 collective-permute-start.29
  108.5 0.7 collective-permute-start.28
  109.2 36.4 %collective-permute-start.30 = (f32[1,1024]{1,0:T(1,128)S(1)}, f32[1,1024]{1,0:T(1,128)S(1)}, u32[]{:S(2)}, u32[]{:S(2)}) collective-permute-start(f32[1,1024]{1,0:T(1,128)S(1)} %shard_map.95.begin_ref), channel_id=1, source_target_pairs={{8,0},{24,16},{40,32},{56,48},{72,64},{88,80},{104,96},{120,112},{... | collective-permute-start | bytes 12296 | tf_op jit(solution)/shard_map/ppermute | solution.py:459
  (5 other events, 31.6 us)

commit v15 on v14

--- a/solution.py
+++ b/solution.py
@@ -10,7 +10,7 @@
 F32 = jnp.float32
 BF16 = jnp.bfloat16
 VMEM_LIMIT = 24 * 1024 * 1024
-ROWS = 512
+ROWS = 1024
 
 
 def three_parts(x):

time: 147 us -> 147 us (level)
  no operation moved by 1% of the time
where the time goes in v15:
time: 147 us; the launch traced here: 146 us
  waiting for transfers between devices  91.4 us (62%)
  starting transfers between devices  39.3 us (27%)
  Pallas kernels  13.6 us (9%)
    ppermute x1, waiting for transfers between devices, shards(): got = lax.ppermute(begin, 'tm', [(b, a) for a, b in pairs])  35.1 us
    ppermute x7, waiting for transfers between devices, ring_rounds(): pieces[count - r] = lax.ppermute(left, ('tm', 'state'), forward)  30.9 us
    ppermute x7, waiting for transfers between devices, ring_rounds(): pieces[r] = lax.ppermute(right, ('tm', 'state'), backward)  24.6 us
    ppermute x7, starting transfers between devices, ring_rounds(): pieces[r] = lax.ppermute(right, ('tm', 'state'), backward)  20.8 us
    ppermute x8, starting transfers between devices, shards(): lax.ppermute(value, 'tm', [(2 * turn + 1, 2 * turn + (3 if turn + 1 < fir...  5.29 us
    ppermute x7, starting transfers between devices, ring_rounds(): pieces[count - r] = lax.ppermute(left, ('tm', 'state'), forward)  4.9 us
    pallas_call x1, Pallas kernels, shards(): call(functools.partial(four_kernel, count, have), (matrix, slab, slab, ma...  3.45 us
  transfers between devices with their start and end apart: 31, of which 13 were waited for; matrix products, arithmetic and copies ran while one was open for 0% of the time, Pallas kernels for 6%

profile of v15, /device:TPU:30, one launch (start us, length us, event | category | flops | bytes accessed | tf_op | source)
XLA Modules:
  0.0 146.2 jit_solution(7999791520343469359)
XLA Ops:
  0.0 1.4 fusion
  1.5 2.0 %collective-permute-start.1 = (bf16[256,1024]{1,0:T(8,128)(2,1)S(1)}, bf16[256,1024]{1,0:T(8,128)(2,1)S(1)}, u32[]{:S(2)}, u32[]{:S(2)}) collective-permute-start(bf16[256,1024]{1,0:T(8,128)(2,1)S(1)} %bitcast.2), channel_id=1, source_target_pairs={{0,1},{1,2},{2,3},{3,4},{4,5},{5,6},{6,7},{7,0},{8,15},{9,8},{10,9... | collective-permute-start | bytes 1572872 | tf_op jit(solution)/shard_map/ppermute | solution.py:353
  3.4 4.0 %collective-permute-start = (bf16[256,1024]{1,0:T(8,128)(2,1)S(1)}, bf16[256,1024]{1,0:T(8,128)(2,1)S(1)}, u32[]{:S(2)}, u32[]{:S(2)}) collective-permute-start(bf16[256,1024]{1,0:T(8,128)(2,1)S(1)} %bitcast.3), channel_id=1, source_target_pairs={{1,0},{2,1},{3,2},{4,3},{5,4},{6,5},{7,6},{0,7},{15,8},{8,9},{9,10... | collective-permute-start | bytes 1572872 | tf_op jit(solution)/shard_map/ppermute | solution.py:355
  7.5 1.6 %shard_map.73.refs_0_ = bf16[272,1024]{1,0:T(8,128)(2,1)S(1)} custom-call(s32[4,32]{1,0:T(4,128)S(1)} %copy-done.2, s32[4,32]{1,0:T(4,128)S(1)} %copy-done.3, bf16[4,4096]{1,0:T(4,128)(2,1)S(1)} %multiply_convert_fusion.values_ref, bf16[4,32,64,64]{3,2,1,0:T(8,128)(2,1)S(1)} %copy-done, bf16[2,128,1024]{2,1,0:T(8,128)(2,1)S(1)} %get-tuple-element.83.maps_ref), custom_call_target="tpu_custom_call" | custom-call | flops 10000000 | bytes 2097152 | tf_op jit(solution)/shard_map/pallas_call | solution.py:375
  9.1 2.0 %collective-permute-start.7 = (bf16[272,1024]{1,0:T(8,128)(2,1)S(1)}, bf16[272,1024]{1,0:T(8,128)(2,1)S(1)}, u32[]{:S(2)}, u32[]{:S(2)}) collective-permute-start(bf16[272,1024]{1,0:T(8,128)(2,1)S(1)} %shard_map.73.refs_0_), channel_id=1, source_target_pairs={{1,0},{2,1},{3,2},{4,3},{5,4},{6,5},{7,6},{0,7},{15,8},{8,9},{9,10... | collective-permute-start | bytes 1671176 | tf_op jit(solution)/shard_map/ppermute | solution.py:355
  11.1 7.2 %collective-permute-done.1.refs_7_ = bf16[256,1024]{1,0:T(8,128)(2,1)S(1)} collective-permute-done((bf16[256,1024]{1,0:T(8,128)(2,1)S(1)}, bf16[256,1024]{1,0:T(8,128)(2,1)S(1)}, u32[]{:S(2)}, u32[]{:S(2)}) %collective-permute-start.1) | collective-permute-done | bytes 524320 | tf_op jit(solution)/shard_map/ppermute | solution.py:353
  18.6 1.6 %collective-permute-start.10 = (bf16[272,1024]{1,0:T(8,128)(2,1)S(1)}, bf16[272,1024]{1,0:T(8,128)(2,1)S(1)}, u32[]{:S(2)}, u32[]{:S(2)}) collective-permute-start(bf16[272,1024]{1,0:T(8,128)(2,1)S(1)} %shard_map.73.refs_0_), channel_id=1, source_target_pairs={{0,1},{1,2},{2,3},{3,4},{4,5},{5,6},{6,7},{7,0},{8,15},{9,8},{10,9... | collective-permute-start | bytes 1671176 | tf_op jit(solution)/shard_map/ppermute | solution.py:353
  20.2 7.2 %collective-permute-done.7.refs_1_ = bf16[272,1024]{1,0:T(8,128)(2,1)S(1)} collective-permute-done((bf16[272,1024]{1,0:T(8,128)(2,1)S(1)}, bf16[272,1024]{1,0:T(8,128)(2,1)S(1)}, u32[]{:S(2)}, u32[]{:S(2)}) %collective-permute-start.7) | collective-permute-done | bytes 557088 | tf_op jit(solution)/shard_map/ppermute | solution.py:355
  27.3 3.7 %collective-permute-start.8 = (bf16[272,1024]{1,0:T(8,128)(2,1)S(1)}, bf16[272,1024]{1,0:T(8,128)(2,1)S(1)}, u32[]{:S(2)}, u32[]{:S(2)}) collective-permute-start(bf16[272,1024]{1,0:T(8,128)(2,1)S(1)} %collective-permute-done.7.refs_1_), channel_id=1, source_target_pairs={{1,0},{2,1},{3,2},{4,3},{5,4},{6,5},{7,6},{0,7},{15,8},{8,9},{9,10... | collective-permute-start | bytes 1671176 | tf_op jit(solution)/shard_map/ppermute | solution.py:355
  31.8 1.3 collective-permute-start.5
  33.0 10.0 %collective-permute-done.10.refs_5_.refs_7_ = bf16[272,1024]{1,0:T(8,128)(2,1)S(1)} collective-permute-done((bf16[272,1024]{1,0:T(8,128)(2,1)S(1)}, bf16[272,1024]{1,0:T(8,128)(2,1)S(1)}, u32[]{:S(2)}, u32[]{:S(2)}) %collective-permute-start.10) | collective-permute-done | bytes 557088 | tf_op jit(solution)/shard_map/ppermute | solution.py:353
  43.1 1.0 collective-permute-done.8.refs_2_
  44.1 3.7 %collective-permute-start.9 = (bf16[272,1024]{1,0:T(8,128)(2,1)S(1)}, bf16[272,1024]{1,0:T(8,128)(2,1)S(1)}, u32[]{:S(2)}, u32[]{:S(2)}) collective-permute-start(bf16[272,1024]{1,0:T(8,128)(2,1)S(1)} %collective-permute-done.8.refs_2_), channel_id=1, source_target_pairs={{1,0},{2,1},{3,2},{4,3},{5,4},{6,5},{7,6},{0,7},{15,8},{8,9},{9,10... | collective-permute-start | bytes 1671176 | tf_op jit(solution)/shard_map/ppermute | solution.py:355
  47.8 7.5 %collective-permute-done.2.refs_2_ = bf16[256,1024]{1,0:T(8,128)(2,1)S(1)} collective-permute-done((bf16[256,1024]{1,0:T(8,128)(2,1)S(1)}, bf16[256,1024]{1,0:T(8,128)(2,1)S(1)}, u32[]{:S(2)}, u32[]{:S(2)}) %collective-permute-start.2) | collective-permute-done | bytes 524320 | tf_op jit(solution)/shard_map/ppermute | solution.py:355
  55.3 3.7 %collective-permute-start.3 = (bf16[256,1024]{1,0:T(8,128)(2,1)S(1)}, bf16[256,1024]{1,0:T(8,128)(2,1)S(1)}, u32[]{:S(2)}, u32[]{:S(2)}) collective-permute-start(bf16[256,1024]{1,0:T(8,128)(2,1)S(1)} %collective-permute-done.2.refs_2_), channel_id=1, source_target_pairs={{1,0},{2,1},{3,2},{4,3},{5,4},{6,5},{7,6},{0,7},{15,8},{8,9},{9,10... | collective-permute-start | bytes 1572872 | tf_op jit(solution)/shard_map/ppermute | solution.py:355
  59.0 7.2 %collective-permute-done.11.refs_4_.refs_6_ = bf16[272,1024]{1,0:T(8,128)(2,1)S(1)} collective-permute-done((bf16[272,1024]{1,0:T(8,128)(2,1)S(1)}, bf16[272,1024]{1,0:T(8,128)(2,1)S(1)}, u32[]{:S(2)}, u32[]{:S(2)}) %collective-permute-start.11) | collective-permute-done | bytes 557088 | tf_op jit(solution)/shard_map/ppermute | solution.py:353
  66.2 1.0 collective-permute-done.9.refs_3_
  67.3 3.7 %collective-permute-start.12 = (bf16[272,1024]{1,0:T(8,128)(2,1)S(1)}, bf16[272,1024]{1,0:T(8,128)(2,1)S(1)}, u32[]{:S(2)}, u32[]{:S(2)}) collective-permute-start(bf16[272,1024]{1,0:T(8,128)(2,1)S(1)} %collective-permute-done.9.refs_3_), channel_id=1, source_target_pairs={{1,0},{2,1},{3,2},{4,3},{5,4},{6,5},{7,6},{0,7},{15,8},{8,9},{9,10... | collective-permute-start | bytes 1671176 | tf_op jit(solution)/shard_map/ppermute | solution.py:355
  71.0 7.5 %collective-permute-done.3.refs_3_ = bf16[256,1024]{1,0:T(8,128)(2,1)S(1)} collective-permute-done((bf16[256,1024]{1,0:T(8,128)(2,1)S(1)}, bf16[256,1024]{1,0:T(8,128)(2,1)S(1)}, u32[]{:S(2)}, u32[]{:S(2)}) %collective-permute-start.3) | collective-permute-done | bytes 524320 | tf_op jit(solution)/shard_map/ppermute | solution.py:355
  78.5 2.9 %shard_map.74 = (bf16[1024,1024]{1,0:T(8,128)(2,1)S(1)}, bf16[128,1024]{1,0:T(8,128)(2,1)S(1)}, bf16[1024,1024]{1,0:T(8,128)(2,1)S(1)}) custom-call(bf16[256,1024]{1,0:T(8,128)(2,1)S(1)} %bitcast.4, bf16[256,1024]{1,0:T(8,128)(2,1)S(1)} %collective-permute-done.refs_1_, bf16[256,1024]{1,0:T(8,128)(2,1)S(1)} %collective-permute-done.2.refs_2_, ...), custom_call_target="tpu_custom_call" | custom-call | flops 2147483648 | bytes 6291456 | tf_op jit(solution)/shard_map/pallas_call | solution.py:388
  81.4 2.2 %shard_map.75 = (bf16[1024,1024]{1,0:T(8,128)(2,1)S(1)}, bf16[1024,1024]{1,0:T(8,128)(2,1)S(1)}, bf16[1024,1024]{1,0:T(8,128)(2,1)S(1)}) custom-call(bf16[1024,1024]{1,0:T(8,128)(2,1)S(1)} %get-tuple-element.46.two_ref, bf16[272,1024]{1,0:T(8,128)(2,1)S(1)} %shard_map.73.refs_0_, bf16[272,1024]{1,0:T(8,128)(2,1)S(1)} %collective-permute-done.7.refs_1_, ...), custom_call_target="tpu_custom_call" | custom-call | flops 2147483648 | bytes 6291456 | tf_op jit(solution)/shard_map/pallas_call | solution.py:393
  83.6 5.8 %collective-permute-done.13.refs_5_ = bf16[272,1024]{1,0:T(8,128)(2,1)S(1)} collective-permute-done((bf16[272,1024]{1,0:T(8,128)(2,1)S(1)}, bf16[272,1024]{1,0:T(8,128)(2,1)S(1)}, u32[]{:S(2)}, u32[]{:S(2)}) %collective-permute-start.13) | collective-permute-done | bytes 557088 | tf_op jit(solution)/shard_map/ppermute | solution.py:353
  89.4 3.5 %shard_map.76 = (bf16[1024,1024]{1,0:T(8,128)(2,1)S(1)}, bf16[128,1024]{1,0:T(8,128)(2,1)S(1)}, bf16[128,1024]{1,0:T(8,128)(2,1)S(1)}, bf16[1024,1024]{1,0:T(8,1...) custom-call(bf16[1024,1024]{1,0:T(8,128)(2,1)S(1)} %get-tuple-elemen, ...), custom_call_target="tpu_custom_call", output_to_operand_aliasing={{3}: (1, {}), {4}: (2, {}), {5}: (3, {})} | custom-call | flops 2147483648 | bytes 6291456 | tf_op jit(solution)/shard_map/pallas_call | solution.py:397
  92.9 1.4 collective-permute-start.14
  94.3 1.8 %shard_map.78 = (f32[4,1024]{1,0:T(4,128)S(1)}, bf16[16,1024]{1,0:T(8,128)(2,1)S(1)}) custom-call(f32[16,1024]{1,0:T(8,128)S(1)} %get-tuple-element.53.drive_ref, bf16[1024,1024]{1,0:T(8,128)(2,1)S(1)} %get-tuple-element.54.second_ref, bf16[1024,1024]{1,0:T(8,128)(2,1)S(1)} %get-tuple-element.55.third_ref, bf16[1024,1024]{1,0:T(8,128)(2,1)S(1)} %get-tuple-element.51.fourth_ref), custom_call_target="tpu_custom_call" | custom-call | flops 100663296 | bytes 6291456 | tf_op jit(solution)/shard_map/pallas_call | solution.py:407
  96.1 1.3 collective-permute-start.15
  97.4 0.8 collective-permute-done.15.other_term_ref
  98.2 0.8 collective-permute-start.24
  99.3 0.7 collective-permute-start.25
  109.0 1.3 collective-permute-start.30
  110.3 35.1 %collective-permute-done.30.got_ref = f32[1,1024]{1,0:T(1,128)S(1)} collective-permute-done((f32[1,1024]{1,0:T(1,128)S(1)}, f32[1,1024]{1,0:T(1,128)S(1)}, u32[]{:S(2)}, u32[]{:S(2)}) %collective-permute-start.30) | collective-permute-done | bytes 4128 | tf_op jit(solution)/shard_map/ppermute | solution.py:459
  145.4 0.8 shard_map.96
  (68 shorter events, 10.0 us)
Async XLA Ops:
  0.0 7.5 %copy-start.2 = (s32[4,32]{1,0:T(4,128)S(1)}, s32[4,32]{1,0:T(4,128)}, u32[]{:S(2)}) copy-start(s32[4,32]{1,0:T(4,128)} %rows_ref.1) | copy-start | bytes 1540
  1.5 16.8 %collective-permute-start.1 = (bf16[256,1024]{1,0:T(8,128)(2,1)S(1)}, bf16[256,1024]{1,0:T(8,128)(2,1)S(1)}, u32[]{:S(2)}, u32[]{:S(2)}) collective-permute-start(bf16[256,1024]{1,0:T(8,128)(2,1)S(1)} %bitcast.2), channel_id=1, source_target_pairs={{0,1},{1,2},{2,3},{3,4},{4,5},{5,6},{6,7},{7,0},{8,15},{9,8},{10,9... | collective-permute-start | bytes 1572872 | tf_op jit(solution)/shard_map/ppermute | solution.py:353
  3.4 15.1 %collective-permute-start = (bf16[256,1024]{1,0:T(8,128)(2,1)S(1)}, bf16[256,1024]{1,0:T(8,128)(2,1)S(1)}, u32[]{:S(2)}, u32[]{:S(2)}) collective-permute-start(bf16[256,1024]{1,0:T(8,128)(2,1)S(1)} %bitcast.3), channel_id=1, source_target_pairs={{1,0},{2,1},{3,2},{4,3},{5,4},{6,5},{7,6},{0,7},{15,8},{8,9},{9,10... | collective-permute-start | bytes 1572872 | tf_op jit(solution)/shard_map/ppermute | solution.py:355
  9.1 18.2 %collective-permute-start.7 = (bf16[272,1024]{1,0:T(8,128)(2,1)S(1)}, bf16[272,1024]{1,0:T(8,128)(2,1)S(1)}, u32[]{:S(2)}, u32[]{:S(2)}) collective-permute-start(bf16[272,1024]{1,0:T(8,128)(2,1)S(1)} %shard_map.73.refs_0_), channel_id=1, source_target_pairs={{1,0},{2,1},{3,2},{4,3},{5,4},{6,5},{7,6},{0,7},{15,8},{8,9},{9,10... | collective-permute-start | bytes 1671176 | tf_op jit(solution)/shard_map/ppermute | solution.py:355
  18.6 13.2 %collective-permute-start.4 = (bf16[256,1024]{1,0:T(8,128)(2,1)S(1)}, bf16[256,1024]{1,0:T(8,128)(2,1)S(1)}, u32[]{:S(2)}, u32[]{:S(2)}) collective-permute-start(bf16[256,1024]{1,0:T(8,128)(2,1)S(1)} %collective-permute-done.1.refs_7_), channel_id=1, source_target_pairs={{0,1},{1,2},{2,3},{3,4},{4,5},{5,6},{6,7},{7,0},{8,15},{9,8},{10,9... | collective-permute-start | bytes 1572872 | tf_op jit(solution)/shard_map/ppermute | solution.py:353
  18.6 24.5 %collective-permute-start.10 = (bf16[272,1024]{1,0:T(8,128)(2,1)S(1)}, bf16[272,1024]{1,0:T(8,128)(2,1)S(1)}, u32[]{:S(2)}, u32[]{:S(2)}) collective-permute-start(bf16[272,1024]{1,0:T(8,128)(2,1)S(1)} %shard_map.73.refs_0_), channel_id=1, source_target_pairs={{0,1},{1,2},{2,3},{3,4},{4,5},{5,6},{6,7},{7,0},{8,15},{9,8},{10,9... | collective-permute-start | bytes 1671176 | tf_op jit(solution)/shard_map/ppermute | solution.py:353
  27.3 16.8 %collective-permute-start.8 = (bf16[272,1024]{1,0:T(8,128)(2,1)S(1)}, bf16[272,1024]{1,0:T(8,128)(2,1)S(1)}, u32[]{:S(2)}, u32[]{:S(2)}) collective-permute-start(bf16[272,1024]{1,0:T(8,128)(2,1)S(1)} %collective-permute-done.7.refs_1_), channel_id=1, source_target_pairs={{1,0},{2,1},{3,2},{4,3},{5,4},{6,5},{7,6},{0,7},{15,8},{8,9},{9,10... | collective-permute-start | bytes 1671176 | tf_op jit(solution)/shard_map/ppermute | solution.py:355
  31.0 24.3 %collective-permute-start.2 = (bf16[256,1024]{1,0:T(8,128)(2,1)S(1)}, bf16[256,1024]{1,0:T(8,128)(2,1)S(1)}, u32[]{:S(2)}, u32[]{:S(2)}) collective-permute-start(bf16[256,1024]{1,0:T(8,128)(2,1)S(1)} %collective-permute-done.refs_1_), channel_id=1, source_target_pairs={{1,0},{2,1},{3,2},{4,3},{5,4},{6,5},{7,6},{0,7},{15,8},{8,9},{9,10... | collective-permute-start | bytes 1572872 | tf_op jit(solution)/shard_map/ppermute | solution.py:355
  31.8 27.3 %collective-permute-start.5 = (bf16[256,1024]{1,0:T(8,128)(2,1)S(1)}, bf16[256,1024]{1,0:T(8,128)(2,1)S(1)}, u32[]{:S(2)}, u32[]{:S(2)}) collective-permute-start(bf16[256,1024]{1,0:T(8,128)(2,1)S(1)} %collective-permute-done.4.refs_6_), channel_id=1, source_target_pairs={{0,1},{1,2},{2,3},{3,4},{4,5},{5,6},{6,7},{7,0},{8,15},{9,8},{10,9... | collective-permute-start | bytes 1572872 | tf_op jit(solution)/shard_map/ppermute | solution.py:353
  43.1 23.2 %collective-permute-start.11 = (bf16[272,1024]{1,0:T(8,128)(2,1)S(1)}, bf16[272,1024]{1,0:T(8,128)(2,1)S(1)}, u32[]{:S(2)}, u32[]{:S(2)}) collective-permute-start(bf16[272,1024]{1,0:T(8,128)(2,1)S(1)} %collective-permute-done.10.refs_5_.refs_7_), channel_id=1, source_target_pairs={{0,1},{1,2},{2,3},{3,4},{4,5},{5,6},{6,7},{7,0},{8,15},{9,8},{10,9... | collective-permute-start | bytes 1671176 | tf_op jit(solution)/shard_map/ppermute | solution.py:353
  44.1 23.2 %collective-permute-start.9 = (bf16[272,1024]{1,0:T(8,128)(2,1)S(1)}, bf16[272,1024]{1,0:T(8,128)(2,1)S(1)}, u32[]{:S(2)}, u32[]{:S(2)}) collective-permute-start(bf16[272,1024]{1,0:T(8,128)(2,1)S(1)} %collective-permute-done.8.refs_2_), channel_id=1, source_target_pairs={{1,0},{2,1},{3,2},{4,3},{5,4},{6,5},{7,6},{0,7},{15,8},{8,9},{9,10... | collective-permute-start | bytes 1671176 | tf_op jit(solution)/shard_map/ppermute | solution.py:355
  55.3 23.2 %collective-permute-start.3 = (bf16[256,1024]{1,0:T(8,128)(2,1)S(1)}, bf16[256,1024]{1,0:T(8,128)(2,1)S(1)}, u32[]{:S(2)}, u32[]{:S(2)}) collective-permute-start(bf16[256,1024]{1,0:T(8,128)(2,1)S(1)} %collective-permute-done.2.refs_2_), channel_id=1, source_target_pairs={{1,0},{2,1},{3,2},{4,3},{5,4},{6,5},{7,6},{0,7},{15,8},{8,9},{9,10... | collective-permute-start | bytes 1572872 | tf_op jit(solution)/shard_map/ppermute | solution.py:355
  59.0 19.5 %collective-permute-start.6 = (bf16[256,1024]{1,0:T(8,128)(2,1)S(1)}, bf16[256,1024]{1,0:T(8,128)(2,1)S(1)}, u32[]{:S(2)}, u32[]{:S(2)}) collective-permute-start(bf16[256,1024]{1,0:T(8,128)(2,1)S(1)} %collective-permute-done.5.refs_5_), channel_id=1, source_target_pairs={{0,1},{1,2},{2,3},{3,4},{4,5},{5,6},{6,7},{7,0},{8,15},{9,8},{10,9... | collective-permute-start | bytes 1572872 | tf_op jit(solution)/shard_map/ppermute | solution.py:353
  66.2 23.2 %collective-permute-start.13 = (bf16[272,1024]{1,0:T(8,128)(2,1)S(1)}, bf16[272,1024]{1,0:T(8,128)(2,1)S(1)}, u32[]{:S(2)}, u32[]{:S(2)}) collective-permute-start(bf16[272,1024]{1,0:T(8,128)(2,1)S(1)} %collective-permute-done.11.refs_4_.refs_6_), channel_id=1, source_target_pairs={{0,1},{1,2},{2,3},{3,4},{4,5},{5,6},{6,7},{7,0},{8,15},{9,8},{10,9... | collective-permute-start | bytes 1671176 | tf_op jit(solution)/shard_map/ppermute | solution.py:353
  67.3 22.1 %collective-permute-start.12 = (bf16[272,1024]{1,0:T(8,128)(2,1)S(1)}, bf16[272,1024]{1,0:T(8,128)(2,1)S(1)}, u32[]{:S(2)}, u32[]{:S(2)}) collective-permute-start(bf16[272,1024]{1,0:T(8,128)(2,1)S(1)} %collective-permute-done.9.refs_3_), channel_id=1, source_target_pairs={{1,0},{2,1},{3,2},{4,3},{5,4},{6,5},{7,6},{0,7},{15,8},{8,9},{9,10... | collective-permute-start | bytes 1671176 | tf_op jit(solution)/shard_map/ppermute | solution.py:355
  92.9 5.3 %collective-permute-start.14 = (bf16[1024,1024]{1,0:T(8,128)(2,1)S(1)}, bf16[1024,1024]{1,0:T(8,128)(2,1)S(1)}, u32[]{:S(2)}, u32[]{:S(2)}) collective-permute-start(bf16[1024,1024]{1,0:T(8,128)(2,1)S(1)} %get-tuple-element.57), channel_id=1, source_target_pairs={{0,8},{16,24},{32,40},{48,56},{64,72},{80,88},{96,104},{112,120},{... | collective-permute-start | bytes 6291464 | tf_op jit(solution)/shard_map/ppermute | solution.py:405
  96.1 2.1 %collective-permute-start.15 = (bf16[16,1024]{1,0:T(8,128)(2,1)S(1)}, bf16[16,1024]{1,0:T(8,128)(2,1)S(1)}, u32[]{:S(2)}, u32[]{:S(2)}) collective-permute-start(bf16[16,1024]{1,0:T(8,128)(2,1)S(1)} %get-tuple-element.56.own_term_ref), channel_id=1, source_target_pairs={{0,8},{16,24},{32,40},{48,56},{64,72},{80,88},{96,104},{112,120},{... | collective-permute-start | bytes 98312 | tf_op jit(solution)/shard_map/ppermute | solution.py:410
  98.2 7.9 %collective-permute-start.24 = (bf16[512,1024]{1,0:T(8,128)(2,1)S(1)}, bf16[512,1024]{1,0:T(8,128)(2,1)S(1)}, u32[]{:S(2)}, u32[]{:S(2)}) collective-permute-start(bf16[512,1024]{1,0:T(8,128)(2,1)S(1)} %shard_map.82.turned0_ref), channel_id=1, source_target_pairs={{136,152},{168,184},{200,216},{232,248},{137,153},{169,185},{201,2... | collective-permute-start | bytes 3145736 | tf_op jit(solution)/shard_map/ppermute | solution.py:420
  99.3 6.8 %collective-permute-start.25 = (bf16[528,1024]{1,0:T(8,128)(2,1)S(1)}, bf16[528,1024]{1,0:T(8,128)(2,1)S(1)}, u32[]{:S(2)}, u32[]{:S(2)}) collective-permute-start(bf16[528,1024]{1,0:T(8,128)(2,1)S(1)} %shard_map.79.turned1_ref), channel_id=1, source_target_pairs={{136,152},{168,184},{200,216},{232,248},{137,153},{169,185},{201,2... | collective-permute-start | bytes 3244040 | tf_op jit(solution)/shard_map/ppermute | solution.py:422
  100.1 0.7 collective-permute-start.16
  100.8 0.7 collective-permute-start.17
  101.5 0.7 collective-permute-start.18
  102.2 0.7 collective-permute-start.19
  102.9 1.0 collective-permute-start.20
  104.0 0.7 collective-permute-start.21
  104.7 0.7 collective-permute-start.22
  105.4 0.8 collective-permute-start.23
  106.2 0.7 collective-permute-start.26
  106.9 0.7 collective-permute-start.27
  107.6 1.3 collective-permute-start.29
  108.3 0.7 collective-permute-start.28
  109.0 36.4 %collective-permute-start.30 = (f32[1,1024]{1,0:T(1,128)S(1)}, f32[1,1024]{1,0:T(1,128)S(1)}, u32[]{:S(2)}, u32[]{:S(2)}) collective-permute-start(f32[1,1024]{1,0:T(1,128)S(1)} %shard_map.95.begin_ref), channel_id=1, source_target_pairs={{8,0},{24,16},{40,32},{56,48},{72,64},{88,80},{104,96},{120,112},{... | collective-permute-start | bytes 12296 | tf_op jit(solution)/shard_map/ppermute | solution.py:459
  (5 other events, 31.8 us)
